TPU v7x, 512 devices: a whole 4x8x8 slice. The times are simulated.
512 devices in a mesh: dp: 64 (over z, x, core), tensor: 8 (over y).
Axes of the slice: x: 4, y: 8, z: 8, core: 2. Of those that a mesh axis runs over, the one named last changes fastest.
Arguments:
- hidden: bfloat16 [8192, 4096], P('dp', 'tensor'), may hold values from -6 to 6
- gain: bfloat16 [4096], P('tensor'), may hold values from 0.5 to 1.5
- w_query: bfloat16 [4096, 4096], P('dp', 'tensor'), may hold values from -0.09375 to 0.09375
- w_key: bfloat16 [4096, 1024], P('dp', 'tensor'), may hold values from -0.09375 to 0.09375
- w_value: bfloat16 [4096, 1024], P('dp', 'tensor'), may hold values from -0.09375 to 0.09375
- cotangent: bfloat16 [16384, 4096], P('dp', 'tensor'), may hold values from -6 to 6
- seq_length: int32 [64, 4], replicated, may hold values from 16 to 64, as said below
- home_offset: int32 [64, 4], replicated, may hold values from 0 to 112, as said below
- dest_shard: int32 [64, 4], replicated, may hold values from 0 to 63, as said below
- dest_offset: int32 [64, 4], replicated, may hold values from 0 to 192, as said below
Outputs:
- attention_output: bfloat16 [16384, 4096], P('dp', 'tensor')
- grad_hidden: bfloat16 [8192, 4096], P('dp', 'tensor')
- grad_value_weight: float32 [4096, 1024], P('dp', 'tensor')
Inputs may be any that keep to these rules, and one draw needn't show every extreme that they name: `seq_length`: the 4 sequences of a shard fill its 128 rows exactly; every length is at least 16 and at most 64, and some sequence has length 64. `home_offset`: the sequences of a shard lie back to back from row 0 in the order of c. `dest_shard`: sequence c of shard h goes to shard (h + e) mod 64, e one of -1, 1, 32 and 33; every shard sends exactly one sequence to each of these 4 shards. `dest_offset`: the sequences that arrive at a shard lie back to back from row 0 of its 256 rows, in the order e = -1, 1, 32, 33; at some shard they fill all 256 rows.
All inputs are finite; a program needn't handle non-finite values.
Results may differ from a plain program's by a relative error of at most 0.02.
Values may be sent and summed in bfloat16 or wider, within the bound.
No kernel may reach another device: no remote copies, remote signals or barrier semaphores. Data moves between devices by JAX's collectives and lax.ppermute only.
A program may use at most 64 MiB of HBM per device.

v0:
```python
import jax
import jax.numpy as jnp
from jax import lax
from jax.sharding import PartitionSpec as P

D = 4096
HEAD = 128
TOK_DEV = 128
MAXLEN = 64
CAP = 256


EPSILON = 1e-05
ROPE_BASE = 500000.0


def passed_along(value, axis, by):
    size = lax.axis_size(axis)
    return lax.ppermute(value, axis, [(i, (i + by) % size) for i in range(size)])


def rope_tables(position):
    half_head = HEAD // 2
    exponent = jnp.arange(half_head, dtype=jnp.float32) * (2.0 / HEAD)
    inverse = jnp.power(jnp.float32(ROPE_BASE), -exponent)
    angles = position.astype(jnp.float32)[:, None] * inverse[None, :]
    return (jnp.cos(angles)[:, None, :], jnp.sin(angles)[:, None, :])


def rotate(values, cosine, sine_part):
    half_head = values.shape[-1] // 2
    lower_half = values[..., :half_head]
    upper_half = values[..., half_head:]
    return jnp.concatenate(
        [
            lower_half * cosine - upper_half * sine_part,
            upper_half * cosine + lower_half * sine_part,
        ],
        -1,
    )


def unrotate(values, cosine, sine_part):
    half_head = values.shape[-1] // 2
    lower_half = values[..., :half_head]
    upper_half = values[..., half_head:]
    return jnp.concatenate(
        [
            lower_half * cosine + upper_half * sine_part,
            upper_half * cosine - lower_half * sine_part,
        ],
        -1,
    )


def attention_block(normed, w_query, w_key, w_value, cotangent, segment, position, occupied):
    row_count = normed.shape[0]
    kv_heads = w_key.shape[1] // HEAD
    q_heads = w_query.shape[1] // HEAD
    group_size = q_heads // kv_heads
    cosine, sine_part = rope_tables(position)
    query_rows = jnp.dot(normed, w_query, preferred_element_type=jnp.float32).reshape(
        row_count, q_heads, HEAD
    )
    key_rows = jnp.dot(normed, w_key, preferred_element_type=jnp.float32).reshape(
        row_count, kv_heads, HEAD
    )
    value_rows = (
        jnp.dot(normed, w_value, preferred_element_type=jnp.float32)
        .astype(jnp.bfloat16)
        .reshape(row_count, kv_heads, HEAD)
    )
    query_rows = (
        rotate(query_rows, cosine, sine_part)
        .astype(jnp.bfloat16)
        .reshape(row_count, kv_heads, group_size, HEAD)
    )
    key_rows = rotate(key_rows, cosine, sine_part).astype(jnp.bfloat16)
    factor = HEAD ** (-0.5)
    scores = (
        jnp.einsum("qhgd,khd->hgqk", query_rows, key_rows, preferred_element_type=jnp.float32)
        * factor
    )
    allowed = (segment[:, None] == segment[None, :]) & (position[None, :] <= position[:, None])
    scores = jnp.where(allowed[None, None], scores, jnp.float32(-1e30))
    row_max = jnp.max(scores, -1, keepdims=True)
    exp_terms = jnp.exp(scores - row_max)
    attn_prob = exp_terms / jnp.sum(exp_terms, -1, keepdims=True)
    prob_low = attn_prob.astype(jnp.bfloat16)
    mixed_rows = jnp.einsum(
        "hgqk,khd->qhgd", prob_low, value_rows, preferred_element_type=jnp.float32
    )
    attn_out = jnp.where(
        occupied[:, None], mixed_rows.reshape(row_count, q_heads * HEAD), jnp.float32(0.0)
    ).astype(jnp.bfloat16)
    grad_out = jnp.where(occupied[:, None], cotangent, jnp.zeros((), jnp.bfloat16)).reshape(
        row_count, kv_heads, group_size, HEAD
    )
    grad_value = jnp.einsum(
        "hgqk,qhgd->khd", prob_low, grad_out, preferred_element_type=jnp.float32
    ).astype(jnp.bfloat16)
    grad_probs = jnp.einsum(
        "qhgd,khd->hgqk", grad_out, value_rows, preferred_element_type=jnp.float32
    )
    centre = jnp.sum(grad_probs * attn_prob, -1, keepdims=True)
    grad_scores = (attn_prob * (grad_probs - centre) * factor).astype(jnp.bfloat16)
    grad_query = jnp.einsum(
        "hgqk,khd->qhgd", grad_scores, key_rows, preferred_element_type=jnp.float32
    ).reshape(row_count, q_heads, HEAD)
    grad_key = jnp.einsum(
        "hgqk,qhgd->khd", grad_scores, query_rows, preferred_element_type=jnp.float32
    )
    grad_query = (
        unrotate(grad_query, cosine, sine_part)
        .astype(jnp.bfloat16)
        .reshape(row_count, q_heads * HEAD)
    )
    grad_key = (
        unrotate(grad_key, cosine, sine_part)
        .astype(jnp.bfloat16)
        .reshape(row_count, kv_heads * HEAD)
    )
    return (attn_out, grad_query, grad_key, grad_value.reshape(row_count, kv_heads * HEAD))


def cut_blocks(matrix, starts, lengths):
    within = jnp.arange(MAXLEN, dtype=jnp.int32)
    picks = jnp.minimum(starts[:, None] + within[None, :], matrix.shape[0] - 1)
    in_seq = within[None, :] < lengths[:, None]
    return jnp.where(in_seq[:, :, None], matrix[picks], jnp.zeros((), matrix.dtype))


def on_device(
    hidden,
    gain,
    w_query,
    w_key,
    w_value,
    cotangent,
    seq_length,
    home_offset,
    dest_shard,
    dest_offset,
):
    shards = lax.axis_size("dp")
    my_shard = lax.axis_index("dp")
    width_here = hidden.shape[1]
    shift_list = [-1, 1, shards // 2, shards // 2 + 1]
    stride_array = jnp.array(shift_list, dtype=jnp.int32)
    stride_mod = jnp.array([stride % shards for stride in shift_list], dtype=jnp.int32)
    slot_count = len(shift_list)
    slot_index = jnp.arange(slot_count, dtype=jnp.int32)[:, None]
    wq_full, wk_full, wv_full = (
        lax.all_gather(w_query, "dp", axis=0, tiled=True),
        lax.all_gather(w_key, "dp", axis=0, tiled=True),
        lax.all_gather(w_value, "dp", axis=0, tiled=True),
    )
    own_len = seq_length[my_shard]
    own_off = home_offset[my_shard]
    own_move = (dest_shard[my_shard] - my_shard + shards) % shards
    chosen = (own_move[None, :] == stride_mod[:, None]).astype(jnp.int32)
    outgoing = cut_blocks(
        hidden, jnp.sum(chosen * own_off[None, :], 1), jnp.sum(chosen * own_len[None, :], 1)
    )
    buffers = jnp.zeros((shards, MAXLEN, width_here), hidden.dtype)
    for number, stride in enumerate(shift_list):
        buffers = lax.dynamic_update_slice_in_dim(
            buffers, outgoing[number][None], (my_shard + stride + shards) % shards, 0
        )
    received = lax.all_to_all(buffers, "dp", split_axis=0, concat_axis=0, tiled=True)
    arrived = jnp.stack(
        [
            lax.dynamic_index_in_dim(
                received, (my_shard - stride + shards) % shards, 0, keepdims=False
            )
            for stride in shift_list
        ]
    )
    sources = (my_shard - stride_array + shards) % shards
    source_move = (dest_shard[sources] - sources[:, None] + shards) % shards
    matches = (source_move == stride_mod[:, None]).astype(jnp.int32)
    in_len = jnp.sum(matches * seq_length[sources], 1)
    in_start = jnp.sum(matches * dest_offset[sources], 1)
    dest_slot = jnp.arange(CAP, dtype=jnp.int32)
    member = (
        (dest_slot[None, :] >= in_start[:, None])
        & (dest_slot[None, :] < (in_start + in_len)[:, None])
    ).astype(jnp.int32)
    occupied = jnp.sum(member, 0) > 0
    segment = jnp.where(occupied, jnp.sum(member * slot_index, 0), -1)
    position = jnp.sum(member * (dest_slot[None, :] - in_start[:, None]), 0)
    fetch_rows = jnp.sum(member * (slot_index * MAXLEN + dest_slot[None, :] - in_start[:, None]), 0)
    local_rows = jnp.where(
        occupied[:, None], arrived.reshape(-1, width_here)[fetch_rows], jnp.zeros((), hidden.dtype)
    )
    full_rows, gain_full = (
        lax.all_gather(local_rows, "tensor", axis=1, tiled=True),
        lax.all_gather(gain, "tensor", axis=0, tiled=True),
    )
    values = full_rows.astype(jnp.float32)
    inverse_rms = lax.rsqrt(jnp.mean(values * values, 1, keepdims=True) + EPSILON)
    normed = (values * inverse_rms * gain_full.astype(jnp.float32)).astype(jnp.bfloat16)
    attn_out, grad_query, grad_key, grad_value = attention_block(
        normed, wq_full, wk_full, wv_full, cotangent, segment, position, occupied
    )
    partial_value = jnp.einsum("rc,dc->rd", grad_query, wq_full, preferred_element_type=jnp.float32)
    partial_value = partial_value + jnp.einsum(
        "rc,dc->rd", grad_key, wk_full, preferred_element_type=jnp.float32
    )
    partial_value = partial_value + jnp.einsum(
        "rc,dc->rd", grad_value, wv_full, preferred_element_type=jnp.float32
    )
    grad_value_weight = lax.psum_scatter(
        jnp.einsum("rd,rc->dc", normed, grad_value, preferred_element_type=jnp.float32),
        "dp",
        scatter_dimension=0,
        tiled=True,
    )
    slot_of_seq = jnp.sum(chosen * slot_index, 0)
    home_slot = jnp.arange(TOK_DEV, dtype=jnp.int32)
    belong = (
        (home_slot[None, :] >= own_off[:, None])
        & (home_slot[None, :] < (own_off + own_len)[:, None])
    ).astype(jnp.int32)
    gather_back = jnp.sum(
        belong * (slot_of_seq[:, None] * MAXLEN + home_slot[None, :] - own_off[:, None]), 0
    )
    gain_here = gain.astype(jnp.float32)
    summed = lax.psum_scatter(
        partial_value.astype(jnp.bfloat16), "tensor", scatter_dimension=1, tiled=True
    ).astype(jnp.float32)
    weighted = summed * gain_here
    local_vals = local_rows.astype(jnp.float32)
    row_dot = lax.psum(jnp.sum(weighted * local_vals, 1), "tensor")
    grad_rows = (
        inverse_rms * weighted - local_vals * inverse_rms**3 * row_dot[:, None] / D
    ).astype(jnp.bfloat16)
    sending = cut_blocks(grad_rows, in_start, in_len)
    returned = jnp.stack(
        [passed_along(sending[number], "dp", -stride) for number, stride in enumerate(shift_list)]
    )
    grad_hidden = returned.reshape(-1, width_here)[gather_back]
    return (attn_out, grad_hidden, grad_value_weight)


def solution(mesh):
    return jax.shard_map(
        on_device,
        mesh=mesh,
        in_specs=(
            P("dp", "tensor"),
            P("tensor"),
            P("dp", "tensor"),
            P("dp", "tensor"),
            P("dp", "tensor"),
            P("dp", "tensor"),
            P(),
            P(),
            P(),
            P(),
        ),
        out_specs=(P("dp", "tensor"), P("dp", "tensor"), P("dp", "tensor")),
        check_vma=False,
    )
```

profile of v0, /device:TPU:1, one launch (start us, length us, event | category | flops | bytes accessed | tf_op | source)
XLA Modules:
  0.0 648.3 jit_solution(5192040141124039154)
XLA Ops:
  18.8 2.5 broadcast_in_dim.62
  23.9 15.0 %all-to-all-start = ((bf16[64,64,512]{2,1,0:T(8,128)(2,1)}), bf16[64,64,512]{2,1,0:T(8,128)(2,1)}, u32[]{:S(2)}, u32[]{:S(2)}) async-start(bf16[64,64,512]{2,1,0:T(8,128)(2,1)} %slice_dynamic-update-slice_fusion), calls=%async_computation | async-start | bytes 8388608 | tf_op jit(solution)/shard_map/all_to_all | solution.py:170
  39.2 94.1 %all-to-all-done = bf16[64,64,512]{2,1,0:T(8,128)(2,1)} async-done(((bf16[64,64,512]{2,1,0:T(8,128)(2,1)}), bf16[64,64,512]{2,1,0:T(8,128)(2,1)}, u32[]{:S(2)}, u32[]{:S(2)}) %all-to-all-start) | async-done | bytes 4194336 | tf_op jit(solution)/shard_map/all_to_all | solution.py:170
  138.5 19.2 %all-gather = bf16[8,1,512]{2,1,0:T(2,128)(2,1)S(1)} all-gather(bf16[1,1,512]{2,1,0:T(2,128)(2,1)S(1)} %reshape.558), channel_id=1, replica_groups=mesh['dp'=64,'tensor'=8] {'tensor'}, dimensions={0}, use_global_device_ids=true | all-gather | bytes 9216 | tf_op jit(solution)/shard_map/all_gather | solution.py:198
  159.1 15.3 %all-gather.6.cloned.1.call-done = bf16[256,4096]{1,0:T(8,128)(2,1)} async-done(((bf16[256,512]{1,0:T(8,128)(2,1)}), bf16[256,4096]{1,0:T(8,128)(2,1)}) %all-gather.6.cloned.1.call-update) | async-done | bytes 2097168 | tf_op jit(solution)/shard_map/all_gather | solution.py:197
  174.3 2.1 fusion.1
  177.0 88.8 %all-gather.12.cloned.1.call-done = bf16[4096,512]{1,0:T(8,128)(2,1)} async-done(((bf16[64,512]{1,0:T(8,128)(2,1)}), bf16[4096,512]{1,0:T(8,128)(2,1)}) %all-gather.12.cloned.1.call-update) | async-done | bytes 4194320 | tf_op jit(solution)/shard_map/all_gather | solution.py:154
  265.8 5.1 fusion.69
  272.1 76.3 %all-gather.10.cloned.1.call-done = bf16[4096,128]{1,0:T(8,128)(2,1)} async-done(((bf16[64,128]{1,0:T(8,128)(2,1)}), bf16[4096,128]{1,0:T(8,128)(2,1)}) %all-gather.10.cloned.1.call-update) | async-done | bytes 1048592 | tf_op jit(solution)/shard_map/all_gather | solution.py:155
  348.5 2.2 convolution_bitcast_fusion.4
  354.1 77.3 %all-gather.8.cloned.1.call-done = bf16[4096,128]{1,0:T(8,128)(2,1)} async-done(((bf16[64,128]{1,0:T(8,128)(2,1)}), bf16[4096,128]{1,0:T(8,128)(2,1)}) %all-gather.8.cloned.1.call-update) | async-done | bytes 1048592 | tf_op jit(solution)/shard_map/all_gather | solution.py:156
  431.5 2.0 fusion.8
  436.4 2.0 broadcast_select_fusion
  440.2 2.0 fusion.7
  445.5 2.1 fusion.38
  449.0 2.0 fusion
  451.4 2.3 fusion.67
  454.0 34.5 %reduce-scatter.3.cloned.1.call-done = bf16[256,512]{1,0:T(8,128)(2,1)} async-done(((bf16[256,4096]{1,0:T(8,128)(2,1)}), bf16[256,512]{1,0:T(8,128)(2,1)}) %reduce-scatter.3.cloned.1.call-update) | async-done | bytes 262160 | tf_op jit(solution)/shard_map/reduce_scatter | solution.py:229
  489.7 11.8 %psum.7 = f32[256]{0:T(256)S(1)} all-reduce(f32[256]{0:T(256)S(1)} %fusion.15), channel_id=1, replica_groups=mesh['dp'=64,'tensor'=8] {'tensor'}, use_global_device_ids=true, to_apply=%region_14.15 | all-reduce | flops 256 | bytes 2048 | tf_op jit(solution)/shard_map/psum | solution.py:234
  504.0 11.5 %collective-permute-start = (bf16[64,512]{1,0:T(8,128)(2,1)S(1)}, bf16[64,512]{1,0:T(8,128)(2,1)S(1)}, u32[]{:S(2)}, u32[]{:S(2)}) collective-permute-start(bf16[64,512]{1,0:T(8,128)(2,1)S(1)} %get-tuple-element.26), channel_id=1, source_target_pairs={{0,8},{8,16},{16,24},{24,32},{32,40},{40,48},{48,56},{56,64},{64,7... | collective-permute-start | bytes 196616 | tf_op jit(solution)/shard_map/ppermute | solution.py:19
  517.4 7.7 %collective-permute-start.2 = (bf16[64,512]{1,0:T(8,128)(2,1)S(1)}, bf16[64,512]{1,0:T(8,128)(2,1)S(1)}, u32[]{:S(2)}, u32[]{:S(2)}) collective-permute-start(bf16[64,512]{1,0:T(8,128)(2,1)S(1)} %get-tuple-element.28), channel_id=1, source_target_pairs={{0,256},{8,264},{16,272},{24,280},{32,288},{40,296},{48,304},{56,3... | collective-permute-start | bytes 196616 | tf_op jit(solution)/shard_map/ppermute | solution.py:19
  525.1 5.8 collective-permute-start.3
  531.0 5.0 collective-permute-done.3
  537.5 104.0 %reduce-scatter.5.cloned.1.call-done = f32[64,128]{1,0:T(8,128)} async-done(((f32[4096,128]{1,0:T(8,128)}), f32[64,128]{1,0:T(8,128)}) %reduce-scatter.5.cloned.1.call-update) | async-done | bytes 32784 | tf_op jit(solution)/shard_map/reduce_scatter | solution.py:213
  (176 shorter events, 42.6 us)
Async XLA Ops:
  7.2 10.4 %copy-start = (bf16[128,512]{1,0:T(8,128)(2,1)S(1)}, bf16[128,512]{1,0:T(8,128)(2,1)}, u32[]{:S(2)}) copy-start(bf16[128,512]{1,0:T(8,128)(2,1)} %param.12) | copy-start | bytes 393220
  9.7 9.0 %copy-start.36 = (s32[4]{0:T(128)}, s32[4]{0:T(128)S(1)}, u32[]{:S(2)}) copy-start(s32[4]{0:T(128)S(1)} %fusion.52) | copy-start | bytes 52
  16.7 22.3 %copy-start.38 = (s32[4]{0:T(128)}, s32[4]{0:T(128)S(1)}, u32[]{:S(2)}) copy-start(s32[4]{0:T(128)S(1)} %get-tuple-element.10) | copy-start | bytes 52
  23.9 109.4 %all-to-all-start = ((bf16[64,64,512]{2,1,0:T(8,128)(2,1)}), bf16[64,64,512]{2,1,0:T(8,128)(2,1)}, u32[]{:S(2)}, u32[]{:S(2)}) async-start(bf16[64,64,512]{2,1,0:T(8,128)(2,1)} %slice_dynamic-update-slice_fusion), calls=%async_computation | async-start | bytes 8388608 | tf_op jit(solution)/shard_map/all_to_all | solution.py:170
  38.9 99.5 %copy-start.34 = (bf16[512]{0:T(512)(128)(2,1)S(1)}, bf16[512]{0:T(512)(128)(2,1)}, u32[]{:S(2)}) copy-start(bf16[512]{0:T(512)(128)(2,1)} %param.13) | copy-start | bytes 3076
  38.9 135.4 %all-gather.6.cloned.1.call-start = ((), (), s32[]{:S(2)}) async-start(), calls=%async_computation.3 | async-start | bytes 2359296 | tf_op jit(solution)/shard_map/all_gather | solution.py:197
  39.2 226.6 %copy-start.25 = (pred[256]{0:T(512)(128)(4,1)}, pred[256]{0:T(512)(128)(4,1)S(1)}, u32[]{:S(2)}) copy-start(pred[256]{0:T(512)(128)(4,1)S(1)} %get-tuple-element.13) | copy-start | bytes 772
  136.3 129.5 %all-gather.12.cloned.1.call-start = ((), (), s32[]{:S(2)}) async-start(), calls=%async_computation.6 | async-start | bytes 4259840 | tf_op jit(solution)/shard_map/all_gather | solution.py:154
  137.1 211.4 %all-gather.10.cloned.1.call-start = ((), (), s32[]{:S(2)}) async-start(), calls=%async_computation.5 | async-start | bytes 1064960 | tf_op jit(solution)/shard_map/all_gather | solution.py:155
  137.8 293.7 %all-gather.8.cloned.1.call-start = ((), (), s32[]{:S(2)}) async-start(), calls=%async_computation.4 | async-start | bytes 1064960 | tf_op jit(solution)/shard_map/all_gather | solution.py:156
  138.4 350.2 %reduce-scatter.3.cloned.1.call-start = ((), (), s32[]{:S(2)}) async-start(), calls=%async_computation.7 | async-start | bytes 2359296 | tf_op jit(solution)/shard_map/reduce_scatter | solution.py:229
  138.4 212.3 %copy-start.30 = (f32[64]{0:T(128)}, f32[64]{0:T(128)S(1)}, u32[]{:S(2)}) copy-start(f32[64]{0:T(128)S(1)} %negate_power_fusion) | copy-start | bytes 772
  157.7 193.0 %copy-start.24 = (f32[256]{0:T(256)}, f32[256]{0:T(256)S(1)}, u32[]{:S(2)}) copy-start(f32[256]{0:T(256)S(1)} %convert_element_type.81) | copy-start | bytes 3076
  159.0 192.4 %copy-start.7 = (f32[256,64]{1,0:T(8,128)}, f32[256,64]{1,0:T(8,128)S(1)}, u32[]{:S(2)}) copy-start(f32[256,64]{1,0:T(8,128)S(1)} %get-tuple-element.34) | copy-start | bytes 196612
  159.0 192.4 %copy-start.9 = (f32[256,64]{1,0:T(8,128)}, f32[256,64]{1,0:T(8,128)S(1)}, u32[]{:S(2)}) copy-start(f32[256,64]{1,0:T(8,128)S(1)} %get-tuple-element.35) | copy-start | bytes 196612
  177.0 171.5 %copy-start.27 = (f32[256]{0:T(256)}, f32[256]{0:T(256)S(1)}, u32[]{:S(2)}) copy-start(f32[256]{0:T(256)S(1)} %get-tuple-element.37) | copy-start | bytes 3076
  265.8 82.7 %copy-start.1 = (bf16[256,4096]{1,0:T(8,128)(2,1)S(1)}, bf16[256,4096]{1,0:T(8,128)(2,1)}, u32[]{:S(2)}) copy-start(bf16[256,4096]{1,0:T(8,128)(2,1)} %all-gather.6.cloned.1.call-done) | copy-start | bytes 6291460
  451.1 37.5 %copy-start.26 = (pred[256]{0:T(512)(128)(4,1)S(1)}, pred[256]{0:T(512)(128)(4,1)}, u32[]{:S(2)}) copy-start(pred[256]{0:T(512)(128)(4,1)} %copy-done.25) | copy-start | bytes 772
  451.1 50.5 %copy-start.33 = (f32[256]{0:T(256)S(1)}, f32[256]{0:T(256)}, u32[]{:S(2)}) copy-start(f32[256]{0:T(256)} %get-tuple-element.36) | copy-start | bytes 3076
  451.1 190.4 %reduce-scatter.5.cloned.1.call-start = ((), (), s32[]{:S(2)}) async-start(), calls=%async_computation.8 | async-start | bytes 2129920 | tf_op jit(solution)/shard_map/reduce_scatter | solution.py:213
  504.0 26.9 %collective-permute-start = (bf16[64,512]{1,0:T(8,128)(2,1)S(1)}, bf16[64,512]{1,0:T(8,128)(2,1)S(1)}, u32[]{:S(2)}, u32[]{:S(2)}) collective-permute-start(bf16[64,512]{1,0:T(8,128)(2,1)S(1)} %get-tuple-element.26), channel_id=1, source_target_pairs={{0,8},{8,16},{16,24},{24,32},{32,40},{40,48},{48,56},{56,64},{64,7... | collective-permute-start | bytes 196616 | tf_op jit(solution)/shard_map/ppermute | solution.py:19
  515.5 15.4 %collective-permute-start.1 = (bf16[64,512]{1,0:T(8,128)(2,1)S(1)}, bf16[64,512]{1,0:T(8,128)(2,1)S(1)}, u32[]{:S(2)}, u32[]{:S(2)}) collective-permute-start(bf16[64,512]{1,0:T(8,128)(2,1)S(1)} %get-tuple-element.29), channel_id=1, source_target_pairs={{0,504},{8,0},{16,8},{24,16},{32,24},{40,32},{48,40},{56,48},{64,5... | collective-permute-start | bytes 196616 | tf_op jit(solution)/shard_map/ppermute | solution.py:19
  517.4 13.5 %collective-permute-start.2 = (bf16[64,512]{1,0:T(8,128)(2,1)S(1)}, bf16[64,512]{1,0:T(8,128)(2,1)S(1)}, u32[]{:S(2)}, u32[]{:S(2)}) collective-permute-start(bf16[64,512]{1,0:T(8,128)(2,1)S(1)} %get-tuple-element.28), channel_id=1, source_target_pairs={{0,256},{8,264},{16,272},{24,280},{32,288},{40,296},{48,304},{56,3... | collective-permute-start | bytes 196616 | tf_op jit(solution)/shard_map/ppermute | solution.py:19
  525.1 10.8 %collective-permute-start.3 = (bf16[64,512]{1,0:T(8,128)(2,1)S(1)}, bf16[64,512]{1,0:T(8,128)(2,1)S(1)}, u32[]{:S(2)}, u32[]{:S(2)}) collective-permute-start(bf16[64,512]{1,0:T(8,128)(2,1)S(1)} %get-tuple-element.27), channel_id=1, source_target_pairs={{0,248},{8,256},{16,264},{24,272},{32,280},{40,288},{48,296},{56,3... | collective-permute-start | bytes 196616 | tf_op jit(solution)/shard_map/ppermute | solution.py:19
  (30 other events, 61.9 us)
Sparse Core Ops, SparseCore 0:
  136.4 37.8 all-gather.5
  177.7 88.0 all-gather.11
  269.2 79.2 all-gather.9
  351.7 79.7 all-gather.7
  451.2 37.2 reduce-scatter.2
  493.6 147.8 reduce-scatter.4
where the time goes:
time: 653 us; the launch traced here: 648 us
  waiting for transfers between devices  497 us (76%)
  starting transfers between devices  42.4 us (6%)
  blocking collectives  31.1 us (5%)
  local copies, waits for them, and re-layouts  23.7 us (4%)
  matrix products  21.6 us (3%)
  other arithmetic  17.2 us (3%)
  between operations  14.9 us (2%)
    reduce_scatter x1, waiting for transfers between devices, on_device(): lax.psum_scatter(jnp.einsum('rd,rc->dc', normed, grad_value, preferred_el...  104 us
    all_to_all x1, waiting for transfers between devices, on_device(): lax.all_to_all(buffers, 'dp', split_axis=0, concat_axis=0, tiled=True)  94.1 us
    all_gather x1, waiting for transfers between devices, on_device(): lax.all_gather(w_query, 'dp', axis=0, tiled=True)  88.8 us
    all_gather x1, waiting for transfers between devices, on_device(): lax.all_gather(w_value, 'dp', axis=0, tiled=True)  77.3 us
    all_gather x1, waiting for transfers between devices, on_device(): lax.all_gather(w_key, 'dp', axis=0, tiled=True)  76.3 us
    reduce_scatter x1, waiting for transfers between devices, on_device(): lax.psum_scatter(partial_value.astype(jnp.bfloat16), 'tensor', scatter_di...  34.5 us
    ppermute x4, starting transfers between devices, passed_along(): lax.ppermute(value, axis, [(i, (i + by) % size) for i in range(size)])  26.9 us
    all_gather x1, blocking collectives, on_device(): lax.all_gather(gain, 'tensor', axis=0, tiled=True)  19.2 us
  transfers between devices with their start and end apart: 11, of which 8 were waited for; matrix products, arithmetic and copies ran while one was open for 3% of the time, Pallas kernels for 0%

commit v1 on v0

v1 whole, which is shorter than its diff:
```python
import functools

import jax
import jax.numpy as jnp
from jax import lax
from jax.experimental import pallas as pl
from jax.experimental.pallas import tpu as pltpu
from jax.sharding import PartitionSpec as P

D = 4096
HEAD = 128
TOK_DEV = 128
MAXLEN = 64
CAP = 256
SLOTS = 4
EXTRA = 16
EPSILON = 1e-05
ROPE_BASE = 500000.0
BF = jnp.bfloat16
F32 = jnp.float32
VMEM_BYTES = 48 * 1024 * 1024


def passed_along(value, axis, by):
    size = lax.axis_size(axis)
    return lax.ppermute(value, axis, [(i, (i + by) % size) for i in range(size)])


def picked(onehot, rows):
    return jnp.dot(onehot, rows, preferred_element_type=F32).astype(rows.dtype)


def dot_nn(a, b):
    return lax.dot_general(a, b, (((1,), (0,)), ((), ())), preferred_element_type=F32)


def dot_nt(a, b):
    return lax.dot_general(a, b, (((1,), (1,)), ((), ())), preferred_element_type=F32)


def dot_tn(a, b):
    return lax.dot_general(a, b, (((0,), (0,)), ((), ())), preferred_element_type=F32)


def layer_kernel(
    q_heads,
    rows_ref,
    w_ref,
    cot_ref,
    cos_ref,
    sin_ref,
    allowed_ref,
    cut_ref,
    attn_ref,
    terms_ref,
    value_terms_ref,
    inverse_ref,
    normed_ref,
    grads_ref,
):
    peers = rows_ref.shape[0]
    width = rows_ref.shape[2]
    kv_at = q_heads * HEAD
    squares = jnp.zeros((TOK_DEV, 1), F32)
    for j in range(peers):
        part = rows_ref[j, :TOK_DEV, :].astype(F32)
        squares = squares + jnp.sum(part * part, 1, keepdims=True)
    inverse = lax.rsqrt(squares / D + EPSILON)
    inverse_ref[...] = jnp.broadcast_to(inverse, inverse_ref.shape)
    projected = jnp.zeros((TOK_DEV, w_ref.shape[1]), F32)
    for j in range(peers):
        gain = rows_ref[j, TOK_DEV : TOK_DEV + EXTRA, :].astype(F32)[0:1, :]
        part = (rows_ref[j, :TOK_DEV, :].astype(F32) * inverse * gain).astype(BF)
        normed_ref[:, j * width : (j + 1) * width] = part
        projected = projected + dot_nn(part, w_ref[j * width : (j + 1) * width, :])
    cosine = cos_ref[...]
    sine = sin_ref[...]
    factor = HEAD ** (-0.5)
    allowed = allowed_ref[...] > 0.5
    key_raw = projected[:, kv_at : kv_at + HEAD]
    value_raw = projected[:, kv_at + HEAD :]
    key = (key_raw * cosine + pltpu.roll(key_raw, HEAD // 2, 1) * sine).astype(BF)
    value = value_raw.astype(BF)
    grad_key = jnp.zeros((TOK_DEV, HEAD), F32)
    grad_value = jnp.zeros((TOK_DEV, HEAD), F32)
    dots = jnp.zeros((TOK_DEV, HEAD), F32)
    cut = cut_ref[...]
    for g in range(q_heads):
        at = slice(g * HEAD, (g + 1) * HEAD)
        query_raw = projected[:, at]
        query = (query_raw * cosine + pltpu.roll(query_raw, HEAD // 2, 1) * sine).astype(BF)
        scores = jnp.where(allowed, dot_nt(query, key) * factor, F32(-1e30))
        exp_terms = jnp.exp(scores - jnp.max(scores, -1, keepdims=True))
        probs = exp_terms / jnp.sum(exp_terms, -1, keepdims=True)
        probs_low = probs.astype(BF)
        mixed = dot_nn(probs_low, value).astype(BF)
        attn_ref[:, at] = dot_nn(cut, mixed).astype(BF)
        grad_out = cot_ref[:, at]
        grad_value = grad_value + dot_tn(probs_low, grad_out)
        grad_probs = dot_nt(grad_out, value)
        centre = jnp.sum(grad_probs * probs, -1, keepdims=True)
        grad_scores = (probs * (grad_probs - centre) * factor).astype(BF)
        grad_query = dot_nn(grad_scores, key)
        grad_key = grad_key + dot_tn(grad_scores, query)
        grad_query = (grad_query * cosine - pltpu.roll(grad_query, HEAD // 2, 1) * sine).astype(BF)
        grads_ref[:, at] = grad_query
        dots = dots + grad_query.astype(F32) * query_raw
    grad_key = (grad_key * cosine - pltpu.roll(grad_key, HEAD // 2, 1) * sine).astype(BF)
    grad_value = grad_value.astype(BF)
    grads_ref[:, kv_at : kv_at + HEAD] = grad_key
    grads_ref[:, kv_at + HEAD :] = grad_value
    dots = dots + grad_key.astype(F32) * key_raw + grad_value.astype(F32) * value_raw
    share = jnp.sum(dots, 1, keepdims=True) / inverse
    share = jnp.transpose(jnp.broadcast_to(share, (TOK_DEV, TOK_DEV)))[0:EXTRA, :]
    high = share.astype(BF)
    low = (share - high.astype(F32)).astype(BF)
    blank = jnp.zeros((EXTRA, width - 2 * TOK_DEV), BF)
    tail = jnp.concatenate([high, low, blank], 1)
    grads = grads_ref[...]
    for j in range(peers):
        cols = slice(j * width, (j + 1) * width)
        value_terms_ref[cols, :] = dot_tn(normed_ref[:, cols], grad_value).astype(BF)
    for j in range(peers):
        cols = slice(j * width, (j + 1) * width)
        terms_ref[j, :TOK_DEV, :] = dot_nt(grads, w_ref[cols, :]).astype(BF)
        terms_ref[j, TOK_DEV:, :] = tail


def finish_kernel(terms_ref, hidden_ref, gain_ref, inverse_ref, out_ref):
    total = terms_ref[0].astype(F32)
    for j in range(1, terms_ref.shape[0]):
        total = total + terms_ref[j].astype(F32)
    share = total[TOK_DEV : TOK_DEV + 8, :]
    share = share[0:1, :TOK_DEV] + share[0:1, TOK_DEV : 2 * TOK_DEV]
    row_dot = jnp.transpose(jnp.broadcast_to(share, (TOK_DEV, TOK_DEV)))[:, 0:1]
    inverse = inverse_ref[:, 0:1]
    weighted = total[:TOK_DEV, :] * gain_ref[...].astype(F32)
    here = hidden_ref[...].astype(F32)
    out_ref[...] = (inverse * weighted - here * (inverse * inverse * inverse * row_dot / D)).astype(BF)


def in_vmem(count):
    return [pl.BlockSpec(memory_space=pltpu.VMEM)] * count


def on_device(
    hidden, gain, w_query, w_key, w_value, cotangent, seq_length, home_offset, dest_shard, dest_offset
):
    shards = lax.axis_size("dp")
    peers = lax.axis_size("tensor")
    me = lax.axis_index("dp")
    strides = [-1, 1, shards // 2, shards // 2 + 1]
    width = hidden.shape[1]
    q_cols = w_query.shape[1]
    k_cols = w_key.shape[1]
    q_heads = q_cols // HEAD

    weights = lax.all_gather(
        jnp.concatenate([w_query, w_key, w_value], 1), "dp", axis=0, tiled=True
    )
    packed = jnp.concatenate([hidden, jnp.broadcast_to(gain[None, :], (EXTRA, width))], 0)
    rows_full = lax.all_to_all(
        jnp.broadcast_to(packed[None], (peers, TOK_DEV + EXTRA, width)),
        "tensor", split_axis=0, concat_axis=0, tiled=True,
    )

    own_len = seq_length[me]
    own_off = home_offset[me]
    own_move = (dest_shard[me] - me + shards) % shards
    stride_mod = jnp.array([s % shards for s in strides], jnp.int32)
    chosen = (own_move[None, :] == stride_mod[:, None]).astype(jnp.int32)
    slot_len = jnp.sum(chosen * own_len[None, :], 1)
    slot_off = jnp.sum(chosen * own_off[None, :], 1)
    sources = (me - jnp.array(strides, jnp.int32) + shards) % shards
    source_move = (dest_shard[sources] - sources[:, None] + shards) % shards
    matches = (source_move == stride_mod[:, None]).astype(jnp.int32)
    in_len = jnp.sum(matches * seq_length[sources], 1)
    in_start = jnp.sum(matches * dest_offset[sources], 1)

    t = jnp.arange(MAXLEN, dtype=jnp.int32)
    dest_row = jnp.arange(CAP, dtype=jnp.int32)
    home_row = jnp.arange(TOK_DEV, dtype=jnp.int32)
    dest_onehot = (dest_row[None, None, :] == (in_start[:, None] + t[None, :])[:, :, None]) & (
        t[None, :, None] < in_len[:, None, None]
    )
    home_onehot = (home_row[None, None, :] == (slot_off[:, None] + t[None, :])[:, :, None]) & (
        t[None, :, None] < slot_len[:, None, None]
    )
    dest_onehot = dest_onehot.reshape(SLOTS * MAXLEN, CAP).astype(BF)
    home_onehot = home_onehot.reshape(SLOTS * MAXLEN, TOK_DEV).astype(BF)
    belongs = (home_row[None, :] >= slot_off[:, None]) & (
        home_row[None, :] < (slot_off + slot_len)[:, None]
    )
    segment = jnp.sum(belongs * jnp.arange(SLOTS, dtype=jnp.int32)[:, None], 0)
    position = jnp.sum(belongs * (home_row[None, :] - slot_off[:, None]), 0)
    allowed = (segment[:, None] == segment[None, :]) & (position[None, :] <= position[:, None])
    half = HEAD // 2
    exponent = jnp.arange(half, dtype=F32) * (2.0 / HEAD)
    angles = position.astype(F32)[:, None] * jnp.power(F32(ROPE_BASE), -exponent)[None, :]
    cosine, sine = jnp.cos(angles), jnp.sin(angles)
    cosine = jnp.concatenate([cosine, cosine], 1)
    sine = jnp.concatenate([-sine, sine], 1)

    cot_cut = picked(dest_onehot, cotangent).reshape(SLOTS, MAXLEN, q_cols)
    cot_back = jnp.concatenate(
        [passed_along(cot_cut[n], "dp", -s) for n, s in enumerate(strides)], 0
    )
    grad_out = picked(home_onehot.T, cot_back)

    attn_cut, terms, value_terms, inverse = pl.pallas_call(
        functools.partial(layer_kernel, q_heads),
        out_shape=(
            jax.ShapeDtypeStruct((SLOTS * MAXLEN, q_cols), BF),
            jax.ShapeDtypeStruct((peers, TOK_DEV + EXTRA, width), BF),
            jax.ShapeDtypeStruct((D, k_cols), BF),
            jax.ShapeDtypeStruct((TOK_DEV, HEAD), F32),
        ),
        in_specs=in_vmem(7),
        out_specs=tuple(in_vmem(4)),
        scratch_shapes=[
            pltpu.VMEM((TOK_DEV, D), BF),
            pltpu.VMEM((TOK_DEV, q_cols + 2 * k_cols), BF),
        ],
        compiler_params=pltpu.CompilerParams(vmem_limit_bytes=VMEM_BYTES),
        name="layer",
    )(rows_full, weights, grad_out, cosine, sine, allowed.astype(F32), home_onehot)

    rows_each = D // shards
    halves = value_terms.reshape(shards // 2, 2, rows_each, k_cols)
    core = me % 2
    kept = jnp.where(core == 0, halves[:, 0], halves[:, 1])
    given = jnp.where(core == 0, halves[:, 1], halves[:, 0])
    got = lax.ppermute(given, "dp", [(i, i ^ 1) for i in range(shards)])
    pair = (kept.astype(F32) + got.astype(F32)).astype(BF)
    parts = lax.all_to_all(
        pair, "dp", split_axis=0, concat_axis=0, tiled=True,
        axis_index_groups=[list(range(c, shards, 2)) for c in range(2)],
    )
    grad_value_weight = jnp.sum(parts.astype(F32), 0)

    summed = lax.all_to_all(terms, "tensor", split_axis=0, concat_axis=0, tiled=True)
    grad_hidden = pl.pallas_call(
        finish_kernel,
        out_shape=jax.ShapeDtypeStruct((TOK_DEV, width), BF),
        in_specs=in_vmem(4),
        out_specs=in_vmem(1)[0],
        compiler_params=pltpu.CompilerParams(vmem_limit_bytes=VMEM_BYTES),
        name="finish",
    )(summed, hidden, gain[None, :], inverse)

    attn_cut = attn_cut.reshape(SLOTS, MAXLEN, q_cols)
    attn_sent = jnp.concatenate(
        [passed_along(attn_cut[n], "dp", s) for n, s in enumerate(strides)], 0
    )
    attn_out = picked(dest_onehot.T, attn_sent)
    return (attn_out, grad_hidden, grad_value_weight)


def solution(mesh):
    return jax.shard_map(
        on_device,
        mesh=mesh,
        in_specs=(P("dp", "tensor"), P("tensor")) + (P("dp", "tensor"),) * 4 + (P(),) * 4,
        out_specs=(P("dp", "tensor"), P("dp", "tensor"), P("dp", "tensor")),
        check_vma=False,
    )
```

time: 653 us -> 190 us (0.29)
  waiting for transfers between devices: 497 us -> 73.7 us
  matrix products: 21.6 us -> 1.69 us
  local copies, waits for them, and re-layouts: 23.7 us -> 4.59 us
  starting transfers between devices: 42.4 us -> 57.6 us
  other arithmetic: 17.2 us -> 5.02 us
  Pallas kernels: 0 us -> 11.5 us
  blocking collectives: 31.1 us -> 21.3 us
    all_gather x4 -> x1, waiting for transfers between devices: 258 us -> 55.5 us  [on_device(): lax.all_gather(jnp.concatenate([w_query, w_key, w_value], 1), 'dp', axis=...]
    reduce_scatter x2 -> x0, waiting for transfers between devices: 138 us -> none  [the longest x1 104 us: on_device(): lax.psum_scatter(jnp.einsum('rd,rc->dc', normed, grad_value, preferred_el...]
    all_to_all x1 -> x2, waiting for transfers between devices: 94.1 us -> 9.73 us  [the longest x1 9.73 us: on_device(): lax.all_to_all(terms, 'tensor', split_axis=0, concat_axis=0, tiled=True)]
    all_to_all x0 -> x1, blocking collectives: none -> 21.3 us  [on_device(): lax.all_to_all(pair, 'dp', split_axis=0, concat_axis=0, tiled=True, axis_...]
    dot_general x13 -> x3, matrix products: 21.6 us -> 1.69 us  [picked(): return jnp.dot(onehot, rows, preferred_element_type=F32).astype(rows.dtype)]
    all_gather x1 -> x0, blocking collectives: 19.2 us -> none  [on_device(): lax.all_gather(gain, 'tensor', axis=0, tiled=True)]
    ppermute x4 -> x8, starting transfers between devices: 26.9 us -> 41 us  [passed_along(): lax.ppermute(value, axis, [(i, (i + by) % size) for i in range(size)])]
    psum x1 -> x0, blocking collectives: 11.8 us -> none  [on_device(): row_dot = lax.psum(jnp.sum(weighted * local_vals, 1), 'tensor')]
  transfers between devices with their start and end apart: 11 -> 12, of which waited for: 8 -> 6; matrix products, arithmetic and copies ran while one was open for 3% -> 5% of each run, Pallas kernels for 0% -> 0%
where the time goes in v1:
time: 190 us
  waiting for transfers between devices  73.7 us (39%)
  starting transfers between devices  57.6 us (30%)
  blocking collectives  21.3 us (11%)
  between operations  14.3 us (8%)
  Pallas kernels  11.5 us (6%)
  other arithmetic  5.02 us (3%)
  local copies, waits for them, and re-layouts  4.59 us (2%)
    all_gather x1, waiting for transfers between devices, on_device(): lax.all_gather(jnp.concatenate([w_query, w_key, w_value], 1), 'dp', axis=...  55.5 us
    ppermute x8, starting transfers between devices, passed_along(): lax.ppermute(value, axis, [(i, (i + by) % size) for i in range(size)])  41 us
    all_to_all x1, blocking collectives, on_device(): lax.all_to_all(pair, 'dp', split_axis=0, concat_axis=0, tiled=True, axis_...  21.3 us
    pallas_call x1, Pallas kernels, on_device(): pl.pallas_call(functools.partial(layer_kernel, q_heads), out_shape=(jax.S...  10.7 us
    all_to_all x1, waiting for transfers between devices, on_device(): lax.all_to_all(terms, 'tensor', split_axis=0, concat_axis=0, tiled=True)  9.73 us
    all_to_all x1, starting transfers between devices, on_device(): lax.all_to_all(jnp.broadcast_to(packed[None], (peers, TOK_DEV + EXTRA, wi...  7.79 us
    ppermute x8, waiting for transfers between devices, passed_along(): lax.ppermute(value, axis, [(i, (i + by) % size) for i in range(size)])  6.85 us
    all_to_all x1, starting transfers between devices, on_device(): lax.all_to_all(terms, 'tensor', split_axis=0, concat_axis=0, tiled=True)  6.6 us
  transfers between devices with their start and end apart: 12, of which 6 were waited for; matrix products, arithmetic and copies ran while one was open for 5% of the time, Pallas kernels for 0%

profile of v1, /device:TPU:1, one launch (start us, length us, event | category | flops | bytes accessed | tf_op | source)
XLA Modules:
  0.0 189.8 jit_solution(7411390654167621003)
XLA Ops:
  7.2 1.6 pad_maximum_fusion.1
  9.5 0.9 pad_maximum_fusion
  10.4 1.1 broadcast_in_dim.10
  11.6 7.8 %all-to-all-start = ((bf16[8,144,512]{2,1,0:T(8,128)(2,1)}), bf16[8,144,512]{2,1,0:T(8,128)(2,1)S(1)}, u32[]{:S(2)}, u32[]{:S(2)}) async-start(bf16[8,144,512]{2,1,0:T(8,128)(2,1)} %broadcast_in_dim.10), calls=%async_computation | async-start | bytes 2359296 | tf_op jit(solution)/shard_map/all_to_all | solution.py:162
  22.8 4.0 %collective-permute-start = (bf16[64,512]{1,0:T(8,128)(2,1)S(1)}, bf16[64,512]{1,0:T(8,128)(2,1)S(1)}, u32[]{:S(2)}, u32[]{:S(2)}) collective-permute-start(bf16[64,512]{1,0:T(8,128)(2,1)S(1)} %get-tuple-element.23), channel_id=1, source_target_pairs={{0,8},{8,16},{16,24},{24,32},{32,40},{40,48},{48,56},{56,64},{64,7... | collective-permute-start | bytes 196616 | tf_op jit(solution)/shard_map/ppermute | solution.py:26
  26.8 2.7 %collective-permute-start.1 = (bf16[64,512]{1,0:T(8,128)(2,1)S(1)}, bf16[64,512]{1,0:T(8,128)(2,1)S(1)}, u32[]{:S(2)}, u32[]{:S(2)}) collective-permute-start(bf16[64,512]{1,0:T(8,128)(2,1)S(1)} %get-tuple-element.26), channel_id=1, source_target_pairs={{0,504},{8,0},{16,8},{24,16},{32,24},{40,32},{48,40},{56,48},{64,5... | collective-permute-start | bytes 196616 | tf_op jit(solution)/shard_map/ppermute | solution.py:26
  29.5 9.9 %collective-permute-start.2 = (bf16[64,512]{1,0:T(8,128)(2,1)S(1)}, bf16[64,512]{1,0:T(8,128)(2,1)S(1)}, u32[]{:S(2)}, u32[]{:S(2)}) collective-permute-start(bf16[64,512]{1,0:T(8,128)(2,1)S(1)} %get-tuple-element.25), channel_id=1, source_target_pairs={{0,256},{8,264},{16,272},{24,280},{32,288},{40,296},{48,304},{56,3... | collective-permute-start | bytes 196616 | tf_op jit(solution)/shard_map/ppermute | solution.py:26
  39.4 8.0 %collective-permute-start.3 = (bf16[64,512]{1,0:T(8,128)(2,1)S(1)}, bf16[64,512]{1,0:T(8,128)(2,1)S(1)}, u32[]{:S(2)}, u32[]{:S(2)}) collective-permute-start(bf16[64,512]{1,0:T(8,128)(2,1)S(1)} %get-tuple-element.24), channel_id=1, source_target_pairs={{0,248},{8,256},{16,264},{24,272},{32,280},{40,288},{48,296},{56,3... | collective-permute-start | bytes 196616 | tf_op jit(solution)/shard_map/ppermute | solution.py:26
  48.6 3.0 %collective-permute-done.3 = bf16[64,512]{1,0:T(8,128)(2,1)S(1)} collective-permute-done((bf16[64,512]{1,0:T(8,128)(2,1)S(1)}, bf16[64,512]{1,0:T(8,128)(2,1)S(1)}, u32[]{:S(2)}, u32[]{:S(2)}) %collective-permute-start.3) | collective-permute-done | bytes 65568 | tf_op jit(solution)/shard_map/ppermute | solution.py:26
  51.9 55.5 %all-gather.2.cloned.1.call-done.w_ref = bf16[4096,768]{1,0:T(8,128)(2,1)} async-done(((bf16[64,768]{1,0:T(8,128)(2,1)}), bf16[4096,768]{1,0:T(8,128)(2,1)}) %all-gather.2.cloned.1.call-update) | async-done | bytes 6291472 | tf_op jit(solution)/shard_map/all_gather | solution.py:158
  107.4 10.7 %layer.1 = (bf16[256,512]{1,0:T(8,128)(2,1)S(1)}, bf16[8,144,512]{2,1,0:T(8,128)(2,1)}, bf16[4096,128]{1,0:T(8,128)(2,1)S(1)}, f32[128,128]{1,0:T(8,128)S(1)}) custom-call(bf16[8,144,512]{2,1,0:T(8,128)(2,1)S(1)} %all-to-all-done.rows_ref, bf16[4096,768]{1,0:T(8,128)(2,1)} %all-gather.2.cloned.1.call-done.w_ref, ...), custom_call_target="tpu_custom_call" | custom-call | tf_op jit(solution)/shard_map/layer/pallas_call | solution.py:210
  118.2 2.2 %collective-permute-start.8 = (bf16[32,64,128]{2,1,0:T(8,128)(2,1)S(1)}, bf16[32,64,128]{2,1,0:T(8,128)(2,1)S(1)}, u32[]{:S(2)}, u32[]{:S(2)}) collective-permute-start(bf16[32,64,128]{2,1,0:T(8,128)(2,1)S(1)} %fusion.1), channel_id=1, source_target_pairs={{0,8},{8,0},{16,24},{24,16},{32,40},{40,32},{48,56},{56,48},{64,72... | collective-permute-start | bytes 1572872 | tf_op jit(solution)/shard_map/ppermute | solution.py:233
  120.3 1.6 collective-permute-done.8
  122.2 21.3 %all_to_all.15 = bf16[32,64,128]{2,1,0:T(8,128)(2,1)S(1)} all-to-all(bf16[32,64,128]{2,1,0:T(8,128)(2,1)S(1)} %fusion), channel_id=1, replica_groups={{0,16,32,48,64,80,96,112,128,144,160,176,192,208,224,240,256,272,288,30..., dimensions={0} | all-to-all | bytes 1048576 | tf_op jit(solution)/shard_map/all_to_all | solution.py:235
  143.5 6.6 %all-to-all-start.1 = ((bf16[8,144,512]{2,1,0:T(8,128)(2,1)}), bf16[8,144,512]{2,1,0:T(8,128)(2,1)S(1)}, u32[]{:S(2)}, u32[]{:S(2)}) async-start(bf16[8,144,512]{2,1,0:T(8,128)(2,1)} %get-tuple-element.8), calls=%async_computation.1 | async-start | bytes 2359296 | tf_op jit(solution)/shard_map/all_to_all | solution.py:241
  150.1 4.5 %collective-permute-start.4 = (bf16[64,512]{1,0:T(8,128)(2,1)S(1)}, bf16[64,512]{1,0:T(8,128)(2,1)S(1)}, u32[]{:S(2)}, u32[]{:S(2)}) collective-permute-start(bf16[64,512]{1,0:T(8,128)(2,1)S(1)} %get-tuple-element.19), channel_id=1, source_target_pairs={{0,504},{8,0},{16,8},{24,16},{32,24},{40,32},{48,40},{56,48},{64,5... | collective-permute-start | bytes 196616 | tf_op jit(solution)/shard_map/ppermute | solution.py:26
  154.6 2.3 %collective-permute-start.5 = (bf16[64,512]{1,0:T(8,128)(2,1)S(1)}, bf16[64,512]{1,0:T(8,128)(2,1)S(1)}, u32[]{:S(2)}, u32[]{:S(2)}) collective-permute-start(bf16[64,512]{1,0:T(8,128)(2,1)S(1)} %get-tuple-element.22), channel_id=1, source_target_pairs={{0,8},{8,16},{16,24},{24,32},{32,40},{40,48},{48,56},{56,64},{64,7... | collective-permute-start | bytes 196616 | tf_op jit(solution)/shard_map/ppermute | solution.py:26
  157.0 3.3 %collective-permute-start.6 = (bf16[64,512]{1,0:T(8,128)(2,1)S(1)}, bf16[64,512]{1,0:T(8,128)(2,1)S(1)}, u32[]{:S(2)}, u32[]{:S(2)}) collective-permute-start(bf16[64,512]{1,0:T(8,128)(2,1)S(1)} %get-tuple-element.21), channel_id=1, source_target_pairs={{0,256},{8,264},{16,272},{24,280},{32,288},{40,296},{48,304},{56,3... | collective-permute-start | bytes 196616 | tf_op jit(solution)/shard_map/ppermute | solution.py:26
  160.3 6.4 %collective-permute-start.7 = (bf16[64,512]{1,0:T(8,128)(2,1)S(1)}, bf16[64,512]{1,0:T(8,128)(2,1)S(1)}, u32[]{:S(2)}, u32[]{:S(2)}) collective-permute-start(bf16[64,512]{1,0:T(8,128)(2,1)S(1)} %get-tuple-element.20), channel_id=1, source_target_pairs={{0,264},{8,272},{16,280},{24,288},{32,296},{40,304},{48,312},{56,3... | collective-permute-start | bytes 196616 | tf_op jit(solution)/shard_map/ppermute | solution.py:26
  167.2 3.4 %collective-permute-done.7 = bf16[64,512]{1,0:T(8,128)(2,1)S(1)} collective-permute-done((bf16[64,512]{1,0:T(8,128)(2,1)S(1)}, bf16[64,512]{1,0:T(8,128)(2,1)S(1)}, u32[]{:S(2)}, u32[]{:S(2)}) %collective-permute-start.7) | collective-permute-done | bytes 65568 | tf_op jit(solution)/shard_map/ppermute | solution.py:26
  170.6 1.1 convolution_convert_fusion
  171.7 0.7 convert_reduce_fusion
  172.4 9.7 %all-to-all-done.1.terms_ref = bf16[8,144,512]{2,1,0:T(8,128)(2,1)S(1)} async-done(((bf16[8,144,512]{2,1,0:T(8,128)(2,1)}), bf16[8,144,512]{2,1,0:T(8,128)(2,1)S(1)}, u32[]{:S(2)}, u32[]{:S(2)}) %all-to-all-start.1) | async-done | bytes 1179680 | tf_op jit(solution)/shard_map/all_to_all | solution.py:241
  182.1 0.9 finish.1
  (64 shorter events, 6.5 us)
Async XLA Ops:
  7.2 15.3 %copy-start = (bf16[256,512]{1,0:T(8,128)(2,1)S(1)}, bf16[256,512]{1,0:T(8,128)(2,1)}, u32[]{:S(2)}) copy-start(bf16[256,512]{1,0:T(8,128)(2,1)} %param.17) | copy-start | bytes 786436
  7.2 100.2 %all-gather.2.cloned.1.call-start = ((), (), s32[]{:S(2)}) async-start(), calls=%async_computation.3 | async-start | bytes 6389760 | tf_op jit(solution)/shard_map/all_gather | solution.py:158
  11.6 7.8 %copy-start.3 = (s32[64,4]{0,1:T(4,128)S(1)}, s32[64,4]{0,1:T(4,128)}, u32[]{:S(2)}) copy-start(s32[64,4]{0,1:T(4,128)} %param.18) | copy-start | bytes 3076
  11.6 8.1 %copy-start.6 = (s32[64,4]{0,1:T(4,128)S(1)}, s32[64,4]{0,1:T(4,128)}, u32[]{:S(2)}) copy-start(s32[64,4]{0,1:T(4,128)} %param.19) | copy-start | bytes 3076
  11.6 8.3 %copy-start.2 = (s32[64,4]{0,1:T(4,128)S(1)}, s32[64,4]{0,1:T(4,128)}, u32[]{:S(2)}) copy-start(s32[64,4]{0,1:T(4,128)} %param.20) | copy-start | bytes 3076
  11.6 8.4 %copy-start.5 = (s32[64,4]{0,1:T(4,128)S(1)}, s32[64,4]{0,1:T(4,128)}, u32[]{:S(2)}) copy-start(s32[64,4]{0,1:T(4,128)} %param.21) | copy-start | bytes 3076
  11.6 8.5 %copy-start.7 = (s32[4]{0:T(128)S(1)}, s32[4]{0:T(128)}, u32[]{:S(2)}) copy-start(s32[4]{0:T(128)} %constant.68) | copy-start | bytes 52
  11.6 10.4 %copy-start.8 = (s32[4]{0:T(128)S(1)}, s32[4]{0:T(128)}, u32[]{:S(2)}) copy-start(s32[4]{0:T(128)} %constant.66.clone) | copy-start | bytes 52
  11.6 40.3 %all-to-all-start = ((bf16[8,144,512]{2,1,0:T(8,128)(2,1)}), bf16[8,144,512]{2,1,0:T(8,128)(2,1)S(1)}, u32[]{:S(2)}, u32[]{:S(2)}) async-start(bf16[8,144,512]{2,1,0:T(8,128)(2,1)} %broadcast_in_dim.10), calls=%async_computation | async-start | bytes 2359296 | tf_op jit(solution)/shard_map/all_to_all | solution.py:162
  22.8 25.8 %collective-permute-start = (bf16[64,512]{1,0:T(8,128)(2,1)S(1)}, bf16[64,512]{1,0:T(8,128)(2,1)S(1)}, u32[]{:S(2)}, u32[]{:S(2)}) collective-permute-start(bf16[64,512]{1,0:T(8,128)(2,1)S(1)} %get-tuple-element.23), channel_id=1, source_target_pairs={{0,8},{8,16},{16,24},{24,32},{32,40},{40,48},{48,56},{56,64},{64,7... | collective-permute-start | bytes 196616 | tf_op jit(solution)/shard_map/ppermute | solution.py:26
  26.8 21.8 %collective-permute-start.1 = (bf16[64,512]{1,0:T(8,128)(2,1)S(1)}, bf16[64,512]{1,0:T(8,128)(2,1)S(1)}, u32[]{:S(2)}, u32[]{:S(2)}) collective-permute-start(bf16[64,512]{1,0:T(8,128)(2,1)S(1)} %get-tuple-element.26), channel_id=1, source_target_pairs={{0,504},{8,0},{16,8},{24,16},{32,24},{40,32},{48,40},{56,48},{64,5... | collective-permute-start | bytes 196616 | tf_op jit(solution)/shard_map/ppermute | solution.py:26
  29.5 19.1 %collective-permute-start.2 = (bf16[64,512]{1,0:T(8,128)(2,1)S(1)}, bf16[64,512]{1,0:T(8,128)(2,1)S(1)}, u32[]{:S(2)}, u32[]{:S(2)}) collective-permute-start(bf16[64,512]{1,0:T(8,128)(2,1)S(1)} %get-tuple-element.25), channel_id=1, source_target_pairs={{0,256},{8,264},{16,272},{24,280},{32,288},{40,296},{48,304},{56,3... | collective-permute-start | bytes 196616 | tf_op jit(solution)/shard_map/ppermute | solution.py:26
  39.4 12.2 %collective-permute-start.3 = (bf16[64,512]{1,0:T(8,128)(2,1)S(1)}, bf16[64,512]{1,0:T(8,128)(2,1)S(1)}, u32[]{:S(2)}, u32[]{:S(2)}) collective-permute-start(bf16[64,512]{1,0:T(8,128)(2,1)S(1)} %get-tuple-element.24), channel_id=1, source_target_pairs={{0,248},{8,256},{16,264},{24,272},{32,280},{40,288},{48,296},{56,3... | collective-permute-start | bytes 196616 | tf_op jit(solution)/shard_map/ppermute | solution.py:26
  118.2 3.8 %collective-permute-start.8 = (bf16[32,64,128]{2,1,0:T(8,128)(2,1)S(1)}, bf16[32,64,128]{2,1,0:T(8,128)(2,1)S(1)}, u32[]{:S(2)}, u32[]{:S(2)}) collective-permute-start(bf16[32,64,128]{2,1,0:T(8,128)(2,1)S(1)} %fusion.1), channel_id=1, source_target_pairs={{0,8},{8,0},{16,24},{24,16},{32,40},{40,32},{48,56},{56,48},{64,72... | collective-permute-start | bytes 1572872 | tf_op jit(solution)/shard_map/ppermute | solution.py:233
  143.5 23.2 %copy-start.4 = (bf16[512]{0:T(512)(128)(2,1)S(1)}, bf16[512]{0:T(512)(128)(2,1)}, u32[]{:S(2)}) copy-start(bf16[512]{0:T(512)(128)(2,1)} %param.13) | copy-start | bytes 3076
  143.5 38.6 %all-to-all-start.1 = ((bf16[8,144,512]{2,1,0:T(8,128)(2,1)}), bf16[8,144,512]{2,1,0:T(8,128)(2,1)S(1)}, u32[]{:S(2)}, u32[]{:S(2)}) async-start(bf16[8,144,512]{2,1,0:T(8,128)(2,1)} %get-tuple-element.8), calls=%async_computation.1 | async-start | bytes 2359296 | tf_op jit(solution)/shard_map/all_to_all | solution.py:241
  150.1 32.0 %copy-start.1 = (bf16[128,512]{1,0:T(8,128)(2,1)S(1)}, bf16[128,512]{1,0:T(8,128)(2,1)}, u32[]{:S(2)}) copy-start(bf16[128,512]{1,0:T(8,128)(2,1)} %hidden_ref.1) | copy-start | bytes 393220
  150.1 16.6 %collective-permute-start.4 = (bf16[64,512]{1,0:T(8,128)(2,1)S(1)}, bf16[64,512]{1,0:T(8,128)(2,1)S(1)}, u32[]{:S(2)}, u32[]{:S(2)}) collective-permute-start(bf16[64,512]{1,0:T(8,128)(2,1)S(1)} %get-tuple-element.19), channel_id=1, source_target_pairs={{0,504},{8,0},{16,8},{24,16},{32,24},{40,32},{48,40},{56,48},{64,5... | collective-permute-start | bytes 196616 | tf_op jit(solution)/shard_map/ppermute | solution.py:26
  154.6 12.1 %collective-permute-start.5 = (bf16[64,512]{1,0:T(8,128)(2,1)S(1)}, bf16[64,512]{1,0:T(8,128)(2,1)S(1)}, u32[]{:S(2)}, u32[]{:S(2)}) collective-permute-start(bf16[64,512]{1,0:T(8,128)(2,1)S(1)} %get-tuple-element.22), channel_id=1, source_target_pairs={{0,8},{8,16},{16,24},{24,32},{32,40},{40,48},{48,56},{56,64},{64,7... | collective-permute-start | bytes 196616 | tf_op jit(solution)/shard_map/ppermute | solution.py:26
  157.0 10.2 %collective-permute-start.6 = (bf16[64,512]{1,0:T(8,128)(2,1)S(1)}, bf16[64,512]{1,0:T(8,128)(2,1)S(1)}, u32[]{:S(2)}, u32[]{:S(2)}) collective-permute-start(bf16[64,512]{1,0:T(8,128)(2,1)S(1)} %get-tuple-element.21), channel_id=1, source_target_pairs={{0,256},{8,264},{16,272},{24,280},{32,288},{40,296},{48,304},{56,3... | collective-permute-start | bytes 196616 | tf_op jit(solution)/shard_map/ppermute | solution.py:26
  160.3 10.3 %collective-permute-start.7 = (bf16[64,512]{1,0:T(8,128)(2,1)S(1)}, bf16[64,512]{1,0:T(8,128)(2,1)S(1)}, u32[]{:S(2)}, u32[]{:S(2)}) collective-permute-start(bf16[64,512]{1,0:T(8,128)(2,1)S(1)} %get-tuple-element.20), channel_id=1, source_target_pairs={{0,264},{8,272},{16,280},{24,288},{32,296},{40,304},{48,312},{56,3... | collective-permute-start | bytes 196616 | tf_op jit(solution)/shard_map/ppermute | solution.py:26
Sparse Core Ops, SparseCore 0:
  11.9 95.4 all-gather.1

commit v2 on v1

v2 whole, which is shorter than its diff:
```python
import functools

import jax
import jax.numpy as jnp
import numpy as np
from jax import lax
from jax.experimental import pallas as pl
from jax.experimental.pallas import tpu as pltpu
from jax.sharding import PartitionSpec as P

D = 4096
HEAD = 128
TOK_DEV = 128
MAXLEN = 64
CAP = 256
SLOTS = 4
EXTRA = 16
EPSILON = 1e-05
ROPE_BASE = 500000.0
NZ, NX, NC = 8, 4, 2
BF = jnp.bfloat16
F32 = jnp.float32
VMEM_BYTES = 48 * 1024 * 1024


def moved(value, where):
    pairs = []
    for z in range(NZ):
        for x in range(NX):
            for c in range(NC):
                tz, tx, tc = where(z, x, c)
                pairs.append(((z * NX + x) * NC + c, ((tz % NZ) * NX + tx % NX) * NC + tc))
    return lax.ppermute(value, "dp", pairs)


def other_core(value):
    return moved(value, lambda z, x, c: (z, x, 1 - c))


def along_z(value):
    return moved(value, lambda z, x, c: (z + (1 if c == 0 else -1), x, c))


def passed_along(value, by):
    size = lax.axis_size("dp")
    return lax.ppermute(value, "dp", [(i, (i + by) % size) for i in range(size)])


def dot_nn(a, b):
    return lax.dot_general(a, b, (((1,), (0,)), ((), ())), preferred_element_type=F32)


def dot_nt(a, b):
    return lax.dot_general(a, b, (((1,), (1,)), ((), ())), preferred_element_type=F32)


def dot_tn(a, b):
    return lax.dot_general(a, b, (((0,), (0,)), ((), ())), preferred_element_type=F32)


def place():
    me = lax.axis_index("dp")
    return me, me // (NX * NC), (me // NC) % NX, me % NC


def plan_kernel(
    strides, shards,
    len_ref, off_ref, shard_ref, start_ref, freq_ref, cotangent_ref,
    cut0_ref, cut1_ref, cut2_ref, cut3_ref, home_ref, dest_ref, cos_ref, sin_ref, allowed_ref,
):
    me = lax.axis_index("dp")
    rows = lax.broadcasted_iota(jnp.int32, (TOK_DEV, TOK_DEV), 0)
    cols = lax.broadcasted_iota(jnp.int32, (TOK_DEV, TOK_DEV), 1)
    row_seq, row_pos = jnp.zeros_like(rows), jnp.zeros_like(rows)
    col_seq, col_pos = jnp.zeros_like(rows), jnp.zeros_like(rows)
    cuts = (cut0_ref, cut1_ref, cut2_ref, cut3_ref)
    for e, stride in enumerate(strides):
        target = lax.rem(me + stride + shards, shards)
        source = lax.rem(me - stride + shards, shards)
        length = jnp.int32(0)
        offset = jnp.int32(0)
        in_len = jnp.int32(0)
        in_start = jnp.int32(0)
        for c in range(SLOTS):
            mine = shard_ref[c, me] == target
            length = length + jnp.where(mine, len_ref[c, me], 0)
            offset = offset + jnp.where(mine, off_ref[c, me], 0)
            theirs = shard_ref[c, source] == me
            in_len = in_len + jnp.where(theirs, len_ref[c, source], 0)
            in_start = in_start + jnp.where(theirs, start_ref[c, source], 0)
        inside = (rows >= offset) & (rows < offset + length)
        row_seq = jnp.where(inside, e, row_seq)
        row_pos = jnp.where(inside, rows - offset, row_pos)
        inside = (cols >= offset) & (cols < offset + length)
        col_seq = jnp.where(inside, e, col_seq)
        col_pos = jnp.where(inside, cols - offset, col_pos)
        at = slice(e * MAXLEN, (e + 1) * MAXLEN)
        t = lax.broadcasted_iota(jnp.int32, (MAXLEN, TOK_DEV), 0)
        r = lax.broadcasted_iota(jnp.int32, (MAXLEN, TOK_DEV), 1)
        home_ref[at, :] = jnp.where((r == t + offset) & (t < length), 1.0, 0.0).astype(BF)
        t = lax.broadcasted_iota(jnp.int32, (MAXLEN, CAP), 0)
        r = lax.broadcasted_iota(jnp.int32, (MAXLEN, CAP), 1)
        dest = jnp.where((r == t + in_start) & (t < in_len), 1.0, 0.0).astype(BF)
        dest_ref[at, :] = dest
        cuts[e][...] = dot_nn(dest, cotangent_ref[...]).astype(BF)
    allowed_ref[...] = jnp.where((row_seq == col_seq) & (col_pos <= row_pos), 1.0, 0.0)
    angles = row_pos.astype(F32) * freq_ref[...]
    cos_ref[...] = jnp.cos(angles)
    sine = jnp.sin(angles)
    sin_ref[...] = jnp.where(cols < HEAD // 2, -sine, sine)


def layer_kernel(q_heads, pieces, *refs):
    rows_ref, cos_ref, sin_ref, allowed_ref, home_ref = refs[:5]
    cot_refs = refs[5:9]
    w_refs = refs[9 : 9 + pieces]
    cut0_ref, cut1_ref, cut2_ref, cut3_ref, terms_ref, kept_ref, given_ref, inverse_ref = refs[9 + pieces : 17 + pieces]
    normed_ref, grads_ref = refs[17 + pieces :]
    _, z, x, c = place()
    up = 1 - 2 * c
    where = [(z, 0, w_refs[0], 0), (z, 1, w_refs[0], 256)]
    for k in range(1, NZ // 2):
        first = 1 + 4 * (k - 1)
        behind = lax.rem(z - up * k + NZ, NZ)
        ahead = lax.rem(z + up * k + NZ, NZ)
        where.append((behind, c, w_refs[first], 0))
        where.append((behind, 1 - c, w_refs[first + 1], 0))
        where.append((ahead, 1 - c, w_refs[first + 2], 0))
        where.append((ahead, c, w_refs[first + 3], 0))
    far = lax.rem(z + NZ // 2, NZ)
    where.append((far, c, w_refs[pieces - 2], 0))
    where.append((far, 1 - c, w_refs[pieces - 1], 0))
    deep = rows_ref.shape[3]
    kv_at = q_heads * HEAD
    squares = jnp.zeros((TOK_DEV, 1), F32)
    for j in range(NZ):
        for h in range(2):
            part = rows_ref[j, h, :TOK_DEV, :].astype(F32)
            squares = squares + jnp.sum(part * part, 1, keepdims=True)
    inverse = lax.rsqrt(squares / D + EPSILON)
    inverse_ref[...] = jnp.broadcast_to(inverse, inverse_ref.shape)
    projected = jnp.zeros((TOK_DEV, w_refs[0].shape[1]), F32)
    for n, (block, half, w_ref, at) in enumerate(where):
        gain = rows_ref[block, half, TOK_DEV:, :].astype(F32)[0:1, :]
        part = (rows_ref[block, half, :TOK_DEV, :].astype(F32) * inverse * gain).astype(BF)
        normed_ref[n] = part
        projected = projected + dot_nn(part, w_ref[at : at + deep, :])
    cosine = cos_ref[...]
    sine = sin_ref[...]
    factor = HEAD ** (-0.5)
    allowed = allowed_ref[...] > 0.5
    home = home_ref[...]
    cot = jnp.concatenate([ref[...] for ref in cot_refs], 0)
    cot = dot_tn(home, cot).astype(BF)
    key_raw = projected[:, kv_at : kv_at + HEAD]
    value_raw = projected[:, kv_at + HEAD :]
    key = (key_raw * cosine + pltpu.roll(key_raw, HEAD // 2, 1) * sine).astype(BF)
    value = value_raw.astype(BF)
    grad_key = jnp.zeros((TOK_DEV, HEAD), F32)
    grad_value = jnp.zeros((TOK_DEV, HEAD), F32)
    dots = jnp.zeros((TOK_DEV, HEAD), F32)
    cuts = (cut0_ref, cut1_ref, cut2_ref, cut3_ref)
    for g in range(q_heads):
        at = slice(g * HEAD, (g + 1) * HEAD)
        query_raw = projected[:, at]
        query = (query_raw * cosine + pltpu.roll(query_raw, HEAD // 2, 1) * sine).astype(BF)
        scores = jnp.where(allowed, dot_nt(query, key) * factor, F32(-1e30))
        exp_terms = jnp.exp(scores - jnp.max(scores, -1, keepdims=True))
        probs = exp_terms / jnp.sum(exp_terms, -1, keepdims=True)
        probs_low = probs.astype(BF)
        mixed = dot_nn(probs_low, value).astype(BF)
        mixed = dot_nn(home, mixed).astype(BF)
        for e in range(SLOTS):
            cuts[e][:, at] = mixed[e * MAXLEN : (e + 1) * MAXLEN, :]
        grad_out = cot[:, at]
        grad_value = grad_value + dot_tn(probs_low, grad_out)
        grad_probs = dot_nt(grad_out, value)
        centre = jnp.sum(grad_probs * probs, -1, keepdims=True)
        grad_scores = (probs * (grad_probs - centre) * factor).astype(BF)
        grad_query = dot_nn(grad_scores, key)
        grad_key = grad_key + dot_tn(grad_scores, query)
        grad_query = (grad_query * cosine - pltpu.roll(grad_query, HEAD // 2, 1) * sine).astype(BF)
        grads_ref[:, at] = grad_query
        dots = dots + grad_query.astype(F32) * query_raw
    grad_key = (grad_key * cosine - pltpu.roll(grad_key, HEAD // 2, 1) * sine).astype(BF)
    grad_value = grad_value.astype(BF)
    grads_ref[:, kv_at : kv_at + HEAD] = grad_key
    grads_ref[:, kv_at + HEAD :] = grad_value
    dots = dots + grad_key.astype(F32) * key_raw + grad_value.astype(F32) * value_raw
    share = jnp.sum(dots, 1, keepdims=True) / inverse
    share = jnp.transpose(jnp.broadcast_to(share, (TOK_DEV, TOK_DEV)))[0:EXTRA, :]
    high = share.astype(BF)
    low = (share - high.astype(F32)).astype(BF)
    tail = jnp.concatenate([high, low], 1)
    grads = grads_ref[...]
    for n, (block, half, w_ref, at) in enumerate(where):
        found = dot_tn(normed_ref[n], grad_value).astype(BF)
        for pair in range(2):
            low_rows = found[pair * 128 : pair * 128 + 64, :]
            high_rows = found[pair * 128 + 64 : (pair + 1) * 128, :]
            away = lax.rem(2 * half + pair - x + NX, NX)
            kept_ref[away, block] = jnp.where(c == 0, low_rows, high_rows)
            given_ref[away, block] = jnp.where(c == 0, high_rows, low_rows)
    for n, (block, half, w_ref, at) in enumerate(where):
        terms_ref[block, half, :TOK_DEV, :] = dot_nt(grads, w_ref[at : at + deep, :]).astype(BF)
        terms_ref[block, half, TOK_DEV:, :] = tail


def finish_kernel(terms_ref, hidden_ref, gain_ref, inverse_ref, out_ref):
    inverse = inverse_ref[:, 0:1]
    deep = terms_ref.shape[3]
    row_dot = None
    for h in range(2):
        total = terms_ref[0, h].astype(F32)
        for j in range(1, terms_ref.shape[0]):
            total = total + terms_ref[j, h].astype(F32)
        if row_dot is None:
            share = total[TOK_DEV : TOK_DEV + 8, :]
            share = share[0:1, :TOK_DEV] + share[0:1, TOK_DEV : 2 * TOK_DEV]
            row_dot = jnp.transpose(jnp.broadcast_to(share, (TOK_DEV, TOK_DEV)))[:, 0:1]
        at = slice(h * deep, (h + 1) * deep)
        weighted = total[:TOK_DEV, :] * gain_ref[:, at].astype(F32)
        here = hidden_ref[:, at].astype(F32)
        out_ref[:, at] = (inverse * weighted - here * (inverse * inverse * inverse * row_dot / D)).astype(BF)


def lay_kernel(dest_ref, a_ref, b_ref, c_ref, d_ref, out_ref):
    rows = jnp.concatenate([a_ref[...], b_ref[...], c_ref[...], d_ref[...]], 0)
    out_ref[...] = dot_tn(dest_ref[...], rows).astype(BF)


def in_vmem(count):
    return [pl.BlockSpec(memory_space=pltpu.VMEM)] * count


def kernel_call(body, outs, ins, name, scratch=()):
    shapes = [jax.ShapeDtypeStruct(s, d) for s, d in outs]
    return pl.pallas_call(
        body,
        out_shape=shapes,
        in_specs=ins,
        out_specs=in_vmem(len(shapes)),
        scratch_shapes=list(scratch),
        compiler_params=pltpu.CompilerParams(vmem_limit_bytes=VMEM_BYTES),
        name=name,
    )


def on_device(
    hidden, gain, w_query, w_key, w_value, cotangent, seq_length, home_offset, dest_shard, dest_offset
):
    shards = lax.axis_size("dp")
    peers = lax.axis_size("tensor")
    me, z, x, c = place()
    strides = [-1, 1, shards // 2, shards // 2 + 1]
    width = hidden.shape[1]
    deep = width // 2
    q_cols = w_query.shape[1]
    k_cols = w_key.shape[1]
    q_heads = q_cols // HEAD
    rows_each = D // shards

    own = jnp.concatenate([w_query, w_key, w_value], 1)
    slab = lax.all_gather(
        own, "dp", axis=0, tiled=True,
        axis_index_groups=[[a * NX * NC + b for b in range(NX * NC)] for a in range(NZ)],
    )
    first = jnp.where(c == 0, slab[:deep], slab[deep:])
    second = jnp.where(c == 0, slab[deep:], slab[:deep])
    weights = [slab]
    for _ in range(1, NZ // 2):
        first, second = along_z(first), along_z(second)
        weights += [first, second, other_core(first), other_core(second)]
    first = along_z(first)
    weights += [first, other_core(first)]

    packed = jnp.concatenate([hidden, jnp.broadcast_to(gain[None, :], (EXTRA, width))], 0)
    packed = packed.reshape(TOK_DEV + EXTRA, 2, deep).transpose(1, 0, 2)
    rows_full = lax.all_to_all(
        jnp.broadcast_to(packed[None], (peers,) + packed.shape),
        "tensor", split_axis=0, concat_axis=0, tiled=True,
    )

    half = HEAD // 2
    freq = np.power(np.float32(ROPE_BASE), -(np.arange(half, dtype=np.float32) * np.float32(2.0 / HEAD)))
    freq = jnp.asarray(np.concatenate([freq, freq])[None, :].astype(np.float32))
    smem = [pl.BlockSpec(memory_space=pltpu.SMEM)] * 4
    square = ((TOK_DEV, TOK_DEV), F32)
    cut = ((MAXLEN, q_cols), BF)
    *cot_cuts, home, dest, cosine, sine, allowed = kernel_call(
        functools.partial(plan_kernel, strides, shards),
        [cut] * 4 + [((SLOTS * MAXLEN, TOK_DEV), BF), ((SLOTS * MAXLEN, CAP), BF)] + [square] * 3,
        smem + in_vmem(2),
        "plan",
    )(seq_length.T, home_offset.T, dest_shard.T, dest_offset.T, freq, cotangent)
    cots = [passed_along(cot_cuts[n], -s) for n, s in enumerate(strides)]

    pieces = len(weights)
    share = ((NX, NZ, rows_each, k_cols), BF)
    *attn_cuts, terms, kept, given, inverse = kernel_call(
        functools.partial(layer_kernel, q_heads, pieces),
        [cut] * 4 + [((peers, 2, TOK_DEV + EXTRA, deep), BF), share, share, square],
        in_vmem(9 + pieces),
        "layer",
        [
            pltpu.VMEM((2 * NZ, TOK_DEV, deep), BF),
            pltpu.VMEM((TOK_DEV, q_cols + 2 * k_cols), BF),
        ],
    )(rows_full, cosine, sine, allowed, home, *cots, *weights)

    summed = lax.all_to_all(terms, "tensor", split_axis=0, concat_axis=0, tiled=True)
    (grad_hidden,) = kernel_call(
        finish_kernel, [((TOK_DEV, width), BF)], in_vmem(4), "finish"
    )(summed, hidden, gain[None, :], inverse)

    attn_sent = [passed_along(attn_cuts[n], s) for n, s in enumerate(strides)]
    (attn_out,) = kernel_call(lay_kernel, [((CAP, q_cols), BF)], in_vmem(5), "lay")(dest, *attn_sent)

    pair = kept.astype(F32) + other_core(given).astype(F32)
    total = pair[0]
    for k in range(1, NX):
        total = total + moved(pair[k].astype(BF), lambda z, x, c, k=k: (z, x + k, c)).astype(F32)
    span = NZ // 2
    while span:
        upper = (z // span) % 2
        mine = jnp.where(upper == 0, total[:span], total[span:])
        theirs = jnp.where(upper == 0, total[span:], total[:span])
        if span > 1:
            theirs = theirs.astype(BF)
        total = mine + moved(theirs, lambda z, x, c, s=span: (z ^ s, x, c)).astype(F32)
        span //= 2
    grad_value_weight = total.reshape(rows_each, k_cols)
    return (attn_out, grad_hidden, grad_value_weight)


def solution(mesh):
    return jax.shard_map(
        on_device,
        mesh=mesh,
        in_specs=(P("dp", "tensor"), P("tensor")) + (P("dp", "tensor"),) * 4 + (P(),) * 4,
        out_specs=(P("dp", "tensor"), P("dp", "tensor"), P("dp", "tensor")),
        check_vma=False,
    )
```

time: 190 us -> 213 us (1.12)
  starting transfers between devices: 57.6 us -> 121 us
  waiting for transfers between devices: 73.7 us -> 29.1 us
  local copies, waits for them, and re-layouts: 4.59 us -> 27.5 us
  between operations: 14.3 us -> 1.44 us
  blocking collectives: 21.3 us -> 16.8 us
    ppermute x9 -> x29, starting transfers between devices: 43.2 us -> 106 us  [the longest x21 69.2 us: moved(): return lax.ppermute(value, 'dp', pairs)]
    all_gather x1 -> x0, waiting for transfers between devices: 55.5 us -> none  [on_device(): lax.all_gather(jnp.concatenate([w_query, w_key, w_value], 1), 'dp', axis=...]
    unnamed x21 -> x100, local copies, waits for them, and re-layouts: 0.33 us -> 25.7 us
    all_to_all x1 -> x0, blocking collectives: 21.3 us -> none  [on_device(): lax.all_to_all(pair, 'dp', split_axis=0, concat_axis=0, tiled=True, axis_...]
    ppermute x9 -> x29, waiting for transfers between devices: 8.5 us -> 29.1 us  [the longest x21 14.8 us: moved(): return lax.ppermute(value, 'dp', pairs)]
    all_gather x0 -> x1, blocking collectives: none -> 16.8 us  [on_device(): lax.all_gather(own, 'dp', axis=0, tiled=True, axis_index_groups=[[a * NX...]
    all_to_all x1, waiting for transfers between devices: 9.73 us -> 0.01 us  [on_device(): lax.all_to_all(terms, 'tensor', split_axis=0, concat_axis=0, tiled=True)]
    pallas_call x2 -> x4, Pallas kernels: 11.5 us -> 12.3 us  [the longest x1 9.12 us: on_device(): kernel_call(functools.partial(layer_kernel, q_heads, pieces), [cut] * 4 +...]
  transfers between devices with their start and end apart: 12 -> 31, of which waited for: 6 -> 10; matrix products, arithmetic and copies ran while one was open for 5% -> 1% of each run, Pallas kernels for 0% -> 1%
where the time goes in v2:
time: 213 us; the launch traced here: 211 us
  starting transfers between devices  121 us (57%)
  waiting for transfers between devices  29.1 us (14%)
  local copies, waits for them, and re-layouts  27.5 us (13%)
  blocking collectives  16.8 us (8%)
  Pallas kernels  12.3 us (6%)
  other arithmetic  2.98 us (1%)
    ppermute x21, starting transfers between devices, moved(): return lax.ppermute(value, 'dp', pairs)  69.2 us
    ppermute x8, starting transfers between devices, passed_along(): lax.ppermute(value, 'dp', [(i, (i + by) % size) for i in range(size)])  36.6 us
    unnamed x100, local copies, waits for them, and re-layouts  25.7 us
    all_gather x1, blocking collectives, on_device(): lax.all_gather(own, 'dp', axis=0, tiled=True, axis_index_groups=[[a * NX...  16.8 us
    ppermute x21, waiting for transfers between devices, moved(): return lax.ppermute(value, 'dp', pairs)  14.8 us
    ppermute x8, waiting for transfers between devices, passed_along(): lax.ppermute(value, 'dp', [(i, (i + by) % size) for i in range(size)])  14.4 us
    pallas_call x1, Pallas kernels, on_device(): kernel_call(functools.partial(layer_kernel, q_heads, pieces), [cut] * 4 +...  9.12 us
    all_to_all x1, starting transfers between devices, on_device(): lax.all_to_all(jnp.broadcast_to(packed[None], (peers,) + packed.shape), '...  7.78 us
  transfers between devices with their start and end apart: 31, of which 10 were waited for; matrix products, arithmetic and copies ran while one was open for 1% of the time, Pallas kernels for 1%

profile of v2, /device:TPU:1, one launch (start us, length us, event | category | flops | bytes accessed | tf_op | source)
XLA Modules:
  0.0 211.1 jit_solution(3969874390572936257)
XLA Ops:
  3.4 7.8 %all-to-all-start = ((bf16[8,2,144,256]{3,2,1,0:T(8,128)(2,1)}), bf16[8,2,144,256]{3,2,1,0:T(8,128)(2,1)}, u32[]{:S(2)}, u32[]{:S(2)}) async-start(bf16[8,2,144,256]{3,2,1,0:T(8,128)(2,1)} %broadcast_in_dim.7), calls=%async_computation | async-start | bytes 2359296 | tf_op jit(solution)/shard_map/all_to_all | solution.py:279
  11.2 16.8 %all_gather.3.refs_9_ = bf16[512,768]{1,0:T(8,128)(2,1)S(1)} all-gather(bf16[64,768]{1,0:T(8,128)(2,1)S(1)} %pad_maximum_fusion.1), channel_id=1, replica_groups={{0,8,16,24,32,40,48,56},{64,72,80,88,96,104,112,120},{128,136,144,152,1..., dimensions={0}, use_global_device_ids=true | all-gather | bytes 884736 | tf_op jit(solution)/shard_map/all_gather | solution.py:264
  29.0 8.4 %collective-permute-start.4 = (bf16[256,768]{1,0:T(8,128)(2,1)S(1)}, bf16[256,768]{1,0:T(8,128)(2,1)S(1)}, u32[]{:S(2)}, u32[]{:S(2)}) collective-permute-start(bf16[256,768]{1,0:T(8,128)(2,1)S(1)} %get-tuple-element.40), channel_id=1, source_target_pairs={{0,64},{8,456},{16,80},{24,472},{32,96},{40,488},{48,112},{56,504}... | collective-permute-start | bytes 1179656 | tf_op jit(solution)/shard_map/ppermute | solution.py:33
  42.0 5.0 %collective-permute-start.8 = (bf16[256,768]{1,0:T(8,128)(2,1)S(1)}, bf16[256,768]{1,0:T(8,128)(2,1)S(1)}, u32[]{:S(2)}, u32[]{:S(2)}) collective-permute-start(bf16[256,768]{1,0:T(8,128)(2,1)S(1)} %collective-permute-done.4.refs_10_), channel_id=1, source_target_pairs={{0,64},{8,456},{16,80},{24,472},{32,96},{40,488},{48,112},{56,504}... | collective-permute-start | bytes 1179656 | tf_op jit(solution)/shard_map/ppermute | solution.py:33
  47.0 4.6 %collective-permute-start.9 = (bf16[256,768]{1,0:T(8,128)(2,1)S(1)}, bf16[256,768]{1,0:T(8,128)(2,1)S(1)}, u32[]{:S(2)}, u32[]{:S(2)}) collective-permute-start(bf16[256,768]{1,0:T(8,128)(2,1)S(1)} %collective-permute-done.5.refs_11_), channel_id=1, source_target_pairs={{0,64},{8,456},{16,80},{24,472},{32,96},{40,488},{48,112},{56,504}... | collective-permute-start | bytes 1179656 | tf_op jit(solution)/shard_map/ppermute | solution.py:33
  51.7 5.0 %collective-permute-start.12 = (bf16[256,768]{1,0:T(8,128)(2,1)S(1)}, bf16[256,768]{1,0:T(8,128)(2,1)S(1)}, u32[]{:S(2)}, u32[]{:S(2)}) collective-permute-start(bf16[256,768]{1,0:T(8,128)(2,1)S(1)} %collective-permute-done.8.refs_14_), channel_id=1, source_target_pairs={{0,64},{8,456},{16,80},{24,472},{32,96},{40,488},{48,112},{56,504}... | collective-permute-start | bytes 1179656 | tf_op jit(solution)/shard_map/ppermute | solution.py:33
  61.1 3.9 %collective-permute-start.13 = (bf16[256,768]{1,0:T(8,128)(2,1)S(1)}, bf16[256,768]{1,0:T(8,128)(2,1)S(1)}, u32[]{:S(2)}, u32[]{:S(2)}) collective-permute-start(bf16[256,768]{1,0:T(8,128)(2,1)S(1)} %collective-permute-done.9.refs_15_), channel_id=1, source_target_pairs={{0,64},{8,456},{16,80},{24,472},{32,96},{40,488},{48,112},{56,504}... | collective-permute-start | bytes 1179656 | tf_op jit(solution)/shard_map/ppermute | solution.py:33
  78.0 6.7 %collective-permute-start.1 = (bf16[64,512]{1,0:T(8,128)(2,1)S(1)}, bf16[64,512]{1,0:T(8,128)(2,1)S(1)}, u32[]{:S(2)}, u32[]{:S(2)}) collective-permute-start(bf16[64,512]{1,0:T(8,128)(2,1)S(1)} %get-tuple-element.26), channel_id=1, source_target_pairs={{0,504},{8,0},{16,8},{24,16},{32,24},{40,32},{48,40},{56,48},{64,5... | collective-permute-start | bytes 196616 | tf_op jit(solution)/shard_map/ppermute | solution.py:46
  86.2 4.8 %collective-permute-start.2 = (bf16[64,512]{1,0:T(8,128)(2,1)S(1)}, bf16[64,512]{1,0:T(8,128)(2,1)S(1)}, u32[]{:S(2)}, u32[]{:S(2)}) collective-permute-start(bf16[64,512]{1,0:T(8,128)(2,1)S(1)} %get-tuple-element.27), channel_id=1, source_target_pairs={{0,256},{8,264},{16,272},{24,280},{32,288},{40,296},{48,304},{56,3... | collective-permute-start | bytes 196616 | tf_op jit(solution)/shard_map/ppermute | solution.py:46
  91.0 4.2 %collective-permute-done.2.refs_7_ = bf16[64,512]{1,0:T(8,128)(2,1)S(1)} collective-permute-done((bf16[64,512]{1,0:T(8,128)(2,1)S(1)}, bf16[64,512]{1,0:T(8,128)(2,1)S(1)}, u32[]{:S(2)}, u32[]{:S(2)}) %collective-permute-start.2) | collective-permute-done | bytes 65568 | tf_op jit(solution)/shard_map/ppermute | solution.py:46
  95.8 7.3 %collective-permute-start.3 = (bf16[64,512]{1,0:T(8,128)(2,1)S(1)}, bf16[64,512]{1,0:T(8,128)(2,1)S(1)}, u32[]{:S(2)}, u32[]{:S(2)}) collective-permute-start(bf16[64,512]{1,0:T(8,128)(2,1)S(1)} %get-tuple-element.28), channel_id=1, source_target_pairs={{0,248},{8,256},{16,264},{24,272},{32,280},{40,288},{48,296},{56,3... | collective-permute-start | bytes 196616 | tf_op jit(solution)/shard_map/ppermute | solution.py:46
  103.1 3.2 %collective-permute-done.3.refs_8_ = bf16[64,512]{1,0:T(8,128)(2,1)S(1)} collective-permute-done((bf16[64,512]{1,0:T(8,128)(2,1)S(1)}, bf16[64,512]{1,0:T(8,128)(2,1)S(1)}, u32[]{:S(2)}, u32[]{:S(2)}) %collective-permute-start.3) | collective-permute-done | bytes 65568 | tf_op jit(solution)/shard_map/ppermute | solution.py:46
  132.4 9.1 %layer.1 = (bf16[64,512]{1,0:T(8,128)(2,1)S(1)}, bf16[64,512]{1,0:T(8,128)(2,1)S(1)}, bf16[64,512]{1,0:T(8,128)(2,1)S(1)}, bf16[64,512]{1,0:T(8,128)(2,1)S(1)}, ...) custom-call(bf16[8,2,144,256]{3,2,1,0:T(8,128)(2,1)} %all-to-all-don, ...), custom_call_target="tpu_custom_call" | custom-call | tf_op jit(solution)/shard_map/layer/pallas_call | solution.py:300
  146.6 7.4 %all-to-all-start.1 = ((bf16[8,2,144,256]{3,2,1,0:T(8,128)(2,1)}), bf16[8,2,144,256]{3,2,1,0:T(8,128)(2,1)S(1)}, u32[]{:S(2)}, u32[]{:S(2)}) async-start(bf16[8,2,144,256]{3,2,1,0:T(8,128)(2,1)} %get-tuple-element.33), calls=%async_computation.1 | async-start | bytes 2359296 | tf_op jit(solution)/shard_map/all_to_all | solution.py:311
  156.1 6.7 %collective-permute-start.25 = (bf16[8,64,128]{2,1,0:T(8,128)(2,1)S(1)}, bf16[8,64,128]{2,1,0:T(8,128)(2,1)S(1)}, u32[]{:S(2)}, u32[]{:S(2)}) collective-permute-start(bf16[8,64,128]{2,1,0:T(8,128)(2,1)S(1)} %get-tuple-element.42), channel_id=1, source_target_pairs={{0,48},{8,56},{16,0},{24,8},{32,16},{40,24},{48,32},{56,40},{64,11... | collective-permute-start | bytes 393224 | tf_op jit(solution)/shard_map/ppermute | solution.py:33
  167.3 3.4 %collective-permute-done.24 = bf16[8,64,128]{2,1,0:T(8,128)(2,1)S(1)} collective-permute-done((bf16[8,64,128]{2,1,0:T(8,128)(2,1)S(1)}, bf16[8,64,128]{2,1,0:T(8,128)(2,1)S(1)}, u32[]{:S(2)}, u32[]{:S(2)}) %collective-permute-start.24) | collective-permute-done | bytes 131104 | tf_op jit(solution)/shard_map/ppermute | solution.py:33
  170.7 3.5 %collective-permute-done.23 = bf16[8,64,128]{2,1,0:T(8,128)(2,1)S(1)} collective-permute-done((bf16[8,64,128]{2,1,0:T(8,128)(2,1)S(1)}, bf16[8,64,128]{2,1,0:T(8,128)(2,1)S(1)}, u32[]{:S(2)}, u32[]{:S(2)}) %collective-permute-start.23) | collective-permute-done | bytes 131104 | tf_op jit(solution)/shard_map/ppermute | solution.py:33
  174.3 4.0 %collective-permute-start.26 = (bf16[4,64,128]{2,1,0:T(8,128)(2,1)S(1)}, bf16[4,64,128]{2,1,0:T(8,128)(2,1)S(1)}, u32[]{:S(2)}, u32[]{:S(2)}) collective-permute-start(bf16[4,64,128]{2,1,0:T(8,128)(2,1)S(1)} %select_convert_fusion), channel_id=1, source_target_pairs={{0,256},{8,264},{16,272},{24,280},{32,288},{40,296},{48,304},{56,3... | collective-permute-start | bytes 196616 | tf_op jit(solution)/shard_map/ppermute | solution.py:33
  178.4 5.3 %collective-permute-done.26 = bf16[4,64,128]{2,1,0:T(8,128)(2,1)S(1)} collective-permute-done((bf16[4,64,128]{2,1,0:T(8,128)(2,1)S(1)}, bf16[4,64,128]{2,1,0:T(8,128)(2,1)S(1)}, u32[]{:S(2)}, u32[]{:S(2)}) %collective-permute-start.26) | collective-permute-done | bytes 65568 | tf_op jit(solution)/shard_map/ppermute | solution.py:33
  183.7 3.2 %collective-permute-start.27 = (bf16[2,64,128]{2,1,0:T(8,128)(2,1)S(1)}, bf16[2,64,128]{2,1,0:T(8,128)(2,1)S(1)}, u32[]{:S(2)}, u32[]{:S(2)}) collective-permute-start(bf16[2,64,128]{2,1,0:T(8,128)(2,1)S(1)} %select_convert_fusion.1), channel_id=1, source_target_pairs={{0,128},{8,136},{16,144},{24,152},{32,160},{40,168},{48,176},{56,1... | collective-permute-start | bytes 98312 | tf_op jit(solution)/shard_map/ppermute | solution.py:33
  187.0 4.8 %collective-permute-start.18 = (bf16[64,512]{1,0:T(8,128)(2,1)S(1)}, bf16[64,512]{1,0:T(8,128)(2,1)S(1)}, u32[]{:S(2)}, u32[]{:S(2)}) collective-permute-start(bf16[64,512]{1,0:T(8,128)(2,1)S(1)} %copy-done.42), channel_id=1, source_target_pairs={{0,504},{8,0},{16,8},{24,16},{32,24},{40,32},{48,40},{56,48},{64,5... | collective-permute-start | bytes 196616 | tf_op jit(solution)/shard_map/ppermute | solution.py:46
  193.7 5.0 %collective-permute-start.20 = (bf16[64,512]{1,0:T(8,128)(2,1)S(1)}, bf16[64,512]{1,0:T(8,128)(2,1)S(1)}, u32[]{:S(2)}, u32[]{:S(2)}) collective-permute-start(bf16[64,512]{1,0:T(8,128)(2,1)S(1)} %copy-done.38), channel_id=1, source_target_pairs={{0,256},{8,264},{16,272},{24,280},{32,288},{40,296},{48,304},{56,3... | collective-permute-start | bytes 196616 | tf_op jit(solution)/shard_map/ppermute | solution.py:46
  198.7 3.1 %collective-permute-start.21 = (bf16[64,512]{1,0:T(8,128)(2,1)S(1)}, bf16[64,512]{1,0:T(8,128)(2,1)S(1)}, u32[]{:S(2)}, u32[]{:S(2)}) collective-permute-start(bf16[64,512]{1,0:T(8,128)(2,1)S(1)} %copy-done.36), channel_id=1, source_target_pairs={{0,264},{8,272},{16,280},{24,288},{32,296},{40,304},{48,312},{56,3... | collective-permute-start | bytes 196616 | tf_op jit(solution)/shard_map/ppermute | solution.py:46
  203.8 4.8 %collective-permute-done.21.d_ref = bf16[64,512]{1,0:T(8,128)(2,1)S(1)} collective-permute-done((bf16[64,512]{1,0:T(8,128)(2,1)S(1)}, bf16[64,512]{1,0:T(8,128)(2,1)S(1)}, u32[]{:S(2)}, u32[]{:S(2)}) %collective-permute-start.21) | collective-permute-done | bytes 65568 | tf_op jit(solution)/shard_map/ppermute | solution.py:46
  (159 shorter events, 71.8 us)
Async XLA Ops:
  3.4 118.4 %all-to-all-start = ((bf16[8,2,144,256]{3,2,1,0:T(8,128)(2,1)}), bf16[8,2,144,256]{3,2,1,0:T(8,128)(2,1)}, u32[]{:S(2)}, u32[]{:S(2)}) async-start(bf16[8,2,144,256]{3,2,1,0:T(8,128)(2,1)} %broadcast_in_dim.7), calls=%async_computation | async-start | bytes 2359296 | tf_op jit(solution)/shard_map/all_to_all | solution.py:279
  29.0 13.1 %collective-permute-start.4 = (bf16[256,768]{1,0:T(8,128)(2,1)S(1)}, bf16[256,768]{1,0:T(8,128)(2,1)S(1)}, u32[]{:S(2)}, u32[]{:S(2)}) collective-permute-start(bf16[256,768]{1,0:T(8,128)(2,1)S(1)} %get-tuple-element.40), channel_id=1, source_target_pairs={{0,64},{8,456},{16,80},{24,472},{32,96},{40,488},{48,112},{56,504}... | collective-permute-start | bytes 1179656 | tf_op jit(solution)/shard_map/ppermute | solution.py:33
  37.3 9.7 %collective-permute-start.5 = (bf16[256,768]{1,0:T(8,128)(2,1)S(1)}, bf16[256,768]{1,0:T(8,128)(2,1)S(1)}, u32[]{:S(2)}, u32[]{:S(2)}) collective-permute-start(bf16[256,768]{1,0:T(8,128)(2,1)S(1)} %get-tuple-element.39), channel_id=1, source_target_pairs={{0,64},{8,456},{16,80},{24,472},{32,96},{40,488},{48,112},{56,504}... | collective-permute-start | bytes 1179656 | tf_op jit(solution)/shard_map/ppermute | solution.py:33
  42.0 9.7 %collective-permute-start.8 = (bf16[256,768]{1,0:T(8,128)(2,1)S(1)}, bf16[256,768]{1,0:T(8,128)(2,1)S(1)}, u32[]{:S(2)}, u32[]{:S(2)}) collective-permute-start(bf16[256,768]{1,0:T(8,128)(2,1)S(1)} %collective-permute-done.4.refs_10_), channel_id=1, source_target_pairs={{0,64},{8,456},{16,80},{24,472},{32,96},{40,488},{48,112},{56,504}... | collective-permute-start | bytes 1179656 | tf_op jit(solution)/shard_map/ppermute | solution.py:33
  47.0 14.1 %collective-permute-start.9 = (bf16[256,768]{1,0:T(8,128)(2,1)S(1)}, bf16[256,768]{1,0:T(8,128)(2,1)S(1)}, u32[]{:S(2)}, u32[]{:S(2)}) collective-permute-start(bf16[256,768]{1,0:T(8,128)(2,1)S(1)} %collective-permute-done.5.refs_11_), channel_id=1, source_target_pairs={{0,64},{8,456},{16,80},{24,472},{32,96},{40,488},{48,112},{56,504}... | collective-permute-start | bytes 1179656 | tf_op jit(solution)/shard_map/ppermute | solution.py:33
  51.7 13.3 %collective-permute-start.12 = (bf16[256,768]{1,0:T(8,128)(2,1)S(1)}, bf16[256,768]{1,0:T(8,128)(2,1)S(1)}, u32[]{:S(2)}, u32[]{:S(2)}) collective-permute-start(bf16[256,768]{1,0:T(8,128)(2,1)S(1)} %collective-permute-done.8.refs_14_), channel_id=1, source_target_pairs={{0,64},{8,456},{16,80},{24,472},{32,96},{40,488},{48,112},{56,504}... | collective-permute-start | bytes 1179656 | tf_op jit(solution)/shard_map/ppermute | solution.py:33
  56.8 53.2 %collective-permute-start.6 = (bf16[256,768]{1,0:T(8,128)(2,1)S(1)}, bf16[256,768]{1,0:T(8,128)(2,1)S(1)}, u32[]{:S(2)}, u32[]{:S(2)}) collective-permute-start(bf16[256,768]{1,0:T(8,128)(2,1)S(1)} %collective-permute-done.4.refs_10_), channel_id=1, source_target_pairs={{0,8},{8,0},{16,24},{24,16},{32,40},{40,32},{48,56},{56,48},{64,72... | collective-permute-start | bytes 1179656 | tf_op jit(solution)/shard_map/ppermute | solution.py:33
  58.7 53.2 %collective-permute-start.7 = (bf16[256,768]{1,0:T(8,128)(2,1)S(1)}, bf16[256,768]{1,0:T(8,128)(2,1)S(1)}, u32[]{:S(2)}, u32[]{:S(2)}) collective-permute-start(bf16[256,768]{1,0:T(8,128)(2,1)S(1)} %collective-permute-done.5.refs_11_), channel_id=1, source_target_pairs={{0,8},{8,0},{16,24},{24,16},{32,40},{40,32},{48,56},{56,48},{64,72... | collective-permute-start | bytes 1179656 | tf_op jit(solution)/shard_map/ppermute | solution.py:33
  61.1 53.2 %collective-permute-start.13 = (bf16[256,768]{1,0:T(8,128)(2,1)S(1)}, bf16[256,768]{1,0:T(8,128)(2,1)S(1)}, u32[]{:S(2)}, u32[]{:S(2)}) collective-permute-start(bf16[256,768]{1,0:T(8,128)(2,1)S(1)} %collective-permute-done.9.refs_15_), channel_id=1, source_target_pairs={{0,64},{8,456},{16,80},{24,472},{32,96},{40,488},{48,112},{56,504}... | collective-permute-start | bytes 1179656 | tf_op jit(solution)/shard_map/ppermute | solution.py:33
  65.0 51.3 %collective-permute-start.16 = (bf16[256,768]{1,0:T(8,128)(2,1)S(1)}, bf16[256,768]{1,0:T(8,128)(2,1)S(1)}, u32[]{:S(2)}, u32[]{:S(2)}) collective-permute-start(bf16[256,768]{1,0:T(8,128)(2,1)S(1)} %collective-permute-done.12.refs_18_), channel_id=1, source_target_pairs={{0,64},{8,456},{16,80},{24,472},{32,96},{40,488},{48,112},{56,504}... | collective-permute-start | bytes 1179656 | tf_op jit(solution)/shard_map/ppermute | solution.py:33
  86.2 9.0 %collective-permute-start.2 = (bf16[64,512]{1,0:T(8,128)(2,1)S(1)}, bf16[64,512]{1,0:T(8,128)(2,1)S(1)}, u32[]{:S(2)}, u32[]{:S(2)}) collective-permute-start(bf16[64,512]{1,0:T(8,128)(2,1)S(1)} %get-tuple-element.27), channel_id=1, source_target_pairs={{0,256},{8,264},{16,272},{24,280},{32,288},{40,296},{48,304},{56,3... | collective-permute-start | bytes 196616 | tf_op jit(solution)/shard_map/ppermute | solution.py:46
  95.8 10.5 %collective-permute-start.3 = (bf16[64,512]{1,0:T(8,128)(2,1)S(1)}, bf16[64,512]{1,0:T(8,128)(2,1)S(1)}, u32[]{:S(2)}, u32[]{:S(2)}) collective-permute-start(bf16[64,512]{1,0:T(8,128)(2,1)S(1)} %get-tuple-element.28), channel_id=1, source_target_pairs={{0,248},{8,256},{16,264},{24,272},{32,280},{40,288},{48,296},{56,3... | collective-permute-start | bytes 196616 | tf_op jit(solution)/shard_map/ppermute | solution.py:46
  106.9 11.8 %collective-permute-start.10 = (bf16[256,768]{1,0:T(8,128)(2,1)S(1)}, bf16[256,768]{1,0:T(8,128)(2,1)S(1)}, u32[]{:S(2)}, u32[]{:S(2)}) collective-permute-start(bf16[256,768]{1,0:T(8,128)(2,1)S(1)} %collective-permute-done.8.refs_14_), channel_id=1, source_target_pairs={{0,8},{8,0},{16,24},{24,16},{32,40},{40,32},{48,56},{56,48},{64,72... | collective-permute-start | bytes 1179656 | tf_op jit(solution)/shard_map/ppermute | solution.py:33
  110.0 9.5 %collective-permute-start.11 = (bf16[256,768]{1,0:T(8,128)(2,1)S(1)}, bf16[256,768]{1,0:T(8,128)(2,1)S(1)}, u32[]{:S(2)}, u32[]{:S(2)}) collective-permute-start(bf16[256,768]{1,0:T(8,128)(2,1)S(1)} %collective-permute-done.9.refs_15_), channel_id=1, source_target_pairs={{0,8},{8,0},{16,24},{24,16},{32,40},{40,32},{48,56},{56,48},{64,72... | collective-permute-start | bytes 1179656 | tf_op jit(solution)/shard_map/ppermute | solution.py:33
  144.7 9.3 %collective-permute-start.22 = (bf16[4,8,64,128]{3,2,1,0:T(8,128)(2,1)}, bf16[4,8,64,128]{3,2,1,0:T(8,128)(2,1)S(1)}, u32[]{:S(2)}, u32[]{:S(2)}) collective-permute-start(bf16[4,8,64,128]{3,2,1,0:T(8,128)(2,1)} %get-tuple-element.36), channel_id=1, source_target_pairs={{0,8},{8,0},{16,24},{24,16},{32,40},{40,32},{48,56},{56,48},{64,72... | collective-permute-start | bytes 1572872 | tf_op jit(solution)/shard_map/ppermute | solution.py:33
  146.6 63.6 %all-to-all-start.1 = ((bf16[8,2,144,256]{3,2,1,0:T(8,128)(2,1)}), bf16[8,2,144,256]{3,2,1,0:T(8,128)(2,1)S(1)}, u32[]{:S(2)}, u32[]{:S(2)}) async-start(bf16[8,2,144,256]{3,2,1,0:T(8,128)(2,1)} %get-tuple-element.33), calls=%async_computation.1 | async-start | bytes 2359296 | tf_op jit(solution)/shard_map/all_to_all | solution.py:311
  156.1 11.2 %collective-permute-start.25 = (bf16[8,64,128]{2,1,0:T(8,128)(2,1)S(1)}, bf16[8,64,128]{2,1,0:T(8,128)(2,1)S(1)}, u32[]{:S(2)}, u32[]{:S(2)}) collective-permute-start(bf16[8,64,128]{2,1,0:T(8,128)(2,1)S(1)} %get-tuple-element.42), channel_id=1, source_target_pairs={{0,48},{8,56},{16,0},{24,8},{32,16},{40,24},{48,32},{56,40},{64,11... | collective-permute-start | bytes 393224 | tf_op jit(solution)/shard_map/ppermute | solution.py:33
  164.8 9.4 %collective-permute-start.23 = (bf16[8,64,128]{2,1,0:T(8,128)(2,1)S(1)}, bf16[8,64,128]{2,1,0:T(8,128)(2,1)S(1)}, u32[]{:S(2)}, u32[]{:S(2)}) collective-permute-start(bf16[8,64,128]{2,1,0:T(8,128)(2,1)S(1)} %get-tuple-element.41), channel_id=1, source_target_pairs={{0,16},{8,24},{16,32},{24,40},{32,48},{40,56},{48,0},{56,8},{64,80... | collective-permute-start | bytes 393224 | tf_op jit(solution)/shard_map/ppermute | solution.py:33
  174.3 9.3 %collective-permute-start.26 = (bf16[4,64,128]{2,1,0:T(8,128)(2,1)S(1)}, bf16[4,64,128]{2,1,0:T(8,128)(2,1)S(1)}, u32[]{:S(2)}, u32[]{:S(2)}) collective-permute-start(bf16[4,64,128]{2,1,0:T(8,128)(2,1)S(1)} %select_convert_fusion), channel_id=1, source_target_pairs={{0,256},{8,264},{16,272},{24,280},{32,288},{40,296},{48,304},{56,3... | collective-permute-start | bytes 196616 | tf_op jit(solution)/shard_map/ppermute | solution.py:33
  183.7 18.1 %collective-permute-start.27 = (bf16[2,64,128]{2,1,0:T(8,128)(2,1)S(1)}, bf16[2,64,128]{2,1,0:T(8,128)(2,1)S(1)}, u32[]{:S(2)}, u32[]{:S(2)}) collective-permute-start(bf16[2,64,128]{2,1,0:T(8,128)(2,1)S(1)} %select_convert_fusion.1), channel_id=1, source_target_pairs={{0,128},{8,136},{16,144},{24,152},{32,160},{40,168},{48,176},{56,1... | collective-permute-start | bytes 98312 | tf_op jit(solution)/shard_map/ppermute | solution.py:33
  187.0 16.8 %collective-permute-start.18 = (bf16[64,512]{1,0:T(8,128)(2,1)S(1)}, bf16[64,512]{1,0:T(8,128)(2,1)S(1)}, u32[]{:S(2)}, u32[]{:S(2)}) collective-permute-start(bf16[64,512]{1,0:T(8,128)(2,1)S(1)} %copy-done.42), channel_id=1, source_target_pairs={{0,504},{8,0},{16,8},{24,16},{32,24},{40,32},{48,40},{56,48},{64,5... | collective-permute-start | bytes 196616 | tf_op jit(solution)/shard_map/ppermute | solution.py:46
  191.7 12.1 %collective-permute-start.19 = (bf16[64,512]{1,0:T(8,128)(2,1)S(1)}, bf16[64,512]{1,0:T(8,128)(2,1)S(1)}, u32[]{:S(2)}, u32[]{:S(2)}) collective-permute-start(bf16[64,512]{1,0:T(8,128)(2,1)S(1)} %copy-done.40), channel_id=1, source_target_pairs={{0,8},{8,16},{16,24},{24,32},{32,40},{40,48},{48,56},{56,64},{64,7... | collective-permute-start | bytes 196616 | tf_op jit(solution)/shard_map/ppermute | solution.py:46
  193.7 10.1 %collective-permute-start.20 = (bf16[64,512]{1,0:T(8,128)(2,1)S(1)}, bf16[64,512]{1,0:T(8,128)(2,1)S(1)}, u32[]{:S(2)}, u32[]{:S(2)}) collective-permute-start(bf16[64,512]{1,0:T(8,128)(2,1)S(1)} %copy-done.38), channel_id=1, source_target_pairs={{0,256},{8,264},{16,272},{24,280},{32,288},{40,296},{48,304},{56,3... | collective-permute-start | bytes 196616 | tf_op jit(solution)/shard_map/ppermute | solution.py:46
  198.7 9.9 %collective-permute-start.21 = (bf16[64,512]{1,0:T(8,128)(2,1)S(1)}, bf16[64,512]{1,0:T(8,128)(2,1)S(1)}, u32[]{:S(2)}, u32[]{:S(2)}) collective-permute-start(bf16[64,512]{1,0:T(8,128)(2,1)S(1)} %copy-done.36), channel_id=1, source_target_pairs={{0,264},{8,272},{16,280},{24,288},{32,296},{40,304},{48,312},{56,3... | collective-permute-start | bytes 196616 | tf_op jit(solution)/shard_map/ppermute | solution.py:46
  (57 other events, 647.2 us)

commit v3 on v2

--- a/solution.py
+++ b/solution.py
@@ -20,7 +20,7 @@
 NZ, NX, NC = 8, 4, 2
 BF = jnp.bfloat16
 F32 = jnp.float32
-VMEM_BYTES = 48 * 1024 * 1024
+MIB = 1024 * 1024
 
 
 def moved(value, where):
@@ -46,6 +46,10 @@
     return lax.ppermute(value, "dp", [(i, (i + by) % size) for i in range(size)])
 
 
+def tied(*values):
+    return lax.optimization_barrier(values)
+
+
 def dot_nn(a, b):
     return lax.dot_general(a, b, (((1,), (0,)), ((), ())), preferred_element_type=F32)
 
@@ -64,16 +68,15 @@
 
 
 def plan_kernel(
-    strides, shards,
-    len_ref, off_ref, shard_ref, start_ref, freq_ref, cotangent_ref,
-    cut0_ref, cut1_ref, cut2_ref, cut3_ref, home_ref, dest_ref, cos_ref, sin_ref, allowed_ref,
+    strides, shards, get, put, send, smem, extra,
 ):
+    len_ref, off_ref, shard_ref, start_ref = smem
+    home_ref, dest_ref, cos_ref, sin_ref, allowed_ref = [put(SLOTS + i) for i in range(5)]
     me = lax.axis_index("dp")
     rows = lax.broadcasted_iota(jnp.int32, (TOK_DEV, TOK_DEV), 0)
     cols = lax.broadcasted_iota(jnp.int32, (TOK_DEV, TOK_DEV), 1)
     row_seq, row_pos = jnp.zeros_like(rows), jnp.zeros_like(rows)
     col_seq, col_pos = jnp.zeros_like(rows), jnp.zeros_like(rows)
-    cuts = (cut0_ref, cut1_ref, cut2_ref, cut3_ref)
     for e, stride in enumerate(strides):
         target = lax.rem(me + stride + shards, shards)
         source = lax.rem(me - stride + shards, shards)
@@ -102,20 +105,21 @@
         r = lax.broadcasted_iota(jnp.int32, (MAXLEN, CAP), 1)
         dest = jnp.where((r == t + in_start) & (t < in_len), 1.0, 0.0).astype(BF)
         dest_ref[at, :] = dest
-        cuts[e][...] = dot_nn(dest, cotangent_ref[...]).astype(BF)
+        put(e)[...] = dot_nn(dest, get(1)[...]).astype(BF)
+        send(e)
     allowed_ref[...] = jnp.where((row_seq == col_seq) & (col_pos <= row_pos), 1.0, 0.0)
-    angles = row_pos.astype(F32) * freq_ref[...]
+    angles = row_pos.astype(F32) * get(0)[...]
     cos_ref[...] = jnp.cos(angles)
     sine = jnp.sin(angles)
     sin_ref[...] = jnp.where(cols < HEAD // 2, -sine, sine)
 
 
-def layer_kernel(q_heads, pieces, *refs):
-    rows_ref, cos_ref, sin_ref, allowed_ref, home_ref = refs[:5]
-    cot_refs = refs[5:9]
-    w_refs = refs[9 : 9 + pieces]
-    cut0_ref, cut1_ref, cut2_ref, cut3_ref, terms_ref, kept_ref, given_ref, inverse_ref = refs[9 + pieces : 17 + pieces]
-    normed_ref, grads_ref = refs[17 + pieces :]
+def layer_kernel(q_heads, pieces, peers, get, put, send, smem, extra):
+    normed_ref, grads_ref, terms_ref = extra
+    kept_ref, given_ref, inverse_ref = [put(SLOTS + i) for i in range(3)]
+    out_at = SLOTS + 3
+    peer = lax.axis_index("tensor")
+    w_refs = list(range(9, 9 + pieces))
     _, z, x, c = place()
     up = 1 - 2 * c
     where = [(z, 0, w_refs[0], 0), (z, 1, w_refs[0], 256)]
@@ -130,6 +134,7 @@
     far = lax.rem(z + NZ // 2, NZ)
     where.append((far, c, w_refs[pieces - 2], 0))
     where.append((far, 1 - c, w_refs[pieces - 1], 0))
+    rows_ref = get(0)
     deep = rows_ref.shape[3]
     kv_at = q_heads * HEAD
     squares = jnp.zeros((TOK_DEV, 1), F32)
@@ -139,18 +144,18 @@
             squares = squares + jnp.sum(part * part, 1, keepdims=True)
     inverse = lax.rsqrt(squares / D + EPSILON)
     inverse_ref[...] = jnp.broadcast_to(inverse, inverse_ref.shape)
-    projected = jnp.zeros((TOK_DEV, w_refs[0].shape[1]), F32)
+    projected = jnp.zeros((TOK_DEV, kv_at + 2 * HEAD), F32)
     for n, (block, half, w_ref, at) in enumerate(where):
         gain = rows_ref[block, half, TOK_DEV:, :].astype(F32)[0:1, :]
         part = (rows_ref[block, half, :TOK_DEV, :].astype(F32) * inverse * gain).astype(BF)
         normed_ref[n] = part
-        projected = projected + dot_nn(part, w_ref[at : at + deep, :])
-    cosine = cos_ref[...]
-    sine = sin_ref[...]
+        projected = projected + dot_nn(part, get(w_ref)[at : at + deep, :])
+    cosine = get(1)[...]
+    sine = get(2)[...]
     factor = HEAD ** (-0.5)
-    allowed = allowed_ref[...] > 0.5
-    home = home_ref[...]
-    cot = jnp.concatenate([ref[...] for ref in cot_refs], 0)
+    allowed = get(3)[...] > 0.5
+    home = get(4)[...]
+    cot = jnp.concatenate([get(5 + e)[...] for e in range(SLOTS)], 0)
     cot = dot_tn(home, cot).astype(BF)
     key_raw = projected[:, kv_at : kv_at + HEAD]
     value_raw = projected[:, kv_at + HEAD :]
@@ -159,7 +164,6 @@
     grad_key = jnp.zeros((TOK_DEV, HEAD), F32)
     grad_value = jnp.zeros((TOK_DEV, HEAD), F32)
     dots = jnp.zeros((TOK_DEV, HEAD), F32)
-    cuts = (cut0_ref, cut1_ref, cut2_ref, cut3_ref)
     for g in range(q_heads):
         at = slice(g * HEAD, (g + 1) * HEAD)
         query_raw = projected[:, at]
@@ -171,7 +175,7 @@
         mixed = dot_nn(probs_low, value).astype(BF)
         mixed = dot_nn(home, mixed).astype(BF)
         for e in range(SLOTS):
-            cuts[e][:, at] = mixed[e * MAXLEN : (e + 1) * MAXLEN, :]
+            put(e)[:, at] = mixed[e * MAXLEN : (e + 1) * MAXLEN, :]
         grad_out = cot[:, at]
         grad_value = grad_value + dot_tn(probs_low, grad_out)
         grad_probs = dot_nt(grad_out, value)
@@ -187,6 +191,8 @@
     grads_ref[:, kv_at : kv_at + HEAD] = grad_key
     grads_ref[:, kv_at + HEAD :] = grad_value
     dots = dots + grad_key.astype(F32) * key_raw + grad_value.astype(F32) * value_raw
+    for e in range(SLOTS):
+        send(e)
     share = jnp.sum(dots, 1, keepdims=True) / inverse
     share = jnp.transpose(jnp.broadcast_to(share, (TOK_DEV, TOK_DEV)))[0:EXTRA, :]
     high = share.astype(BF)
@@ -198,22 +204,29 @@
         for pair in range(2):
             low_rows = found[pair * 128 : pair * 128 + 64, :]
             high_rows = found[pair * 128 + 64 : (pair + 1) * 128, :]
-            away = lax.rem(2 * half + pair - x + NX, NX)
-            kept_ref[away, block] = jnp.where(c == 0, low_rows, high_rows)
-            given_ref[away, block] = jnp.where(c == 0, high_rows, low_rows)
+            owner = block * NX + 2 * half + pair
+            kept_ref[owner] = jnp.where(c == 0, low_rows, high_rows)
+            given_ref[owner] = jnp.where(c == 0, high_rows, low_rows)
+    for i in range(3):
+        send(SLOTS + i)
     for n, (block, half, w_ref, at) in enumerate(where):
-        terms_ref[block, half, :TOK_DEV, :] = dot_nt(grads, w_ref[at : at + deep, :]).astype(BF)
+        terms_ref[block, half, :TOK_DEV, :] = dot_nt(grads, get(w_ref)[at : at + deep, :]).astype(BF)
         terms_ref[block, half, TOK_DEV:, :] = tail
-
-
-def finish_kernel(terms_ref, hidden_ref, gain_ref, inverse_ref, out_ref):
-    inverse = inverse_ref[:, 0:1]
-    deep = terms_ref.shape[3]
+    for k in range(peers):
+        put(out_at + k)[...] = terms_ref[lax.rem(peer + k, peers)]
+        send(out_at + k)
+
+
+def finish_kernel(peers, get, put, send, smem, extra):
+    hidden_ref, gain_ref, out_ref = get(0), get(1), put(0)
+    inverse = get(2)[:, 0:1]
+    term_refs = [get(3 + k) for k in range(peers)]
+    deep = term_refs[0].shape[2]
     row_dot = None
     for h in range(2):
-        total = terms_ref[0, h].astype(F32)
-        for j in range(1, terms_ref.shape[0]):
-            total = total + terms_ref[j, h].astype(F32)
+        total = term_refs[0][h].astype(F32)
+        for ref in term_refs[1:]:
+            total = total + ref[h].astype(F32)
         if row_dot is None:
             share = total[TOK_DEV : TOK_DEV + 8, :]
             share = share[0:1, :TOK_DEV] + share[0:1, TOK_DEV : 2 * TOK_DEV]
@@ -224,26 +237,61 @@
         out_ref[:, at] = (inverse * weighted - here * (inverse * inverse * inverse * row_dot / D)).astype(BF)
 
 
-def lay_kernel(dest_ref, a_ref, b_ref, c_ref, d_ref, out_ref):
-    rows = jnp.concatenate([a_ref[...], b_ref[...], c_ref[...], d_ref[...]], 0)
-    out_ref[...] = dot_tn(dest_ref[...], rows).astype(BF)
-
-
-def in_vmem(count):
-    return [pl.BlockSpec(memory_space=pltpu.VMEM)] * count
-
-
-def kernel_call(body, outs, ins, name, scratch=()):
+def lay_kernel(get, put, send, smem, extra):
+    rows = jnp.concatenate([get(1 + e)[...] for e in range(SLOTS)], 0)
+    put(0)[...] = dot_tn(get(0)[...], rows).astype(BF)
+
+
+def kernel_call(body, outs, args, name, mib, scalars=0, scratch=()):
     shapes = [jax.ShapeDtypeStruct(s, d) for s, d in outs]
+    arrays = args[scalars:]
+    n_in, n_out = len(arrays), len(shapes)
+
+    def kernel(*refs):
+        smem, refs = refs[:scalars], refs[scalars:]
+        ins, refs = refs[:n_in], refs[n_in:]
+        out, refs = refs[:n_out], refs[n_out:]
+        in_buf, refs = refs[:n_in], refs[n_in:]
+        out_buf, refs = refs[:n_out], refs[n_out:]
+        in_sem, out_sem, extra = refs[0], refs[1], refs[2:]
+        loads = [pltpu.make_async_copy(ins[i], in_buf[i], in_sem.at[i]) for i in range(n_in)]
+        stores = [pltpu.make_async_copy(out_buf[i], out[i], out_sem.at[i]) for i in range(n_out)]
+        for load in loads:
+            load.start()
+        waited, sent = set(), set()
+
+        def get(i):
+            if i not in waited:
+                waited.add(i)
+                loads[i].wait()
+            return in_buf[i]
+
+        def send(i):
+            if i not in sent:
+                sent.add(i)
+                stores[i].start()
+
+        body(get, lambda i: out_buf[i], send, smem, extra)
+        for i in range(n_in):
+            get(i)
+        for i in range(n_out):
+            send(i)
+        for store in stores:
+            store.wait()
+
+    hbm = pl.BlockSpec(memory_space=pltpu.HBM)
     return pl.pallas_call(
-        body,
+        kernel,
         out_shape=shapes,
-        in_specs=ins,
-        out_specs=in_vmem(len(shapes)),
-        scratch_shapes=list(scratch),
-        compiler_params=pltpu.CompilerParams(vmem_limit_bytes=VMEM_BYTES),
+        in_specs=[pl.BlockSpec(memory_space=pltpu.SMEM)] * scalars + [hbm] * n_in,
+        out_specs=[hbm] * n_out,
+        scratch_shapes=[pltpu.VMEM(v.shape, v.dtype) for v in arrays]
+        + [pltpu.VMEM(v.shape, v.dtype) for v in shapes]
+        + [pltpu.SemaphoreType.DMA((n_in,)), pltpu.SemaphoreType.DMA((n_out,))]
+        + list(scratch),
+        compiler_params=pltpu.CompilerParams(vmem_limit_bytes=mib * MIB),
         name=name,
-    )
+    )(*args)
 
 
 def on_device(
@@ -267,69 +315,79 @@
     )
     first = jnp.where(c == 0, slab[:deep], slab[deep:])
     second = jnp.where(c == 0, slab[deep:], slab[:deep])
-    weights = [slab]
-    for _ in range(1, NZ // 2):
-        first, second = along_z(first), along_z(second)
-        weights += [first, second, other_core(first), other_core(second)]
-    first = along_z(first)
-    weights += [first, other_core(first)]
-
-    packed = jnp.concatenate([hidden, jnp.broadcast_to(gain[None, :], (EXTRA, width))], 0)
-    packed = packed.reshape(TOK_DEV + EXTRA, 2, deep).transpose(1, 0, 2)
-    rows_full = lax.all_to_all(
-        jnp.broadcast_to(packed[None], (peers,) + packed.shape),
-        "tensor", split_axis=0, concat_axis=0, tiled=True,
-    )
 
     half = HEAD // 2
     freq = np.power(np.float32(ROPE_BASE), -(np.arange(half, dtype=np.float32) * np.float32(2.0 / HEAD)))
     freq = jnp.asarray(np.concatenate([freq, freq])[None, :].astype(np.float32))
-    smem = [pl.BlockSpec(memory_space=pltpu.SMEM)] * 4
     square = ((TOK_DEV, TOK_DEV), F32)
     cut = ((MAXLEN, q_cols), BF)
+    slab, cotangent = tied(slab, cotangent)
     *cot_cuts, home, dest, cosine, sine, allowed = kernel_call(
         functools.partial(plan_kernel, strides, shards),
         [cut] * 4 + [((SLOTS * MAXLEN, TOK_DEV), BF), ((SLOTS * MAXLEN, CAP), BF)] + [square] * 3,
-        smem + in_vmem(2),
-        "plan",
-    )(seq_length.T, home_offset.T, dest_shard.T, dest_offset.T, freq, cotangent)
-    cots = [passed_along(cot_cuts[n], -s) for n, s in enumerate(strides)]
+        [seq_length.T, home_offset.T, dest_shard.T, dest_offset.T, freq, cotangent],
+        "plan", 60, 4,
+    )
+    packed = jnp.concatenate([hidden, jnp.broadcast_to(gain[None, :], (EXTRA, width))], 0)
+    packed = packed.reshape(TOK_DEV + EXTRA, 2, deep).transpose(1, 0, 2)
+    packed = jnp.broadcast_to(packed[None], (peers,) + packed.shape)
+
+    def sent_home(n):
+        return passed_along(cot_cuts[n], -strides[n])
+
+    weights, cots = [slab], []
+    first, second, *landed, packed = tied(
+        along_z(first), along_z(second), sent_home(0), sent_home(1), sent_home(2), packed
+    )
+    cots += landed
+    rows_full = lax.all_to_all(packed, "tensor", split_axis=0, concat_axis=0, tiled=True)
+    weights += [first, second]
+    first, second, *landed = tied(
+        along_z(first), along_z(second), other_core(first), other_core(second)
+    )
+    weights += landed + [first, second]
+    first, second, *landed = tied(
+        along_z(first), along_z(second), other_core(first), other_core(second)
+    )
+    weights += landed + [first, second]
+    first, *landed, last = tied(
+        along_z(first), other_core(first), other_core(second), sent_home(3)
+    )
+    cots.append(last)
+    weights += landed + [first, other_core(first)]
 
     pieces = len(weights)
-    share = ((NX, NZ, rows_each, k_cols), BF)
-    *attn_cuts, terms, kept, given, inverse = kernel_call(
-        functools.partial(layer_kernel, q_heads, pieces),
-        [cut] * 4 + [((peers, 2, TOK_DEV + EXTRA, deep), BF), share, share, square],
-        in_vmem(9 + pieces),
-        "layer",
+    share = ((NZ * NX, rows_each, k_cols), BF)
+    block = ((2, TOK_DEV + EXTRA, deep), BF)
+    *attn_cuts, kept, given, inverse, t0, t1, t2, t3, t4, t5, t6, t7 = kernel_call(
+        functools.partial(layer_kernel, q_heads, pieces, peers),
+        [cut] * 4 + [share, share, square] + [block] * peers,
+        [rows_full, cosine, sine, allowed, home, *cots, *weights],
+        "layer", 60, 0,
         [
             pltpu.VMEM((2 * NZ, TOK_DEV, deep), BF),
             pltpu.VMEM((TOK_DEV, q_cols + 2 * k_cols), BF),
+            pltpu.VMEM((peers, 2, TOK_DEV + EXTRA, deep), BF),
         ],
-    )(rows_full, cosine, sine, allowed, home, *cots, *weights)
-
-    summed = lax.all_to_all(terms, "tensor", split_axis=0, concat_axis=0, tiled=True)
+    )
+
+    pair = (kept.astype(F32) + other_core(given).astype(F32)).astype(BF)
+    terms = [t0] + [
+        lax.ppermute(t, "tensor", [(i, (i + k) % peers) for i in range(peers)])
+        for k, t in enumerate((t1, t2, t3, t4, t5, t6, t7), 1)
+    ]
+    terms[1], terms[2], pair, *attn_cuts = tied(terms[1], terms[2], pair, *attn_cuts)
+    parts = lax.all_to_all(
+        pair, "dp", split_axis=0, concat_axis=0, tiled=True,
+        axis_index_groups=[list(range(b, shards, NC)) for b in range(NC)],
+    )
+    grad_value_weight = jnp.sum(parts.astype(F32), 0)
     (grad_hidden,) = kernel_call(
-        finish_kernel, [((TOK_DEV, width), BF)], in_vmem(4), "finish"
-    )(summed, hidden, gain[None, :], inverse)
-
+        functools.partial(finish_kernel, peers), [((TOK_DEV, width), BF)],
+        [hidden, gain[None, :], inverse, *terms], "finish", 8,
+    )
     attn_sent = [passed_along(attn_cuts[n], s) for n, s in enumerate(strides)]
-    (attn_out,) = kernel_call(lay_kernel, [((CAP, q_cols), BF)], in_vmem(5), "lay")(dest, *attn_sent)
-
-    pair = kept.astype(F32) + other_core(given).astype(F32)
-    total = pair[0]
-    for k in range(1, NX):
-        total = total + moved(pair[k].astype(BF), lambda z, x, c, k=k: (z, x + k, c)).astype(F32)
-    span = NZ // 2
-    while span:
-        upper = (z // span) % 2
-        mine = jnp.where(upper == 0, total[:span], total[span:])
-        theirs = jnp.where(upper == 0, total[span:], total[:span])
-        if span > 1:
-            theirs = theirs.astype(BF)
-        total = mine + moved(theirs, lambda z, x, c, s=span: (z ^ s, x, c)).astype(F32)
-        span //= 2
-    grad_value_weight = total.reshape(rows_each, k_cols)
+    (attn_out,) = kernel_call(lay_kernel, [((CAP, q_cols), BF)], [dest, *attn_sent], "lay", 8)
     return (attn_out, grad_hidden, grad_value_weight)
 
 

time: 213 us -> 196 us (0.920)
  local copies, waits for them, and re-layouts: 27.5 us -> 2.38 us
  waiting for transfers between devices: 29.1 us -> 15.9 us
  starting transfers between devices: 121 us -> 131 us
  Pallas kernels: 12.3 us -> 17.3 us
  blocking collectives: 16.8 us -> 20.3 us
    ppermute x0 -> x7, starting transfers between devices: none -> 29.2 us  [on_device(): lax.ppermute(t, 'tensor', [(i, (i + k) % peers) for i in range(peers)])]
    unnamed x100 -> x68, local copies, waits for them, and re-layouts: 25.7 us -> 1.14 us
    ppermute x21 -> x15, starting transfers between devices: 69.2 us -> 47.8 us  [moved(): return lax.ppermute(value, 'dp', pairs)]
    ppermute x21 -> x15, waiting for transfers between devices: 14.8 us -> 5.08 us  [moved(): return lax.ppermute(value, 'dp', pairs)]
    ppermute x8, waiting for transfers between devices: 14.4 us -> 6.3 us  [passed_along(): lax.ppermute(value, 'dp', [(i, (i + by) % size) for i in range(size)])]
    pallas_call x4, Pallas kernels: 12.3 us -> 17.3 us  [kernel_call(): pl.pallas_call(kernel, out_shape=shapes, in_specs=[pl.BlockSpec(memory_sp...]
    ppermute x0 -> x7, waiting for transfers between devices: none -> 4.5 us  [on_device(): lax.ppermute(t, 'tensor', [(i, (i + k) % peers) for i in range(peers)])]
    all_gather x1, blocking collectives: 16.8 us -> 20.3 us  [on_device(): lax.all_gather(own, 'dp', axis=0, tiled=True, axis_index_groups=[[a * NX...]
  transfers between devices with their start and end apart: 31 -> 32, of which waited for: 10 -> 8; matrix products, arithmetic and copies ran while one was open for 1% -> 1% of each run, Pallas kernels for 1% -> 4%
where the time goes in v3:
time: 196 us; the launch traced here: 193 us
  starting transfers between devices  131 us (67%)
  blocking collectives  20.3 us (10%)
  Pallas kernels  17.3 us (9%)
  waiting for transfers between devices  15.9 us (8%)
  other arithmetic  3.85 us (2%)
  local copies, waits for them, and re-layouts  2.38 us (1%)
    ppermute x15, starting transfers between devices, moved(): return lax.ppermute(value, 'dp', pairs)  47.8 us
    ppermute x8, starting transfers between devices, passed_along(): lax.ppermute(value, 'dp', [(i, (i + by) % size) for i in range(size)])  39.2 us
    ppermute x7, starting transfers between devices, on_device(): lax.ppermute(t, 'tensor', [(i, (i + k) % peers) for i in range(peers)])  29.2 us
    all_gather x1, blocking collectives, on_device(): lax.all_gather(own, 'dp', axis=0, tiled=True, axis_index_groups=[[a * NX...  20.3 us
    pallas_call x4, Pallas kernels, kernel_call(): pl.pallas_call(kernel, out_shape=shapes, in_specs=[pl.BlockSpec(memory_sp...  17.3 us
    all_to_all x1, starting transfers between devices, on_device(): lax.all_to_all(pair, 'dp', split_axis=0, concat_axis=0, tiled=True, axis_...  8.22 us
    all_to_all x1, starting transfers between devices, on_device(): lax.all_to_all(packed, 'tensor', split_axis=0, concat_axis=0, tiled=True)  6.96 us
    ppermute x8, waiting for transfers between devices, passed_along(): lax.ppermute(value, 'dp', [(i, (i + by) % size) for i in range(size)])  6.3 us
  transfers between devices with their start and end apart: 32, of which 8 were waited for; matrix products, arithmetic and copies ran while one was open for 1% of the time, Pallas kernels for 4%

profile of v3, /device:TPU:1, one launch (start us, length us, event | category | flops | bytes accessed | tf_op | source)
XLA Modules:
  0.0 192.7 jit_solution(15611668001391115642)
XLA Ops:
  1.6 20.3 %all_gather.3.refs_9_ = bf16[512,768]{1,0:T(8,128)(2,1)S(1)} all-gather(bf16[64,768]{1,0:T(8,128)(2,1)S(1)} %pad_maximum_fusion.1), channel_id=1, replica_groups={{0,8,16,24,32,40,48,56},{64,72,80,88,96,104,112,120},{128,136,144,152,1..., dimensions={0}, use_global_device_ids=true | all-gather | bytes 884736 | tf_op jit(solution)/shard_map/all_gather | solution.py:312
  21.9 5.6 %collective-permute-start = (bf16[256,768]{1,0:T(8,128)(2,1)S(1)}, bf16[256,768]{1,0:T(8,128)(2,1)S(1)}, u32[]{:S(2)}, u32[]{:S(2)}) collective-permute-start(bf16[256,768]{1,0:T(8,128)(2,1)S(1)} %get-tuple-element.106), channel_id=1, source_target_pairs={{0,64},{8,456},{16,80},{24,472},{32,96},{40,488},{48,112},{56,504}... | collective-permute-start | bytes 1179656 | tf_op jit(solution)/shard_map/ppermute | solution.py:33
  37.2 5.1 %collective-permute-start.4 = (bf16[64,512]{1,0:T(8,128)(2,1)}, bf16[64,512]{1,0:T(8,128)(2,1)S(1)}, u32[]{:S(2)}, u32[]{:S(2)}) collective-permute-start(bf16[64,512]{1,0:T(8,128)(2,1)} %get-tuple-element.58), channel_id=1, source_target_pairs={{0,256},{8,264},{16,272},{24,280},{32,288},{40,296},{48,304},{56,3... | collective-permute-start | bytes 196616 | tf_op jit(solution)/shard_map/ppermute | solution.py:46
  42.4 3.9 %collective-permute-done.4.refs_7_ = bf16[64,512]{1,0:T(8,128)(2,1)S(1)} collective-permute-done((bf16[64,512]{1,0:T(8,128)(2,1)}, bf16[64,512]{1,0:T(8,128)(2,1)S(1)}, u32[]{:S(2)}, u32[]{:S(2)}) %collective-permute-start.4) | collective-permute-done | bytes 65568 | tf_op jit(solution)/shard_map/ppermute | solution.py:46
  47.6 7.0 %all-to-all-start = ((bf16[8,2,144,256]{3,2,1,0:T(8,128)(2,1)}), bf16[8,2,144,256]{3,2,1,0:T(8,128)(2,1)S(1)}, u32[]{:S(2)}, u32[]{:S(2)}) async-start(bf16[8,2,144,256]{3,2,1,0:T(8,128)(2,1)} %broadcast_in_dim.7), calls=%async_computation | async-start | bytes 2359296 | tf_op jit(solution)/shard_map/all_to_all | solution.py:343
  57.2 3.2 %collective-permute-start.6 = (bf16[256,768]{1,0:T(8,128)(2,1)S(1)}, bf16[256,768]{1,0:T(8,128)(2,1)S(1)}, u32[]{:S(2)}, u32[]{:S(2)}) collective-permute-start(bf16[256,768]{1,0:T(8,128)(2,1)S(1)} %collective-permute-done.1.refs_11_), channel_id=1, source_target_pairs={{0,64},{8,456},{16,80},{24,472},{32,96},{40,488},{48,112},{56,504}... | collective-permute-start | bytes 1179656 | tf_op jit(solution)/shard_map/ppermute | solution.py:33
  60.4 7.1 %collective-permute-start.7 = (bf16[256,768]{1,0:T(8,128)(2,1)S(1)}, bf16[256,768]{1,0:T(8,128)(2,1)S(1)}, u32[]{:S(2)}, u32[]{:S(2)}) collective-permute-start(bf16[256,768]{1,0:T(8,128)(2,1)S(1)} %collective-permute-done.refs_10_), channel_id=1, source_target_pairs={{0,8},{8,0},{16,24},{24,16},{32,40},{40,32},{48,56},{56,48},{64,72... | collective-permute-start | bytes 1179656 | tf_op jit(solution)/shard_map/ppermute | solution.py:33
  76.0 5.4 %collective-permute-start.11 = (bf16[256,768]{1,0:T(8,128)(2,1)S(1)}, bf16[256,768]{1,0:T(8,128)(2,1)S(1)}, u32[]{:S(2)}, u32[]{:S(2)}) collective-permute-start(bf16[256,768]{1,0:T(8,128)(2,1)S(1)} %collective-permute-done.5.refs_14_), channel_id=1, source_target_pairs={{0,8},{8,0},{16,24},{24,16},{32,40},{40,32},{48,56},{56,48},{64,72... | collective-permute-start | bytes 1179656 | tf_op jit(solution)/shard_map/ppermute | solution.py:33
  88.0 4.1 %collective-permute-start.14 = (bf16[256,768]{1,0:T(8,128)(2,1)S(1)}, bf16[256,768]{1,0:T(8,128)(2,1)S(1)}, u32[]{:S(2)}, u32[]{:S(2)}) collective-permute-start(bf16[256,768]{1,0:T(8,128)(2,1)S(1)} %collective-permute-done.9.refs_18_), channel_id=1, source_target_pairs={{0,8},{8,0},{16,24},{24,16},{32,40},{40,32},{48,56},{56,48},{64,72... | collective-permute-start | bytes 1179656 | tf_op jit(solution)/shard_map/ppermute | solution.py:33
  94.1 8.2 %collective-permute-start.16 = (bf16[64,512]{1,0:T(8,128)(2,1)S(1)}, bf16[64,512]{1,0:T(8,128)(2,1)S(1)}, u32[]{:S(2)}, u32[]{:S(2)}) collective-permute-start(bf16[64,512]{1,0:T(8,128)(2,1)S(1)} %copy-done.33), channel_id=1, source_target_pairs={{0,248},{8,256},{16,264},{24,272},{32,280},{40,288},{48,296},{56,3... | collective-permute-start | bytes 196616 | tf_op jit(solution)/shard_map/ppermute | solution.py:46
  109.4 9.9 %layer.1 = (bf16[64,512]{1,0:T(8,128)(2,1)}, bf16[64,512]{1,0:T(8,128)(2,1)}, bf16[64,512]{1,0:T(8,128)(2,1)}, bf16[64,512]{1,0:T(8,128)(2,1)}, bf16[32,64,128]{...) custom-call(bf16[8,2,144,256]{3,2,1,0:T(8,128)(2,1)} %copy-done.5, ...), custom_call_target="tpu_custom_call" | custom-call | tf_op jit(solution)/shard_map/layer/pallas_call | solution.py:283
  121.3 3.6 %collective-permute-start.18 = (bf16[2,144,256]{2,1,0:T(8,128)(2,1)}, bf16[2,144,256]{2,1,0:T(8,128)(2,1)S(1)}, u32[]{:S(2)}, u32[]{:S(2)}) collective-permute-start(bf16[2,144,256]{2,1,0:T(8,128)(2,1)} %get-tuple-element.83), channel_id=1, source_target_pairs={{0,1},{1,2},{2,3},{3,4},{4,5},{5,6},{6,7},{7,0},{8,9},{9,10},{10,1... | collective-permute-start | bytes 442376 | tf_op jit(solution)/shard_map/ppermute | solution.py:376
  125.0 4.0 %collective-permute-start.19 = (bf16[2,144,256]{2,1,0:T(8,128)(2,1)}, bf16[2,144,256]{2,1,0:T(8,128)(2,1)S(1)}, u32[]{:S(2)}, u32[]{:S(2)}) collective-permute-start(bf16[2,144,256]{2,1,0:T(8,128)(2,1)} %get-tuple-element.84), channel_id=1, source_target_pairs={{0,2},{1,3},{2,4},{3,5},{4,6},{5,7},{6,0},{7,1},{8,10},{9,11},{10,... | collective-permute-start | bytes 442376 | tf_op jit(solution)/shard_map/ppermute | solution.py:376
  131.3 4.5 %collective-permute-done.19.refs_5_ = bf16[2,144,256]{2,1,0:T(8,128)(2,1)S(1)} collective-permute-done((bf16[2,144,256]{2,1,0:T(8,128)(2,1)}, bf16[2,144,256]{2,1,0:T(8,128)(2,1)S(1)}, u32[]{:S(2)}, u32[]{:S(2)}) %collective-permute-start.19) | collective-permute-done | bytes 147488 | tf_op jit(solution)/shard_map/ppermute | solution.py:376
  135.8 8.2 %all-to-all-start.1 = ((bf16[32,64,128]{2,1,0:T(8,128)(2,1)}), bf16[32,64,128]{2,1,0:T(8,128)(2,1)S(1)}, u32[]{:S(2)}, u32[]{:S(2)}) async-start(bf16[32,64,128]{2,1,0:T(8,128)(2,1)} %add_convert_fusion), calls=%async_computation.1 | async-start | bytes 1048576 | tf_op jit(solution)/shard_map/all_to_all | solution.py:380
  144.0 5.6 %collective-permute-start.25 = (bf16[2,144,256]{2,1,0:T(8,128)(2,1)S(1)}, bf16[2,144,256]{2,1,0:T(8,128)(2,1)S(1)}, u32[]{:S(2)}, u32[]{:S(2)}) collective-permute-start(bf16[2,144,256]{2,1,0:T(8,128)(2,1)S(1)} %copy-done.28), channel_id=1, source_target_pairs={{0,3},{1,4},{2,5},{3,6},{4,7},{5,0},{6,1},{7,2},{8,11},{9,12},{10,... | collective-permute-start | bytes 442376 | tf_op jit(solution)/shard_map/ppermute | solution.py:376
  149.6 4.1 %collective-permute-start.26 = (bf16[2,144,256]{2,1,0:T(8,128)(2,1)S(1)}, bf16[2,144,256]{2,1,0:T(8,128)(2,1)S(1)}, u32[]{:S(2)}, u32[]{:S(2)}) collective-permute-start(bf16[2,144,256]{2,1,0:T(8,128)(2,1)S(1)} %copy-done.27), channel_id=1, source_target_pairs={{0,4},{1,5},{2,6},{3,7},{4,0},{5,1},{6,2},{7,3},{8,12},{9,13},{10,... | collective-permute-start | bytes 442376 | tf_op jit(solution)/shard_map/ppermute | solution.py:376
  153.8 3.7 %collective-permute-start.27 = (bf16[2,144,256]{2,1,0:T(8,128)(2,1)S(1)}, bf16[2,144,256]{2,1,0:T(8,128)(2,1)S(1)}, u32[]{:S(2)}, u32[]{:S(2)}) collective-permute-start(bf16[2,144,256]{2,1,0:T(8,128)(2,1)S(1)} %copy-done.26), channel_id=1, source_target_pairs={{0,5},{1,6},{2,7},{3,0},{4,1},{5,2},{6,3},{7,4},{8,13},{9,14},{10,... | collective-permute-start | bytes 442376 | tf_op jit(solution)/shard_map/ppermute | solution.py:376
  157.5 4.3 %collective-permute-start.28 = (bf16[2,144,256]{2,1,0:T(8,128)(2,1)S(1)}, bf16[2,144,256]{2,1,0:T(8,128)(2,1)S(1)}, u32[]{:S(2)}, u32[]{:S(2)}) collective-permute-start(bf16[2,144,256]{2,1,0:T(8,128)(2,1)S(1)} %copy-done.25), channel_id=1, source_target_pairs={{0,6},{1,7},{2,0},{3,1},{4,2},{5,3},{6,4},{7,5},{8,14},{9,15},{10,... | collective-permute-start | bytes 442376 | tf_op jit(solution)/shard_map/ppermute | solution.py:376
  161.8 3.9 %collective-permute-start.29 = (bf16[2,144,256]{2,1,0:T(8,128)(2,1)S(1)}, bf16[2,144,256]{2,1,0:T(8,128)(2,1)S(1)}, u32[]{:S(2)}, u32[]{:S(2)}) collective-permute-start(bf16[2,144,256]{2,1,0:T(8,128)(2,1)S(1)} %copy-done.24), channel_id=1, source_target_pairs={{0,7},{1,0},{2,1},{3,2},{4,3},{5,4},{6,5},{7,6},{8,15},{9,8},{10,9... | collective-permute-start | bytes 442376 | tf_op jit(solution)/shard_map/ppermute | solution.py:376
  165.7 4.5 %collective-permute-start.21 = (bf16[64,512]{1,0:T(8,128)(2,1)S(1)}, bf16[64,512]{1,0:T(8,128)(2,1)S(1)}, u32[]{:S(2)}, u32[]{:S(2)}) collective-permute-start(bf16[64,512]{1,0:T(8,128)(2,1)S(1)} %copy-done.32), channel_id=1, source_target_pairs={{0,504},{8,0},{16,8},{24,16},{32,24},{40,32},{48,40},{56,48},{64,5... | collective-permute-start | bytes 196616 | tf_op jit(solution)/shard_map/ppermute | solution.py:46
  170.3 3.3 %collective-permute-start.22 = (bf16[64,512]{1,0:T(8,128)(2,1)S(1)}, bf16[64,512]{1,0:T(8,128)(2,1)S(1)}, u32[]{:S(2)}, u32[]{:S(2)}) collective-permute-start(bf16[64,512]{1,0:T(8,128)(2,1)S(1)} %copy-done.31), channel_id=1, source_target_pairs={{0,8},{8,16},{16,24},{24,32},{32,40},{40,48},{48,56},{56,64},{64,7... | collective-permute-start | bytes 196616 | tf_op jit(solution)/shard_map/ppermute | solution.py:46
  173.6 7.0 %collective-permute-start.23 = (bf16[64,512]{1,0:T(8,128)(2,1)S(1)}, bf16[64,512]{1,0:T(8,128)(2,1)S(1)}, u32[]{:S(2)}, u32[]{:S(2)}) collective-permute-start(bf16[64,512]{1,0:T(8,128)(2,1)S(1)} %copy-done.30), channel_id=1, source_target_pairs={{0,256},{8,264},{16,272},{24,280},{32,288},{40,296},{48,304},{56,3... | collective-permute-start | bytes 196616 | tf_op jit(solution)/shard_map/ppermute | solution.py:46
  180.7 6.7 %collective-permute-start.24 = (bf16[64,512]{1,0:T(8,128)(2,1)S(1)}, bf16[64,512]{1,0:T(8,128)(2,1)S(1)}, u32[]{:S(2)}, u32[]{:S(2)}) collective-permute-start(bf16[64,512]{1,0:T(8,128)(2,1)S(1)} %copy-done.29), channel_id=1, source_target_pairs={{0,264},{8,272},{16,280},{24,288},{32,296},{40,304},{48,312},{56,3... | collective-permute-start | bytes 196616 | tf_op jit(solution)/shard_map/ppermute | solution.py:46
  (122 shorter events, 47.9 us)
Async XLA Ops:
  21.9 24.4 %collective-permute-start = (bf16[256,768]{1,0:T(8,128)(2,1)S(1)}, bf16[256,768]{1,0:T(8,128)(2,1)S(1)}, u32[]{:S(2)}, u32[]{:S(2)}) collective-permute-start(bf16[256,768]{1,0:T(8,128)(2,1)S(1)} %get-tuple-element.106), channel_id=1, source_target_pairs={{0,64},{8,456},{16,80},{24,472},{32,96},{40,488},{48,112},{56,504}... | collective-permute-start | bytes 1179656 | tf_op jit(solution)/shard_map/ppermute | solution.py:33
  27.5 18.8 %collective-permute-start.1 = (bf16[256,768]{1,0:T(8,128)(2,1)S(1)}, bf16[256,768]{1,0:T(8,128)(2,1)S(1)}, u32[]{:S(2)}, u32[]{:S(2)}) collective-permute-start(bf16[256,768]{1,0:T(8,128)(2,1)S(1)} %get-tuple-element.105), channel_id=1, source_target_pairs={{0,64},{8,456},{16,80},{24,472},{32,96},{40,488},{48,112},{56,504}... | collective-permute-start | bytes 1179656 | tf_op jit(solution)/shard_map/ppermute | solution.py:33
  47.6 60.7 %all-to-all-start = ((bf16[8,2,144,256]{3,2,1,0:T(8,128)(2,1)}), bf16[8,2,144,256]{3,2,1,0:T(8,128)(2,1)S(1)}, u32[]{:S(2)}, u32[]{:S(2)}) async-start(bf16[8,2,144,256]{3,2,1,0:T(8,128)(2,1)} %broadcast_in_dim.7), calls=%async_computation | async-start | bytes 2359296 | tf_op jit(solution)/shard_map/all_to_all | solution.py:343
  54.5 14.9 %collective-permute-start.5 = (bf16[256,768]{1,0:T(8,128)(2,1)S(1)}, bf16[256,768]{1,0:T(8,128)(2,1)S(1)}, u32[]{:S(2)}, u32[]{:S(2)}) collective-permute-start(bf16[256,768]{1,0:T(8,128)(2,1)S(1)} %collective-permute-done.refs_10_), channel_id=1, source_target_pairs={{0,64},{8,456},{16,80},{24,472},{32,96},{40,488},{48,112},{56,504}... | collective-permute-start | bytes 1179656 | tf_op jit(solution)/shard_map/ppermute | solution.py:33
  57.2 12.3 %collective-permute-start.6 = (bf16[256,768]{1,0:T(8,128)(2,1)S(1)}, bf16[256,768]{1,0:T(8,128)(2,1)S(1)}, u32[]{:S(2)}, u32[]{:S(2)}) collective-permute-start(bf16[256,768]{1,0:T(8,128)(2,1)S(1)} %collective-permute-done.1.refs_11_), channel_id=1, source_target_pairs={{0,64},{8,456},{16,80},{24,472},{32,96},{40,488},{48,112},{56,504}... | collective-permute-start | bytes 1179656 | tf_op jit(solution)/shard_map/ppermute | solution.py:33
  71.2 12.2 %collective-permute-start.9 = (bf16[256,768]{1,0:T(8,128)(2,1)S(1)}, bf16[256,768]{1,0:T(8,128)(2,1)S(1)}, u32[]{:S(2)}, u32[]{:S(2)}) collective-permute-start(bf16[256,768]{1,0:T(8,128)(2,1)S(1)} %collective-permute-done.5.refs_14_), channel_id=1, source_target_pairs={{0,64},{8,456},{16,80},{24,472},{32,96},{40,488},{48,112},{56,504}... | collective-permute-start | bytes 1179656 | tf_op jit(solution)/shard_map/ppermute | solution.py:33
  73.8 10.4 %collective-permute-start.10 = (bf16[256,768]{1,0:T(8,128)(2,1)S(1)}, bf16[256,768]{1,0:T(8,128)(2,1)S(1)}, u32[]{:S(2)}, u32[]{:S(2)}) collective-permute-start(bf16[256,768]{1,0:T(8,128)(2,1)S(1)} %collective-permute-done.6.refs_15_), channel_id=1, source_target_pairs={{0,64},{8,456},{16,80},{24,472},{32,96},{40,488},{48,112},{56,504}... | collective-permute-start | bytes 1179656 | tf_op jit(solution)/shard_map/ppermute | solution.py:33
  85.0 19.5 %collective-permute-start.13 = (bf16[256,768]{1,0:T(8,128)(2,1)S(1)}, bf16[256,768]{1,0:T(8,128)(2,1)S(1)}, u32[]{:S(2)}, u32[]{:S(2)}) collective-permute-start(bf16[256,768]{1,0:T(8,128)(2,1)S(1)} %collective-permute-done.9.refs_18_), channel_id=1, source_target_pairs={{0,64},{8,456},{16,80},{24,472},{32,96},{40,488},{48,112},{56,504}... | collective-permute-start | bytes 1179656 | tf_op jit(solution)/shard_map/ppermute | solution.py:33
  88.0 16.5 %collective-permute-start.14 = (bf16[256,768]{1,0:T(8,128)(2,1)S(1)}, bf16[256,768]{1,0:T(8,128)(2,1)S(1)}, u32[]{:S(2)}, u32[]{:S(2)}) collective-permute-start(bf16[256,768]{1,0:T(8,128)(2,1)S(1)} %collective-permute-done.9.refs_18_), channel_id=1, source_target_pairs={{0,8},{8,0},{16,24},{24,16},{32,40},{40,32},{48,56},{56,48},{64,72... | collective-permute-start | bytes 1179656 | tf_op jit(solution)/shard_map/ppermute | solution.py:33
  92.2 12.4 %collective-permute-start.15 = (bf16[256,768]{1,0:T(8,128)(2,1)S(1)}, bf16[256,768]{1,0:T(8,128)(2,1)S(1)}, u32[]{:S(2)}, u32[]{:S(2)}) collective-permute-start(bf16[256,768]{1,0:T(8,128)(2,1)S(1)} %collective-permute-done.10.refs_19_), channel_id=1, source_target_pairs={{0,8},{8,0},{16,24},{24,16},{32,40},{40,32},{48,56},{56,48},{64,72... | collective-permute-start | bytes 1179656 | tf_op jit(solution)/shard_map/ppermute | solution.py:33
  94.1 10.4 %collective-permute-start.16 = (bf16[64,512]{1,0:T(8,128)(2,1)S(1)}, bf16[64,512]{1,0:T(8,128)(2,1)S(1)}, u32[]{:S(2)}, u32[]{:S(2)}) collective-permute-start(bf16[64,512]{1,0:T(8,128)(2,1)S(1)} %copy-done.33), channel_id=1, source_target_pairs={{0,248},{8,256},{16,264},{24,272},{32,280},{40,288},{48,296},{56,3... | collective-permute-start | bytes 196616 | tf_op jit(solution)/shard_map/ppermute | solution.py:46
  119.3 9.7 %collective-permute-start.20 = (bf16[32,64,128]{2,1,0:T(8,128)(2,1)}, bf16[32,64,128]{2,1,0:T(8,128)(2,1)S(1)}, u32[]{:S(2)}, u32[]{:S(2)}) collective-permute-start(bf16[32,64,128]{2,1,0:T(8,128)(2,1)} %get-tuple-element.86), channel_id=1, source_target_pairs={{0,8},{8,0},{16,24},{24,16},{32,40},{40,32},{48,56},{56,48},{64,72... | collective-permute-start | bytes 1572872 | tf_op jit(solution)/shard_map/ppermute | solution.py:33
  121.3 10.0 %collective-permute-start.18 = (bf16[2,144,256]{2,1,0:T(8,128)(2,1)}, bf16[2,144,256]{2,1,0:T(8,128)(2,1)S(1)}, u32[]{:S(2)}, u32[]{:S(2)}) collective-permute-start(bf16[2,144,256]{2,1,0:T(8,128)(2,1)} %get-tuple-element.83), channel_id=1, source_target_pairs={{0,1},{1,2},{2,3},{3,4},{4,5},{5,6},{6,7},{7,0},{8,9},{9,10},{10,1... | collective-permute-start | bytes 442376 | tf_op jit(solution)/shard_map/ppermute | solution.py:376
  125.0 10.8 %collective-permute-start.19 = (bf16[2,144,256]{2,1,0:T(8,128)(2,1)}, bf16[2,144,256]{2,1,0:T(8,128)(2,1)S(1)}, u32[]{:S(2)}, u32[]{:S(2)}) collective-permute-start(bf16[2,144,256]{2,1,0:T(8,128)(2,1)} %get-tuple-element.84), channel_id=1, source_target_pairs={{0,2},{1,3},{2,4},{3,5},{4,6},{5,7},{6,0},{7,1},{8,10},{9,11},{10,... | collective-permute-start | bytes 442376 | tf_op jit(solution)/shard_map/ppermute | solution.py:376
  135.8 56.2 %all-to-all-start.1 = ((bf16[32,64,128]{2,1,0:T(8,128)(2,1)}), bf16[32,64,128]{2,1,0:T(8,128)(2,1)S(1)}, u32[]{:S(2)}, u32[]{:S(2)}) async-start(bf16[32,64,128]{2,1,0:T(8,128)(2,1)} %add_convert_fusion), calls=%async_computation.1 | async-start | bytes 1048576 | tf_op jit(solution)/shard_map/all_to_all | solution.py:380
  144.0 21.7 %collective-permute-start.25 = (bf16[2,144,256]{2,1,0:T(8,128)(2,1)S(1)}, bf16[2,144,256]{2,1,0:T(8,128)(2,1)S(1)}, u32[]{:S(2)}, u32[]{:S(2)}) collective-permute-start(bf16[2,144,256]{2,1,0:T(8,128)(2,1)S(1)} %copy-done.28), channel_id=1, source_target_pairs={{0,3},{1,4},{2,5},{3,6},{4,7},{5,0},{6,1},{7,2},{8,11},{9,12},{10,... | collective-permute-start | bytes 442376 | tf_op jit(solution)/shard_map/ppermute | solution.py:376
  149.6 20.6 %collective-permute-start.26 = (bf16[2,144,256]{2,1,0:T(8,128)(2,1)S(1)}, bf16[2,144,256]{2,1,0:T(8,128)(2,1)S(1)}, u32[]{:S(2)}, u32[]{:S(2)}) collective-permute-start(bf16[2,144,256]{2,1,0:T(8,128)(2,1)S(1)} %copy-done.27), channel_id=1, source_target_pairs={{0,4},{1,5},{2,6},{3,7},{4,0},{5,1},{6,2},{7,3},{8,12},{9,13},{10,... | collective-permute-start | bytes 442376 | tf_op jit(solution)/shard_map/ppermute | solution.py:376
  153.8 19.8 %collective-permute-start.27 = (bf16[2,144,256]{2,1,0:T(8,128)(2,1)S(1)}, bf16[2,144,256]{2,1,0:T(8,128)(2,1)S(1)}, u32[]{:S(2)}, u32[]{:S(2)}) collective-permute-start(bf16[2,144,256]{2,1,0:T(8,128)(2,1)S(1)} %copy-done.26), channel_id=1, source_target_pairs={{0,5},{1,6},{2,7},{3,0},{4,1},{5,2},{6,3},{7,4},{8,13},{9,14},{10,... | collective-permute-start | bytes 442376 | tf_op jit(solution)/shard_map/ppermute | solution.py:376
  157.5 23.1 %collective-permute-start.28 = (bf16[2,144,256]{2,1,0:T(8,128)(2,1)S(1)}, bf16[2,144,256]{2,1,0:T(8,128)(2,1)S(1)}, u32[]{:S(2)}, u32[]{:S(2)}) collective-permute-start(bf16[2,144,256]{2,1,0:T(8,128)(2,1)S(1)} %copy-done.25), channel_id=1, source_target_pairs={{0,6},{1,7},{2,0},{3,1},{4,2},{5,3},{6,4},{7,5},{8,14},{9,15},{10,... | collective-permute-start | bytes 442376 | tf_op jit(solution)/shard_map/ppermute | solution.py:376
  161.8 25.6 %collective-permute-start.29 = (bf16[2,144,256]{2,1,0:T(8,128)(2,1)S(1)}, bf16[2,144,256]{2,1,0:T(8,128)(2,1)S(1)}, u32[]{:S(2)}, u32[]{:S(2)}) collective-permute-start(bf16[2,144,256]{2,1,0:T(8,128)(2,1)S(1)} %copy-done.24), channel_id=1, source_target_pairs={{0,7},{1,0},{2,1},{3,2},{4,3},{5,4},{6,5},{7,6},{8,15},{9,8},{10,9... | collective-permute-start | bytes 442376 | tf_op jit(solution)/shard_map/ppermute | solution.py:376
  165.7 24.5 %collective-permute-start.21 = (bf16[64,512]{1,0:T(8,128)(2,1)S(1)}, bf16[64,512]{1,0:T(8,128)(2,1)S(1)}, u32[]{:S(2)}, u32[]{:S(2)}) collective-permute-start(bf16[64,512]{1,0:T(8,128)(2,1)S(1)} %copy-done.32), channel_id=1, source_target_pairs={{0,504},{8,0},{16,8},{24,16},{32,24},{40,32},{48,40},{56,48},{64,5... | collective-permute-start | bytes 196616 | tf_op jit(solution)/shard_map/ppermute | solution.py:46
  170.3 19.9 %collective-permute-start.22 = (bf16[64,512]{1,0:T(8,128)(2,1)S(1)}, bf16[64,512]{1,0:T(8,128)(2,1)S(1)}, u32[]{:S(2)}, u32[]{:S(2)}) collective-permute-start(bf16[64,512]{1,0:T(8,128)(2,1)S(1)} %copy-done.31), channel_id=1, source_target_pairs={{0,8},{8,16},{16,24},{24,32},{32,40},{40,48},{48,56},{56,64},{64,7... | collective-permute-start | bytes 196616 | tf_op jit(solution)/shard_map/ppermute | solution.py:46
  173.6 16.6 %collective-permute-start.23 = (bf16[64,512]{1,0:T(8,128)(2,1)S(1)}, bf16[64,512]{1,0:T(8,128)(2,1)S(1)}, u32[]{:S(2)}, u32[]{:S(2)}) collective-permute-start(bf16[64,512]{1,0:T(8,128)(2,1)S(1)} %copy-done.30), channel_id=1, source_target_pairs={{0,256},{8,264},{16,272},{24,280},{32,288},{40,296},{48,304},{56,3... | collective-permute-start | bytes 196616 | tf_op jit(solution)/shard_map/ppermute | solution.py:46
  180.7 9.8 %collective-permute-start.24 = (bf16[64,512]{1,0:T(8,128)(2,1)S(1)}, bf16[64,512]{1,0:T(8,128)(2,1)S(1)}, u32[]{:S(2)}, u32[]{:S(2)}) collective-permute-start(bf16[64,512]{1,0:T(8,128)(2,1)S(1)} %copy-done.29), channel_id=1, source_target_pairs={{0,264},{8,272},{16,280},{24,288},{32,296},{40,304},{48,312},{56,3... | collective-permute-start | bytes 196616 | tf_op jit(solution)/shard_map/ppermute | solution.py:46
  (42 other events, 972.7 us)

commit v4 on v3

--- a/solution.py
+++ b/solution.py
@@ -6,7 +6,7 @@
 from jax import lax
 from jax.experimental import pallas as pl
 from jax.experimental.pallas import tpu as pltpu
-from jax.sharding import PartitionSpec as P
+from jax.sharding import Mesh, PartitionSpec as P
 
 D = 4096
 HEAD = 128
@@ -18,6 +18,7 @@
 EPSILON = 1e-05
 ROPE_BASE = 500000.0
 NZ, NX, NC = 8, 4, 2
+DP = ("z", "x", "core")
 BF = jnp.bfloat16
 F32 = jnp.float32
 MIB = 1024 * 1024
@@ -30,20 +31,16 @@
             for c in range(NC):
                 tz, tx, tc = where(z, x, c)
                 pairs.append(((z * NX + x) * NC + c, ((tz % NZ) * NX + tx % NX) * NC + tc))
-    return lax.ppermute(value, "dp", pairs)
+    return lax.ppermute(value, DP, pairs)
 
 
 def other_core(value):
     return moved(value, lambda z, x, c: (z, x, 1 - c))
 
 
-def along_z(value):
-    return moved(value, lambda z, x, c: (z + (1 if c == 0 else -1), x, c))
-
-
 def passed_along(value, by):
-    size = lax.axis_size("dp")
-    return lax.ppermute(value, "dp", [(i, (i + by) % size) for i in range(size)])
+    size = NZ * NX * NC
+    return lax.ppermute(value, DP, [(i, (i + by) % size) for i in range(size)])
 
 
 def tied(*values):
@@ -63,16 +60,16 @@
 
 
 def place():
-    me = lax.axis_index("dp")
-    return me, me // (NX * NC), (me // NC) % NX, me % NC
+    z, x, c = [lax.axis_index(axis) for axis in DP]
+    return (z * NX + x) * NC + c, z, x, c
 
 
 def plan_kernel(
     strides, shards, get, put, send, smem, extra,
 ):
     len_ref, off_ref, shard_ref, start_ref = smem
-    home_ref, dest_ref, cos_ref, sin_ref, allowed_ref = [put(SLOTS + i) for i in range(5)]
-    me = lax.axis_index("dp")
+    home_ref, dest_ref, cos_ref, sin_ref, allowed_ref = [put(3 + i) for i in range(5)]
+    me = place()[0]
     rows = lax.broadcasted_iota(jnp.int32, (TOK_DEV, TOK_DEV), 0)
     cols = lax.broadcasted_iota(jnp.int32, (TOK_DEV, TOK_DEV), 1)
     row_seq, row_pos = jnp.zeros_like(rows), jnp.zeros_like(rows)
@@ -105,8 +102,8 @@
         r = lax.broadcasted_iota(jnp.int32, (MAXLEN, CAP), 1)
         dest = jnp.where((r == t + in_start) & (t < in_len), 1.0, 0.0).astype(BF)
         dest_ref[at, :] = dest
-        put(e)[...] = dot_nn(dest, get(1)[...]).astype(BF)
-        send(e)
+        ref, lo = ((1, 0), (0, 0), (2, 0), (0, MAXLEN))[e]
+        put(ref)[lo : lo + MAXLEN, :] = dot_nn(dest, get(1)[...]).astype(BF)
     allowed_ref[...] = jnp.where((row_seq == col_seq) & (col_pos <= row_pos), 1.0, 0.0)
     angles = row_pos.astype(F32) * get(0)[...]
     cos_ref[...] = jnp.cos(angles)
@@ -114,26 +111,11 @@
     sin_ref[...] = jnp.where(cols < HEAD // 2, -sine, sine)
 
 
-def layer_kernel(q_heads, pieces, peers, get, put, send, smem, extra):
-    normed_ref, grads_ref, terms_ref = extra
-    kept_ref, given_ref, inverse_ref = [put(SLOTS + i) for i in range(3)]
-    out_at = SLOTS + 3
-    peer = lax.axis_index("tensor")
-    w_refs = list(range(9, 9 + pieces))
+def layer_kernel(q_heads, get, put, send, smem, extra):
+    normed_ref, grads_ref = extra
+    kept_ref, given_ref, inverse_ref, terms_ref = [put(3 + i) for i in range(4)]
     _, z, x, c = place()
-    up = 1 - 2 * c
-    where = [(z, 0, w_refs[0], 0), (z, 1, w_refs[0], 256)]
-    for k in range(1, NZ // 2):
-        first = 1 + 4 * (k - 1)
-        behind = lax.rem(z - up * k + NZ, NZ)
-        ahead = lax.rem(z + up * k + NZ, NZ)
-        where.append((behind, c, w_refs[first], 0))
-        where.append((behind, 1 - c, w_refs[first + 1], 0))
-        where.append((ahead, 1 - c, w_refs[first + 2], 0))
-        where.append((ahead, c, w_refs[first + 3], 0))
-    far = lax.rem(z + NZ // 2, NZ)
-    where.append((far, c, w_refs[pieces - 2], 0))
-    where.append((far, 1 - c, w_refs[pieces - 1], 0))
+    where = [(j, h, ref, j * 256) for j in range(NZ) for h, ref in ((c, 8), (1 - c, 9))]
     rows_ref = get(0)
     deep = rows_ref.shape[3]
     kv_at = q_heads * HEAD
@@ -155,7 +137,9 @@
     factor = HEAD ** (-0.5)
     allowed = get(3)[...] > 0.5
     home = get(4)[...]
-    cot = jnp.concatenate([get(5 + e)[...] for e in range(SLOTS)], 0)
+    cot = jnp.concatenate(
+        [get(6)[...], get(5)[:MAXLEN, :], get(7)[...]], 0
+    )
     cot = dot_tn(home, cot).astype(BF)
     key_raw = projected[:, kv_at : kv_at + HEAD]
     value_raw = projected[:, kv_at + HEAD :]
@@ -174,8 +158,9 @@
         probs_low = probs.astype(BF)
         mixed = dot_nn(probs_low, value).astype(BF)
         mixed = dot_nn(home, mixed).astype(BF)
-        for e in range(SLOTS):
-            put(e)[:, at] = mixed[e * MAXLEN : (e + 1) * MAXLEN, :]
+        put(0)[:, at] = mixed[:MAXLEN, :]
+        put(1)[:, at] = mixed[MAXLEN : 2 * MAXLEN, :]
+        put(2)[:, at] = mixed[2 * MAXLEN :, :]
         grad_out = cot[:, at]
         grad_value = grad_value + dot_tn(probs_low, grad_out)
         grad_probs = dot_nt(grad_out, value)
@@ -191,8 +176,8 @@
     grads_ref[:, kv_at : kv_at + HEAD] = grad_key
     grads_ref[:, kv_at + HEAD :] = grad_value
     dots = dots + grad_key.astype(F32) * key_raw + grad_value.astype(F32) * value_raw
-    for e in range(SLOTS):
-        send(e)
+    for i in range(3):
+        send(i)
     share = jnp.sum(dots, 1, keepdims=True) / inverse
     share = jnp.transpose(jnp.broadcast_to(share, (TOK_DEV, TOK_DEV)))[0:EXTRA, :]
     high = share.astype(BF)
@@ -208,37 +193,30 @@
             kept_ref[owner] = jnp.where(c == 0, low_rows, high_rows)
             given_ref[owner] = jnp.where(c == 0, high_rows, low_rows)
     for i in range(3):
-        send(SLOTS + i)
+        send(3 + i)
     for n, (block, half, w_ref, at) in enumerate(where):
         terms_ref[block, half, :TOK_DEV, :] = dot_nt(grads, get(w_ref)[at : at + deep, :]).astype(BF)
         terms_ref[block, half, TOK_DEV:, :] = tail
-    for k in range(peers):
-        put(out_at + k)[...] = terms_ref[lax.rem(peer + k, peers)]
-        send(out_at + k)
-
-
-def finish_kernel(peers, get, put, send, smem, extra):
-    hidden_ref, gain_ref, out_ref = get(0), get(1), put(0)
+
+
+def finish_kernel(get, put, send, smem, extra):
+    hidden_ref, gain_ref, total_ref, out_ref = get(0), get(1), get(3), put(0)
     inverse = get(2)[:, 0:1]
-    term_refs = [get(3 + k) for k in range(peers)]
-    deep = term_refs[0].shape[2]
-    row_dot = None
+    deep = total_ref.shape[2]
+    share = total_ref[0, TOK_DEV:, :].astype(F32)
+    share = share[0:1, :TOK_DEV] + share[0:1, TOK_DEV : 2 * TOK_DEV]
+    row_dot = jnp.transpose(jnp.broadcast_to(share, (TOK_DEV, TOK_DEV)))[:, 0:1]
     for h in range(2):
-        total = term_refs[0][h].astype(F32)
-        for ref in term_refs[1:]:
-            total = total + ref[h].astype(F32)
-        if row_dot is None:
-            share = total[TOK_DEV : TOK_DEV + 8, :]
-            share = share[0:1, :TOK_DEV] + share[0:1, TOK_DEV : 2 * TOK_DEV]
-            row_dot = jnp.transpose(jnp.broadcast_to(share, (TOK_DEV, TOK_DEV)))[:, 0:1]
         at = slice(h * deep, (h + 1) * deep)
-        weighted = total[:TOK_DEV, :] * gain_ref[:, at].astype(F32)
+        weighted = total_ref[h, :TOK_DEV, :].astype(F32) * gain_ref[:, at].astype(F32)
         here = hidden_ref[:, at].astype(F32)
         out_ref[:, at] = (inverse * weighted - here * (inverse * inverse * inverse * row_dot / D)).astype(BF)
 
 
 def lay_kernel(get, put, send, smem, extra):
-    rows = jnp.concatenate([get(1 + e)[...] for e in range(SLOTS)], 0)
+    rows = jnp.concatenate(
+        [get(1)[...], get(2)[:MAXLEN, :], get(3)[...], get(2)[MAXLEN:, :]], 0
+    )
     put(0)[...] = dot_tn(get(0)[...], rows).astype(BF)
 
 
@@ -297,7 +275,7 @@
 def on_device(
     hidden, gain, w_query, w_key, w_value, cotangent, seq_length, home_offset, dest_shard, dest_offset
 ):
-    shards = lax.axis_size("dp")
+    shards = NZ * NX * NC
     peers = lax.axis_size("tensor")
     me, z, x, c = place()
     strides = [-1, 1, shards // 2, shards // 2 + 1]
@@ -309,93 +287,75 @@
     rows_each = D // shards
 
     own = jnp.concatenate([w_query, w_key, w_value], 1)
-    slab = lax.all_gather(
-        own, "dp", axis=0, tiled=True,
-        axis_index_groups=[[a * NX * NC + b for b in range(NX * NC)] for a in range(NZ)],
-    )
-    first = jnp.where(c == 0, slab[:deep], slab[deep:])
-    second = jnp.where(c == 0, slab[deep:], slab[:deep])
+    slab = lax.all_gather(own, ("x", "core"), axis=0, tiled=True)
+    own_half = jnp.where(c == 0, slab[:deep], slab[deep:])
+    own_half, cotangent, packed = tied(own_half, cotangent, hidden)
+    mine = lax.all_gather(own_half, "z", axis=0, tiled=True)
 
     half = HEAD // 2
     freq = np.power(np.float32(ROPE_BASE), -(np.arange(half, dtype=np.float32) * np.float32(2.0 / HEAD)))
     freq = jnp.asarray(np.concatenate([freq, freq])[None, :].astype(np.float32))
     square = ((TOK_DEV, TOK_DEV), F32)
     cut = ((MAXLEN, q_cols), BF)
-    slab, cotangent = tied(slab, cotangent)
-    *cot_cuts, home, dest, cosine, sine, allowed = kernel_call(
+    wide = ((2 * MAXLEN, q_cols), BF)
+    cot_near, cot_behind, cot_far, home, dest, cosine, sine, allowed = kernel_call(
         functools.partial(plan_kernel, strides, shards),
-        [cut] * 4 + [((SLOTS * MAXLEN, TOK_DEV), BF), ((SLOTS * MAXLEN, CAP), BF)] + [square] * 3,
+        [wide, cut, cut] + [((SLOTS * MAXLEN, TOK_DEV), BF), ((SLOTS * MAXLEN, CAP), BF)] + [square] * 3,
         [seq_length.T, home_offset.T, dest_shard.T, dest_offset.T, freq, cotangent],
         "plan", 60, 4,
     )
-    packed = jnp.concatenate([hidden, jnp.broadcast_to(gain[None, :], (EXTRA, width))], 0)
+    packed = jnp.concatenate([packed, jnp.broadcast_to(gain[None, :], (EXTRA, width))], 0)
     packed = packed.reshape(TOK_DEV + EXTRA, 2, deep).transpose(1, 0, 2)
     packed = jnp.broadcast_to(packed[None], (peers,) + packed.shape)
 
-    def sent_home(n):
-        return passed_along(cot_cuts[n], -strides[n])
-
-    weights, cots = [slab], []
-    first, second, *landed, packed = tied(
-        along_z(first), along_z(second), sent_home(0), sent_home(1), sent_home(2), packed
-    )
-    cots += landed
     rows_full = lax.all_to_all(packed, "tensor", split_axis=0, concat_axis=0, tiled=True)
-    weights += [first, second]
-    first, second, *landed = tied(
-        along_z(first), along_z(second), other_core(first), other_core(second)
-    )
-    weights += landed + [first, second]
-    first, second, *landed = tied(
-        along_z(first), along_z(second), other_core(first), other_core(second)
-    )
-    weights += landed + [first, second]
-    first, *landed, last = tied(
-        along_z(first), other_core(first), other_core(second), sent_home(3)
-    )
-    cots.append(last)
-    weights += landed + [first, other_core(first)]
-
-    pieces = len(weights)
+    cot_near = passed_along(cot_near, -1)
+    cot_behind = passed_along(cot_behind, 1)
+    cot_far = passed_along(jnp.concatenate([cot_far, cot_near[MAXLEN:]], 0), shards // 2)
+
+    mine, rows_full, cot_near, cot_behind, cot_far = tied(
+        mine, rows_full, cot_near, cot_behind, cot_far
+    )
+    theirs = other_core(mine)
+
     share = ((NZ * NX, rows_each, k_cols), BF)
-    block = ((2, TOK_DEV + EXTRA, deep), BF)
-    *attn_cuts, kept, given, inverse, t0, t1, t2, t3, t4, t5, t6, t7 = kernel_call(
-        functools.partial(layer_kernel, q_heads, pieces, peers),
-        [cut] * 4 + [share, share, square] + [block] * peers,
-        [rows_full, cosine, sine, allowed, home, *cots, *weights],
+    block = (2, TOK_DEV + EXTRA, deep)
+    attn_behind, attn_near, attn_far, kept, given, inverse, terms = kernel_call(
+        functools.partial(layer_kernel, q_heads),
+        [cut, cut, wide, share, share, square, ((peers,) + block, BF)],
+        [rows_full, cosine, sine, allowed, home, cot_near, cot_behind, cot_far, mine, theirs],
         "layer", 60, 0,
         [
             pltpu.VMEM((2 * NZ, TOK_DEV, deep), BF),
             pltpu.VMEM((TOK_DEV, q_cols + 2 * k_cols), BF),
-            pltpu.VMEM((peers, 2, TOK_DEV + EXTRA, deep), BF),
         ],
     )
+    total = lax.psum_scatter(terms, "tensor", scatter_dimension=0, tiled=False)
+    (grad_hidden,) = kernel_call(
+        finish_kernel, [((TOK_DEV, width), BF)],
+        [hidden, gain[None, :], inverse, total], "finish", 8,
+    )
 
     pair = (kept.astype(F32) + other_core(given).astype(F32)).astype(BF)
-    terms = [t0] + [
-        lax.ppermute(t, "tensor", [(i, (i + k) % peers) for i in range(peers)])
-        for k, t in enumerate((t1, t2, t3, t4, t5, t6, t7), 1)
-    ]
-    terms[1], terms[2], pair, *attn_cuts = tied(terms[1], terms[2], pair, *attn_cuts)
-    parts = lax.all_to_all(
-        pair, "dp", split_axis=0, concat_axis=0, tiled=True,
-        axis_index_groups=[list(range(b, shards, NC)) for b in range(NC)],
-    )
+    parts = lax.all_to_all(pair, ("z", "x"), split_axis=0, concat_axis=0, tiled=True)
     grad_value_weight = jnp.sum(parts.astype(F32), 0)
-    (grad_hidden,) = kernel_call(
-        functools.partial(finish_kernel, peers), [((TOK_DEV, width), BF)],
-        [hidden, gain[None, :], inverse, *terms], "finish", 8,
-    )
-    attn_sent = [passed_along(attn_cuts[n], s) for n, s in enumerate(strides)]
-    (attn_out,) = kernel_call(lay_kernel, [((CAP, q_cols), BF)], [dest, *attn_sent], "lay", 8)
+
+    attn_far = passed_along(attn_far, shards // 2)
+    attn_near = passed_along(jnp.concatenate([attn_near, attn_far[MAXLEN:]], 0), 1)
+    attn_behind = passed_along(attn_behind, -1)
+    (attn_out,) = kernel_call(
+        lay_kernel, [((CAP, q_cols), BF)], [dest, attn_behind, attn_near, attn_far[:MAXLEN]], "lay", 8
+    )
     return (attn_out, grad_hidden, grad_value_weight)
 
 
 def solution(mesh):
+    fine = Mesh(mesh.devices.reshape(NZ, NX, NC, -1), DP + ("tensor",))
+    both = P(DP, "tensor")
     return jax.shard_map(
         on_device,
-        mesh=mesh,
-        in_specs=(P("dp", "tensor"), P("tensor")) + (P("dp", "tensor"),) * 4 + (P(),) * 4,
-        out_specs=(P("dp", "tensor"), P("dp", "tensor"), P("dp", "tensor")),
+        mesh=fine,
+        in_specs=(both, P("tensor")) + (both,) * 4 + (P(),) * 4,
+        out_specs=(both,) * 3,
         check_vma=False,
     )

time: 196 us -> 159 us (0.81); the launches traced: 193 us -> 158 us
  starting transfers between devices: 131 us -> 45.2 us
  waiting for transfers between devices: 15.9 us -> 53.8 us
  between operations: 1.51 us -> 14.3 us
    ppermute x30 -> x8, starting transfers between devices: 116 us -> 35.1 us  [the longest x6 28.7 us: passed_along(): return lax.ppermute(value, DP, [(i, (i + by) % size) for i in range(size)])]
    ppermute x30 -> x8, waiting for transfers between devices: 15.9 us -> 32.7 us  [the longest x6 25.6 us: passed_along(): return lax.ppermute(value, DP, [(i, (i + by) % size) for i in range(size)])]
    all_gather x0 -> x1, waiting for transfers between devices: none -> 15.2 us  [on_device(): mine = lax.all_gather(own_half, 'z', axis=0, tiled=True)]
    all_to_all x1, waiting for transfers between devices: 0.01 us -> 5.84 us  [on_device(): lax.all_to_all(packed, 'tensor', split_axis=0, concat_axis=0, tiled=True)]
    all_to_all x1, starting transfers between devices: 6.96 us -> 3.56 us  [on_device(): lax.all_to_all(packed, 'tensor', split_axis=0, concat_axis=0, tiled=True)]
  transfers between devices with their start and end apart: 32 -> 12, of which waited for: 8 -> 9; matrix products, arithmetic and copies ran while one was open for 1% -> 2% of each run, Pallas kernels for 4% -> 3%
where the time goes in v4:
time: 159 us; the launch traced here: 158 us
  waiting for transfers between devices  53.8 us (34%)
  starting transfers between devices  45.2 us (28%)
  blocking collectives  20.3 us (13%)
  Pallas kernels  16.7 us (11%)
  between operations  14.3 us (9%)
  other arithmetic  4.31 us (3%)
  local copies, waits for them, and re-layouts  3.1 us (2%)
    ppermute x6, starting transfers between devices, passed_along(): return lax.ppermute(value, DP, [(i, (i + by) % size) for i in range(size)])  28.7 us
    ppermute x6, waiting for transfers between devices, passed_along(): return lax.ppermute(value, DP, [(i, (i + by) % size) for i in range(size)])  25.6 us
    all_gather x1, blocking collectives, on_device(): slab = lax.all_gather(own, ('x', 'core'), axis=0, tiled=True)  20.3 us
    pallas_call x4, Pallas kernels, kernel_call(): pl.pallas_call(kernel, out_shape=shapes, in_specs=[pl.BlockSpec(memory_sp...  16.7 us
    all_gather x1, waiting for transfers between devices, on_device(): mine = lax.all_gather(own_half, 'z', axis=0, tiled=True)  15.2 us
    ppermute x2, waiting for transfers between devices, moved(): return lax.ppermute(value, DP, pairs)  7.12 us
    ppermute x2, starting transfers between devices, moved(): return lax.ppermute(value, DP, pairs)  6.42 us
    all_to_all x1, starting transfers between devices, on_device(): lax.all_to_all(pair, ('z', 'x'), split_axis=0, concat_axis=0, tiled=True)  6.4 us
  transfers between devices with their start and end apart: 12, of which 9 were waited for; matrix products, arithmetic and copies ran while one was open for 2% of the time, Pallas kernels for 3%

profile of v4, /device:TPU:1, one launch (start us, length us, event | category | flops | bytes accessed | tf_op | source)
XLA Modules:
  0.0 157.7 jit_solution(4946701868834518023)
XLA Ops:
  8.1 20.3 %all_gather.6 = bf16[512,768]{1,0:T(8,128)(2,1)S(1)} all-gather(bf16[64,768]{1,0:T(8,128)(2,1)S(1)} %pad_maximum_fusion.3), channel_id=1, replica_groups=mesh['z'=8,'x'=4,'core'=2,'tensor'=8] {'x','core'}, dimensions={0}, use_global_device_ids=true | all-gather | bytes 884736 | tf_op jit(solution)/shard_map/all_gather | solution.py:290
  29.4 1.1 broadcast_in_dim.7
  30.5 3.6 %all-to-all-start = ((bf16[8,2,144,256]{3,2,1,0:T(8,128)(2,1)}), bf16[8,2,144,256]{3,2,1,0:T(8,128)(2,1)S(1)}, u32[]{:S(2)}, u32[]{:S(2)}) async-start(bf16[8,2,144,256]{3,2,1,0:T(8,128)(2,1)} %broadcast_in_dim.7), calls=%async_computation | async-start | bytes 2359296 | tf_op jit(solution)/shard_map/all_to_all | solution.py:311
  34.1 3.1 %plan.1 = (bf16[128,512]{1,0:T(8,128)(2,1)}, bf16[64,512]{1,0:T(8,128)(2,1)}, bf16[64,512]{1,0:T(8,128)(2,1)}, bf16[256,128]{1,0:T(8,128)(2,1)}, bf16[256,256]{1...) custom-call(s32[4,64]{1,0:T(4,128)} %bitcast.15, s32[4,64]{1,0:T(4,128)} %bitcast.16, ...), custom_call_target="tpu_custom_call" | custom-call | tf_op jit(solution)/shard_map/plan/pallas_call | solution.py:261
  37.2 2.1 %collective-permute-start = (bf16[128,512]{1,0:T(8,128)(2,1)}, bf16[128,512]{1,0:T(8,128)(2,1)S(1)}, u32[]{:S(2)}, u32[]{:S(2)}) collective-permute-start(bf16[128,512]{1,0:T(8,128)(2,1)} %get-tuple-element.30), channel_id=1, source_target_pairs={{0,504},{8,0},{16,8},{24,16},{32,24},{40,32},{48,40},{56,48},{64,5... | collective-permute-start | bytes 393224 | tf_op jit(solution)/shard_map/ppermute | solution.py:43
  39.3 4.7 %collective-permute-done.refs_5_ = bf16[128,512]{1,0:T(8,128)(2,1)S(1)} collective-permute-done((bf16[128,512]{1,0:T(8,128)(2,1)}, bf16[128,512]{1,0:T(8,128)(2,1)S(1)}, u32[]{:S(2)}, u32[]{:S(2)}) %collective-permute-start) | collective-permute-done | bytes 131104 | tf_op jit(solution)/shard_map/ppermute | solution.py:43
  44.9 8.9 %collective-permute-start.2 = (bf16[128,512]{1,0:T(8,128)(2,1)S(1)}, bf16[128,512]{1,0:T(8,128)(2,1)S(1)}, u32[]{:S(2)}, u32[]{:S(2)}) collective-permute-start(bf16[128,512]{1,0:T(8,128)(2,1)S(1)} %pad_maximum_fusion.1), channel_id=1, source_target_pairs={{0,256},{8,264},{16,272},{24,280},{32,288},{40,296},{48,304},{56,3... | collective-permute-start | bytes 393224 | tf_op jit(solution)/shard_map/ppermute | solution.py:43
  53.8 1.9 %collective-permute-start.1 = (bf16[64,512]{1,0:T(8,128)(2,1)}, bf16[64,512]{1,0:T(8,128)(2,1)S(1)}, u32[]{:S(2)}, u32[]{:S(2)}) collective-permute-start(bf16[64,512]{1,0:T(8,128)(2,1)} %get-tuple-element.31), channel_id=1, source_target_pairs={{0,8},{8,16},{16,24},{24,32},{32,40},{40,48},{48,56},{56,64},{64,7... | collective-permute-start | bytes 196616 | tf_op jit(solution)/shard_map/ppermute | solution.py:43
  55.7 3.9 %collective-permute-done.1.refs_6_ = bf16[64,512]{1,0:T(8,128)(2,1)S(1)} collective-permute-done((bf16[64,512]{1,0:T(8,128)(2,1)}, bf16[64,512]{1,0:T(8,128)(2,1)S(1)}, u32[]{:S(2)}, u32[]{:S(2)}) %collective-permute-start.1) | collective-permute-done | bytes 65568 | tf_op jit(solution)/shard_map/ppermute | solution.py:43
  60.2 5.8 %all-to-all-done.refs_0_ = bf16[8,2,144,256]{3,2,1,0:T(8,128)(2,1)S(1)} async-done(((bf16[8,2,144,256]{3,2,1,0:T(8,128)(2,1)}), bf16[8,2,144,256]{3,2,1,0:T(8,128)(2,1)S(1)}, u32[]{:S(2)}, u32[]{:S(2)}) %all-to-all-start) | async-done | bytes 1179680 | tf_op jit(solution)/shard_map/all_to_all | solution.py:311
  66.0 15.2 %all-gather.2.cloned.1.call-done.refs_8_ = bf16[2048,768]{1,0:T(8,128)(2,1)} async-done(((bf16[256,768]{1,0:T(8,128)(2,1)}), bf16[2048,768]{1,0:T(8,128)(2,1)}) %all-gather.2.cloned.1.call-update) | async-done | bytes 3145744 | tf_op jit(solution)/shard_map/all_gather | solution.py:293
  81.2 4.1 %collective-permute-start.3 = (bf16[2048,768]{1,0:T(8,128)(2,1)}, bf16[2048,768]{1,0:T(8,128)(2,1)}, u32[]{:S(2)}, u32[]{:S(2)}) collective-permute-start(bf16[2048,768]{1,0:T(8,128)(2,1)} %all-gather.2.cloned.1.call-done.refs_8_), channel_id=1, source_target_pairs={{0,8},{8,0},{16,24},{24,16},{32,40},{40,32},{48,56},{56,48},{64,72... | collective-permute-start | bytes 9437192 | tf_op jit(solution)/shard_map/ppermute | solution.py:34
  85.3 5.6 %collective-permute-done.3.refs_9_ = bf16[2048,768]{1,0:T(8,128)(2,1)} collective-permute-done((bf16[2048,768]{1,0:T(8,128)(2,1)}, bf16[2048,768]{1,0:T(8,128)(2,1)}, u32[]{:S(2)}, u32[]{:S(2)}) %collective-permute-start.3) | collective-permute-done | bytes 3145760 | tf_op jit(solution)/shard_map/ppermute | solution.py:34
  90.9 10.8 %layer.1 = (bf16[64,512]{1,0:T(8,128)(2,1)}, bf16[64,512]{1,0:T(8,128)(2,1)}, bf16[128,512]{1,0:T(8,128)(2,1)}, bf16[32,64,128]{2,1,0:T(8,128)(2,1)}, bf16[32,64...) custom-call(bf16[8,2,144,256]{3,2,1,0:T(8,128)(2,1)} %copy-done.4, ...), custom_call_target="tpu_custom_call" | custom-call | tf_op jit(solution)/shard_map/layer/pallas_call | solution.py:261
  102.8 2.3 %collective-permute-start.7 = (bf16[32,64,128]{2,1,0:T(8,128)(2,1)S(1)}, bf16[32,64,128]{2,1,0:T(8,128)(2,1)S(1)}, u32[]{:S(2)}, u32[]{:S(2)}) collective-permute-start(bf16[32,64,128]{2,1,0:T(8,128)(2,1)S(1)} %copy-done.11), channel_id=1, source_target_pairs={{0,8},{8,0},{16,24},{24,16},{32,40},{40,32},{48,56},{56,48},{64,72... | collective-permute-start | bytes 1572872 | tf_op jit(solution)/shard_map/ppermute | solution.py:34
  105.1 1.5 collective-permute-done.7
  107.6 6.4 %all-to-all-start.1 = ((bf16[32,64,128]{2,1,0:T(8,128)(2,1)}), bf16[32,64,128]{2,1,0:T(8,128)(2,1)S(1)}, u32[]{:S(2)}, u32[]{:S(2)}) async-start(bf16[32,64,128]{2,1,0:T(8,128)(2,1)} %add_convert_fusion), calls=%async_computation.2 | async-start | bytes 1048576 | tf_op jit(solution)/shard_map/all_to_all | solution.py:340
  114.0 7.1 %collective-permute-start.5 = (bf16[128,512]{1,0:T(8,128)(2,1)S(1)}, bf16[128,512]{1,0:T(8,128)(2,1)S(1)}, u32[]{:S(2)}, u32[]{:S(2)}) collective-permute-start(bf16[128,512]{1,0:T(8,128)(2,1)S(1)} %copy-done.12), channel_id=1, source_target_pairs={{0,256},{8,264},{16,272},{24,280},{32,288},{40,296},{48,304},{56,3... | collective-permute-start | bytes 393224 | tf_op jit(solution)/shard_map/ppermute | solution.py:43
  121.1 12.8 %collective-permute-done.5 = bf16[128,512]{1,0:T(8,128)(2,1)S(1)} collective-permute-done((bf16[128,512]{1,0:T(8,128)(2,1)S(1)}, bf16[128,512]{1,0:T(8,128)(2,1)S(1)}, u32[]{:S(2)}, u32[]{:S(2)}) %collective-permute-start.5) | collective-permute-done | bytes 131104 | tf_op jit(solution)/shard_map/ppermute | solution.py:43
  133.9 6.8 %collective-permute-start.6 = (bf16[128,512]{1,0:T(8,128)(2,1)S(1)}, bf16[128,512]{1,0:T(8,128)(2,1)S(1)}, u32[]{:S(2)}, u32[]{:S(2)}) collective-permute-start(bf16[128,512]{1,0:T(8,128)(2,1)S(1)} %pad_maximum_fusion.2), channel_id=1, source_target_pairs={{0,8},{8,16},{16,24},{24,32},{32,40},{40,48},{48,56},{56,64},{64,7... | collective-permute-start | bytes 393224 | tf_op jit(solution)/shard_map/ppermute | solution.py:43
  140.8 1.9 %collective-permute-start.4 = (bf16[64,512]{1,0:T(8,128)(2,1)S(1)}, bf16[64,512]{1,0:T(8,128)(2,1)S(1)}, u32[]{:S(2)}, u32[]{:S(2)}) collective-permute-start(bf16[64,512]{1,0:T(8,128)(2,1)S(1)} %copy-done.13), channel_id=1, source_target_pairs={{0,504},{8,0},{16,8},{24,16},{32,24},{40,32},{48,40},{56,48},{64,5... | collective-permute-start | bytes 196616 | tf_op jit(solution)/shard_map/ppermute | solution.py:43
  142.7 3.6 %collective-permute-done.4.refs_1_ = bf16[64,512]{1,0:T(8,128)(2,1)S(1)} collective-permute-done((bf16[64,512]{1,0:T(8,128)(2,1)S(1)}, bf16[64,512]{1,0:T(8,128)(2,1)S(1)}, u32[]{:S(2)}, u32[]{:S(2)}) %collective-permute-start.4) | collective-permute-done | bytes 65568 | tf_op jit(solution)/shard_map/ppermute | solution.py:43
  146.4 1.5 lay.1
  149.5 1.3 finish.1
  (48 shorter events, 7.0 us)
Async XLA Ops:
  7.2 74.0 %all-gather.2.cloned.1.call-start = ((), (), s32[]{:S(2)}) async-start(), calls=%async_computation.3 | async-start | bytes 3538944 | tf_op jit(solution)/shard_map/all_gather | solution.py:293
  8.1 21.2 %copy-start.10 = (bf16[512]{0:T(512)(128)(2,1)S(1)}, bf16[512]{0:T(512)(128)(2,1)}, u32[]{:S(2)}) copy-start(bf16[512]{0:T(512)(128)(2,1)} %param.12) | copy-start | bytes 3076
  8.1 21.2 %copy-start = (bf16[128,512]{1,0:T(8,128)(2,1)S(1)}, bf16[128,512]{1,0:T(8,128)(2,1)}, u32[]{:S(2)}) copy-start(bf16[128,512]{1,0:T(8,128)(2,1)} %refs_0_.1) | copy-start | bytes 393220
  30.5 35.6 %all-to-all-start = ((bf16[8,2,144,256]{3,2,1,0:T(8,128)(2,1)}), bf16[8,2,144,256]{3,2,1,0:T(8,128)(2,1)S(1)}, u32[]{:S(2)}, u32[]{:S(2)}) async-start(bf16[8,2,144,256]{3,2,1,0:T(8,128)(2,1)} %broadcast_in_dim.7), calls=%async_computation | async-start | bytes 2359296 | tf_op jit(solution)/shard_map/all_to_all | solution.py:311
  34.0 114.6 %reduce-scatter.2.cloned.1.call-start = ((), (), s32[]{:S(2)}) async-start(), calls=%async_computation.4 | async-start | bytes 1327104 | tf_op jit(solution)/shard_map/reduce_scatter | solution.py:333
  37.2 6.8 %collective-permute-start = (bf16[128,512]{1,0:T(8,128)(2,1)}, bf16[128,512]{1,0:T(8,128)(2,1)S(1)}, u32[]{:S(2)}, u32[]{:S(2)}) collective-permute-start(bf16[128,512]{1,0:T(8,128)(2,1)} %get-tuple-element.30), channel_id=1, source_target_pairs={{0,504},{8,0},{16,8},{24,16},{32,24},{40,32},{48,40},{56,48},{64,5... | collective-permute-start | bytes 393224 | tf_op jit(solution)/shard_map/ppermute | solution.py:43
  44.0 46.9 %copy-start.6 = (bf16[128,512]{1,0:T(8,128)(2,1)}, bf16[128,512]{1,0:T(8,128)(2,1)S(1)}, u32[]{:S(2)}) copy-start(bf16[128,512]{1,0:T(8,128)(2,1)S(1)} %collective-permute-done.refs_5_) | copy-start | bytes 393220
  44.9 15.3 %collective-permute-start.2 = (bf16[128,512]{1,0:T(8,128)(2,1)S(1)}, bf16[128,512]{1,0:T(8,128)(2,1)S(1)}, u32[]{:S(2)}, u32[]{:S(2)}) collective-permute-start(bf16[128,512]{1,0:T(8,128)(2,1)S(1)} %pad_maximum_fusion.1), channel_id=1, source_target_pairs={{0,256},{8,264},{16,272},{24,280},{32,288},{40,296},{48,304},{56,3... | collective-permute-start | bytes 393224 | tf_op jit(solution)/shard_map/ppermute | solution.py:43
  53.8 5.8 %collective-permute-start.1 = (bf16[64,512]{1,0:T(8,128)(2,1)}, bf16[64,512]{1,0:T(8,128)(2,1)S(1)}, u32[]{:S(2)}, u32[]{:S(2)}) collective-permute-start(bf16[64,512]{1,0:T(8,128)(2,1)} %get-tuple-element.31), channel_id=1, source_target_pairs={{0,8},{8,16},{16,24},{24,32},{32,40},{40,48},{48,56},{56,64},{64,7... | collective-permute-start | bytes 196616 | tf_op jit(solution)/shard_map/ppermute | solution.py:43
  59.6 31.4 %copy-start.8 = (bf16[64,512]{1,0:T(8,128)(2,1)}, bf16[64,512]{1,0:T(8,128)(2,1)S(1)}, u32[]{:S(2)}) copy-start(bf16[64,512]{1,0:T(8,128)(2,1)S(1)} %collective-permute-done.1.refs_6_) | copy-start | bytes 196612
  60.2 30.8 %copy-start.7 = (bf16[128,512]{1,0:T(8,128)(2,1)}, bf16[128,512]{1,0:T(8,128)(2,1)S(1)}, u32[]{:S(2)}) copy-start(bf16[128,512]{1,0:T(8,128)(2,1)S(1)} %collective-permute-done.2.refs_7_) | copy-start | bytes 393220
  66.0 24.9 %copy-start.4 = (bf16[8,2,144,256]{3,2,1,0:T(8,128)(2,1)}, bf16[8,2,144,256]{3,2,1,0:T(8,128)(2,1)S(1)}, u32[]{:S(2)}) copy-start(bf16[8,2,144,256]{3,2,1,0:T(8,128)(2,1)S(1)} %all-to-all-done.refs_0_) | copy-start | bytes 3538948
  81.2 9.7 %collective-permute-start.3 = (bf16[2048,768]{1,0:T(8,128)(2,1)}, bf16[2048,768]{1,0:T(8,128)(2,1)}, u32[]{:S(2)}, u32[]{:S(2)}) collective-permute-start(bf16[2048,768]{1,0:T(8,128)(2,1)} %all-gather.2.cloned.1.call-done.refs_8_), channel_id=1, source_target_pairs={{0,8},{8,0},{16,24},{24,16},{32,40},{40,32},{48,56},{56,48},{64,72... | collective-permute-start | bytes 9437192 | tf_op jit(solution)/shard_map/ppermute | solution.py:34
  101.7 4.9 %copy-start.5 = (bf16[32,64,128]{2,1,0:T(8,128)(2,1)S(1)}, bf16[32,64,128]{2,1,0:T(8,128)(2,1)}, u32[]{:S(2)}) copy-start(bf16[32,64,128]{2,1,0:T(8,128)(2,1)} %get-tuple-element.47) | copy-start | bytes 1572868
  102.8 3.8 %collective-permute-start.7 = (bf16[32,64,128]{2,1,0:T(8,128)(2,1)S(1)}, bf16[32,64,128]{2,1,0:T(8,128)(2,1)S(1)}, u32[]{:S(2)}, u32[]{:S(2)}) collective-permute-start(bf16[32,64,128]{2,1,0:T(8,128)(2,1)S(1)} %copy-done.11), channel_id=1, source_target_pairs={{0,8},{8,0},{16,24},{24,16},{32,40},{40,32},{48,56},{56,48},{64,72... | collective-permute-start | bytes 1572872 | tf_op jit(solution)/shard_map/ppermute | solution.py:34
  106.6 7.4 %copy-start.12 = (bf16[128,512]{1,0:T(8,128)(2,1)S(1)}, bf16[128,512]{1,0:T(8,128)(2,1)}, u32[]{:S(2)}) copy-start(bf16[128,512]{1,0:T(8,128)(2,1)} %get-tuple-element.44) | copy-start | bytes 393220
  106.6 27.3 %copy-start.9 = (bf16[64,512]{1,0:T(8,128)(2,1)S(1)}, bf16[64,512]{1,0:T(8,128)(2,1)}, u32[]{:S(2)}) copy-start(bf16[64,512]{1,0:T(8,128)(2,1)} %get-tuple-element.43) | copy-start | bytes 196612
  107.6 33.2 %copy-start.13 = (bf16[64,512]{1,0:T(8,128)(2,1)S(1)}, bf16[64,512]{1,0:T(8,128)(2,1)}, u32[]{:S(2)}) copy-start(bf16[64,512]{1,0:T(8,128)(2,1)} %get-tuple-element.42) | copy-start | bytes 196612
  107.6 38.8 %copy-start.2 = (bf16[256,256]{1,0:T(8,128)(2,1)S(1)}, bf16[256,256]{1,0:T(8,128)(2,1)}, u32[]{:S(2)}) copy-start(bf16[256,256]{1,0:T(8,128)(2,1)} %get-tuple-element.27.refs_0_) | copy-start | bytes 393220
  107.6 41.0 %copy-start.3 = (f32[128,128]{1,0:T(8,128)S(1)}, f32[128,128]{1,0:T(8,128)}, u32[]{:S(2)}) copy-start(f32[128,128]{1,0:T(8,128)} %get-tuple-element.45.refs_2_) | copy-start | bytes 196612
  107.6 40.3 %all-to-all-start.1 = ((bf16[32,64,128]{2,1,0:T(8,128)(2,1)}), bf16[32,64,128]{2,1,0:T(8,128)(2,1)S(1)}, u32[]{:S(2)}, u32[]{:S(2)}) async-start(bf16[32,64,128]{2,1,0:T(8,128)(2,1)} %add_convert_fusion), calls=%async_computation.2 | async-start | bytes 1048576 | tf_op jit(solution)/shard_map/all_to_all | solution.py:340
  114.0 19.8 %collective-permute-start.5 = (bf16[128,512]{1,0:T(8,128)(2,1)S(1)}, bf16[128,512]{1,0:T(8,128)(2,1)S(1)}, u32[]{:S(2)}, u32[]{:S(2)}) collective-permute-start(bf16[128,512]{1,0:T(8,128)(2,1)S(1)} %copy-done.12), channel_id=1, source_target_pairs={{0,256},{8,264},{16,272},{24,280},{32,288},{40,296},{48,304},{56,3... | collective-permute-start | bytes 393224 | tf_op jit(solution)/shard_map/ppermute | solution.py:43
  133.9 12.5 %collective-permute-start.6 = (bf16[128,512]{1,0:T(8,128)(2,1)S(1)}, bf16[128,512]{1,0:T(8,128)(2,1)S(1)}, u32[]{:S(2)}, u32[]{:S(2)}) collective-permute-start(bf16[128,512]{1,0:T(8,128)(2,1)S(1)} %pad_maximum_fusion.2), channel_id=1, source_target_pairs={{0,8},{8,16},{16,24},{24,32},{32,40},{40,48},{48,56},{56,64},{64,7... | collective-permute-start | bytes 393224 | tf_op jit(solution)/shard_map/ppermute | solution.py:43
  140.8 5.6 %collective-permute-start.4 = (bf16[64,512]{1,0:T(8,128)(2,1)S(1)}, bf16[64,512]{1,0:T(8,128)(2,1)S(1)}, u32[]{:S(2)}, u32[]{:S(2)}) collective-permute-start(bf16[64,512]{1,0:T(8,128)(2,1)S(1)} %copy-done.13), channel_id=1, source_target_pairs={{0,504},{8,0},{16,8},{24,16},{32,24},{40,32},{48,40},{56,48},{64,5... | collective-permute-start | bytes 196616 | tf_op jit(solution)/shard_map/ppermute | solution.py:43
  (2 other events, 2.0 us)
Sparse Core Ops, SparseCore 0:
  29.4 51.7 all-gather.1
  101.9 34.8 reduce-scatter.1

commit v5 on v4

--- a/solution.py
+++ b/solution.py
@@ -111,14 +111,10 @@
     sin_ref[...] = jnp.where(cols < HEAD // 2, -sine, sine)
 
 
-def layer_kernel(q_heads, get, put, send, smem, extra):
-    normed_ref, grads_ref = extra
-    kept_ref, given_ref, inverse_ref, terms_ref = [put(3 + i) for i in range(4)]
-    _, z, x, c = place()
-    where = [(j, h, ref, j * 256) for j in range(NZ) for h, ref in ((c, 8), (1 - c, 9))]
-    rows_ref = get(0)
+def norm_kernel(get, put, send, smem, extra):
+    c = place()[3]
+    rows_ref, normed_ref, inverse_ref, partial_ref = get(0), put(0), put(1), put(2)
     deep = rows_ref.shape[3]
-    kv_at = q_heads * HEAD
     squares = jnp.zeros((TOK_DEV, 1), F32)
     for j in range(NZ):
         for h in range(2):
@@ -126,12 +122,44 @@
             squares = squares + jnp.sum(part * part, 1, keepdims=True)
     inverse = lax.rsqrt(squares / D + EPSILON)
     inverse_ref[...] = jnp.broadcast_to(inverse, inverse_ref.shape)
-    projected = jnp.zeros((TOK_DEV, kv_at + 2 * HEAD), F32)
-    for n, (block, half, w_ref, at) in enumerate(where):
-        gain = rows_ref[block, half, TOK_DEV:, :].astype(F32)[0:1, :]
-        part = (rows_ref[block, half, :TOK_DEV, :].astype(F32) * inverse * gain).astype(BF)
-        normed_ref[n] = part
-        projected = projected + dot_nn(part, get(w_ref)[at : at + deep, :])
+    for n, half in enumerate((c, 1 - c)):
+        for j in range(NZ):
+            gain = rows_ref[j, half, TOK_DEV:, :].astype(F32)[0:1, :]
+            part = rows_ref[j, half, :TOK_DEV, :].astype(F32) * inverse * gain
+            normed_ref[n, j] = part.astype(BF)
+    send(0)
+    partial = jnp.zeros(partial_ref.shape, F32)
+    for j in range(NZ):
+        partial = partial + dot_nn(normed_ref[0, j], get(1)[j * deep : (j + 1) * deep, :])
+    partial_ref[...] = partial
+
+
+def value_kernel(get, put, send, smem, extra):
+    c = place()[3]
+    kept_ref, given_ref = put(0), put(1)
+    grad_value = get(1)[...]
+    for n, half in enumerate((c, 1 - c)):
+        for j in range(NZ):
+            found = dot_tn(get(0)[n, j], grad_value).astype(BF)
+            for pair in range(2):
+                low_rows = found[pair * 128 : pair * 128 + 64, :]
+                high_rows = found[pair * 128 + 64 : (pair + 1) * 128, :]
+                owner = j * NX + 2 * half + pair
+                kept_ref[owner] = jnp.where(c == 0, low_rows, high_rows)
+                given_ref[owner] = jnp.where(c == 0, high_rows, low_rows)
+
+
+def layer_kernel(q_heads, get, put, send, smem, extra):
+    (grads_ref,) = extra
+    value_out_ref, terms_ref = put(4), put(5)
+    c = place()[3]
+    kv_at = q_heads * HEAD
+    inverse = get(9)[:, 0:1]
+    normed_ref = get(0)
+    deep = normed_ref.shape[3]
+    projected = get(10)[...]
+    for j in range(NZ):
+        projected = projected + dot_nn(normed_ref[1, j], get(11)[j * deep : (j + 1) * deep, :])
     cosine = get(1)[...]
     sine = get(2)[...]
     factor = HEAD ** (-0.5)
@@ -158,9 +186,8 @@
         probs_low = probs.astype(BF)
         mixed = dot_nn(probs_low, value).astype(BF)
         mixed = dot_nn(home, mixed).astype(BF)
-        put(0)[:, at] = mixed[:MAXLEN, :]
-        put(1)[:, at] = mixed[MAXLEN : 2 * MAXLEN, :]
-        put(2)[:, at] = mixed[2 * MAXLEN :, :]
+        for e in range(SLOTS):
+            put(e)[:, at] = mixed[e * MAXLEN : (e + 1) * MAXLEN, :]
         grad_out = cot[:, at]
         grad_value = grad_value + dot_tn(probs_low, grad_out)
         grad_probs = dot_nt(grad_out, value)
@@ -175,28 +202,21 @@
     grad_value = grad_value.astype(BF)
     grads_ref[:, kv_at : kv_at + HEAD] = grad_key
     grads_ref[:, kv_at + HEAD :] = grad_value
+    value_out_ref[...] = grad_value
     dots = dots + grad_key.astype(F32) * key_raw + grad_value.astype(F32) * value_raw
-    for i in range(3):
-        send(i)
+    for e in range(SLOTS):
+        send(e)
     share = jnp.sum(dots, 1, keepdims=True) / inverse
     share = jnp.transpose(jnp.broadcast_to(share, (TOK_DEV, TOK_DEV)))[0:EXTRA, :]
     high = share.astype(BF)
     low = (share - high.astype(F32)).astype(BF)
     tail = jnp.concatenate([high, low], 1)
     grads = grads_ref[...]
-    for n, (block, half, w_ref, at) in enumerate(where):
-        found = dot_tn(normed_ref[n], grad_value).astype(BF)
-        for pair in range(2):
-            low_rows = found[pair * 128 : pair * 128 + 64, :]
-            high_rows = found[pair * 128 + 64 : (pair + 1) * 128, :]
-            owner = block * NX + 2 * half + pair
-            kept_ref[owner] = jnp.where(c == 0, low_rows, high_rows)
-            given_ref[owner] = jnp.where(c == 0, high_rows, low_rows)
-    for i in range(3):
-        send(3 + i)
-    for n, (block, half, w_ref, at) in enumerate(where):
-        terms_ref[block, half, :TOK_DEV, :] = dot_nt(grads, get(w_ref)[at : at + deep, :]).astype(BF)
-        terms_ref[block, half, TOK_DEV:, :] = tail
+    for half, ref in ((c, 8), (1 - c, 11)):
+        for j in range(NZ):
+            found = dot_nt(grads, get(ref)[j * deep : (j + 1) * deep, :])
+            terms_ref[j, half, :TOK_DEV, :] = found.astype(BF)
+            terms_ref[j, half, TOK_DEV:, :] = tail
 
 
 def finish_kernel(get, put, send, smem, extra):
@@ -215,7 +235,7 @@
 
 def lay_kernel(get, put, send, smem, extra):
     rows = jnp.concatenate(
-        [get(1)[...], get(2)[:MAXLEN, :], get(3)[...], get(2)[MAXLEN:, :]], 0
+        [get(1 + e)[...] for e in range(SLOTS)], 0
     )
     put(0)[...] = dot_tn(get(0)[...], rows).astype(BF)
 
@@ -318,33 +338,34 @@
     )
     theirs = other_core(mine)
 
-    share = ((NZ * NX, rows_each, k_cols), BF)
+    normed, inverse, partial = kernel_call(
+        norm_kernel,
+        [((2, NZ, TOK_DEV, deep), BF), square, ((TOK_DEV, q_cols + 2 * k_cols), F32)],
+        [rows_full, mine], "norm", 60,
+    )
     block = (2, TOK_DEV + EXTRA, deep)
-    attn_behind, attn_near, attn_far, kept, given, inverse, terms = kernel_call(
+    *attn_cuts, grad_value, terms = kernel_call(
         functools.partial(layer_kernel, q_heads),
-        [cut, cut, wide, share, share, square, ((peers,) + block, BF)],
-        [rows_full, cosine, sine, allowed, home, cot_near, cot_behind, cot_far, mine, theirs],
+        [cut] * 4 + [((TOK_DEV, k_cols), BF), ((peers,) + block, BF)],
+        [normed, cosine, sine, allowed, home, cot_near, cot_behind, cot_far, mine, inverse, partial, theirs],
         "layer", 60, 0,
-        [
-            pltpu.VMEM((2 * NZ, TOK_DEV, deep), BF),
-            pltpu.VMEM((TOK_DEV, q_cols + 2 * k_cols), BF),
-        ],
+        [pltpu.VMEM((TOK_DEV, q_cols + 2 * k_cols), BF)],
     )
     total = lax.psum_scatter(terms, "tensor", scatter_dimension=0, tiled=False)
     (grad_hidden,) = kernel_call(
         finish_kernel, [((TOK_DEV, width), BF)],
-        [hidden, gain[None, :], inverse, total], "finish", 8,
-    )
-
+        [hidden, gain[None, :], inverse, total], "finish", 60,
+    )
+
+    share = ((NZ * NX, rows_each, k_cols), BF)
+    kept, given = kernel_call(value_kernel, [share, share], [normed, grad_value], "value", 60)
     pair = (kept.astype(F32) + other_core(given).astype(F32)).astype(BF)
     parts = lax.all_to_all(pair, ("z", "x"), split_axis=0, concat_axis=0, tiled=True)
     grad_value_weight = jnp.sum(parts.astype(F32), 0)
 
-    attn_far = passed_along(attn_far, shards // 2)
-    attn_near = passed_along(jnp.concatenate([attn_near, attn_far[MAXLEN:]], 0), 1)
-    attn_behind = passed_along(attn_behind, -1)
+    attn_sent = [passed_along(attn_cuts[n], s) for n, s in enumerate(strides)]
     (attn_out,) = kernel_call(
-        lay_kernel, [((CAP, q_cols), BF)], [dest, attn_behind, attn_near, attn_far[:MAXLEN]], "lay", 8
+        lay_kernel, [((CAP, q_cols), BF)], [dest, *attn_sent], "lay", 8
     )
     return (attn_out, grad_hidden, grad_value_weight)
 

time: 159 us -> 152 us (0.956)
  waiting for transfers between devices: 53.8 us -> 41 us
  Pallas kernels: 16.7 us -> 23.2 us
    ppermute x6 -> x7, waiting for transfers between devices: 25.6 us -> 16.3 us  [passed_along(): return lax.ppermute(value, DP, [(i, (i + by) % size) for i in range(size)])]
    pallas_call x4 -> x6, Pallas kernels: 16.7 us -> 23.2 us  [kernel_call(): pl.pallas_call(kernel, out_shape=shapes, in_specs=[pl.BlockSpec(memory_sp...]
    ppermute x2, waiting for transfers between devices: 7.12 us -> 3.65 us  [moved(): return lax.ppermute(value, DP, pairs)]
    unnamed x28 -> x22, local copies, waits for them, and re-layouts: 1.96 us -> 0.05 us
    ppermute x6 -> x7, starting transfers between devices: 28.7 us -> 28.4 us  [passed_along(): return lax.ppermute(value, DP, [(i, (i + by) % size) for i in range(size)])]
  transfers between devices with their start and end apart: 12 -> 13, of which waited for: 9 -> 9; matrix products, arithmetic and copies ran while one was open for 2% -> 4% of each run, Pallas kernels for 3% -> 7%
where the time goes in v5:
time: 152 us; the launch traced here: 151 us
  starting transfers between devices  44.8 us (29%)
  waiting for transfers between devices  41 us (27%)
  Pallas kernels  23.2 us (15%)
  blocking collectives  20.3 us (13%)
  between operations  14.3 us (9%)
  other arithmetic  5.4 us (4%)
  local copies, waits for them, and re-layouts  1.75 us (1%)
    ppermute x7, starting transfers between devices, passed_along(): return lax.ppermute(value, DP, [(i, (i + by) % size) for i in range(size)])  28.4 us
    pallas_call x6, Pallas kernels, kernel_call(): pl.pallas_call(kernel, out_shape=shapes, in_specs=[pl.BlockSpec(memory_sp...  23.2 us
    all_gather x1, blocking collectives, on_device(): slab = lax.all_gather(own, ('x', 'core'), axis=0, tiled=True)  20.3 us
    ppermute x7, waiting for transfers between devices, passed_along(): return lax.ppermute(value, DP, [(i, (i + by) % size) for i in range(size)])  16.3 us
    all_gather x1, waiting for transfers between devices, on_device(): mine = lax.all_gather(own_half, 'z', axis=0, tiled=True)  15.2 us
    ppermute x2, starting transfers between devices, moved(): return lax.ppermute(value, DP, pairs)  6.43 us
    all_to_all x1, starting transfers between devices, on_device(): lax.all_to_all(pair, ('z', 'x'), split_axis=0, concat_axis=0, tiled=True)  6.28 us
    all_to_all x1, waiting for transfers between devices, on_device(): lax.all_to_all(packed, 'tensor', split_axis=0, concat_axis=0, tiled=True)  5.84 us
  transfers between devices with their start and end apart: 13, of which 9 were waited for; matrix products, arithmetic and copies ran while one was open for 4% of the time, Pallas kernels for 7%

profile of v5, /device:TPU:1, one launch (start us, length us, event | category | flops | bytes accessed | tf_op | source)
XLA Modules:
  0.0 150.8 jit_solution(6042344470153827860)
XLA Ops:
  8.1 20.3 %all_gather.6 = bf16[512,768]{1,0:T(8,128)(2,1)S(1)} all-gather(bf16[64,768]{1,0:T(8,128)(2,1)S(1)} %pad_maximum_fusion.2), channel_id=1, replica_groups=mesh['z'=8,'x'=4,'core'=2,'tensor'=8] {'x','core'}, dimensions={0}, use_global_device_ids=true | all-gather | bytes 884736 | tf_op jit(solution)/shard_map/all_gather | solution.py:310
  30.5 3.6 %all-to-all-start = ((bf16[8,2,144,256]{3,2,1,0:T(8,128)(2,1)}), bf16[8,2,144,256]{3,2,1,0:T(8,128)(2,1)S(1)}, u32[]{:S(2)}, u32[]{:S(2)}) async-start(bf16[8,2,144,256]{3,2,1,0:T(8,128)(2,1)} %broadcast_in_dim.7), calls=%async_computation | async-start | bytes 2359296 | tf_op jit(solution)/shard_map/all_to_all | solution.py:331
  34.1 3.1 %plan.1 = (bf16[128,512]{1,0:T(8,128)(2,1)}, bf16[64,512]{1,0:T(8,128)(2,1)}, bf16[64,512]{1,0:T(8,128)(2,1)}, bf16[256,128]{1,0:T(8,128)(2,1)}, bf16[256,256]{1...) custom-call(s32[4,64]{1,0:T(4,128)} %bitcast.15, s32[4,64]{1,0:T(4,128)} %bitcast.16, ...), custom_call_target="tpu_custom_call" | custom-call | tf_op jit(solution)/shard_map/plan/pallas_call | solution.py:281
  37.2 2.1 %collective-permute-start = (bf16[128,512]{1,0:T(8,128)(2,1)}, bf16[128,512]{1,0:T(8,128)(2,1)S(1)}, u32[]{:S(2)}, u32[]{:S(2)}) collective-permute-start(bf16[128,512]{1,0:T(8,128)(2,1)} %get-tuple-element.34), channel_id=1, source_target_pairs={{0,504},{8,0},{16,8},{24,16},{32,24},{40,32},{48,40},{56,48},{64,5... | collective-permute-start | bytes 393224 | tf_op jit(solution)/shard_map/ppermute | solution.py:43
  39.3 4.7 %collective-permute-done.refs_5_ = bf16[128,512]{1,0:T(8,128)(2,1)S(1)} collective-permute-done((bf16[128,512]{1,0:T(8,128)(2,1)}, bf16[128,512]{1,0:T(8,128)(2,1)S(1)}, u32[]{:S(2)}, u32[]{:S(2)}) %collective-permute-start) | collective-permute-done | bytes 131104 | tf_op jit(solution)/shard_map/ppermute | solution.py:43
  44.9 8.9 %collective-permute-start.2 = (bf16[128,512]{1,0:T(8,128)(2,1)S(1)}, bf16[128,512]{1,0:T(8,128)(2,1)S(1)}, u32[]{:S(2)}, u32[]{:S(2)}) collective-permute-start(bf16[128,512]{1,0:T(8,128)(2,1)S(1)} %pad_maximum_fusion.1), channel_id=1, source_target_pairs={{0,256},{8,264},{16,272},{24,280},{32,288},{40,296},{48,304},{56,3... | collective-permute-start | bytes 393224 | tf_op jit(solution)/shard_map/ppermute | solution.py:43
  53.8 1.9 %collective-permute-start.1 = (bf16[64,512]{1,0:T(8,128)(2,1)}, bf16[64,512]{1,0:T(8,128)(2,1)S(1)}, u32[]{:S(2)}, u32[]{:S(2)}) collective-permute-start(bf16[64,512]{1,0:T(8,128)(2,1)} %get-tuple-element.35), channel_id=1, source_target_pairs={{0,8},{8,16},{16,24},{24,32},{32,40},{40,48},{48,56},{56,64},{64,7... | collective-permute-start | bytes 196616 | tf_op jit(solution)/shard_map/ppermute | solution.py:43
  55.7 3.8 %collective-permute-done.1.refs_6_ = bf16[64,512]{1,0:T(8,128)(2,1)S(1)} collective-permute-done((bf16[64,512]{1,0:T(8,128)(2,1)}, bf16[64,512]{1,0:T(8,128)(2,1)S(1)}, u32[]{:S(2)}, u32[]{:S(2)}) %collective-permute-start.1) | collective-permute-done | bytes 65568 | tf_op jit(solution)/shard_map/ppermute | solution.py:43
  60.2 5.8 %all-to-all-done.refs_0_ = bf16[8,2,144,256]{3,2,1,0:T(8,128)(2,1)S(1)} async-done(((bf16[8,2,144,256]{3,2,1,0:T(8,128)(2,1)}), bf16[8,2,144,256]{3,2,1,0:T(8,128)(2,1)S(1)}, u32[]{:S(2)}, u32[]{:S(2)}) %all-to-all-start) | async-done | bytes 1179680 | tf_op jit(solution)/shard_map/all_to_all | solution.py:331
  66.0 15.2 %all-gather.2.cloned.1.call-done.refs_1_.refs_8_ = bf16[2048,768]{1,0:T(8,128)(2,1)} async-done(((bf16[256,768]{1,0:T(8,128)(2,1)}), bf16[2048,768]{1,0:T(8,128)(2,1)}) %all-gather.2.cloned.1.call-update) | async-done | bytes 3145744 | tf_op jit(solution)/shard_map/all_gather | solution.py:313
  81.2 4.1 %collective-permute-start.3 = (bf16[2048,768]{1,0:T(8,128)(2,1)}, bf16[2048,768]{1,0:T(8,128)(2,1)}, u32[]{:S(2)}, u32[]{:S(2)}) collective-permute-start(bf16[2048,768]{1,0:T(8,128)(2,1)} %all-gather.2.cloned.1.call-done.refs_1_.refs_8_), channel_id=1, source_target_pairs={{0,8},{8,0},{16,24},{24,16},{32,40},{40,32},{48,56},{56,48},{64,72... | collective-permute-start | bytes 9437192 | tf_op jit(solution)/shard_map/ppermute | solution.py:34
  85.3 3.7 %norm.1 = (bf16[2,8,128,256]{3,2,1,0:T(8,128)(2,1)}, f32[128,128]{1,0:T(8,128)}, f32[128,768]{1,0:T(8,128)}) custom-call(bf16[8,2,144,256]{3,2,1,0:T(8,128)(2,1)} %copy-done.1, bf16[2048,768]{1,0:T(8,128)(2,1)} %all-gather.2.cloned.1.call-done.refs_1_.refs_8_), custom_call_target="tpu_custom_call" | custom-call | tf_op jit(solution)/shard_map/norm/pallas_call | solution.py:281
  89.0 1.9 %collective-permute-done.3.refs_11_ = bf16[2048,768]{1,0:T(8,128)(2,1)} collective-permute-done((bf16[2048,768]{1,0:T(8,128)(2,1)}, bf16[2048,768]{1,0:T(8,128)(2,1)}, u32[]{:S(2)}, u32[]{:S(2)}) %collective-permute-start.3) | collective-permute-done | bytes 3145760 | tf_op jit(solution)/shard_map/ppermute | solution.py:34
  90.9 10.3 %layer.1 = (bf16[64,512]{1,0:T(8,128)(2,1)}, bf16[64,512]{1,0:T(8,128)(2,1)}, bf16[64,512]{1,0:T(8,128)(2,1)}, bf16[64,512]{1,0:T(8,128)(2,1)}, bf16[128,128]{1,...) custom-call(bf16[2,8,128,256]{3,2,1,0:T(8,128)(2,1)} %get-tuple-element.39.refs_0_, f32[128,128]{1,0:T(8,128)} %get-tuple-element.40.refs_1_, ...), custom_call_target="tpu_custom_call" | custom-call | tf_op jit(solution)/shard_map/layer/pallas_call | solution.py:281
  101.2 2.8 %value.1 = (bf16[32,64,128]{2,1,0:T(8,128)(2,1)}, bf16[32,64,128]{2,1,0:T(8,128)(2,1)}) custom-call(bf16[2,8,128,256]{3,2,1,0:T(8,128)(2,1)} %get-tuple-element.39.refs_0_, bf16[128,128]{1,0:T(8,128)(2,1)} %get-tuple-element.54.refs_1_), custom_call_target="tpu_custom_call" | custom-call | tf_op jit(solution)/shard_map/value/pallas_call | solution.py:281
  104.0 2.3 %collective-permute-start.8 = (bf16[32,64,128]{2,1,0:T(8,128)(2,1)}, bf16[32,64,128]{2,1,0:T(8,128)(2,1)S(1)}, u32[]{:S(2)}, u32[]{:S(2)}) collective-permute-start(bf16[32,64,128]{2,1,0:T(8,128)(2,1)} %get-tuple-element.56), channel_id=1, source_target_pairs={{0,8},{8,0},{16,24},{24,16},{32,40},{40,32},{48,56},{56,48},{64,72... | collective-permute-start | bytes 1572872 | tf_op jit(solution)/shard_map/ppermute | solution.py:34
  108.1 2.1 %add_convert_fusion = bf16[32,64,128]{2,1,0:T(8,128)(2,1)} fusion(bf16[32,64,128]{2,1,0:T(8,128)(2,1)S(1)} %collective-permute-done.8, bf16[32,64,128]{2,1,0:T(8,128)(2,1)} %get-tuple-element.55), kind=kLoop, calls=%fused_computation.1 | loop fusion | flops 1048576 | bytes 1572864 | tf_op jit(solution)/shard_map/convert_element_type | solution.py:362
  110.2 6.3 %all-to-all-start.1 = ((bf16[32,64,128]{2,1,0:T(8,128)(2,1)}), bf16[32,64,128]{2,1,0:T(8,128)(2,1)S(1)}, u32[]{:S(2)}, u32[]{:S(2)}) async-start(bf16[32,64,128]{2,1,0:T(8,128)(2,1)} %add_convert_fusion), calls=%async_computation.2 | async-start | bytes 1048576 | tf_op jit(solution)/shard_map/all_to_all | solution.py:363
  116.5 2.6 %collective-permute-start.4 = (bf16[64,512]{1,0:T(8,128)(2,1)S(1)}, bf16[64,512]{1,0:T(8,128)(2,1)S(1)}, u32[]{:S(2)}, u32[]{:S(2)}) collective-permute-start(bf16[64,512]{1,0:T(8,128)(2,1)S(1)} %copy-done.10), channel_id=1, source_target_pairs={{0,504},{8,0},{16,8},{24,16},{32,24},{40,32},{48,40},{56,48},{64,5... | collective-permute-start | bytes 196616 | tf_op jit(solution)/shard_map/ppermute | solution.py:43
  119.0 3.3 %collective-permute-start.5 = (bf16[64,512]{1,0:T(8,128)(2,1)S(1)}, bf16[64,512]{1,0:T(8,128)(2,1)S(1)}, u32[]{:S(2)}, u32[]{:S(2)}) collective-permute-start(bf16[64,512]{1,0:T(8,128)(2,1)S(1)} %copy-done.9), channel_id=1, source_target_pairs={{0,8},{8,16},{16,24},{24,32},{32,40},{40,48},{48,56},{56,64},{64,7... | collective-permute-start | bytes 196616 | tf_op jit(solution)/shard_map/ppermute | solution.py:43
  122.4 7.0 %collective-permute-start.6 = (bf16[64,512]{1,0:T(8,128)(2,1)S(1)}, bf16[64,512]{1,0:T(8,128)(2,1)S(1)}, u32[]{:S(2)}, u32[]{:S(2)}) collective-permute-start(bf16[64,512]{1,0:T(8,128)(2,1)S(1)} %copy-done.8), channel_id=1, source_target_pairs={{0,256},{8,264},{16,272},{24,280},{32,288},{40,296},{48,304},{56,3... | collective-permute-start | bytes 196616 | tf_op jit(solution)/shard_map/ppermute | solution.py:43
  129.4 2.7 %collective-permute-start.7 = (bf16[64,512]{1,0:T(8,128)(2,1)S(1)}, bf16[64,512]{1,0:T(8,128)(2,1)S(1)}, u32[]{:S(2)}, u32[]{:S(2)}) collective-permute-start(bf16[64,512]{1,0:T(8,128)(2,1)S(1)} %copy-done.7), channel_id=1, source_target_pairs={{0,264},{8,272},{16,280},{24,288},{32,296},{40,304},{48,312},{56,3... | collective-permute-start | bytes 196616 | tf_op jit(solution)/shard_map/ppermute | solution.py:43
  132.7 3.0 %collective-permute-done.6.refs_3_ = bf16[64,512]{1,0:T(8,128)(2,1)S(1)} collective-permute-done((bf16[64,512]{1,0:T(8,128)(2,1)S(1)}, bf16[64,512]{1,0:T(8,128)(2,1)S(1)}, u32[]{:S(2)}, u32[]{:S(2)}) %collective-permute-start.6) | collective-permute-done | bytes 65568 | tf_op jit(solution)/shard_map/ppermute | solution.py:43
  135.7 4.1 %collective-permute-done.7.refs_4_ = bf16[64,512]{1,0:T(8,128)(2,1)S(1)} collective-permute-done((bf16[64,512]{1,0:T(8,128)(2,1)S(1)}, bf16[64,512]{1,0:T(8,128)(2,1)S(1)}, u32[]{:S(2)}, u32[]{:S(2)}) %collective-permute-start.7) | collective-permute-done | bytes 65568 | tf_op jit(solution)/shard_map/ppermute | solution.py:43
  (44 shorter events, 10.9 us)
Async XLA Ops:
  7.2 74.0 %all-gather.2.cloned.1.call-start = ((), (), s32[]{:S(2)}) async-start(), calls=%async_computation.3 | async-start | bytes 3538944 | tf_op jit(solution)/shard_map/all_gather | solution.py:313
  8.1 21.2 %copy-start.6 = (bf16[512]{0:T(512)(128)(2,1)S(1)}, bf16[512]{0:T(512)(128)(2,1)}, u32[]{:S(2)}) copy-start(bf16[512]{0:T(512)(128)(2,1)} %param.12) | copy-start | bytes 3076
  8.1 21.2 %copy-start.2 = (bf16[128,512]{1,0:T(8,128)(2,1)S(1)}, bf16[128,512]{1,0:T(8,128)(2,1)}, u32[]{:S(2)}) copy-start(bf16[128,512]{1,0:T(8,128)(2,1)} %refs_0_.1) | copy-start | bytes 393220
  30.5 35.6 %all-to-all-start = ((bf16[8,2,144,256]{3,2,1,0:T(8,128)(2,1)}), bf16[8,2,144,256]{3,2,1,0:T(8,128)(2,1)S(1)}, u32[]{:S(2)}, u32[]{:S(2)}) async-start(bf16[8,2,144,256]{3,2,1,0:T(8,128)(2,1)} %broadcast_in_dim.7), calls=%async_computation | async-start | bytes 2359296 | tf_op jit(solution)/shard_map/all_to_all | solution.py:331
  34.0 108.0 %reduce-scatter.2.cloned.1.call-start = ((), (), s32[]{:S(2)}) async-start(), calls=%async_computation.4 | async-start | bytes 1327104 | tf_op jit(solution)/shard_map/reduce_scatter | solution.py:354
  37.2 6.8 %collective-permute-start = (bf16[128,512]{1,0:T(8,128)(2,1)}, bf16[128,512]{1,0:T(8,128)(2,1)S(1)}, u32[]{:S(2)}, u32[]{:S(2)}) collective-permute-start(bf16[128,512]{1,0:T(8,128)(2,1)} %get-tuple-element.34), channel_id=1, source_target_pairs={{0,504},{8,0},{16,8},{24,16},{32,24},{40,32},{48,40},{56,48},{64,5... | collective-permute-start | bytes 393224 | tf_op jit(solution)/shard_map/ppermute | solution.py:43
  44.0 45.0 %copy-start.3 = (bf16[128,512]{1,0:T(8,128)(2,1)}, bf16[128,512]{1,0:T(8,128)(2,1)S(1)}, u32[]{:S(2)}) copy-start(bf16[128,512]{1,0:T(8,128)(2,1)S(1)} %collective-permute-done.refs_5_) | copy-start | bytes 393220
  44.9 15.3 %collective-permute-start.2 = (bf16[128,512]{1,0:T(8,128)(2,1)S(1)}, bf16[128,512]{1,0:T(8,128)(2,1)S(1)}, u32[]{:S(2)}, u32[]{:S(2)}) collective-permute-start(bf16[128,512]{1,0:T(8,128)(2,1)S(1)} %pad_maximum_fusion.1), channel_id=1, source_target_pairs={{0,256},{8,264},{16,272},{24,280},{32,288},{40,296},{48,304},{56,3... | collective-permute-start | bytes 393224 | tf_op jit(solution)/shard_map/ppermute | solution.py:43
  53.8 5.8 %collective-permute-start.1 = (bf16[64,512]{1,0:T(8,128)(2,1)}, bf16[64,512]{1,0:T(8,128)(2,1)S(1)}, u32[]{:S(2)}, u32[]{:S(2)}) collective-permute-start(bf16[64,512]{1,0:T(8,128)(2,1)} %get-tuple-element.35), channel_id=1, source_target_pairs={{0,8},{8,16},{16,24},{24,32},{32,40},{40,48},{48,56},{56,64},{64,7... | collective-permute-start | bytes 196616 | tf_op jit(solution)/shard_map/ppermute | solution.py:43
  59.6 31.4 %copy-start.5 = (bf16[64,512]{1,0:T(8,128)(2,1)}, bf16[64,512]{1,0:T(8,128)(2,1)S(1)}, u32[]{:S(2)}) copy-start(bf16[64,512]{1,0:T(8,128)(2,1)S(1)} %collective-permute-done.1.refs_6_) | copy-start | bytes 196612
  60.2 30.8 %copy-start.4 = (bf16[128,512]{1,0:T(8,128)(2,1)}, bf16[128,512]{1,0:T(8,128)(2,1)S(1)}, u32[]{:S(2)}) copy-start(bf16[128,512]{1,0:T(8,128)(2,1)S(1)} %collective-permute-done.2.refs_7_) | copy-start | bytes 393220
  66.0 19.3 %copy-start.1 = (bf16[8,2,144,256]{3,2,1,0:T(8,128)(2,1)}, bf16[8,2,144,256]{3,2,1,0:T(8,128)(2,1)S(1)}, u32[]{:S(2)}) copy-start(bf16[8,2,144,256]{3,2,1,0:T(8,128)(2,1)S(1)} %all-to-all-done.refs_0_) | copy-start | bytes 3538948
  81.2 9.7 %collective-permute-start.3 = (bf16[2048,768]{1,0:T(8,128)(2,1)}, bf16[2048,768]{1,0:T(8,128)(2,1)}, u32[]{:S(2)}, u32[]{:S(2)}) collective-permute-start(bf16[2048,768]{1,0:T(8,128)(2,1)} %all-gather.2.cloned.1.call-done.refs_1_.refs_8_), channel_id=1, source_target_pairs={{0,8},{8,0},{16,24},{24,16},{32,40},{40,32},{48,56},{56,48},{64,72... | collective-permute-start | bytes 9437192 | tf_op jit(solution)/shard_map/ppermute | solution.py:34
  104.0 4.0 %collective-permute-start.8 = (bf16[32,64,128]{2,1,0:T(8,128)(2,1)}, bf16[32,64,128]{2,1,0:T(8,128)(2,1)S(1)}, u32[]{:S(2)}, u32[]{:S(2)}) collective-permute-start(bf16[32,64,128]{2,1,0:T(8,128)(2,1)} %get-tuple-element.56), channel_id=1, source_target_pairs={{0,8},{8,0},{16,24},{24,16},{32,40},{40,32},{48,56},{56,48},{64,72... | collective-permute-start | bytes 1572872 | tf_op jit(solution)/shard_map/ppermute | solution.py:34
  108.0 8.4 %copy-start.10 = (bf16[64,512]{1,0:T(8,128)(2,1)S(1)}, bf16[64,512]{1,0:T(8,128)(2,1)}, u32[]{:S(2)}) copy-start(bf16[64,512]{1,0:T(8,128)(2,1)} %get-tuple-element.49) | copy-start | bytes 196612
  108.0 11.0 %copy-start.9 = (bf16[64,512]{1,0:T(8,128)(2,1)S(1)}, bf16[64,512]{1,0:T(8,128)(2,1)}, u32[]{:S(2)}) copy-start(bf16[64,512]{1,0:T(8,128)(2,1)} %get-tuple-element.50) | copy-start | bytes 196612
  108.0 14.3 %copy-start.8 = (bf16[64,512]{1,0:T(8,128)(2,1)S(1)}, bf16[64,512]{1,0:T(8,128)(2,1)}, u32[]{:S(2)}) copy-start(bf16[64,512]{1,0:T(8,128)(2,1)} %get-tuple-element.51) | copy-start | bytes 196612
  108.0 21.3 %copy-start.7 = (bf16[64,512]{1,0:T(8,128)(2,1)S(1)}, bf16[64,512]{1,0:T(8,128)(2,1)}, u32[]{:S(2)}) copy-start(bf16[64,512]{1,0:T(8,128)(2,1)} %get-tuple-element.52) | copy-start | bytes 196612
  108.1 31.8 %copy-start = (bf16[256,256]{1,0:T(8,128)(2,1)S(1)}, bf16[256,256]{1,0:T(8,128)(2,1)}, u32[]{:S(2)}) copy-start(bf16[256,256]{1,0:T(8,128)(2,1)} %get-tuple-element.31.refs_0_) | copy-start | bytes 393220
  110.2 31.2 %all-to-all-start.1 = ((bf16[32,64,128]{2,1,0:T(8,128)(2,1)}), bf16[32,64,128]{2,1,0:T(8,128)(2,1)S(1)}, u32[]{:S(2)}, u32[]{:S(2)}) async-start(bf16[32,64,128]{2,1,0:T(8,128)(2,1)} %add_convert_fusion), calls=%async_computation.2 | async-start | bytes 1048576 | tf_op jit(solution)/shard_map/all_to_all | solution.py:363
  116.5 16.2 %collective-permute-start.4 = (bf16[64,512]{1,0:T(8,128)(2,1)S(1)}, bf16[64,512]{1,0:T(8,128)(2,1)S(1)}, u32[]{:S(2)}, u32[]{:S(2)}) collective-permute-start(bf16[64,512]{1,0:T(8,128)(2,1)S(1)} %copy-done.10), channel_id=1, source_target_pairs={{0,504},{8,0},{16,8},{24,16},{32,24},{40,32},{48,40},{56,48},{64,5... | collective-permute-start | bytes 196616 | tf_op jit(solution)/shard_map/ppermute | solution.py:43
  119.0 13.6 %collective-permute-start.5 = (bf16[64,512]{1,0:T(8,128)(2,1)S(1)}, bf16[64,512]{1,0:T(8,128)(2,1)S(1)}, u32[]{:S(2)}, u32[]{:S(2)}) collective-permute-start(bf16[64,512]{1,0:T(8,128)(2,1)S(1)} %copy-done.9), channel_id=1, source_target_pairs={{0,8},{8,16},{16,24},{24,32},{32,40},{40,48},{48,56},{56,64},{64,7... | collective-permute-start | bytes 196616 | tf_op jit(solution)/shard_map/ppermute | solution.py:43
  122.4 13.3 %collective-permute-start.6 = (bf16[64,512]{1,0:T(8,128)(2,1)S(1)}, bf16[64,512]{1,0:T(8,128)(2,1)S(1)}, u32[]{:S(2)}, u32[]{:S(2)}) collective-permute-start(bf16[64,512]{1,0:T(8,128)(2,1)S(1)} %copy-done.8), channel_id=1, source_target_pairs={{0,256},{8,264},{16,272},{24,280},{32,288},{40,296},{48,304},{56,3... | collective-permute-start | bytes 196616 | tf_op jit(solution)/shard_map/ppermute | solution.py:43
  129.4 10.4 %collective-permute-start.7 = (bf16[64,512]{1,0:T(8,128)(2,1)S(1)}, bf16[64,512]{1,0:T(8,128)(2,1)S(1)}, u32[]{:S(2)}, u32[]{:S(2)}) collective-permute-start(bf16[64,512]{1,0:T(8,128)(2,1)S(1)} %copy-done.7), channel_id=1, source_target_pairs={{0,264},{8,272},{16,280},{24,288},{32,296},{40,304},{48,312},{56,3... | collective-permute-start | bytes 196616 | tf_op jit(solution)/shard_map/ppermute | solution.py:43
Sparse Core Ops, SparseCore 0:
  29.4 51.7 all-gather.1
  101.4 34.7 reduce-scatter.1

commit v6 on v5

--- a/solution.py
+++ b/solution.py
@@ -64,11 +64,27 @@
     return (z * NX + x) * NC + c, z, x, c
 
 
+def feature_order(width):
+    natural = lax.broadcasted_iota(jnp.int32, (width, width), 0)
+    place_in = lax.broadcasted_iota(jnp.int32, (width, width), 1)
+    core = place_in >> 8
+    x = (place_in >> 6) & (NX - 1)
+    return jnp.where(natural == x * (NC * 64) + core * 64 + (place_in & 63), 1.0, 0.0).astype(BF)
+
+
 def plan_kernel(
     strides, shards, get, put, send, smem, extra,
 ):
     len_ref, off_ref, shard_ref, start_ref = smem
-    home_ref, dest_ref, cos_ref, sin_ref, allowed_ref = [put(3 + i) for i in range(5)]
+    home_ref, dest_ref, cos_ref, sin_ref, allowed_ref, packed_ref = [put(3 + i) for i in range(6)]
+    order = feature_order(packed_ref.shape[2] * packed_ref.shape[0])
+    deep = packed_ref.shape[2]
+    features = dot_nn(get(2)[...], order).astype(BF)
+    gains = dot_nn(jnp.broadcast_to(get(3)[...], (EXTRA, 2 * deep)), order).astype(BF)
+    for h in range(2):
+        packed_ref[h, :TOK_DEV, :] = features[:, h * deep : (h + 1) * deep]
+        packed_ref[h, TOK_DEV:, :] = gains[:, h * deep : (h + 1) * deep]
+    send(8)
     me = place()[0]
     rows = lax.broadcasted_iota(jnp.int32, (TOK_DEV, TOK_DEV), 0)
     cols = lax.broadcasted_iota(jnp.int32, (TOK_DEV, TOK_DEV), 1)
@@ -135,18 +151,13 @@
 
 
 def value_kernel(get, put, send, smem, extra):
-    c = place()[3]
     kept_ref, given_ref = put(0), put(1)
     grad_value = get(1)[...]
-    for n, half in enumerate((c, 1 - c)):
+    for n, ref in enumerate((kept_ref, given_ref)):
         for j in range(NZ):
             found = dot_tn(get(0)[n, j], grad_value).astype(BF)
-            for pair in range(2):
-                low_rows = found[pair * 128 : pair * 128 + 64, :]
-                high_rows = found[pair * 128 + 64 : (pair + 1) * 128, :]
-                owner = j * NX + 2 * half + pair
-                kept_ref[owner] = jnp.where(c == 0, low_rows, high_rows)
-                given_ref[owner] = jnp.where(c == 0, high_rows, low_rows)
+            for x in range(NX):
+                ref[j * NX + x] = found[x * 64 : (x + 1) * 64, :]
 
 
 def layer_kernel(q_heads, get, put, send, smem, extra):
@@ -163,7 +174,6 @@
     cosine = get(1)[...]
     sine = get(2)[...]
     factor = HEAD ** (-0.5)
-    allowed = get(3)[...] > 0.5
     home = get(4)[...]
     cot = jnp.concatenate(
         [get(6)[...], get(5)[:MAXLEN, :], get(7)[...]], 0
@@ -173,31 +183,34 @@
     value_raw = projected[:, kv_at + HEAD :]
     key = (key_raw * cosine + pltpu.roll(key_raw, HEAD // 2, 1) * sine).astype(BF)
     value = value_raw.astype(BF)
-    grad_key = jnp.zeros((TOK_DEV, HEAD), F32)
-    grad_value = jnp.zeros((TOK_DEV, HEAD), F32)
+    heads = [slice(g * HEAD, (g + 1) * HEAD) for g in range(q_heads)]
+    piles = [slice(g * TOK_DEV, (g + 1) * TOK_DEV) for g in range(q_heads)]
+    cosines = jnp.concatenate([cosine] * q_heads, 0)
+    sines = jnp.concatenate([sine] * q_heads, 0)
+    query_raw = jnp.concatenate([projected[:, at] for at in heads], 0)
+    query = (query_raw * cosines + pltpu.roll(query_raw, HEAD // 2, 1) * sines).astype(BF)
+    grad_out = jnp.concatenate([cot[:, at] for at in heads], 0)
+    scores = dot_nt(query, key) * factor
+    scores = jnp.where(jnp.concatenate([get(3)[...]] * q_heads, 0) > 0.5, scores, F32(-1e30))
+    exp_terms = jnp.exp(scores - jnp.max(scores, -1, keepdims=True))
+    probs = exp_terms / jnp.sum(exp_terms, -1, keepdims=True)
+    probs_low = probs.astype(BF)
+    grad_probs = dot_nt(grad_out, value)
+    mixed = dot_nn(probs_low, value).astype(BF)
+    mixed = dot_nn(home, jnp.concatenate([mixed[at, :] for at in piles], 1)).astype(BF)
+    for e in range(SLOTS):
+        put(e)[...] = mixed[e * MAXLEN : (e + 1) * MAXLEN, :]
+    grad_value = dot_tn(probs_low, grad_out)
+    centre = jnp.sum(grad_probs * probs, -1, keepdims=True)
+    grad_scores = (probs * (grad_probs - centre) * factor).astype(BF)
+    grad_query = dot_nn(grad_scores, key)
+    grad_key = dot_tn(grad_scores, query)
+    grad_query = (grad_query * cosines - pltpu.roll(grad_query, HEAD // 2, 1) * sines).astype(BF)
+    pile_dots = grad_query.astype(F32) * query_raw
     dots = jnp.zeros((TOK_DEV, HEAD), F32)
-    for g in range(q_heads):
-        at = slice(g * HEAD, (g + 1) * HEAD)
-        query_raw = projected[:, at]
-        query = (query_raw * cosine + pltpu.roll(query_raw, HEAD // 2, 1) * sine).astype(BF)
-        scores = jnp.where(allowed, dot_nt(query, key) * factor, F32(-1e30))
-        exp_terms = jnp.exp(scores - jnp.max(scores, -1, keepdims=True))
-        probs = exp_terms / jnp.sum(exp_terms, -1, keepdims=True)
-        probs_low = probs.astype(BF)
-        mixed = dot_nn(probs_low, value).astype(BF)
-        mixed = dot_nn(home, mixed).astype(BF)
-        for e in range(SLOTS):
-            put(e)[:, at] = mixed[e * MAXLEN : (e + 1) * MAXLEN, :]
-        grad_out = cot[:, at]
-        grad_value = grad_value + dot_tn(probs_low, grad_out)
-        grad_probs = dot_nt(grad_out, value)
-        centre = jnp.sum(grad_probs * probs, -1, keepdims=True)
-        grad_scores = (probs * (grad_probs - centre) * factor).astype(BF)
-        grad_query = dot_nn(grad_scores, key)
-        grad_key = grad_key + dot_tn(grad_scores, query)
-        grad_query = (grad_query * cosine - pltpu.roll(grad_query, HEAD // 2, 1) * sine).astype(BF)
-        grads_ref[:, at] = grad_query
-        dots = dots + grad_query.astype(F32) * query_raw
+    for at, pile in zip(heads, piles):
+        grads_ref[:, at] = grad_query[pile, :]
+        dots = dots + pile_dots[pile, :]
     grad_key = (grad_key * cosine - pltpu.roll(grad_key, HEAD // 2, 1) * sine).astype(BF)
     grad_value = grad_value.astype(BF)
     grads_ref[:, kv_at : kv_at + HEAD] = grad_key
@@ -220,17 +233,19 @@
 
 
 def finish_kernel(get, put, send, smem, extra):
-    hidden_ref, gain_ref, total_ref, out_ref = get(0), get(1), get(3), put(0)
-    inverse = get(2)[:, 0:1]
-    deep = total_ref.shape[2]
+    packed_ref, inverse, total_ref = get(0), get(1)[:, 0:1], get(2)
     share = total_ref[0, TOK_DEV:, :].astype(F32)
     share = share[0:1, :TOK_DEV] + share[0:1, TOK_DEV : 2 * TOK_DEV]
     row_dot = jnp.transpose(jnp.broadcast_to(share, (TOK_DEV, TOK_DEV)))[:, 0:1]
+    row_dot = inverse * inverse * inverse * row_dot / D
+    halves = []
     for h in range(2):
-        at = slice(h * deep, (h + 1) * deep)
-        weighted = total_ref[h, :TOK_DEV, :].astype(F32) * gain_ref[:, at].astype(F32)
-        here = hidden_ref[:, at].astype(F32)
-        out_ref[:, at] = (inverse * weighted - here * (inverse * inverse * inverse * row_dot / D)).astype(BF)
+        gain = packed_ref[h, TOK_DEV:, :].astype(F32)[0:1, :]
+        weighted = total_ref[h, :TOK_DEV, :].astype(F32) * gain
+        here = packed_ref[h, :TOK_DEV, :].astype(F32)
+        halves.append((inverse * weighted - here * row_dot).astype(BF))
+    grad = jnp.concatenate(halves, 1)
+    put(0)[...] = dot_nt(grad, feature_order(grad.shape[1])).astype(BF)
 
 
 def lay_kernel(get, put, send, smem, extra):
@@ -307,9 +322,8 @@
     rows_each = D // shards
 
     own = jnp.concatenate([w_query, w_key, w_value], 1)
-    slab = lax.all_gather(own, ("x", "core"), axis=0, tiled=True)
-    own_half = jnp.where(c == 0, slab[:deep], slab[deep:])
-    own_half, cotangent, packed = tied(own_half, cotangent, hidden)
+    own_half = lax.all_gather(own, "x", axis=0, tiled=True)
+    own_half, cotangent = tied(own_half, cotangent)
     mine = lax.all_gather(own_half, "z", axis=0, tiled=True)
 
     half = HEAD // 2
@@ -318,17 +332,15 @@
     square = ((TOK_DEV, TOK_DEV), F32)
     cut = ((MAXLEN, q_cols), BF)
     wide = ((2 * MAXLEN, q_cols), BF)
-    cot_near, cot_behind, cot_far, home, dest, cosine, sine, allowed = kernel_call(
+    cot_near, cot_behind, cot_far, home, dest, cosine, sine, allowed, packed = kernel_call(
         functools.partial(plan_kernel, strides, shards),
-        [wide, cut, cut] + [((SLOTS * MAXLEN, TOK_DEV), BF), ((SLOTS * MAXLEN, CAP), BF)] + [square] * 3,
-        [seq_length.T, home_offset.T, dest_shard.T, dest_offset.T, freq, cotangent],
+        [wide, cut, cut] + [((SLOTS * MAXLEN, TOK_DEV), BF), ((SLOTS * MAXLEN, CAP), BF)] + [square] * 3
+        + [((2, TOK_DEV + EXTRA, deep), BF)],
+        [seq_length.T, home_offset.T, dest_shard.T, dest_offset.T, freq, cotangent, hidden, gain[None, :]],
         "plan", 60, 4,
     )
-    packed = jnp.concatenate([packed, jnp.broadcast_to(gain[None, :], (EXTRA, width))], 0)
-    packed = packed.reshape(TOK_DEV + EXTRA, 2, deep).transpose(1, 0, 2)
-    packed = jnp.broadcast_to(packed[None], (peers,) + packed.shape)
-
-    rows_full = lax.all_to_all(packed, "tensor", split_axis=0, concat_axis=0, tiled=True)
+    copies = jnp.broadcast_to(packed[None], (peers,) + packed.shape)
+    rows_full = lax.all_to_all(copies, "tensor", split_axis=0, concat_axis=0, tiled=True)
     cot_near = passed_along(cot_near, -1)
     cot_behind = passed_along(cot_behind, 1)
     cot_far = passed_along(jnp.concatenate([cot_far, cot_near[MAXLEN:]], 0), shards // 2)
@@ -354,7 +366,7 @@
     total = lax.psum_scatter(terms, "tensor", scatter_dimension=0, tiled=False)
     (grad_hidden,) = kernel_call(
         finish_kernel, [((TOK_DEV, width), BF)],
-        [hidden, gain[None, :], inverse, total], "finish", 60,
+        [packed, inverse, total], "finish", 60,
     )
 
     share = ((NZ * NX, rows_each, k_cols), BF)

time: 152 us -> 150 us (0.987)
  starting transfers between devices: 44.8 us -> 54.5 us
  blocking collectives: 20.3 us -> 11.6 us
  waiting for transfers between devices: 41 us -> 39 us
  other arithmetic: 5.4 us -> 3.68 us
  local copies, waits for them, and re-layouts: 1.75 us -> 3.33 us
    all_gather x1, blocking collectives: 20.3 us -> 11.6 us  [on_device(): own_half = lax.all_gather(own, 'x', axis=0, tiled=True)]
    ppermute x7, starting transfers between devices: 28.4 us -> 34.7 us  [passed_along(): return lax.ppermute(value, DP, [(i, (i + by) % size) for i in range(size)])]
    all_to_all x1, waiting for transfers between devices: 5.84 us -> 0.88 us  [on_device(): lax.all_to_all(copies, 'tensor', split_axis=0, concat_axis=0, tiled=True)]
    all_to_all x1, starting transfers between devices: 3.56 us -> 7.73 us  [on_device(): lax.all_to_all(copies, 'tensor', split_axis=0, concat_axis=0, tiled=True)]
    all_gather x1, waiting for transfers between devices: 15.2 us -> 18.2 us  [on_device(): mine = lax.all_gather(own_half, 'z', axis=0, tiled=True)]
  transfers between devices with their start and end apart: 13 -> 13, of which waited for: 9 -> 9; matrix products, arithmetic and copies ran while one was open for 4% -> 4% of each run, Pallas kernels for 7% -> 8%
where the time goes in v6:
time: 150 us; the launch traced here: 149 us
  starting transfers between devices  54.5 us (36%)
  waiting for transfers between devices  39 us (26%)
  Pallas kernels  22.2 us (15%)
  between operations  14.3 us (10%)
  blocking collectives  11.6 us (8%)
  other arithmetic  3.68 us (2%)
  local copies, waits for them, and re-layouts  3.33 us (2%)
    ppermute x7, starting transfers between devices, passed_along(): return lax.ppermute(value, DP, [(i, (i + by) % size) for i in range(size)])  34.7 us
    pallas_call x6, Pallas kernels, kernel_call(): pl.pallas_call(kernel, out_shape=shapes, in_specs=[pl.BlockSpec(memory_sp...  22.2 us
    all_gather x1, waiting for transfers between devices, on_device(): mine = lax.all_gather(own_half, 'z', axis=0, tiled=True)  18.2 us
    ppermute x7, waiting for transfers between devices, passed_along(): return lax.ppermute(value, DP, [(i, (i + by) % size) for i in range(size)])  16.2 us
    all_gather x1, blocking collectives, on_device(): own_half = lax.all_gather(own, 'x', axis=0, tiled=True)  11.6 us
    all_to_all x1, starting transfers between devices, on_device(): lax.all_to_all(copies, 'tensor', split_axis=0, concat_axis=0, tiled=True)  7.73 us
    all_to_all x1, starting transfers between devices, on_device(): lax.all_to_all(pair, ('z', 'x'), split_axis=0, concat_axis=0, tiled=True)  6.29 us
    ppermute x2, starting transfers between devices, moved(): return lax.ppermute(value, DP, pairs)  5.68 us
  transfers between devices with their start and end apart: 13, of which 9 were waited for; matrix products, arithmetic and copies ran while one was open for 4% of the time, Pallas kernels for 8%

profile of v6, /device:TPU:1, one launch (start us, length us, event | category | flops | bytes accessed | tf_op | source)
XLA Modules:
  0.0 148.6 jit_solution(13836109926516560900)
XLA Ops:
  8.1 11.6 %all_gather.6 = bf16[256,768]{1,0:T(8,128)(2,1)} all-gather(bf16[64,768]{1,0:T(8,128)(2,1)S(1)} %pad_maximum_fusion.1), channel_id=1, replica_groups=mesh['z'=8,'x'=4,'core'=2,'tensor'=8] {'x'}, dimensions={0}, use_global_device_ids=true | all-gather | bytes 491520 | tf_op jit(solution)/shard_map/all_gather | solution.py:325
  20.9 3.6 %plan.1 = (bf16[128,512]{1,0:T(8,128)(2,1)}, bf16[64,512]{1,0:T(8,128)(2,1)}, bf16[64,512]{1,0:T(8,128)(2,1)}, bf16[256,128]{1,0:T(8,128)(2,1)}, bf16[256,256]{1...) custom-call(s32[4,64]{1,0:T(4,128)} %bitcast.6, ...), custom_call_target="tpu_custom_call" | custom-call | tf_op jit(solution)/shard_map/plan/pallas_call | solution.py:296
  24.6 2.0 %broadcast_in_dim.10 = bf16[8,2,144,256]{3,2,1,0:T(8,128)(2,1)} broadcast(bf16[2,144,256]{2,1,0:T(8,128)(2,1)} %get-tuple-element.33.refs_0_), dimensions={1,2,3} | broadcast | bytes 1327104 | tf_op jit(solution)/shard_map/broadcast_in_dim | solution.py:342
  26.6 7.7 %all-to-all-start = ((bf16[8,2,144,256]{3,2,1,0:T(8,128)(2,1)}), bf16[8,2,144,256]{3,2,1,0:T(8,128)(2,1)S(1)}, u32[]{:S(2)}, u32[]{:S(2)}) async-start(bf16[8,2,144,256]{3,2,1,0:T(8,128)(2,1)} %broadcast_in_dim.10), calls=%async_computation | async-start | bytes 2359296 | tf_op jit(solution)/shard_map/all_to_all | solution.py:343
  34.4 6.5 %collective-permute-start = (bf16[128,512]{1,0:T(8,128)(2,1)S(1)}, bf16[128,512]{1,0:T(8,128)(2,1)S(1)}, u32[]{:S(2)}, u32[]{:S(2)}) collective-permute-start(bf16[128,512]{1,0:T(8,128)(2,1)S(1)} %copy-done.6), channel_id=1, source_target_pairs={{0,504},{8,0},{16,8},{24,16},{32,24},{40,32},{48,40},{56,48},{64,5... | collective-permute-start | bytes 393224 | tf_op jit(solution)/shard_map/ppermute | solution.py:43
  40.8 2.7 %collective-permute-done.refs_5_ = bf16[128,512]{1,0:T(8,128)(2,1)S(1)} collective-permute-done((bf16[128,512]{1,0:T(8,128)(2,1)S(1)}, bf16[128,512]{1,0:T(8,128)(2,1)S(1)}, u32[]{:S(2)}, u32[]{:S(2)}) %collective-permute-start) | collective-permute-done | bytes 131104 | tf_op jit(solution)/shard_map/ppermute | solution.py:43
  43.6 10.7 %collective-permute-start.2 = (bf16[128,512]{1,0:T(8,128)(2,1)S(1)}, bf16[128,512]{1,0:T(8,128)(2,1)S(1)}, u32[]{:S(2)}, u32[]{:S(2)}) collective-permute-start(bf16[128,512]{1,0:T(8,128)(2,1)S(1)} %pad_maximum_fusion), channel_id=1, source_target_pairs={{0,256},{8,264},{16,272},{24,280},{32,288},{40,296},{48,304},{56,3... | collective-permute-start | bytes 393224 | tf_op jit(solution)/shard_map/ppermute | solution.py:43
  54.4 1.9 %collective-permute-start.1 = (bf16[64,512]{1,0:T(8,128)(2,1)S(1)}, bf16[64,512]{1,0:T(8,128)(2,1)S(1)}, u32[]{:S(2)}, u32[]{:S(2)}) collective-permute-start(bf16[64,512]{1,0:T(8,128)(2,1)S(1)} %copy-done.11), channel_id=1, source_target_pairs={{0,8},{8,16},{16,24},{24,32},{32,40},{40,48},{48,56},{56,64},{64,7... | collective-permute-start | bytes 196616 | tf_op jit(solution)/shard_map/ppermute | solution.py:43
  58.1 4.0 %collective-permute-done.2.refs_7_ = bf16[128,512]{1,0:T(8,128)(2,1)S(1)} collective-permute-done((bf16[128,512]{1,0:T(8,128)(2,1)S(1)}, bf16[128,512]{1,0:T(8,128)(2,1)S(1)}, u32[]{:S(2)}, u32[]{:S(2)}) %collective-permute-start.2) | collective-permute-done | bytes 131104 | tf_op jit(solution)/shard_map/ppermute | solution.py:43
  63.0 18.2 %all-gather.2.cloned.1.call-done.refs_1_.refs_8_ = bf16[2048,768]{1,0:T(8,128)(2,1)} async-done(((bf16[256,768]{1,0:T(8,128)(2,1)}), bf16[2048,768]{1,0:T(8,128)(2,1)}) %all-gather.2.cloned.1.call-update) | async-done | bytes 3145744 | tf_op jit(solution)/shard_map/all_gather | solution.py:327
  81.1 3.4 %collective-permute-start.3 = (bf16[2048,768]{1,0:T(8,128)(2,1)}, bf16[2048,768]{1,0:T(8,128)(2,1)}, u32[]{:S(2)}, u32[]{:S(2)}) collective-permute-start(bf16[2048,768]{1,0:T(8,128)(2,1)} %all-gather.2.cloned.1.call-done.refs_1_.refs_8_), channel_id=1, source_target_pairs={{0,8},{8,0},{16,24},{24,16},{32,40},{40,32},{48,56},{56,48},{64,72... | collective-permute-start | bytes 9437192 | tf_op jit(solution)/shard_map/ppermute | solution.py:34
  84.6 3.7 %norm.1 = (bf16[2,8,128,256]{3,2,1,0:T(8,128)(2,1)}, f32[128,128]{1,0:T(8,128)}, f32[128,768]{1,0:T(8,128)}) custom-call(bf16[8,2,144,256]{3,2,1,0:T(8,128)(2,1)} %copy-done.1, bf16[2048,768]{1,0:T(8,128)(2,1)} %all-gather.2.cloned.1.call-done.refs_1_.refs_8_), custom_call_target="tpu_custom_call" | custom-call | tf_op jit(solution)/shard_map/norm/pallas_call | solution.py:296
  90.2 8.7 %layer.1 = (bf16[64,512]{1,0:T(8,128)(2,1)}, bf16[64,512]{1,0:T(8,128)(2,1)}, bf16[64,512]{1,0:T(8,128)(2,1)}, bf16[64,512]{1,0:T(8,128)(2,1)}, bf16[128,128]{1,...) custom-call(bf16[2,8,128,256]{3,2,1,0:T(8,128)(2,1)} %get-tuple-element.39.refs_0_, f32[128,128]{1,0:T(8,128)} %get-tuple-element.40.refs_1_, ...), custom_call_target="tpu_custom_call" | custom-call | tf_op jit(solution)/shard_map/layer/pallas_call | solution.py:296
  99.0 2.6 %value.1 = (bf16[32,64,128]{2,1,0:T(8,128)(2,1)}, bf16[32,64,128]{2,1,0:T(8,128)(2,1)}) custom-call(bf16[2,8,128,256]{3,2,1,0:T(8,128)(2,1)} %get-tuple-element.39.refs_0_, bf16[128,128]{1,0:T(8,128)(2,1)} %get-tuple-element.54.refs_1_), custom_call_target="tpu_custom_call" | custom-call | tf_op jit(solution)/shard_map/value/pallas_call | solution.py:296
  101.6 2.3 %collective-permute-start.8 = (bf16[32,64,128]{2,1,0:T(8,128)(2,1)}, bf16[32,64,128]{2,1,0:T(8,128)(2,1)S(1)}, u32[]{:S(2)}, u32[]{:S(2)}) collective-permute-start(bf16[32,64,128]{2,1,0:T(8,128)(2,1)} %get-tuple-element.56), channel_id=1, source_target_pairs={{0,8},{8,0},{16,24},{24,16},{32,40},{40,32},{48,56},{56,48},{64,72... | collective-permute-start | bytes 1572872 | tf_op jit(solution)/shard_map/ppermute | solution.py:34
  105.6 2.1 %add_convert_fusion = bf16[32,64,128]{2,1,0:T(8,128)(2,1)} fusion(bf16[32,64,128]{2,1,0:T(8,128)(2,1)S(1)} %collective-permute-done.8, bf16[32,64,128]{2,1,0:T(8,128)(2,1)} %get-tuple-element.55), kind=kLoop, calls=%fused_computation.1 | loop fusion | flops 1048576 | bytes 1572864 | tf_op jit(solution)/shard_map/convert_element_type | solution.py:374
  107.7 6.3 %all-to-all-start.1 = ((bf16[32,64,128]{2,1,0:T(8,128)(2,1)}), bf16[32,64,128]{2,1,0:T(8,128)(2,1)S(1)}, u32[]{:S(2)}, u32[]{:S(2)}) async-start(bf16[32,64,128]{2,1,0:T(8,128)(2,1)} %add_convert_fusion), calls=%async_computation.2 | async-start | bytes 1048576 | tf_op jit(solution)/shard_map/all_to_all | solution.py:375
  114.0 2.6 %collective-permute-start.4 = (bf16[64,512]{1,0:T(8,128)(2,1)S(1)}, bf16[64,512]{1,0:T(8,128)(2,1)S(1)}, u32[]{:S(2)}, u32[]{:S(2)}) collective-permute-start(bf16[64,512]{1,0:T(8,128)(2,1)S(1)} %copy-done.10), channel_id=1, source_target_pairs={{0,504},{8,0},{16,8},{24,16},{32,24},{40,32},{48,40},{56,48},{64,5... | collective-permute-start | bytes 196616 | tf_op jit(solution)/shard_map/ppermute | solution.py:43
  116.6 3.3 %collective-permute-start.5 = (bf16[64,512]{1,0:T(8,128)(2,1)S(1)}, bf16[64,512]{1,0:T(8,128)(2,1)S(1)}, u32[]{:S(2)}, u32[]{:S(2)}) collective-permute-start(bf16[64,512]{1,0:T(8,128)(2,1)S(1)} %copy-done.9), channel_id=1, source_target_pairs={{0,8},{8,16},{16,24},{24,32},{32,40},{40,48},{48,56},{56,64},{64,7... | collective-permute-start | bytes 196616 | tf_op jit(solution)/shard_map/ppermute | solution.py:43
  119.9 7.0 %collective-permute-start.6 = (bf16[64,512]{1,0:T(8,128)(2,1)S(1)}, bf16[64,512]{1,0:T(8,128)(2,1)S(1)}, u32[]{:S(2)}, u32[]{:S(2)}) collective-permute-start(bf16[64,512]{1,0:T(8,128)(2,1)S(1)} %copy-done.8), channel_id=1, source_target_pairs={{0,256},{8,264},{16,272},{24,280},{32,288},{40,296},{48,304},{56,3... | collective-permute-start | bytes 196616 | tf_op jit(solution)/shard_map/ppermute | solution.py:43
  126.9 2.7 %collective-permute-start.7 = (bf16[64,512]{1,0:T(8,128)(2,1)S(1)}, bf16[64,512]{1,0:T(8,128)(2,1)S(1)}, u32[]{:S(2)}, u32[]{:S(2)}) collective-permute-start(bf16[64,512]{1,0:T(8,128)(2,1)S(1)} %copy-done.7), channel_id=1, source_target_pairs={{0,264},{8,272},{16,280},{24,288},{32,296},{40,304},{48,312},{56,3... | collective-permute-start | bytes 196616 | tf_op jit(solution)/shard_map/ppermute | solution.py:43
  129.6 3.6 %collective-permute-done.6.refs_3_ = bf16[64,512]{1,0:T(8,128)(2,1)S(1)} collective-permute-done((bf16[64,512]{1,0:T(8,128)(2,1)S(1)}, bf16[64,512]{1,0:T(8,128)(2,1)S(1)}, u32[]{:S(2)}, u32[]{:S(2)}) %collective-permute-start.6) | collective-permute-done | bytes 65568 | tf_op jit(solution)/shard_map/ppermute | solution.py:43
  133.2 4.1 %collective-permute-done.7.refs_4_ = bf16[64,512]{1,0:T(8,128)(2,1)S(1)} collective-permute-done((bf16[64,512]{1,0:T(8,128)(2,1)S(1)}, bf16[64,512]{1,0:T(8,128)(2,1)S(1)}, u32[]{:S(2)}, u32[]{:S(2)}) %collective-permute-start.7) | collective-permute-done | bytes 65568 | tf_op jit(solution)/shard_map/ppermute | solution.py:43
  139.6 2.1 %finish.1 = bf16[128,512]{1,0:T(8,128)(2,1)} custom-call(bf16[2,144,256]{2,1,0:T(8,128)(2,1)} %get-tuple-element.33.refs_0_, f32[128,128]{1,0:T(8,128)} %get-tuple-element.47.refs_9_.refs_1_, bf16[2,144,256]{2,1,0:T(8,128)(2,1)} %bitcast.5), custom_call_target="tpu_custom_call" | custom-call | tf_op jit(solution)/shard_map/finish/pallas_call | solution.py:296
  (42 shorter events, 10.8 us)
Async XLA Ops:
  7.2 74.0 %all-gather.2.cloned.1.call-start = ((), (), s32[]{:S(2)}) async-start(), calls=%async_computation.3 | async-start | bytes 3538944 | tf_op jit(solution)/shard_map/all_gather | solution.py:327
  26.6 17.0 %copy-start.5 = (bf16[64,512]{1,0:T(8,128)(2,1)S(1)}, bf16[64,512]{1,0:T(8,128)(2,1)}, u32[]{:S(2)}) copy-start(bf16[64,512]{1,0:T(8,128)(2,1)} %get-tuple-element.36) | copy-start | bytes 196612
  26.6 27.8 %copy-start.11 = (bf16[64,512]{1,0:T(8,128)(2,1)S(1)}, bf16[64,512]{1,0:T(8,128)(2,1)}, u32[]{:S(2)}) copy-start(bf16[64,512]{1,0:T(8,128)(2,1)} %get-tuple-element.35) | copy-start | bytes 196612
  26.6 36.4 %all-to-all-start = ((bf16[8,2,144,256]{3,2,1,0:T(8,128)(2,1)}), bf16[8,2,144,256]{3,2,1,0:T(8,128)(2,1)S(1)}, u32[]{:S(2)}, u32[]{:S(2)}) async-start(bf16[8,2,144,256]{3,2,1,0:T(8,128)(2,1)} %broadcast_in_dim.10), calls=%async_computation | async-start | bytes 2359296 | tf_op jit(solution)/shard_map/all_to_all | solution.py:343
  34.3 105.3 %reduce-scatter.2.cloned.1.call-start = ((), (), s32[]{:S(2)}) async-start(), calls=%async_computation.4 | async-start | bytes 1327104 | tf_op jit(solution)/shard_map/reduce_scatter | solution.py:366
  34.4 9.2 %collective-permute-start = (bf16[128,512]{1,0:T(8,128)(2,1)S(1)}, bf16[128,512]{1,0:T(8,128)(2,1)S(1)}, u32[]{:S(2)}, u32[]{:S(2)}) collective-permute-start(bf16[128,512]{1,0:T(8,128)(2,1)S(1)} %copy-done.6), channel_id=1, source_target_pairs={{0,504},{8,0},{16,8},{24,16},{32,24},{40,32},{48,40},{56,48},{64,5... | collective-permute-start | bytes 393224 | tf_op jit(solution)/shard_map/ppermute | solution.py:43
  43.6 44.7 %copy-start.2 = (bf16[128,512]{1,0:T(8,128)(2,1)}, bf16[128,512]{1,0:T(8,128)(2,1)S(1)}, u32[]{:S(2)}) copy-start(bf16[128,512]{1,0:T(8,128)(2,1)S(1)} %collective-permute-done.refs_5_) | copy-start | bytes 393220
  43.6 18.5 %collective-permute-start.2 = (bf16[128,512]{1,0:T(8,128)(2,1)S(1)}, bf16[128,512]{1,0:T(8,128)(2,1)S(1)}, u32[]{:S(2)}, u32[]{:S(2)}) collective-permute-start(bf16[128,512]{1,0:T(8,128)(2,1)S(1)} %pad_maximum_fusion), channel_id=1, source_target_pairs={{0,256},{8,264},{16,272},{24,280},{32,288},{40,296},{48,304},{56,3... | collective-permute-start | bytes 393224 | tf_op jit(solution)/shard_map/ppermute | solution.py:43
  54.4 3.7 %collective-permute-start.1 = (bf16[64,512]{1,0:T(8,128)(2,1)S(1)}, bf16[64,512]{1,0:T(8,128)(2,1)S(1)}, u32[]{:S(2)}, u32[]{:S(2)}) collective-permute-start(bf16[64,512]{1,0:T(8,128)(2,1)S(1)} %copy-done.11), channel_id=1, source_target_pairs={{0,8},{8,16},{16,24},{24,32},{32,40},{40,48},{48,56},{56,64},{64,7... | collective-permute-start | bytes 196616 | tf_op jit(solution)/shard_map/ppermute | solution.py:43
  58.1 32.1 %copy-start.4 = (bf16[64,512]{1,0:T(8,128)(2,1)}, bf16[64,512]{1,0:T(8,128)(2,1)S(1)}, u32[]{:S(2)}) copy-start(bf16[64,512]{1,0:T(8,128)(2,1)S(1)} %collective-permute-done.1.refs_6_) | copy-start | bytes 196612
  62.1 28.1 %copy-start.3 = (bf16[128,512]{1,0:T(8,128)(2,1)}, bf16[128,512]{1,0:T(8,128)(2,1)S(1)}, u32[]{:S(2)}) copy-start(bf16[128,512]{1,0:T(8,128)(2,1)S(1)} %collective-permute-done.2.refs_7_) | copy-start | bytes 393220
  63.0 21.6 %copy-start.1 = (bf16[8,2,144,256]{3,2,1,0:T(8,128)(2,1)}, bf16[8,2,144,256]{3,2,1,0:T(8,128)(2,1)S(1)}, u32[]{:S(2)}) copy-start(bf16[8,2,144,256]{3,2,1,0:T(8,128)(2,1)S(1)} %all-to-all-done.refs_0_) | copy-start | bytes 3538948
  81.1 9.0 %collective-permute-start.3 = (bf16[2048,768]{1,0:T(8,128)(2,1)}, bf16[2048,768]{1,0:T(8,128)(2,1)}, u32[]{:S(2)}, u32[]{:S(2)}) collective-permute-start(bf16[2048,768]{1,0:T(8,128)(2,1)} %all-gather.2.cloned.1.call-done.refs_1_.refs_8_), channel_id=1, source_target_pairs={{0,8},{8,0},{16,24},{24,16},{32,40},{40,32},{48,56},{56,48},{64,72... | collective-permute-start | bytes 9437192 | tf_op jit(solution)/shard_map/ppermute | solution.py:34
  101.6 4.0 %collective-permute-start.8 = (bf16[32,64,128]{2,1,0:T(8,128)(2,1)}, bf16[32,64,128]{2,1,0:T(8,128)(2,1)S(1)}, u32[]{:S(2)}, u32[]{:S(2)}) collective-permute-start(bf16[32,64,128]{2,1,0:T(8,128)(2,1)} %get-tuple-element.56), channel_id=1, source_target_pairs={{0,8},{8,0},{16,24},{24,16},{32,40},{40,32},{48,56},{56,48},{64,72... | collective-permute-start | bytes 1572872 | tf_op jit(solution)/shard_map/ppermute | solution.py:34
  105.6 8.4 %copy-start.10 = (bf16[64,512]{1,0:T(8,128)(2,1)S(1)}, bf16[64,512]{1,0:T(8,128)(2,1)}, u32[]{:S(2)}) copy-start(bf16[64,512]{1,0:T(8,128)(2,1)} %get-tuple-element.49) | copy-start | bytes 196612
  105.6 11.0 %copy-start.9 = (bf16[64,512]{1,0:T(8,128)(2,1)S(1)}, bf16[64,512]{1,0:T(8,128)(2,1)}, u32[]{:S(2)}) copy-start(bf16[64,512]{1,0:T(8,128)(2,1)} %get-tuple-element.50) | copy-start | bytes 196612
  105.6 14.3 %copy-start.8 = (bf16[64,512]{1,0:T(8,128)(2,1)S(1)}, bf16[64,512]{1,0:T(8,128)(2,1)}, u32[]{:S(2)}) copy-start(bf16[64,512]{1,0:T(8,128)(2,1)} %get-tuple-element.51) | copy-start | bytes 196612
  105.6 21.3 %copy-start.7 = (bf16[64,512]{1,0:T(8,128)(2,1)S(1)}, bf16[64,512]{1,0:T(8,128)(2,1)}, u32[]{:S(2)}) copy-start(bf16[64,512]{1,0:T(8,128)(2,1)} %get-tuple-element.52) | copy-start | bytes 196612
  105.6 31.8 %copy-start = (bf16[256,256]{1,0:T(8,128)(2,1)S(1)}, bf16[256,256]{1,0:T(8,128)(2,1)}, u32[]{:S(2)}) copy-start(bf16[256,256]{1,0:T(8,128)(2,1)} %get-tuple-element.31.refs_0_) | copy-start | bytes 393220
  107.7 31.2 %all-to-all-start.1 = ((bf16[32,64,128]{2,1,0:T(8,128)(2,1)}), bf16[32,64,128]{2,1,0:T(8,128)(2,1)S(1)}, u32[]{:S(2)}, u32[]{:S(2)}) async-start(bf16[32,64,128]{2,1,0:T(8,128)(2,1)} %add_convert_fusion), calls=%async_computation.2 | async-start | bytes 1048576 | tf_op jit(solution)/shard_map/all_to_all | solution.py:375
  114.0 15.6 %collective-permute-start.4 = (bf16[64,512]{1,0:T(8,128)(2,1)S(1)}, bf16[64,512]{1,0:T(8,128)(2,1)S(1)}, u32[]{:S(2)}, u32[]{:S(2)}) collective-permute-start(bf16[64,512]{1,0:T(8,128)(2,1)S(1)} %copy-done.10), channel_id=1, source_target_pairs={{0,504},{8,0},{16,8},{24,16},{32,24},{40,32},{48,40},{56,48},{64,5... | collective-permute-start | bytes 196616 | tf_op jit(solution)/shard_map/ppermute | solution.py:43
  116.6 13.1 %collective-permute-start.5 = (bf16[64,512]{1,0:T(8,128)(2,1)S(1)}, bf16[64,512]{1,0:T(8,128)(2,1)S(1)}, u32[]{:S(2)}, u32[]{:S(2)}) collective-permute-start(bf16[64,512]{1,0:T(8,128)(2,1)S(1)} %copy-done.9), channel_id=1, source_target_pairs={{0,8},{8,16},{16,24},{24,32},{32,40},{40,48},{48,56},{56,64},{64,7... | collective-permute-start | bytes 196616 | tf_op jit(solution)/shard_map/ppermute | solution.py:43
  119.9 13.3 %collective-permute-start.6 = (bf16[64,512]{1,0:T(8,128)(2,1)S(1)}, bf16[64,512]{1,0:T(8,128)(2,1)S(1)}, u32[]{:S(2)}, u32[]{:S(2)}) collective-permute-start(bf16[64,512]{1,0:T(8,128)(2,1)S(1)} %copy-done.8), channel_id=1, source_target_pairs={{0,256},{8,264},{16,272},{24,280},{32,288},{40,296},{48,304},{56,3... | collective-permute-start | bytes 196616 | tf_op jit(solution)/shard_map/ppermute | solution.py:43
  126.9 10.4 %collective-permute-start.7 = (bf16[64,512]{1,0:T(8,128)(2,1)S(1)}, bf16[64,512]{1,0:T(8,128)(2,1)S(1)}, u32[]{:S(2)}, u32[]{:S(2)}) collective-permute-start(bf16[64,512]{1,0:T(8,128)(2,1)S(1)} %copy-done.7), channel_id=1, source_target_pairs={{0,264},{8,272},{16,280},{24,288},{32,296},{40,304},{48,312},{56,3... | collective-permute-start | bytes 196616 | tf_op jit(solution)/shard_map/ppermute | solution.py:43
  (1 other events, 7.8 us)
Sparse Core Ops, SparseCore 0:
  19.8 61.3 all-gather.1
  99.1 34.6 reduce-scatter.1

commit v7 on v6

--- a/solution.py
+++ b/solution.py
@@ -77,14 +77,19 @@
 ):
     len_ref, off_ref, shard_ref, start_ref = smem
     home_ref, dest_ref, cos_ref, sin_ref, allowed_ref, packed_ref = [put(3 + i) for i in range(6)]
-    order = feature_order(packed_ref.shape[2] * packed_ref.shape[0])
-    deep = packed_ref.shape[2]
+    deep = packed_ref.shape[1]
+    order = feature_order(2 * deep)
     features = dot_nn(get(2)[...], order).astype(BF)
-    gains = dot_nn(jnp.broadcast_to(get(3)[...], (EXTRA, 2 * deep)), order).astype(BF)
+    gains = dot_nn(jnp.broadcast_to(get(3)[...], (EXTRA, 2 * deep)), order)
     for h in range(2):
-        packed_ref[h, :TOK_DEV, :] = features[:, h * deep : (h + 1) * deep]
-        packed_ref[h, TOK_DEV:, :] = gains[:, h * deep : (h + 1) * deep]
+        packed_ref[h * TOK_DEV : (h + 1) * TOK_DEV, :] = features[:, h * deep : (h + 1) * deep]
+    gains = jnp.concatenate(
+        [gains[: EXTRA // 2, :deep], gains[: EXTRA // 2, deep:]], 0
+    )
+    packed_ref[2 * TOK_DEV :, :] = gains.astype(BF)
     send(8)
+    put(9)[...] = order
+    send(9)
     me = place()[0]
     rows = lax.broadcasted_iota(jnp.int32, (TOK_DEV, TOK_DEV), 0)
     cols = lax.broadcasted_iota(jnp.int32, (TOK_DEV, TOK_DEV), 1)
@@ -130,24 +135,23 @@
 def norm_kernel(get, put, send, smem, extra):
     c = place()[3]
     rows_ref, normed_ref, inverse_ref, partial_ref = get(0), put(0), put(1), put(2)
-    deep = rows_ref.shape[3]
+    deep = rows_ref.shape[2]
     squares = jnp.zeros((TOK_DEV, 1), F32)
     for j in range(NZ):
         for h in range(2):
-            part = rows_ref[j, h, :TOK_DEV, :].astype(F32)
+            part = rows_ref[j, h * TOK_DEV : (h + 1) * TOK_DEV, :].astype(F32)
             squares = squares + jnp.sum(part * part, 1, keepdims=True)
     inverse = lax.rsqrt(squares / D + EPSILON)
     inverse_ref[...] = jnp.broadcast_to(inverse, inverse_ref.shape)
     for n, half in enumerate((c, 1 - c)):
         for j in range(NZ):
-            gain = rows_ref[j, half, TOK_DEV:, :].astype(F32)[0:1, :]
-            part = rows_ref[j, half, :TOK_DEV, :].astype(F32) * inverse * gain
-            normed_ref[n, j] = part.astype(BF)
+            gains = rows_ref[j, 2 * TOK_DEV :, :].astype(F32)
+            gain = jnp.where(half == 0, gains[0:1, :], gains[EXTRA // 2 : EXTRA // 2 + 1, :])
+            at = pl.ds(pl.multiple_of(half * TOK_DEV, TOK_DEV), TOK_DEV)
+            part = rows_ref[j, at, :].astype(F32) * inverse * gain
+            normed_ref[n, :, j * deep : (j + 1) * deep] = part.astype(BF)
     send(0)
-    partial = jnp.zeros(partial_ref.shape, F32)
-    for j in range(NZ):
-        partial = partial + dot_nn(normed_ref[0, j], get(1)[j * deep : (j + 1) * deep, :])
-    partial_ref[...] = partial
+    partial_ref[...] = dot_nn(normed_ref[0], get(1)[...])
 
 
 def value_kernel(get, put, send, smem, extra):
@@ -155,7 +159,7 @@
     grad_value = get(1)[...]
     for n, ref in enumerate((kept_ref, given_ref)):
         for j in range(NZ):
-            found = dot_tn(get(0)[n, j], grad_value).astype(BF)
+            found = dot_tn(get(0)[n, :, j * 256 : (j + 1) * 256], grad_value).astype(BF)
             for x in range(NX):
                 ref[j * NX + x] = found[x * 64 : (x + 1) * 64, :]
 
@@ -166,11 +170,8 @@
     c = place()[3]
     kv_at = q_heads * HEAD
     inverse = get(9)[:, 0:1]
-    normed_ref = get(0)
-    deep = normed_ref.shape[3]
-    projected = get(10)[...]
-    for j in range(NZ):
-        projected = projected + dot_nn(normed_ref[1, j], get(11)[j * deep : (j + 1) * deep, :])
+    deep = terms_ref.shape[2]
+    projected = get(10)[...] + dot_nn(get(0)[1], get(8)[...])
     cosine = get(1)[...]
     sine = get(2)[...]
     factor = HEAD ** (-0.5)
@@ -225,27 +226,29 @@
     low = (share - high.astype(F32)).astype(BF)
     tail = jnp.concatenate([high, low], 1)
     grads = grads_ref[...]
-    for half, ref in ((c, 8), (1 - c, 11)):
+    for half, ref in ((1 - c, 8), (c, 11)):
         for j in range(NZ):
             found = dot_nt(grads, get(ref)[j * deep : (j + 1) * deep, :])
-            terms_ref[j, half, :TOK_DEV, :] = found.astype(BF)
-            terms_ref[j, half, TOK_DEV:, :] = tail
+            terms_ref[j, pl.ds(pl.multiple_of(half * TOK_DEV, TOK_DEV), TOK_DEV), :] = found.astype(BF)
+    for j in range(NZ):
+        terms_ref[j, 2 * TOK_DEV :, :] = tail
 
 
 def finish_kernel(get, put, send, smem, extra):
     packed_ref, inverse, total_ref = get(0), get(1)[:, 0:1], get(2)
-    share = total_ref[0, TOK_DEV:, :].astype(F32)
+    share = total_ref[2 * TOK_DEV :, :].astype(F32)
     share = share[0:1, :TOK_DEV] + share[0:1, TOK_DEV : 2 * TOK_DEV]
     row_dot = jnp.transpose(jnp.broadcast_to(share, (TOK_DEV, TOK_DEV)))[:, 0:1]
     row_dot = inverse * inverse * inverse * row_dot / D
     halves = []
     for h in range(2):
-        gain = packed_ref[h, TOK_DEV:, :].astype(F32)[0:1, :]
-        weighted = total_ref[h, :TOK_DEV, :].astype(F32) * gain
-        here = packed_ref[h, :TOK_DEV, :].astype(F32)
+        gain = packed_ref[2 * TOK_DEV :, :].astype(F32)[h * (EXTRA // 2) : h * (EXTRA // 2) + 1, :]
+        rows = slice(h * TOK_DEV, (h + 1) * TOK_DEV)
+        weighted = total_ref[rows, :].astype(F32) * gain
+        here = packed_ref[rows, :].astype(F32)
         halves.append((inverse * weighted - here * row_dot).astype(BF))
     grad = jnp.concatenate(halves, 1)
-    put(0)[...] = dot_nt(grad, feature_order(grad.shape[1])).astype(BF)
+    put(0)[...] = dot_nt(grad, get(3)[...]).astype(BF)
 
 
 def lay_kernel(get, put, send, smem, extra):
@@ -322,7 +325,9 @@
     rows_each = D // shards
 
     own = jnp.concatenate([w_query, w_key, w_value], 1)
-    own_half = lax.all_gather(own, "x", axis=0, tiled=True)
+    own_half = lax.all_to_all(
+        jnp.broadcast_to(own[None], (NX,) + own.shape), "x", split_axis=0, concat_axis=0, tiled=True
+    ).reshape(NX * own.shape[0], own.shape[1])
     own_half, cotangent = tied(own_half, cotangent)
     mine = lax.all_gather(own_half, "z", axis=0, tiled=True)
 
@@ -330,12 +335,13 @@
     freq = np.power(np.float32(ROPE_BASE), -(np.arange(half, dtype=np.float32) * np.float32(2.0 / HEAD)))
     freq = jnp.asarray(np.concatenate([freq, freq])[None, :].astype(np.float32))
     square = ((TOK_DEV, TOK_DEV), F32)
+    block = (2 * TOK_DEV + EXTRA, deep)
     cut = ((MAXLEN, q_cols), BF)
     wide = ((2 * MAXLEN, q_cols), BF)
-    cot_near, cot_behind, cot_far, home, dest, cosine, sine, allowed, packed = kernel_call(
+    cot_near, cot_behind, cot_far, home, dest, cosine, sine, allowed, packed, order = kernel_call(
         functools.partial(plan_kernel, strides, shards),
         [wide, cut, cut] + [((SLOTS * MAXLEN, TOK_DEV), BF), ((SLOTS * MAXLEN, CAP), BF)] + [square] * 3
-        + [((2, TOK_DEV + EXTRA, deep), BF)],
+        + [(block, BF), ((width, width), BF)],
         [seq_length.T, home_offset.T, dest_shard.T, dest_offset.T, freq, cotangent, hidden, gain[None, :]],
         "plan", 60, 4,
     )
@@ -352,21 +358,20 @@
 
     normed, inverse, partial = kernel_call(
         norm_kernel,
-        [((2, NZ, TOK_DEV, deep), BF), square, ((TOK_DEV, q_cols + 2 * k_cols), F32)],
+        [((2, TOK_DEV, NZ * deep), BF), square, ((TOK_DEV, q_cols + 2 * k_cols), F32)],
         [rows_full, mine], "norm", 60,
     )
-    block = (2, TOK_DEV + EXTRA, deep)
     *attn_cuts, grad_value, terms = kernel_call(
         functools.partial(layer_kernel, q_heads),
         [cut] * 4 + [((TOK_DEV, k_cols), BF), ((peers,) + block, BF)],
-        [normed, cosine, sine, allowed, home, cot_near, cot_behind, cot_far, mine, inverse, partial, theirs],
+        [normed, cosine, sine, allowed, home, cot_near, cot_behind, cot_far, theirs, inverse, partial, mine],
         "layer", 60, 0,
         [pltpu.VMEM((TOK_DEV, q_cols + 2 * k_cols), BF)],
     )
     total = lax.psum_scatter(terms, "tensor", scatter_dimension=0, tiled=False)
     (grad_hidden,) = kernel_call(
         finish_kernel, [((TOK_DEV, width), BF)],
-        [packed, inverse, total], "finish", 60,
+        [packed, inverse, total, order], "finish", 60,
     )
 
     share = ((NZ * NX, rows_each, k_cols), BF)

time: 150 us -> 146 us (0.973)
  starting transfers between devices: 54.5 us -> 52.8 us
    all_gather x1 -> x0, blocking collectives: 11.6 us -> none  [on_device(): own_half = lax.all_gather(own, 'x', axis=0, tiled=True)]
    all_to_all x0 -> x1, blocking collectives: none -> 11 us  [on_device(): lax.all_to_all(jnp.broadcast_to(own[None], (NX,) + own.shape), 'x', split...]
    all_to_all x1, waiting for transfers between devices: 0.88 us -> 5.54 us  [on_device(): lax.all_to_all(copies, 'tensor', split_axis=0, concat_axis=0, tiled=True)]
    all_gather x1, waiting for transfers between devices: 18.2 us -> 13.8 us  [on_device(): mine = lax.all_gather(own_half, 'z', axis=0, tiled=True)]
    ppermute x7, starting transfers between devices: 34.7 us -> 32.3 us  [passed_along(): return lax.ppermute(value, DP, [(i, (i + by) % size) for i in range(size)])]
where the time goes in v7:
time: 146 us; the launch traced here: 144 us
  starting transfers between devices  52.8 us (36%)
  waiting for transfers between devices  39 us (27%)
  Pallas kernels  21.1 us (14%)
  between operations  14.3 us (10%)
  blocking collectives  11 us (8%)
  other arithmetic  3.71 us (3%)
  local copies, waits for them, and re-layouts  2.64 us (2%)
    ppermute x7, starting transfers between devices, passed_along(): return lax.ppermute(value, DP, [(i, (i + by) % size) for i in range(size)])  32.3 us
    pallas_call x6, Pallas kernels, kernel_call(): pl.pallas_call(kernel, out_shape=shapes, in_specs=[pl.BlockSpec(memory_sp...  21.1 us
    ppermute x7, waiting for transfers between devices, passed_along(): return lax.ppermute(value, DP, [(i, (i + by) % size) for i in range(size)])  15.9 us
    all_gather x1, waiting for transfers between devices, on_device(): mine = lax.all_gather(own_half, 'z', axis=0, tiled=True)  13.8 us
    all_to_all x1, blocking collectives, on_device(): lax.all_to_all(jnp.broadcast_to(own[None], (NX,) + own.shape), 'x', split...  11 us
    all_to_all x1, starting transfers between devices, on_device(): lax.all_to_all(copies, 'tensor', split_axis=0, concat_axis=0, tiled=True)  7.88 us
    ppermute x2, starting transfers between devices, moved(): return lax.ppermute(value, DP, pairs)  6.27 us
    all_to_all x1, starting transfers between devices, on_device(): lax.all_to_all(pair, ('z', 'x'), split_axis=0, concat_axis=0, tiled=True)  6.25 us
  transfers between devices with their start and end apart: 13, of which 9 were waited for; matrix products, arithmetic and copies ran while one was open for 4% of the time, Pallas kernels for 8%

profile of v7, /device:TPU:1, one launch (start us, length us, event | category | flops | bytes accessed | tf_op | source)
XLA Modules:
  0.0 144.5 jit_solution(9281324687990449808)
XLA Ops:
  8.1 11.0 %all_to_all.15 = bf16[4,64,768]{2,1,0:T(8,128)(2,1)} all-to-all(bf16[4,64,768]{2,1,0:T(8,128)(2,1)S(1)} %broadcast_in_dim.6), channel_id=1, replica_groups=mesh['z'=8,'x'=4,'core'=2,'tensor'=8] {'x'}, dimensions={0} | all-to-all | bytes 786432 | tf_op jit(solution)/shard_map/all_to_all | solution.py:328
  19.7 3.6 %plan.1 = (bf16[128,512]{1,0:T(8,128)(2,1)}, bf16[64,512]{1,0:T(8,128)(2,1)}, bf16[64,512]{1,0:T(8,128)(2,1)}, bf16[256,128]{1,0:T(8,128)(2,1)}, bf16[256,256]{1...) custom-call(s32[4,64]{1,0:T(4,128)} %bitcast.8, ...), custom_call_target="tpu_custom_call" | custom-call | tf_op jit(solution)/shard_map/plan/pallas_call | solution.py:299
  25.4 7.9 %all-to-all-start.1 = ((bf16[8,272,256]{2,1,0:T(8,128)(2,1)}), bf16[8,272,256]{2,1,0:T(8,128)(2,1)S(1)}, u32[]{:S(2)}, u32[]{:S(2)}) async-start(bf16[8,272,256]{2,1,0:T(8,128)(2,1)} %broadcast_in_dim.8), calls=%async_computation.1 | async-start | bytes 2228224 | tf_op jit(solution)/shard_map/all_to_all | solution.py:349
  33.3 4.1 %collective-permute-start = (bf16[128,512]{1,0:T(8,128)(2,1)S(1)}, bf16[128,512]{1,0:T(8,128)(2,1)S(1)}, u32[]{:S(2)}, u32[]{:S(2)}) collective-permute-start(bf16[128,512]{1,0:T(8,128)(2,1)S(1)} %copy-done.7), channel_id=1, source_target_pairs={{0,504},{8,0},{16,8},{24,16},{32,24},{40,32},{48,40},{56,48},{64,5... | collective-permute-start | bytes 393224 | tf_op jit(solution)/shard_map/ppermute | solution.py:43
  37.4 3.1 %collective-permute-done.refs_5_ = bf16[128,512]{1,0:T(8,128)(2,1)S(1)} collective-permute-done((bf16[128,512]{1,0:T(8,128)(2,1)S(1)}, bf16[128,512]{1,0:T(8,128)(2,1)S(1)}, u32[]{:S(2)}, u32[]{:S(2)}) %collective-permute-start) | collective-permute-done | bytes 131104 | tf_op jit(solution)/shard_map/ppermute | solution.py:43
  40.5 10.7 %collective-permute-start.2 = (bf16[128,512]{1,0:T(8,128)(2,1)S(1)}, bf16[128,512]{1,0:T(8,128)(2,1)S(1)}, u32[]{:S(2)}, u32[]{:S(2)}) collective-permute-start(bf16[128,512]{1,0:T(8,128)(2,1)S(1)} %pad_maximum_fusion), channel_id=1, source_target_pairs={{0,256},{8,264},{16,272},{24,280},{32,288},{40,296},{48,304},{56,3... | collective-permute-start | bytes 393224 | tf_op jit(solution)/shard_map/ppermute | solution.py:43
  53.2 3.0 %collective-permute-done.1.refs_6_ = bf16[64,512]{1,0:T(8,128)(2,1)S(1)} collective-permute-done((bf16[64,512]{1,0:T(8,128)(2,1)S(1)}, bf16[64,512]{1,0:T(8,128)(2,1)S(1)}, u32[]{:S(2)}, u32[]{:S(2)}) %collective-permute-start.1) | collective-permute-done | bytes 65568 | tf_op jit(solution)/shard_map/ppermute | solution.py:43
  56.2 2.1 %collective-permute-done.2.refs_7_ = bf16[128,512]{1,0:T(8,128)(2,1)S(1)} collective-permute-done((bf16[128,512]{1,0:T(8,128)(2,1)S(1)}, bf16[128,512]{1,0:T(8,128)(2,1)S(1)}, u32[]{:S(2)}, u32[]{:S(2)}) %collective-permute-start.2) | collective-permute-done | bytes 131104 | tf_op jit(solution)/shard_map/ppermute | solution.py:43
  58.3 5.5 %all-to-all-done.1.refs_0_ = bf16[8,272,256]{2,1,0:T(8,128)(2,1)S(1)} async-done(((bf16[8,272,256]{2,1,0:T(8,128)(2,1)}), bf16[8,272,256]{2,1,0:T(8,128)(2,1)S(1)}, u32[]{:S(2)}, u32[]{:S(2)}) %all-to-all-start.1) | async-done | bytes 1114144 | tf_op jit(solution)/shard_map/all_to_all | solution.py:349
  63.8 13.8 %all-gather.2.cloned.1.call-done.refs_1_.refs_11_ = bf16[2048,768]{1,0:T(8,128)(2,1)} async-done(((bf16[256,768]{1,0:T(8,128)(2,1)}), bf16[2048,768]{1,0:T(8,128)(2,1)}) %all-gather.2.cloned.1.call-update) | async-done | bytes 3145744 | tf_op jit(solution)/shard_map/all_gather | solution.py:332
  77.6 4.0 %collective-permute-start.3 = (bf16[2048,768]{1,0:T(8,128)(2,1)}, bf16[2048,768]{1,0:T(8,128)(2,1)}, u32[]{:S(2)}, u32[]{:S(2)}) collective-permute-start(bf16[2048,768]{1,0:T(8,128)(2,1)} %all-gather.2.cloned.1.call-done.refs_1_.refs_11_), channel_id=1, source_target_pairs={{0,8},{8,0},{16,24},{24,16},{32,40},{40,32},{48,56},{56,48},{64,72... | collective-permute-start | bytes 9437192 | tf_op jit(solution)/shard_map/ppermute | solution.py:34
  81.6 3.6 %norm.1 = (bf16[2,128,2048]{2,1,0:T(8,128)(2,1)}, f32[128,128]{1,0:T(8,128)}, f32[128,768]{1,0:T(8,128)}) custom-call(bf16[8,272,256]{2,1,0:T(8,128)(2,1)} %copy-done.1, bf16[2048,768]{1,0:T(8,128)(2,1)} %all-gather.2.cloned.1.call-done.refs_1_.refs_11_), custom_call_target="tpu_custom_call" | custom-call | tf_op jit(solution)/shard_map/norm/pallas_call | solution.py:299
  87.2 7.5 %layer.1 = (bf16[64,512]{1,0:T(8,128)(2,1)}, bf16[64,512]{1,0:T(8,128)(2,1)}, bf16[64,512]{1,0:T(8,128)(2,1)}, bf16[64,512]{1,0:T(8,128)(2,1)}, bf16[128,128]{1,0:T(8,128)(2,1)}, /*index=5*/bf16[8,272,256]{2,1,0:T(8,128)(2,1)}) custom-call(bf16[2,128,2048]{2,1,0:T(8,128)(2,1)} %get-tuple-element.40.refs_0_, f32[128,128]{1,0:T(8,128)} %get-tuple-element.41.refs_1_, ...), custom_call_target="tpu_custom_call" | custom-call | tf_op jit(solution)/shard_map/layer/pallas_call | solution.py:299
  94.8 2.6 %value.1 = (bf16[32,64,128]{2,1,0:T(8,128)(2,1)}, bf16[32,64,128]{2,1,0:T(8,128)(2,1)}) custom-call(bf16[2,128,2048]{2,1,0:T(8,128)(2,1)} %get-tuple-element.40.refs_0_, bf16[128,128]{1,0:T(8,128)(2,1)} %get-tuple-element.56.refs_1_), custom_call_target="tpu_custom_call" | custom-call | tf_op jit(solution)/shard_map/value/pallas_call | solution.py:299
  97.4 2.3 %collective-permute-start.8 = (bf16[32,64,128]{2,1,0:T(8,128)(2,1)}, bf16[32,64,128]{2,1,0:T(8,128)(2,1)S(1)}, u32[]{:S(2)}, u32[]{:S(2)}) collective-permute-start(bf16[32,64,128]{2,1,0:T(8,128)(2,1)} %get-tuple-element.58), channel_id=1, source_target_pairs={{0,8},{8,0},{16,24},{24,16},{32,40},{40,32},{48,56},{56,48},{64,72... | collective-permute-start | bytes 1572872 | tf_op jit(solution)/shard_map/ppermute | solution.py:34
  101.4 2.1 %add_convert_fusion = bf16[32,64,128]{2,1,0:T(8,128)(2,1)} fusion(bf16[32,64,128]{2,1,0:T(8,128)(2,1)S(1)} %collective-permute-done.8, bf16[32,64,128]{2,1,0:T(8,128)(2,1)} %get-tuple-element.57), kind=kLoop, calls=%fused_computation.1 | loop fusion | flops 1048576 | bytes 1572864 | tf_op jit(solution)/shard_map/convert_element_type | solution.py:379
  103.5 6.3 %all-to-all-start.2 = ((bf16[32,64,128]{2,1,0:T(8,128)(2,1)}), bf16[32,64,128]{2,1,0:T(8,128)(2,1)S(1)}, u32[]{:S(2)}, u32[]{:S(2)}) async-start(bf16[32,64,128]{2,1,0:T(8,128)(2,1)} %add_convert_fusion), calls=%async_computation.3 | async-start | bytes 1048576 | tf_op jit(solution)/shard_map/all_to_all | solution.py:380
  109.8 2.6 %collective-permute-start.4 = (bf16[64,512]{1,0:T(8,128)(2,1)S(1)}, bf16[64,512]{1,0:T(8,128)(2,1)S(1)}, u32[]{:S(2)}, u32[]{:S(2)}) collective-permute-start(bf16[64,512]{1,0:T(8,128)(2,1)S(1)} %copy-done.11), channel_id=1, source_target_pairs={{0,504},{8,0},{16,8},{24,16},{32,24},{40,32},{48,40},{56,48},{64,5... | collective-permute-start | bytes 196616 | tf_op jit(solution)/shard_map/ppermute | solution.py:43
  112.4 3.3 %collective-permute-start.5 = (bf16[64,512]{1,0:T(8,128)(2,1)S(1)}, bf16[64,512]{1,0:T(8,128)(2,1)S(1)}, u32[]{:S(2)}, u32[]{:S(2)}) collective-permute-start(bf16[64,512]{1,0:T(8,128)(2,1)S(1)} %copy-done.10), channel_id=1, source_target_pairs={{0,8},{8,16},{16,24},{24,32},{32,40},{40,48},{48,56},{56,64},{64,7... | collective-permute-start | bytes 196616 | tf_op jit(solution)/shard_map/ppermute | solution.py:43
  115.7 7.0 %collective-permute-start.6 = (bf16[64,512]{1,0:T(8,128)(2,1)S(1)}, bf16[64,512]{1,0:T(8,128)(2,1)S(1)}, u32[]{:S(2)}, u32[]{:S(2)}) collective-permute-start(bf16[64,512]{1,0:T(8,128)(2,1)S(1)} %copy-done.9), channel_id=1, source_target_pairs={{0,256},{8,264},{16,272},{24,280},{32,288},{40,296},{48,304},{56,3... | collective-permute-start | bytes 196616 | tf_op jit(solution)/shard_map/ppermute | solution.py:43
  122.7 2.7 %collective-permute-start.7 = (bf16[64,512]{1,0:T(8,128)(2,1)S(1)}, bf16[64,512]{1,0:T(8,128)(2,1)S(1)}, u32[]{:S(2)}, u32[]{:S(2)}) collective-permute-start(bf16[64,512]{1,0:T(8,128)(2,1)S(1)} %copy-done.8), channel_id=1, source_target_pairs={{0,264},{8,272},{16,280},{24,288},{32,296},{40,304},{48,312},{56,3... | collective-permute-start | bytes 196616 | tf_op jit(solution)/shard_map/ppermute | solution.py:43
  125.5 3.6 %collective-permute-done.6.refs_3_ = bf16[64,512]{1,0:T(8,128)(2,1)S(1)} collective-permute-done((bf16[64,512]{1,0:T(8,128)(2,1)S(1)}, bf16[64,512]{1,0:T(8,128)(2,1)S(1)}, u32[]{:S(2)}, u32[]{:S(2)}) %collective-permute-start.6) | collective-permute-done | bytes 65568 | tf_op jit(solution)/shard_map/ppermute | solution.py:43
  129.0 4.1 %collective-permute-done.7.refs_4_ = bf16[64,512]{1,0:T(8,128)(2,1)S(1)} collective-permute-done((bf16[64,512]{1,0:T(8,128)(2,1)S(1)}, bf16[64,512]{1,0:T(8,128)(2,1)S(1)}, u32[]{:S(2)}, u32[]{:S(2)}) %collective-permute-start.7) | collective-permute-done | bytes 65568 | tf_op jit(solution)/shard_map/ppermute | solution.py:43
  135.4 2.2 %finish.1 = bf16[128,512]{1,0:T(8,128)(2,1)} custom-call(bf16[272,256]{1,0:T(8,128)(2,1)} %get-tuple-element.34.refs_0_, f32[128,128]{1,0:T(8,128)} %get-tuple-element.48.refs_9_.refs_1_, bf16[272,256]{1,0:T(8,128)(2,1)} %bitcast.7, bf16[512,512]{1,0:T(8,128)(2,1)} %get-tuple-element.55.refs_3_), custom_call_target="tpu_custom_call" | custom-call | tf_op jit(solution)/shard_map/finish/pallas_call | solution.py:299
  (45 shorter events, 11.5 us)
Async XLA Ops:
  7.2 12.0 %copy-start.6 = (bf16[512]{0:T(512)(128)(2,1)S(1)}, bf16[512]{0:T(512)(128)(2,1)}, u32[]{:S(2)}) copy-start(bf16[512]{0:T(512)(128)(2,1)} %param.12) | copy-start | bytes 3076
  7.2 70.4 %all-gather.2.cloned.1.call-start = ((), (), s32[]{:S(2)}) async-start(), calls=%async_computation.4 | async-start | bytes 3538944 | tf_op jit(solution)/shard_map/all_gather | solution.py:332
  25.4 15.1 %copy-start.5 = (bf16[64,512]{1,0:T(8,128)(2,1)S(1)}, bf16[64,512]{1,0:T(8,128)(2,1)}, u32[]{:S(2)}) copy-start(bf16[64,512]{1,0:T(8,128)(2,1)} %get-tuple-element.37) | copy-start | bytes 196612
  25.4 25.9 %copy-start.12 = (bf16[64,512]{1,0:T(8,128)(2,1)S(1)}, bf16[64,512]{1,0:T(8,128)(2,1)}, u32[]{:S(2)}) copy-start(bf16[64,512]{1,0:T(8,128)(2,1)} %get-tuple-element.36) | copy-start | bytes 196612
  25.4 38.5 %all-to-all-start.1 = ((bf16[8,272,256]{2,1,0:T(8,128)(2,1)}), bf16[8,272,256]{2,1,0:T(8,128)(2,1)S(1)}, u32[]{:S(2)}, u32[]{:S(2)}) async-start(bf16[8,272,256]{2,1,0:T(8,128)(2,1)} %broadcast_in_dim.8), calls=%async_computation.1 | async-start | bytes 2228224 | tf_op jit(solution)/shard_map/all_to_all | solution.py:349
  33.2 102.2 %reduce-scatter.2.cloned.1.call-start = ((), (), s32[]{:S(2)}) async-start(), calls=%async_computation.5 | async-start | bytes 1253376 | tf_op jit(solution)/shard_map/reduce_scatter | solution.py:371
  33.3 7.2 %collective-permute-start = (bf16[128,512]{1,0:T(8,128)(2,1)S(1)}, bf16[128,512]{1,0:T(8,128)(2,1)S(1)}, u32[]{:S(2)}, u32[]{:S(2)}) collective-permute-start(bf16[128,512]{1,0:T(8,128)(2,1)S(1)} %copy-done.7), channel_id=1, source_target_pairs={{0,504},{8,0},{16,8},{24,16},{32,24},{40,32},{48,40},{56,48},{64,5... | collective-permute-start | bytes 393224 | tf_op jit(solution)/shard_map/ppermute | solution.py:43
  40.5 44.7 %copy-start.2 = (bf16[128,512]{1,0:T(8,128)(2,1)}, bf16[128,512]{1,0:T(8,128)(2,1)S(1)}, u32[]{:S(2)}) copy-start(bf16[128,512]{1,0:T(8,128)(2,1)S(1)} %collective-permute-done.refs_5_) | copy-start | bytes 393220
  40.5 17.8 %collective-permute-start.2 = (bf16[128,512]{1,0:T(8,128)(2,1)S(1)}, bf16[128,512]{1,0:T(8,128)(2,1)S(1)}, u32[]{:S(2)}, u32[]{:S(2)}) collective-permute-start(bf16[128,512]{1,0:T(8,128)(2,1)S(1)} %pad_maximum_fusion), channel_id=1, source_target_pairs={{0,256},{8,264},{16,272},{24,280},{32,288},{40,296},{48,304},{56,3... | collective-permute-start | bytes 393224 | tf_op jit(solution)/shard_map/ppermute | solution.py:43
  51.3 5.0 %collective-permute-start.1 = (bf16[64,512]{1,0:T(8,128)(2,1)S(1)}, bf16[64,512]{1,0:T(8,128)(2,1)S(1)}, u32[]{:S(2)}, u32[]{:S(2)}) collective-permute-start(bf16[64,512]{1,0:T(8,128)(2,1)S(1)} %copy-done.12), channel_id=1, source_target_pairs={{0,8},{8,16},{16,24},{24,32},{32,40},{40,48},{48,56},{56,64},{64,7... | collective-permute-start | bytes 196616 | tf_op jit(solution)/shard_map/ppermute | solution.py:43
  56.2 31.0 %copy-start.4 = (bf16[64,512]{1,0:T(8,128)(2,1)}, bf16[64,512]{1,0:T(8,128)(2,1)S(1)}, u32[]{:S(2)}) copy-start(bf16[64,512]{1,0:T(8,128)(2,1)S(1)} %collective-permute-done.1.refs_6_) | copy-start | bytes 196612
  58.3 28.9 %copy-start.3 = (bf16[128,512]{1,0:T(8,128)(2,1)}, bf16[128,512]{1,0:T(8,128)(2,1)S(1)}, u32[]{:S(2)}) copy-start(bf16[128,512]{1,0:T(8,128)(2,1)S(1)} %collective-permute-done.2.refs_7_) | copy-start | bytes 393220
  63.8 17.8 %copy-start.1 = (bf16[8,272,256]{2,1,0:T(8,128)(2,1)}, bf16[8,272,256]{2,1,0:T(8,128)(2,1)S(1)}, u32[]{:S(2)}) copy-start(bf16[8,272,256]{2,1,0:T(8,128)(2,1)S(1)} %all-to-all-done.1.refs_0_) | copy-start | bytes 3342340
  77.6 9.6 %collective-permute-start.3 = (bf16[2048,768]{1,0:T(8,128)(2,1)}, bf16[2048,768]{1,0:T(8,128)(2,1)}, u32[]{:S(2)}, u32[]{:S(2)}) collective-permute-start(bf16[2048,768]{1,0:T(8,128)(2,1)} %all-gather.2.cloned.1.call-done.refs_1_.refs_11_), channel_id=1, source_target_pairs={{0,8},{8,0},{16,24},{24,16},{32,40},{40,32},{48,56},{56,48},{64,72... | collective-permute-start | bytes 9437192 | tf_op jit(solution)/shard_map/ppermute | solution.py:34
  97.4 4.0 %collective-permute-start.8 = (bf16[32,64,128]{2,1,0:T(8,128)(2,1)}, bf16[32,64,128]{2,1,0:T(8,128)(2,1)S(1)}, u32[]{:S(2)}, u32[]{:S(2)}) collective-permute-start(bf16[32,64,128]{2,1,0:T(8,128)(2,1)} %get-tuple-element.58), channel_id=1, source_target_pairs={{0,8},{8,0},{16,24},{24,16},{32,40},{40,32},{48,56},{56,48},{64,72... | collective-permute-start | bytes 1572872 | tf_op jit(solution)/shard_map/ppermute | solution.py:34
  101.4 11.0 %copy-start.10 = (bf16[64,512]{1,0:T(8,128)(2,1)S(1)}, bf16[64,512]{1,0:T(8,128)(2,1)}, u32[]{:S(2)}) copy-start(bf16[64,512]{1,0:T(8,128)(2,1)} %get-tuple-element.51) | copy-start | bytes 196612
  101.4 14.3 %copy-start.9 = (bf16[64,512]{1,0:T(8,128)(2,1)S(1)}, bf16[64,512]{1,0:T(8,128)(2,1)}, u32[]{:S(2)}) copy-start(bf16[64,512]{1,0:T(8,128)(2,1)} %get-tuple-element.52) | copy-start | bytes 196612
  101.4 21.3 %copy-start.8 = (bf16[64,512]{1,0:T(8,128)(2,1)S(1)}, bf16[64,512]{1,0:T(8,128)(2,1)}, u32[]{:S(2)}) copy-start(bf16[64,512]{1,0:T(8,128)(2,1)} %get-tuple-element.53) | copy-start | bytes 196612
  101.4 31.8 %copy-start = (bf16[256,256]{1,0:T(8,128)(2,1)S(1)}, bf16[256,256]{1,0:T(8,128)(2,1)}, u32[]{:S(2)}) copy-start(bf16[256,256]{1,0:T(8,128)(2,1)} %get-tuple-element.32.refs_0_) | copy-start | bytes 393220
  103.5 31.2 %all-to-all-start.2 = ((bf16[32,64,128]{2,1,0:T(8,128)(2,1)}), bf16[32,64,128]{2,1,0:T(8,128)(2,1)S(1)}, u32[]{:S(2)}, u32[]{:S(2)}) async-start(bf16[32,64,128]{2,1,0:T(8,128)(2,1)} %add_convert_fusion), calls=%async_computation.3 | async-start | bytes 1048576 | tf_op jit(solution)/shard_map/all_to_all | solution.py:380
  109.8 15.6 %collective-permute-start.4 = (bf16[64,512]{1,0:T(8,128)(2,1)S(1)}, bf16[64,512]{1,0:T(8,128)(2,1)S(1)}, u32[]{:S(2)}, u32[]{:S(2)}) collective-permute-start(bf16[64,512]{1,0:T(8,128)(2,1)S(1)} %copy-done.11), channel_id=1, source_target_pairs={{0,504},{8,0},{16,8},{24,16},{32,24},{40,32},{48,40},{56,48},{64,5... | collective-permute-start | bytes 196616 | tf_op jit(solution)/shard_map/ppermute | solution.py:43
  112.4 13.1 %collective-permute-start.5 = (bf16[64,512]{1,0:T(8,128)(2,1)S(1)}, bf16[64,512]{1,0:T(8,128)(2,1)S(1)}, u32[]{:S(2)}, u32[]{:S(2)}) collective-permute-start(bf16[64,512]{1,0:T(8,128)(2,1)S(1)} %copy-done.10), channel_id=1, source_target_pairs={{0,8},{8,16},{16,24},{24,32},{32,40},{40,48},{48,56},{56,64},{64,7... | collective-permute-start | bytes 196616 | tf_op jit(solution)/shard_map/ppermute | solution.py:43
  115.7 13.3 %collective-permute-start.6 = (bf16[64,512]{1,0:T(8,128)(2,1)S(1)}, bf16[64,512]{1,0:T(8,128)(2,1)S(1)}, u32[]{:S(2)}, u32[]{:S(2)}) collective-permute-start(bf16[64,512]{1,0:T(8,128)(2,1)S(1)} %copy-done.9), channel_id=1, source_target_pairs={{0,256},{8,264},{16,272},{24,280},{32,288},{40,296},{48,304},{56,3... | collective-permute-start | bytes 196616 | tf_op jit(solution)/shard_map/ppermute | solution.py:43
  122.7 10.4 %collective-permute-start.7 = (bf16[64,512]{1,0:T(8,128)(2,1)S(1)}, bf16[64,512]{1,0:T(8,128)(2,1)S(1)}, u32[]{:S(2)}, u32[]{:S(2)}) collective-permute-start(bf16[64,512]{1,0:T(8,128)(2,1)S(1)} %copy-done.8), channel_id=1, source_target_pairs={{0,264},{8,272},{16,280},{24,288},{32,296},{40,304},{48,312},{56,3... | collective-permute-start | bytes 196616 | tf_op jit(solution)/shard_map/ppermute | solution.py:43
  (2 other events, 16.3 us)
Sparse Core Ops, SparseCore 0:
  19.3 58.2 all-gather.1
  94.9 34.6 reduce-scatter.1

commit v8 on v7

--- a/solution.py
+++ b/solution.py
@@ -135,6 +135,11 @@
 def norm_kernel(get, put, send, smem, extra):
     c = place()[3]
     rows_ref, normed_ref, inverse_ref, partial_ref = get(0), put(0), put(1), put(2)
+    cot = jnp.concatenate([get(4)[...], get(3)[:MAXLEN, :], get(5)[...]], 0)
+    cot = dot_tn(get(2)[...], cot).astype(BF)
+    for g in range(cot.shape[1] // HEAD):
+        put(3)[g * TOK_DEV : (g + 1) * TOK_DEV, :] = cot[:, g * HEAD : (g + 1) * HEAD]
+    send(3)
     deep = rows_ref.shape[2]
     squares = jnp.zeros((TOK_DEV, 1), F32)
     for j in range(NZ):
@@ -169,17 +174,13 @@
     value_out_ref, terms_ref = put(4), put(5)
     c = place()[3]
     kv_at = q_heads * HEAD
-    inverse = get(9)[:, 0:1]
+    inverse = get(7)[:, 0:1]
     deep = terms_ref.shape[2]
-    projected = get(10)[...] + dot_nn(get(0)[1], get(8)[...])
+    projected = get(8)[...] + dot_nn(get(0)[1], get(6)[...])
     cosine = get(1)[...]
     sine = get(2)[...]
     factor = HEAD ** (-0.5)
     home = get(4)[...]
-    cot = jnp.concatenate(
-        [get(6)[...], get(5)[:MAXLEN, :], get(7)[...]], 0
-    )
-    cot = dot_tn(home, cot).astype(BF)
     key_raw = projected[:, kv_at : kv_at + HEAD]
     value_raw = projected[:, kv_at + HEAD :]
     key = (key_raw * cosine + pltpu.roll(key_raw, HEAD // 2, 1) * sine).astype(BF)
@@ -190,7 +191,7 @@
     sines = jnp.concatenate([sine] * q_heads, 0)
     query_raw = jnp.concatenate([projected[:, at] for at in heads], 0)
     query = (query_raw * cosines + pltpu.roll(query_raw, HEAD // 2, 1) * sines).astype(BF)
-    grad_out = jnp.concatenate([cot[:, at] for at in heads], 0)
+    grad_out = get(5)[...]
     scores = dot_nt(query, key) * factor
     scores = jnp.where(jnp.concatenate([get(3)[...]] * q_heads, 0) > 0.5, scores, F32(-1e30))
     exp_terms = jnp.exp(scores - jnp.max(scores, -1, keepdims=True))
@@ -226,12 +227,12 @@
     low = (share - high.astype(F32)).astype(BF)
     tail = jnp.concatenate([high, low], 1)
     grads = grads_ref[...]
-    for half, ref in ((1 - c, 8), (c, 11)):
-        for j in range(NZ):
-            found = dot_nt(grads, get(ref)[j * deep : (j + 1) * deep, :])
-            terms_ref[j, pl.ds(pl.multiple_of(half * TOK_DEV, TOK_DEV), TOK_DEV), :] = found.astype(BF)
     for j in range(NZ):
         terms_ref[j, 2 * TOK_DEV :, :] = tail
+        for half, ref in ((1 - c, 6), (c, 9)):
+            at = pl.ds(pl.multiple_of(half * TOK_DEV, TOK_DEV), TOK_DEV)
+            terms_ref[j, at, :] = dot_nt(grads, get(ref)[j * deep : (j + 1) * deep, :]).astype(BF)
+        send(5, j)
 
 
 def finish_kernel(get, put, send, smem, extra):
@@ -258,10 +259,11 @@
     put(0)[...] = dot_tn(get(0)[...], rows).astype(BF)
 
 
-def kernel_call(body, outs, args, name, mib, scalars=0, scratch=()):
+def kernel_call(body, outs, args, name, mib, scalars=0, scratch=(), cut_out=None):
     shapes = [jax.ShapeDtypeStruct(s, d) for s, d in outs]
     arrays = args[scalars:]
     n_in, n_out = len(arrays), len(shapes)
+    n_cut = 0 if cut_out is None else shapes[cut_out].shape[0]
 
     def kernel(*refs):
         smem, refs = refs[:scalars], refs[scalars:]
@@ -271,7 +273,14 @@
         out_buf, refs = refs[:n_out], refs[n_out:]
         in_sem, out_sem, extra = refs[0], refs[1], refs[2:]
         loads = [pltpu.make_async_copy(ins[i], in_buf[i], in_sem.at[i]) for i in range(n_in)]
-        stores = [pltpu.make_async_copy(out_buf[i], out[i], out_sem.at[i]) for i in range(n_out)]
+        stores = {}
+        for i in range(n_out):
+            if i == cut_out:
+                for j in range(shapes[i].shape[0]):
+                    sem = out_sem.at[n_out + j]
+                    stores[i, j] = pltpu.make_async_copy(out_buf[i].at[j], out[i].at[j], sem)
+            else:
+                stores[i, None] = pltpu.make_async_copy(out_buf[i], out[i], out_sem.at[i])
         for load in loads:
             load.start()
         waited, sent = set(), set()
@@ -282,17 +291,17 @@
                 loads[i].wait()
             return in_buf[i]
 
-        def send(i):
-            if i not in sent:
-                sent.add(i)
-                stores[i].start()
+        def send(i, j=None):
+            if (i, j) not in sent:
+                sent.add((i, j))
+                stores[i, j].start()
 
         body(get, lambda i: out_buf[i], send, smem, extra)
         for i in range(n_in):
             get(i)
-        for i in range(n_out):
-            send(i)
-        for store in stores:
+        for i, j in stores:
+            send(i, j)
+        for store in stores.values():
             store.wait()
 
     hbm = pl.BlockSpec(memory_space=pltpu.HBM)
@@ -303,7 +312,7 @@
         out_specs=[hbm] * n_out,
         scratch_shapes=[pltpu.VMEM(v.shape, v.dtype) for v in arrays]
         + [pltpu.VMEM(v.shape, v.dtype) for v in shapes]
-        + [pltpu.SemaphoreType.DMA((n_in,)), pltpu.SemaphoreType.DMA((n_out,))]
+        + [pltpu.SemaphoreType.DMA((n_in,)), pltpu.SemaphoreType.DMA((n_out + n_cut,))]
         + list(scratch),
         compiler_params=pltpu.CompilerParams(vmem_limit_bytes=mib * MIB),
         name=name,
@@ -356,17 +365,17 @@
     )
     theirs = other_core(mine)
 
-    normed, inverse, partial = kernel_call(
+    normed, inverse, partial, grad_out = kernel_call(
         norm_kernel,
-        [((2, TOK_DEV, NZ * deep), BF), square, ((TOK_DEV, q_cols + 2 * k_cols), F32)],
-        [rows_full, mine], "norm", 60,
+        [((2, TOK_DEV, NZ * deep), BF), square, ((TOK_DEV, q_cols + 2 * k_cols), F32), ((q_heads * TOK_DEV, HEAD), BF)],
+        [rows_full, mine, home, cot_near, cot_behind, cot_far], "norm", 60,
     )
     *attn_cuts, grad_value, terms = kernel_call(
         functools.partial(layer_kernel, q_heads),
         [cut] * 4 + [((TOK_DEV, k_cols), BF), ((peers,) + block, BF)],
-        [normed, cosine, sine, allowed, home, cot_near, cot_behind, cot_far, theirs, inverse, partial, mine],
+        [normed, cosine, sine, allowed, home, grad_out, theirs, inverse, partial, mine],
         "layer", 60, 0,
-        [pltpu.VMEM((TOK_DEV, q_cols + 2 * k_cols), BF)],
+        [pltpu.VMEM((TOK_DEV, q_cols + 2 * k_cols), BF)], 5,
     )
     total = lax.psum_scatter(terms, "tensor", scatter_dimension=0, tiled=False)
     (grad_hidden,) = kernel_call(
@@ -375,7 +384,7 @@
     )
 
     share = ((NZ * NX, rows_each, k_cols), BF)
-    kept, given = kernel_call(value_kernel, [share, share], [normed, grad_value], "value", 60)
+    kept, given = kernel_call(value_kernel, [share, share], [normed, grad_value], "value", 12)
     pair = (kept.astype(F32) + other_core(given).astype(F32)).astype(BF)
     parts = lax.all_to_all(pair, ("z", "x"), split_axis=0, concat_axis=0, tiled=True)
     grad_value_weight = jnp.sum(parts.astype(F32), 0)

time: 146 us -> 144 us (0.986)
  transfers between devices with their start and end apart: 13 -> 13, of which waited for: 9 -> 9; matrix products, arithmetic and copies ran while one was open for 4% -> 3% of each run, Pallas kernels for 8% -> 7%
where the time goes in v8:
time: 144 us; the launch traced here: 142 us
  starting transfers between devices  52.8 us (37%)
  waiting for transfers between devices  37.9 us (26%)
  Pallas kernels  20 us (14%)
  between operations  14.4 us (10%)
  blocking collectives  11 us (8%)
  local copies, waits for them, and re-layouts  3.83 us (3%)
  other arithmetic  2.62 us (2%)
    ppermute x7, starting transfers between devices, passed_along(): return lax.ppermute(value, DP, [(i, (i + by) % size) for i in range(size)])  32.3 us
    pallas_call x6, Pallas kernels, kernel_call(): pl.pallas_call(kernel, out_shape=shapes, in_specs=[pl.BlockSpec(memory_sp...  20 us
    ppermute x7, waiting for transfers between devices, passed_along(): return lax.ppermute(value, DP, [(i, (i + by) % size) for i in range(size)])  15.9 us
    all_gather x1, waiting for transfers between devices, on_device(): mine = lax.all_gather(own_half, 'z', axis=0, tiled=True)  13.8 us
    all_to_all x1, blocking collectives, on_device(): lax.all_to_all(jnp.broadcast_to(own[None], (NX,) + own.shape), 'x', split...  11 us
    all_to_all x1, starting transfers between devices, on_device(): lax.all_to_all(copies, 'tensor', split_axis=0, concat_axis=0, tiled=True)  7.88 us
    ppermute x2, starting transfers between devices, moved(): return lax.ppermute(value, DP, pairs)  6.26 us
    all_to_all x1, starting transfers between devices, on_device(): lax.all_to_all(pair, ('z', 'x'), split_axis=0, concat_axis=0, tiled=True)  6.24 us
  transfers between devices with their start and end apart: 13, of which 9 were waited for; matrix products, arithmetic and copies ran while one was open for 3% of the time, Pallas kernels for 7%

profile of v8, /device:TPU:1, one launch (start us, length us, event | category | flops | bytes accessed | tf_op | source)
XLA Modules:
  0.0 142.5 jit_solution(8805557937059549997)
XLA Ops:
  8.1 11.0 %all_to_all.15 = bf16[4,64,768]{2,1,0:T(8,128)(2,1)} all-to-all(bf16[4,64,768]{2,1,0:T(8,128)(2,1)S(1)} %broadcast_in_dim.6), channel_id=1, replica_groups=mesh['z'=8,'x'=4,'core'=2,'tensor'=8] {'x'}, dimensions={0} | all-to-all | bytes 786432 | tf_op jit(solution)/shard_map/all_to_all | solution.py:337
  19.7 3.6 %plan.1 = (bf16[128,512]{1,0:T(8,128)(2,1)}, bf16[64,512]{1,0:T(8,128)(2,1)}, bf16[64,512]{1,0:T(8,128)(2,1)}, bf16[256,128]{1,0:T(8,128)(2,1)}, bf16[256,256]{1...) custom-call(s32[4,64]{1,0:T(4,128)} %bitcast.8, ...), custom_call_target="tpu_custom_call" | custom-call | tf_op jit(solution)/shard_map/plan/pallas_call | solution.py:308
  23.4 2.0 %broadcast_in_dim.8 = bf16[8,272,256]{2,1,0:T(8,128)(2,1)} broadcast(bf16[272,256]{1,0:T(8,128)(2,1)} %get-tuple-element.35.refs_0_), dimensions={1,2} | broadcast | bytes 1253376 | tf_op jit(solution)/shard_map/broadcast_in_dim | solution.py:357
  25.4 7.9 %all-to-all-start.1 = ((bf16[8,272,256]{2,1,0:T(8,128)(2,1)}), bf16[8,272,256]{2,1,0:T(8,128)(2,1)S(1)}, u32[]{:S(2)}, u32[]{:S(2)}) async-start(bf16[8,272,256]{2,1,0:T(8,128)(2,1)} %broadcast_in_dim.8), calls=%async_computation.1 | async-start | bytes 2228224 | tf_op jit(solution)/shard_map/all_to_all | solution.py:358
  33.3 4.1 %collective-permute-start = (bf16[128,512]{1,0:T(8,128)(2,1)S(1)}, bf16[128,512]{1,0:T(8,128)(2,1)S(1)}, u32[]{:S(2)}, u32[]{:S(2)}) collective-permute-start(bf16[128,512]{1,0:T(8,128)(2,1)S(1)} %copy-done.9), channel_id=1, source_target_pairs={{0,504},{8,0},{16,8},{24,16},{32,24},{40,32},{48,40},{56,48},{64,5... | collective-permute-start | bytes 393224 | tf_op jit(solution)/shard_map/ppermute | solution.py:43
  37.4 3.1 %collective-permute-done.refs_3_ = bf16[128,512]{1,0:T(8,128)(2,1)S(1)} collective-permute-done((bf16[128,512]{1,0:T(8,128)(2,1)S(1)}, bf16[128,512]{1,0:T(8,128)(2,1)S(1)}, u32[]{:S(2)}, u32[]{:S(2)}) %collective-permute-start) | collective-permute-done | bytes 131104 | tf_op jit(solution)/shard_map/ppermute | solution.py:43
  40.5 10.7 %collective-permute-start.2 = (bf16[128,512]{1,0:T(8,128)(2,1)S(1)}, bf16[128,512]{1,0:T(8,128)(2,1)S(1)}, u32[]{:S(2)}, u32[]{:S(2)}) collective-permute-start(bf16[128,512]{1,0:T(8,128)(2,1)S(1)} %pad_maximum_fusion), channel_id=1, source_target_pairs={{0,256},{8,264},{16,272},{24,280},{32,288},{40,296},{48,304},{56,3... | collective-permute-start | bytes 393224 | tf_op jit(solution)/shard_map/ppermute | solution.py:43
  51.3 1.9 %collective-permute-start.1 = (bf16[64,512]{1,0:T(8,128)(2,1)S(1)}, bf16[64,512]{1,0:T(8,128)(2,1)S(1)}, u32[]{:S(2)}, u32[]{:S(2)}) collective-permute-start(bf16[64,512]{1,0:T(8,128)(2,1)S(1)} %copy-done.14), channel_id=1, source_target_pairs={{0,8},{8,16},{16,24},{24,32},{32,40},{40,48},{48,56},{56,64},{64,7... | collective-permute-start | bytes 196616 | tf_op jit(solution)/shard_map/ppermute | solution.py:43
  53.2 3.0 %collective-permute-done.1.refs_4_ = bf16[64,512]{1,0:T(8,128)(2,1)S(1)} collective-permute-done((bf16[64,512]{1,0:T(8,128)(2,1)S(1)}, bf16[64,512]{1,0:T(8,128)(2,1)S(1)}, u32[]{:S(2)}, u32[]{:S(2)}) %collective-permute-start.1) | collective-permute-done | bytes 65568 | tf_op jit(solution)/shard_map/ppermute | solution.py:43
  56.2 2.1 %collective-permute-done.2.refs_5_ = bf16[128,512]{1,0:T(8,128)(2,1)S(1)} collective-permute-done((bf16[128,512]{1,0:T(8,128)(2,1)S(1)}, bf16[128,512]{1,0:T(8,128)(2,1)S(1)}, u32[]{:S(2)}, u32[]{:S(2)}) %collective-permute-start.2) | collective-permute-done | bytes 131104 | tf_op jit(solution)/shard_map/ppermute | solution.py:43
  58.3 5.5 %all-to-all-done.1.refs_0_ = bf16[8,272,256]{2,1,0:T(8,128)(2,1)S(1)} async-done(((bf16[8,272,256]{2,1,0:T(8,128)(2,1)}), bf16[8,272,256]{2,1,0:T(8,128)(2,1)S(1)}, u32[]{:S(2)}, u32[]{:S(2)}) %all-to-all-start.1) | async-done | bytes 1114144 | tf_op jit(solution)/shard_map/all_to_all | solution.py:358
  63.8 13.8 %all-gather.2.cloned.1.call-done.refs_1_.refs_9_ = bf16[2048,768]{1,0:T(8,128)(2,1)} async-done(((bf16[256,768]{1,0:T(8,128)(2,1)}), bf16[2048,768]{1,0:T(8,128)(2,1)}) %all-gather.2.cloned.1.call-update) | async-done | bytes 3145744 | tf_op jit(solution)/shard_map/all_gather | solution.py:341
  77.6 4.0 %collective-permute-start.3 = (bf16[2048,768]{1,0:T(8,128)(2,1)}, bf16[2048,768]{1,0:T(8,128)(2,1)}, u32[]{:S(2)}, u32[]{:S(2)}) collective-permute-start(bf16[2048,768]{1,0:T(8,128)(2,1)} %all-gather.2.cloned.1.call-done.refs_1_.refs_9_), channel_id=1, source_target_pairs={{0,8},{8,0},{16,24},{24,16},{32,40},{40,32},{48,56},{56,48},{64,72... | collective-permute-start | bytes 9437192 | tf_op jit(solution)/shard_map/ppermute | solution.py:34
  81.6 4.4 %norm.1 = (bf16[2,128,2048]{2,1,0:T(8,128)(2,1)}, f32[128,128]{1,0:T(8,128)}, f32[128,768]{1,0:T(8,128)}, bf16[512,128]{1,0:T(8,128)(2,1)}) custom-call(bf16[8,272,256]{2,1,0:T(8,128)(2,1)} %copy-done.3, bf16[2048,768]{1,0:T(8,128)(2,1)} %all-gather.2.cloned.1.call-done.refs_1_.refs_9_, bf16[256,128]{1,0:T(8,128)(2,1)} %get-tuple-element.41.refs_2_.refs_4_, ...), custom_call_target="tpu_custom_call" | custom-call | tf_op jit(solution)/shard_map/norm/pallas_call | solution.py:308
  87.2 7.5 %layer.1 = (bf16[64,512]{1,0:T(8,128)(2,1)}, bf16[64,512]{1,0:T(8,128)(2,1)}, bf16[64,512]{1,0:T(8,128)(2,1)}, bf16[64,512]{1,0:T(8,128)(2,1)}, bf16[128,128]{1,0:T(8,128)(2,1)}, /*index=5*/bf16[8,272,256]{2,1,0:T(8,128)(2,1)}) custom-call(bf16[2,128,2048]{2,1,0:T(8,128)(2,1)} %get-tuple-element.45.refs_0_, f32[128,128]{1,0:T(8,128)} %get-tuple-element.46.refs_1_, ...), custom_call_target="tpu_custom_call" | custom-call | tf_op jit(solution)/shard_map/layer/pallas_call | solution.py:308
  96.7 2.3 %collective-permute-start.8 = (bf16[32,64,128]{2,1,0:T(8,128)(2,1)S(1)}, bf16[32,64,128]{2,1,0:T(8,128)(2,1)S(1)}, u32[]{:S(2)}, u32[]{:S(2)}) collective-permute-start(bf16[32,64,128]{2,1,0:T(8,128)(2,1)S(1)} %get-tuple-element.60), channel_id=1, source_target_pairs={{0,8},{8,0},{16,24},{24,16},{32,40},{40,32},{48,56},{56,48},{64,72... | collective-permute-start | bytes 1572872 | tf_op jit(solution)/shard_map/ppermute | solution.py:34
  101.5 6.2 %all-to-all-start.2 = ((bf16[32,64,128]{2,1,0:T(8,128)(2,1)}), bf16[32,64,128]{2,1,0:T(8,128)(2,1)S(1)}, u32[]{:S(2)}, u32[]{:S(2)}) async-start(bf16[32,64,128]{2,1,0:T(8,128)(2,1)} %add_convert_fusion), calls=%async_computation.3 | async-start | bytes 1048576 | tf_op jit(solution)/shard_map/all_to_all | solution.py:389
  107.8 2.6 %collective-permute-start.4 = (bf16[64,512]{1,0:T(8,128)(2,1)S(1)}, bf16[64,512]{1,0:T(8,128)(2,1)S(1)}, u32[]{:S(2)}, u32[]{:S(2)}) collective-permute-start(bf16[64,512]{1,0:T(8,128)(2,1)S(1)} %copy-done.13), channel_id=1, source_target_pairs={{0,504},{8,0},{16,8},{24,16},{32,24},{40,32},{48,40},{56,48},{64,5... | collective-permute-start | bytes 196616 | tf_op jit(solution)/shard_map/ppermute | solution.py:43
  110.4 3.3 %collective-permute-start.5 = (bf16[64,512]{1,0:T(8,128)(2,1)S(1)}, bf16[64,512]{1,0:T(8,128)(2,1)S(1)}, u32[]{:S(2)}, u32[]{:S(2)}) collective-permute-start(bf16[64,512]{1,0:T(8,128)(2,1)S(1)} %copy-done.12), channel_id=1, source_target_pairs={{0,8},{8,16},{16,24},{24,32},{32,40},{40,48},{48,56},{56,64},{64,7... | collective-permute-start | bytes 196616 | tf_op jit(solution)/shard_map/ppermute | solution.py:43
  113.7 7.0 %collective-permute-start.6 = (bf16[64,512]{1,0:T(8,128)(2,1)S(1)}, bf16[64,512]{1,0:T(8,128)(2,1)S(1)}, u32[]{:S(2)}, u32[]{:S(2)}) collective-permute-start(bf16[64,512]{1,0:T(8,128)(2,1)S(1)} %copy-done.11), channel_id=1, source_target_pairs={{0,256},{8,264},{16,272},{24,280},{32,288},{40,296},{48,304},{56,3... | collective-permute-start | bytes 196616 | tf_op jit(solution)/shard_map/ppermute | solution.py:43
  120.7 2.7 %collective-permute-start.7 = (bf16[64,512]{1,0:T(8,128)(2,1)S(1)}, bf16[64,512]{1,0:T(8,128)(2,1)S(1)}, u32[]{:S(2)}, u32[]{:S(2)}) collective-permute-start(bf16[64,512]{1,0:T(8,128)(2,1)S(1)} %copy-done.10), channel_id=1, source_target_pairs={{0,264},{8,272},{16,280},{24,288},{32,296},{40,304},{48,312},{56,3... | collective-permute-start | bytes 196616 | tf_op jit(solution)/shard_map/ppermute | solution.py:43
  123.4 3.6 %collective-permute-done.6.refs_3_ = bf16[64,512]{1,0:T(8,128)(2,1)S(1)} collective-permute-done((bf16[64,512]{1,0:T(8,128)(2,1)S(1)}, bf16[64,512]{1,0:T(8,128)(2,1)S(1)}, u32[]{:S(2)}, u32[]{:S(2)}) %collective-permute-start.6) | collective-permute-done | bytes 65568 | tf_op jit(solution)/shard_map/ppermute | solution.py:43
  127.0 4.2 %collective-permute-done.7.refs_4_ = bf16[64,512]{1,0:T(8,128)(2,1)S(1)} collective-permute-done((bf16[64,512]{1,0:T(8,128)(2,1)S(1)}, bf16[64,512]{1,0:T(8,128)(2,1)S(1)}, u32[]{:S(2)}, u32[]{:S(2)}) %collective-permute-start.7) | collective-permute-done | bytes 65568 | tf_op jit(solution)/shard_map/ppermute | solution.py:43
  133.4 2.2 %finish.1 = bf16[128,512]{1,0:T(8,128)(2,1)} custom-call(bf16[272,256]{1,0:T(8,128)(2,1)} %get-tuple-element.35.refs_0_, f32[128,128]{1,0:T(8,128)} %get-tuple-element.50.refs_7_.refs_1_, bf16[272,256]{1,0:T(8,128)(2,1)} %bitcast.7, bf16[512,512]{1,0:T(8,128)(2,1)} %get-tuple-element.57.refs_3_), custom_call_target="tpu_custom_call" | custom-call | tf_op jit(solution)/shard_map/finish/pallas_call | solution.py:308
  (49 shorter events, 9.5 us)
Async XLA Ops:
  7.2 12.0 %copy-start.8 = (bf16[512]{0:T(512)(128)(2,1)S(1)}, bf16[512]{0:T(512)(128)(2,1)}, u32[]{:S(2)}) copy-start(bf16[512]{0:T(512)(128)(2,1)} %param.12) | copy-start | bytes 3076
  7.2 70.4 %all-gather.2.cloned.1.call-start = ((), (), s32[]{:S(2)}) async-start(), calls=%async_computation.4 | async-start | bytes 3538944 | tf_op jit(solution)/shard_map/all_gather | solution.py:341
  25.3 15.2 %copy-start.7 = (bf16[64,512]{1,0:T(8,128)(2,1)S(1)}, bf16[64,512]{1,0:T(8,128)(2,1)}, u32[]{:S(2)}) copy-start(bf16[64,512]{1,0:T(8,128)(2,1)} %get-tuple-element.38) | copy-start | bytes 196612
  25.4 25.9 %copy-start.14 = (bf16[64,512]{1,0:T(8,128)(2,1)S(1)}, bf16[64,512]{1,0:T(8,128)(2,1)}, u32[]{:S(2)}) copy-start(bf16[64,512]{1,0:T(8,128)(2,1)} %get-tuple-element.37) | copy-start | bytes 196612
  25.4 38.5 %all-to-all-start.1 = ((bf16[8,272,256]{2,1,0:T(8,128)(2,1)}), bf16[8,272,256]{2,1,0:T(8,128)(2,1)S(1)}, u32[]{:S(2)}, u32[]{:S(2)}) async-start(bf16[8,272,256]{2,1,0:T(8,128)(2,1)} %broadcast_in_dim.8), calls=%async_computation.1 | async-start | bytes 2228224 | tf_op jit(solution)/shard_map/all_to_all | solution.py:358
  33.2 100.1 %reduce-scatter.2.cloned.1.call-start = ((), (), s32[]{:S(2)}) async-start(), calls=%async_computation.5 | async-start | bytes 1253376 | tf_op jit(solution)/shard_map/reduce_scatter | solution.py:380
  33.3 7.2 %collective-permute-start = (bf16[128,512]{1,0:T(8,128)(2,1)S(1)}, bf16[128,512]{1,0:T(8,128)(2,1)S(1)}, u32[]{:S(2)}, u32[]{:S(2)}) collective-permute-start(bf16[128,512]{1,0:T(8,128)(2,1)S(1)} %copy-done.9), channel_id=1, source_target_pairs={{0,504},{8,0},{16,8},{24,16},{32,24},{40,32},{48,40},{56,48},{64,5... | collective-permute-start | bytes 393224 | tf_op jit(solution)/shard_map/ppermute | solution.py:43
  40.5 41.1 %copy-start.4 = (bf16[128,512]{1,0:T(8,128)(2,1)}, bf16[128,512]{1,0:T(8,128)(2,1)S(1)}, u32[]{:S(2)}) copy-start(bf16[128,512]{1,0:T(8,128)(2,1)S(1)} %collective-permute-done.refs_3_) | copy-start | bytes 393220
  40.5 17.7 %collective-permute-start.2 = (bf16[128,512]{1,0:T(8,128)(2,1)S(1)}, bf16[128,512]{1,0:T(8,128)(2,1)S(1)}, u32[]{:S(2)}, u32[]{:S(2)}) collective-permute-start(bf16[128,512]{1,0:T(8,128)(2,1)S(1)} %pad_maximum_fusion), channel_id=1, source_target_pairs={{0,256},{8,264},{16,272},{24,280},{32,288},{40,296},{48,304},{56,3... | collective-permute-start | bytes 393224 | tf_op jit(solution)/shard_map/ppermute | solution.py:43
  51.3 5.0 %collective-permute-start.1 = (bf16[64,512]{1,0:T(8,128)(2,1)S(1)}, bf16[64,512]{1,0:T(8,128)(2,1)S(1)}, u32[]{:S(2)}, u32[]{:S(2)}) collective-permute-start(bf16[64,512]{1,0:T(8,128)(2,1)S(1)} %copy-done.14), channel_id=1, source_target_pairs={{0,8},{8,16},{16,24},{24,32},{32,40},{40,48},{48,56},{56,64},{64,7... | collective-permute-start | bytes 196616 | tf_op jit(solution)/shard_map/ppermute | solution.py:43
  56.2 25.4 %copy-start.6 = (bf16[64,512]{1,0:T(8,128)(2,1)}, bf16[64,512]{1,0:T(8,128)(2,1)S(1)}, u32[]{:S(2)}) copy-start(bf16[64,512]{1,0:T(8,128)(2,1)S(1)} %collective-permute-done.1.refs_4_) | copy-start | bytes 196612
  58.3 23.3 %copy-start.5 = (bf16[128,512]{1,0:T(8,128)(2,1)}, bf16[128,512]{1,0:T(8,128)(2,1)S(1)}, u32[]{:S(2)}) copy-start(bf16[128,512]{1,0:T(8,128)(2,1)S(1)} %collective-permute-done.2.refs_5_) | copy-start | bytes 393220
  63.8 17.8 %copy-start.3 = (bf16[8,272,256]{2,1,0:T(8,128)(2,1)}, bf16[8,272,256]{2,1,0:T(8,128)(2,1)S(1)}, u32[]{:S(2)}) copy-start(bf16[8,272,256]{2,1,0:T(8,128)(2,1)S(1)} %all-to-all-done.1.refs_0_) | copy-start | bytes 3342340
  77.6 9.6 %collective-permute-start.3 = (bf16[2048,768]{1,0:T(8,128)(2,1)}, bf16[2048,768]{1,0:T(8,128)(2,1)}, u32[]{:S(2)}, u32[]{:S(2)}) collective-permute-start(bf16[2048,768]{1,0:T(8,128)(2,1)} %all-gather.2.cloned.1.call-done.refs_1_.refs_9_), channel_id=1, source_target_pairs={{0,8},{8,0},{16,24},{24,16},{32,40},{40,32},{48,56},{56,48},{64,72... | collective-permute-start | bytes 9437192 | tf_op jit(solution)/shard_map/ppermute | solution.py:34
  96.7 3.8 %collective-permute-start.8 = (bf16[32,64,128]{2,1,0:T(8,128)(2,1)S(1)}, bf16[32,64,128]{2,1,0:T(8,128)(2,1)S(1)}, u32[]{:S(2)}, u32[]{:S(2)}) collective-permute-start(bf16[32,64,128]{2,1,0:T(8,128)(2,1)S(1)} %get-tuple-element.60), channel_id=1, source_target_pairs={{0,8},{8,0},{16,24},{24,16},{32,40},{40,32},{48,56},{56,48},{64,72... | collective-permute-start | bytes 1572872 | tf_op jit(solution)/shard_map/ppermute | solution.py:34
  100.5 9.9 %copy-start.12 = (bf16[64,512]{1,0:T(8,128)(2,1)S(1)}, bf16[64,512]{1,0:T(8,128)(2,1)}, u32[]{:S(2)}) copy-start(bf16[64,512]{1,0:T(8,128)(2,1)} %get-tuple-element.53) | copy-start | bytes 196612
  100.5 13.2 %copy-start.11 = (bf16[64,512]{1,0:T(8,128)(2,1)S(1)}, bf16[64,512]{1,0:T(8,128)(2,1)}, u32[]{:S(2)}) copy-start(bf16[64,512]{1,0:T(8,128)(2,1)} %get-tuple-element.54) | copy-start | bytes 196612
  100.5 20.2 %copy-start.10 = (bf16[64,512]{1,0:T(8,128)(2,1)S(1)}, bf16[64,512]{1,0:T(8,128)(2,1)}, u32[]{:S(2)}) copy-start(bf16[64,512]{1,0:T(8,128)(2,1)} %get-tuple-element.55) | copy-start | bytes 196612
  100.5 30.7 %copy-start.1 = (bf16[256,256]{1,0:T(8,128)(2,1)S(1)}, bf16[256,256]{1,0:T(8,128)(2,1)}, u32[]{:S(2)}) copy-start(bf16[256,256]{1,0:T(8,128)(2,1)} %get-tuple-element.33.refs_0_) | copy-start | bytes 393220
  101.5 31.2 %all-to-all-start.2 = ((bf16[32,64,128]{2,1,0:T(8,128)(2,1)}), bf16[32,64,128]{2,1,0:T(8,128)(2,1)S(1)}, u32[]{:S(2)}, u32[]{:S(2)}) async-start(bf16[32,64,128]{2,1,0:T(8,128)(2,1)} %add_convert_fusion), calls=%async_computation.3 | async-start | bytes 1048576 | tf_op jit(solution)/shard_map/all_to_all | solution.py:389
  107.8 15.6 %collective-permute-start.4 = (bf16[64,512]{1,0:T(8,128)(2,1)S(1)}, bf16[64,512]{1,0:T(8,128)(2,1)S(1)}, u32[]{:S(2)}, u32[]{:S(2)}) collective-permute-start(bf16[64,512]{1,0:T(8,128)(2,1)S(1)} %copy-done.13), channel_id=1, source_target_pairs={{0,504},{8,0},{16,8},{24,16},{32,24},{40,32},{48,40},{56,48},{64,5... | collective-permute-start | bytes 196616 | tf_op jit(solution)/shard_map/ppermute | solution.py:43
  110.4 13.1 %collective-permute-start.5 = (bf16[64,512]{1,0:T(8,128)(2,1)S(1)}, bf16[64,512]{1,0:T(8,128)(2,1)S(1)}, u32[]{:S(2)}, u32[]{:S(2)}) collective-permute-start(bf16[64,512]{1,0:T(8,128)(2,1)S(1)} %copy-done.12), channel_id=1, source_target_pairs={{0,8},{8,16},{16,24},{24,32},{32,40},{40,48},{48,56},{56,64},{64,7... | collective-permute-start | bytes 196616 | tf_op jit(solution)/shard_map/ppermute | solution.py:43
  113.7 13.3 %collective-permute-start.6 = (bf16[64,512]{1,0:T(8,128)(2,1)S(1)}, bf16[64,512]{1,0:T(8,128)(2,1)S(1)}, u32[]{:S(2)}, u32[]{:S(2)}) collective-permute-start(bf16[64,512]{1,0:T(8,128)(2,1)S(1)} %copy-done.11), channel_id=1, source_target_pairs={{0,256},{8,264},{16,272},{24,280},{32,288},{40,296},{48,304},{56,3... | collective-permute-start | bytes 196616 | tf_op jit(solution)/shard_map/ppermute | solution.py:43
  120.7 10.4 %collective-permute-start.7 = (bf16[64,512]{1,0:T(8,128)(2,1)S(1)}, bf16[64,512]{1,0:T(8,128)(2,1)S(1)}, u32[]{:S(2)}, u32[]{:S(2)}) collective-permute-start(bf16[64,512]{1,0:T(8,128)(2,1)S(1)} %copy-done.10), channel_id=1, source_target_pairs={{0,264},{8,272},{16,280},{24,288},{32,296},{40,304},{48,312},{56,3... | collective-permute-start | bytes 196616 | tf_op jit(solution)/shard_map/ppermute | solution.py:43
  (4 other events, 17.7 us)
Sparse Core Ops, SparseCore 0:
  19.3 58.2 all-gather.1
  94.9 34.6 reduce-scatter.1

commit v9 on v8

--- a/solution.py
+++ b/solution.py
@@ -374,7 +374,7 @@
         functools.partial(layer_kernel, q_heads),
         [cut] * 4 + [((TOK_DEV, k_cols), BF), ((peers,) + block, BF)],
         [normed, cosine, sine, allowed, home, grad_out, theirs, inverse, partial, mine],
-        "layer", 60, 0,
+        "layer", 50, 0,
         [pltpu.VMEM((TOK_DEV, q_cols + 2 * k_cols), BF)], 5,
     )
     total = lax.psum_scatter(terms, "tensor", scatter_dimension=0, tiled=False)

time: 144 us -> 148 us (1.028)
  local copies, waits for them, and re-layouts: 3.83 us -> 7.81 us
    unnamed x30 -> x36, local copies, waits for them, and re-layouts: 1.24 us -> 5.2 us
where the time goes in v9:
time: 148 us; the launch traced here: 147 us
  starting transfers between devices  52.8 us (36%)
  waiting for transfers between devices  37.9 us (26%)
  Pallas kernels  20.5 us (14%)
  between operations  14.4 us (10%)
  blocking collectives  11 us (7%)
  local copies, waits for them, and re-layouts  7.81 us (5%)
  other arithmetic  2.62 us (2%)
    ppermute x7, starting transfers between devices, passed_along(): return lax.ppermute(value, DP, [(i, (i + by) % size) for i in range(size)])  32.3 us
    pallas_call x6, Pallas kernels, kernel_call(): pl.pallas_call(kernel, out_shape=shapes, in_specs=[pl.BlockSpec(memory_sp...  20.5 us
    ppermute x7, waiting for transfers between devices, passed_along(): return lax.ppermute(value, DP, [(i, (i + by) % size) for i in range(size)])  16.3 us
    all_gather x1, waiting for transfers between devices, on_device(): mine = lax.all_gather(own_half, 'z', axis=0, tiled=True)  13.8 us
    all_to_all x1, blocking collectives, on_device(): lax.all_to_all(jnp.broadcast_to(own[None], (NX,) + own.shape), 'x', split...  11 us
    all_to_all x1, starting transfers between devices, on_device(): lax.all_to_all(copies, 'tensor', split_axis=0, concat_axis=0, tiled=True)  7.88 us
    ppermute x2, starting transfers between devices, moved(): return lax.ppermute(value, DP, pairs)  6.28 us
    all_to_all x1, starting transfers between devices, on_device(): lax.all_to_all(pair, ('z', 'x'), split_axis=0, concat_axis=0, tiled=True)  6.24 us
  transfers between devices with their start and end apart: 13, of which 9 were waited for; matrix products, arithmetic and copies ran while one was open for 3% of the time, Pallas kernels for 7%

profile of v9, /device:TPU:1, one launch (start us, length us, event | category | flops | bytes accessed | tf_op | source)
XLA Modules:
  0.0 146.9 jit_solution(11945271217048821061)
XLA Ops:
  8.1 11.0 %all_to_all.15 = bf16[4,64,768]{2,1,0:T(8,128)(2,1)} all-to-all(bf16[4,64,768]{2,1,0:T(8,128)(2,1)S(1)} %broadcast_in_dim.6), channel_id=1, replica_groups=mesh['z'=8,'x'=4,'core'=2,'tensor'=8] {'x'}, dimensions={0} | all-to-all | bytes 786432 | tf_op jit(solution)/shard_map/all_to_all | solution.py:337
  19.7 3.6 %plan.1 = (bf16[128,512]{1,0:T(8,128)(2,1)}, bf16[64,512]{1,0:T(8,128)(2,1)}, bf16[64,512]{1,0:T(8,128)(2,1)}, bf16[256,128]{1,0:T(8,128)(2,1)}, bf16[256,256]{1...) custom-call(s32[4,64]{1,0:T(4,128)} %bitcast.8, ...), custom_call_target="tpu_custom_call" | custom-call | tf_op jit(solution)/shard_map/plan/pallas_call | solution.py:308
  23.4 2.0 %broadcast_in_dim.8 = bf16[8,272,256]{2,1,0:T(8,128)(2,1)} broadcast(bf16[272,256]{1,0:T(8,128)(2,1)} %get-tuple-element.35.refs_0_), dimensions={1,2} | broadcast | bytes 1253376 | tf_op jit(solution)/shard_map/broadcast_in_dim | solution.py:357
  25.4 7.9 %all-to-all-start.1 = ((bf16[8,272,256]{2,1,0:T(8,128)(2,1)}), bf16[8,272,256]{2,1,0:T(8,128)(2,1)S(1)}, u32[]{:S(2)}, u32[]{:S(2)}) async-start(bf16[8,272,256]{2,1,0:T(8,128)(2,1)} %broadcast_in_dim.8), calls=%async_computation.1 | async-start | bytes 2228224 | tf_op jit(solution)/shard_map/all_to_all | solution.py:358
  33.3 4.1 %collective-permute-start = (bf16[128,512]{1,0:T(8,128)(2,1)S(1)}, bf16[128,512]{1,0:T(8,128)(2,1)S(1)}, u32[]{:S(2)}, u32[]{:S(2)}) collective-permute-start(bf16[128,512]{1,0:T(8,128)(2,1)S(1)} %copy-done.16), channel_id=1, source_target_pairs={{0,504},{8,0},{16,8},{24,16},{32,24},{40,32},{48,40},{56,48},{64,5... | collective-permute-start | bytes 393224 | tf_op jit(solution)/shard_map/ppermute | solution.py:43
  37.4 3.1 %collective-permute-done.refs_3_ = bf16[128,512]{1,0:T(8,128)(2,1)S(1)} collective-permute-done((bf16[128,512]{1,0:T(8,128)(2,1)S(1)}, bf16[128,512]{1,0:T(8,128)(2,1)S(1)}, u32[]{:S(2)}, u32[]{:S(2)}) %collective-permute-start) | collective-permute-done | bytes 131104 | tf_op jit(solution)/shard_map/ppermute | solution.py:43
  40.6 10.7 %collective-permute-start.2 = (bf16[128,512]{1,0:T(8,128)(2,1)S(1)}, bf16[128,512]{1,0:T(8,128)(2,1)S(1)}, u32[]{:S(2)}, u32[]{:S(2)}) collective-permute-start(bf16[128,512]{1,0:T(8,128)(2,1)S(1)} %pad_maximum_fusion), channel_id=1, source_target_pairs={{0,256},{8,264},{16,272},{24,280},{32,288},{40,296},{48,304},{56,3... | collective-permute-start | bytes 393224 | tf_op jit(solution)/shard_map/ppermute | solution.py:43
  51.3 1.9 %collective-permute-start.1 = (bf16[64,512]{1,0:T(8,128)(2,1)S(1)}, bf16[64,512]{1,0:T(8,128)(2,1)S(1)}, u32[]{:S(2)}, u32[]{:S(2)}) collective-permute-start(bf16[64,512]{1,0:T(8,128)(2,1)S(1)} %copy-done.17), channel_id=1, source_target_pairs={{0,8},{8,16},{16,24},{24,32},{32,40},{40,48},{48,56},{56,64},{64,7... | collective-permute-start | bytes 196616 | tf_op jit(solution)/shard_map/ppermute | solution.py:43
  53.2 3.0 %collective-permute-done.1.refs_4_ = bf16[64,512]{1,0:T(8,128)(2,1)S(1)} collective-permute-done((bf16[64,512]{1,0:T(8,128)(2,1)S(1)}, bf16[64,512]{1,0:T(8,128)(2,1)S(1)}, u32[]{:S(2)}, u32[]{:S(2)}) %collective-permute-start.1) | collective-permute-done | bytes 65568 | tf_op jit(solution)/shard_map/ppermute | solution.py:43
  56.2 2.4 %collective-permute-done.2.refs_5_ = bf16[128,512]{1,0:T(8,128)(2,1)S(1)} collective-permute-done((bf16[128,512]{1,0:T(8,128)(2,1)S(1)}, bf16[128,512]{1,0:T(8,128)(2,1)S(1)}, u32[]{:S(2)}, u32[]{:S(2)}) %collective-permute-start.2) | collective-permute-done | bytes 131104 | tf_op jit(solution)/shard_map/ppermute | solution.py:43
  58.6 5.2 %all-to-all-done.1.refs_0_ = bf16[8,272,256]{2,1,0:T(8,128)(2,1)S(1)} async-done(((bf16[8,272,256]{2,1,0:T(8,128)(2,1)}), bf16[8,272,256]{2,1,0:T(8,128)(2,1)S(1)}, u32[]{:S(2)}, u32[]{:S(2)}) %all-to-all-start.1) | async-done | bytes 1114144 | tf_op jit(solution)/shard_map/all_to_all | solution.py:358
  63.9 13.8 %all-gather.2.cloned.1.call-done.refs_1_.refs_9_ = bf16[2048,768]{1,0:T(8,128)(2,1)} async-done(((bf16[256,768]{1,0:T(8,128)(2,1)}), bf16[2048,768]{1,0:T(8,128)(2,1)}) %all-gather.2.cloned.1.call-update) | async-done | bytes 3145744 | tf_op jit(solution)/shard_map/all_gather | solution.py:341
  77.6 4.0 %collective-permute-start.3 = (bf16[2048,768]{1,0:T(8,128)(2,1)}, bf16[2048,768]{1,0:T(8,128)(2,1)}, u32[]{:S(2)}, u32[]{:S(2)}) collective-permute-start(bf16[2048,768]{1,0:T(8,128)(2,1)} %all-gather.2.cloned.1.call-done.refs_1_.refs_9_), channel_id=1, source_target_pairs={{0,8},{8,0},{16,24},{24,16},{32,40},{40,32},{48,56},{56,48},{64,72... | collective-permute-start | bytes 9437192 | tf_op jit(solution)/shard_map/ppermute | solution.py:34
  81.7 4.5 %norm.1 = (bf16[2,128,2048]{2,1,0:T(8,128)(2,1)}, f32[128,128]{1,0:T(8,128)}, f32[128,768]{1,0:T(8,128)}, bf16[512,128]{1,0:T(8,128)(2,1)}) custom-call(bf16[8,272,256]{2,1,0:T(8,128)(2,1)} %copy-done.10, bf16[2048,768]{1,0:T(8,128)(2,1)} %all-gather.2.cloned.1.call-done.refs_1_.refs_9_, bf16[256,128]{1,0:T(8,128)(2,1)} %get-tuple-element.41.refs_2_.refs_4_, ...), custom_call_target="tpu_custom_call" | custom-call | tf_op jit(solution)/shard_map/norm/pallas_call | solution.py:308
  91.2 8.0 %layer.1 = (bf16[64,512]{1,0:T(8,128)(2,1)S(1)}, bf16[64,512]{1,0:T(8,128)(2,1)S(1)}, bf16[64,512]{1,0:T(8,128)(2,1)S(1)}, bf16[64,512]{1,0:T(8,128)(2,1)S(1)}, ...) custom-call(bf16[2,128,2048]{2,1,0:T(8,128)(2,1)S(1)} %copy-done, f32[128,128]{1,0:T(8,128)S(1)} %copy-done.7, ...), custom_call_target="tpu_custom_call" | custom-call | tf_op jit(solution)/shard_map/layer/pallas_call | solution.py:308
  101.2 2.3 %collective-permute-start.8 = (bf16[32,64,128]{2,1,0:T(8,128)(2,1)S(1)}, bf16[32,64,128]{2,1,0:T(8,128)(2,1)S(1)}, u32[]{:S(2)}, u32[]{:S(2)}) collective-permute-start(bf16[32,64,128]{2,1,0:T(8,128)(2,1)S(1)} %get-tuple-element.60), channel_id=1, source_target_pairs={{0,8},{8,0},{16,24},{24,16},{32,40},{40,32},{48,56},{56,48},{64,72... | collective-permute-start | bytes 1572872 | tf_op jit(solution)/shard_map/ppermute | solution.py:34
  106.0 6.2 %all-to-all-start.2 = ((bf16[32,64,128]{2,1,0:T(8,128)(2,1)}), bf16[32,64,128]{2,1,0:T(8,128)(2,1)S(1)}, u32[]{:S(2)}, u32[]{:S(2)}) async-start(bf16[32,64,128]{2,1,0:T(8,128)(2,1)} %add_convert_fusion), calls=%async_computation.3 | async-start | bytes 1048576 | tf_op jit(solution)/shard_map/all_to_all | solution.py:389
  112.2 2.6 %collective-permute-start.4 = (bf16[64,512]{1,0:T(8,128)(2,1)S(1)}, bf16[64,512]{1,0:T(8,128)(2,1)S(1)}, u32[]{:S(2)}, u32[]{:S(2)}) collective-permute-start(bf16[64,512]{1,0:T(8,128)(2,1)S(1)} %get-tuple-element.52), channel_id=1, source_target_pairs={{0,504},{8,0},{16,8},{24,16},{32,24},{40,32},{48,40},{56,48},{64,5... | collective-permute-start | bytes 196616 | tf_op jit(solution)/shard_map/ppermute | solution.py:43
  114.8 3.3 %collective-permute-start.5 = (bf16[64,512]{1,0:T(8,128)(2,1)S(1)}, bf16[64,512]{1,0:T(8,128)(2,1)S(1)}, u32[]{:S(2)}, u32[]{:S(2)}) collective-permute-start(bf16[64,512]{1,0:T(8,128)(2,1)S(1)} %get-tuple-element.53), channel_id=1, source_target_pairs={{0,8},{8,16},{16,24},{24,32},{32,40},{40,48},{48,56},{56,64},{64,7... | collective-permute-start | bytes 196616 | tf_op jit(solution)/shard_map/ppermute | solution.py:43
  118.1 7.0 %collective-permute-start.6 = (bf16[64,512]{1,0:T(8,128)(2,1)S(1)}, bf16[64,512]{1,0:T(8,128)(2,1)S(1)}, u32[]{:S(2)}, u32[]{:S(2)}) collective-permute-start(bf16[64,512]{1,0:T(8,128)(2,1)S(1)} %get-tuple-element.54), channel_id=1, source_target_pairs={{0,256},{8,264},{16,272},{24,280},{32,288},{40,296},{48,304},{56,3... | collective-permute-start | bytes 196616 | tf_op jit(solution)/shard_map/ppermute | solution.py:43
  125.2 2.7 %collective-permute-start.7 = (bf16[64,512]{1,0:T(8,128)(2,1)S(1)}, bf16[64,512]{1,0:T(8,128)(2,1)S(1)}, u32[]{:S(2)}, u32[]{:S(2)}) collective-permute-start(bf16[64,512]{1,0:T(8,128)(2,1)S(1)} %get-tuple-element.55), channel_id=1, source_target_pairs={{0,264},{8,272},{16,280},{24,288},{32,296},{40,304},{48,312},{56,3... | collective-permute-start | bytes 196616 | tf_op jit(solution)/shard_map/ppermute | solution.py:43
  127.9 3.6 %collective-permute-done.6.refs_3_ = bf16[64,512]{1,0:T(8,128)(2,1)S(1)} collective-permute-done((bf16[64,512]{1,0:T(8,128)(2,1)S(1)}, bf16[64,512]{1,0:T(8,128)(2,1)S(1)}, u32[]{:S(2)}, u32[]{:S(2)}) %collective-permute-start.6) | collective-permute-done | bytes 65568 | tf_op jit(solution)/shard_map/ppermute | solution.py:43
  131.5 4.2 %collective-permute-done.7.refs_4_ = bf16[64,512]{1,0:T(8,128)(2,1)S(1)} collective-permute-done((bf16[64,512]{1,0:T(8,128)(2,1)S(1)}, bf16[64,512]{1,0:T(8,128)(2,1)S(1)}, u32[]{:S(2)}, u32[]{:S(2)}) %collective-permute-start.7) | collective-permute-done | bytes 65568 | tf_op jit(solution)/shard_map/ppermute | solution.py:43
  137.9 2.2 %finish.1 = bf16[128,512]{1,0:T(8,128)(2,1)} custom-call(bf16[272,256]{1,0:T(8,128)(2,1)} %get-tuple-element.35.refs_0_, f32[128,128]{1,0:T(8,128)} %get-tuple-element.50.refs_7_.refs_1_, bf16[272,256]{1,0:T(8,128)(2,1)} %bitcast.7, bf16[512,512]{1,0:T(8,128)(2,1)} %get-tuple-element.57.refs_3_), custom_call_target="tpu_custom_call" | custom-call | tf_op jit(solution)/shard_map/finish/pallas_call | solution.py:308
  (55 shorter events, 13.3 us)
Async XLA Ops:
  7.2 12.0 %copy-start.15 = (bf16[512]{0:T(512)(128)(2,1)S(1)}, bf16[512]{0:T(512)(128)(2,1)}, u32[]{:S(2)}) copy-start(bf16[512]{0:T(512)(128)(2,1)} %param.12) | copy-start | bytes 3076
  7.2 70.4 %all-gather.2.cloned.1.call-start = ((), (), s32[]{:S(2)}) async-start(), calls=%async_computation.4 | async-start | bytes 3538944 | tf_op jit(solution)/shard_map/all_gather | solution.py:341
  25.4 7.9 %copy-start.16 = (bf16[128,512]{1,0:T(8,128)(2,1)S(1)}, bf16[128,512]{1,0:T(8,128)(2,1)}, u32[]{:S(2)}) copy-start(bf16[128,512]{1,0:T(8,128)(2,1)} %get-tuple-element.36) | copy-start | bytes 393220
  25.4 15.2 %copy-start.14 = (bf16[64,512]{1,0:T(8,128)(2,1)S(1)}, bf16[64,512]{1,0:T(8,128)(2,1)}, u32[]{:S(2)}) copy-start(bf16[64,512]{1,0:T(8,128)(2,1)} %get-tuple-element.38) | copy-start | bytes 196612
  25.4 25.9 %copy-start.17 = (bf16[64,512]{1,0:T(8,128)(2,1)S(1)}, bf16[64,512]{1,0:T(8,128)(2,1)}, u32[]{:S(2)}) copy-start(bf16[64,512]{1,0:T(8,128)(2,1)} %get-tuple-element.37) | copy-start | bytes 196612
  25.4 38.5 %all-to-all-start.1 = ((bf16[8,272,256]{2,1,0:T(8,128)(2,1)}), bf16[8,272,256]{2,1,0:T(8,128)(2,1)S(1)}, u32[]{:S(2)}, u32[]{:S(2)}) async-start(bf16[8,272,256]{2,1,0:T(8,128)(2,1)} %broadcast_in_dim.8), calls=%async_computation.1 | async-start | bytes 2228224 | tf_op jit(solution)/shard_map/all_to_all | solution.py:358
  33.3 104.6 %reduce-scatter.2.cloned.1.call-start = ((), (), s32[]{:S(2)}) async-start(), calls=%async_computation.5 | async-start | bytes 1253376 | tf_op jit(solution)/shard_map/reduce_scatter | solution.py:380
  33.3 7.2 %collective-permute-start = (bf16[128,512]{1,0:T(8,128)(2,1)S(1)}, bf16[128,512]{1,0:T(8,128)(2,1)S(1)}, u32[]{:S(2)}, u32[]{:S(2)}) collective-permute-start(bf16[128,512]{1,0:T(8,128)(2,1)S(1)} %copy-done.16), channel_id=1, source_target_pairs={{0,504},{8,0},{16,8},{24,16},{32,24},{40,32},{48,40},{56,48},{64,5... | collective-permute-start | bytes 393224 | tf_op jit(solution)/shard_map/ppermute | solution.py:43
  40.5 41.1 %copy-start.11 = (bf16[128,512]{1,0:T(8,128)(2,1)}, bf16[128,512]{1,0:T(8,128)(2,1)S(1)}, u32[]{:S(2)}) copy-start(bf16[128,512]{1,0:T(8,128)(2,1)S(1)} %collective-permute-done.refs_3_) | copy-start | bytes 393220
  40.6 18.1 %collective-permute-start.2 = (bf16[128,512]{1,0:T(8,128)(2,1)S(1)}, bf16[128,512]{1,0:T(8,128)(2,1)S(1)}, u32[]{:S(2)}, u32[]{:S(2)}) collective-permute-start(bf16[128,512]{1,0:T(8,128)(2,1)S(1)} %pad_maximum_fusion), channel_id=1, source_target_pairs={{0,256},{8,264},{16,272},{24,280},{32,288},{40,296},{48,304},{56,3... | collective-permute-start | bytes 393224 | tf_op jit(solution)/shard_map/ppermute | solution.py:43
  51.3 5.0 %collective-permute-start.1 = (bf16[64,512]{1,0:T(8,128)(2,1)S(1)}, bf16[64,512]{1,0:T(8,128)(2,1)S(1)}, u32[]{:S(2)}, u32[]{:S(2)}) collective-permute-start(bf16[64,512]{1,0:T(8,128)(2,1)S(1)} %copy-done.17), channel_id=1, source_target_pairs={{0,8},{8,16},{16,24},{24,32},{32,40},{40,48},{48,56},{56,64},{64,7... | collective-permute-start | bytes 196616 | tf_op jit(solution)/shard_map/ppermute | solution.py:43
  56.2 25.4 %copy-start.13 = (bf16[64,512]{1,0:T(8,128)(2,1)}, bf16[64,512]{1,0:T(8,128)(2,1)S(1)}, u32[]{:S(2)}) copy-start(bf16[64,512]{1,0:T(8,128)(2,1)S(1)} %collective-permute-done.1.refs_4_) | copy-start | bytes 196612
  58.6 23.0 %copy-start.12 = (bf16[128,512]{1,0:T(8,128)(2,1)}, bf16[128,512]{1,0:T(8,128)(2,1)S(1)}, u32[]{:S(2)}) copy-start(bf16[128,512]{1,0:T(8,128)(2,1)S(1)} %collective-permute-done.2.refs_5_) | copy-start | bytes 393220
  63.9 17.8 %copy-start.10 = (bf16[8,272,256]{2,1,0:T(8,128)(2,1)}, bf16[8,272,256]{2,1,0:T(8,128)(2,1)S(1)}, u32[]{:S(2)}) copy-start(bf16[8,272,256]{2,1,0:T(8,128)(2,1)S(1)} %all-to-all-done.1.refs_0_) | copy-start | bytes 3342340
  77.6 9.6 %collective-permute-start.3 = (bf16[2048,768]{1,0:T(8,128)(2,1)}, bf16[2048,768]{1,0:T(8,128)(2,1)}, u32[]{:S(2)}, u32[]{:S(2)}) collective-permute-start(bf16[2048,768]{1,0:T(8,128)(2,1)} %all-gather.2.cloned.1.call-done.refs_1_.refs_9_), channel_id=1, source_target_pairs={{0,8},{8,0},{16,24},{24,16},{32,40},{40,32},{48,56},{56,48},{64,72... | collective-permute-start | bytes 9437192 | tf_op jit(solution)/shard_map/ppermute | solution.py:34
  81.6 5.6 %copy-start.3 = (bf16[256,128]{1,0:T(8,128)(2,1)S(1)}, bf16[256,128]{1,0:T(8,128)(2,1)}, u32[]{:S(2)}) copy-start(bf16[256,128]{1,0:T(8,128)(2,1)} %get-tuple-element.41.refs_2_.refs_4_) | copy-start | bytes 196612
  81.7 5.6 %copy-start.7 = (f32[128,128]{1,0:T(8,128)S(1)}, f32[128,128]{1,0:T(8,128)}, u32[]{:S(2)}) copy-start(f32[128,128]{1,0:T(8,128)} %get-tuple-element.46.refs_1_) | copy-start | bytes 196612
  101.2 3.8 %collective-permute-start.8 = (bf16[32,64,128]{2,1,0:T(8,128)(2,1)S(1)}, bf16[32,64,128]{2,1,0:T(8,128)(2,1)S(1)}, u32[]{:S(2)}, u32[]{:S(2)}) collective-permute-start(bf16[32,64,128]{2,1,0:T(8,128)(2,1)S(1)} %get-tuple-element.60), channel_id=1, source_target_pairs={{0,8},{8,0},{16,24},{24,16},{32,40},{40,32},{48,56},{56,48},{64,72... | collective-permute-start | bytes 1572872 | tf_op jit(solution)/shard_map/ppermute | solution.py:34
  105.0 30.7 %copy-start.6 = (bf16[256,256]{1,0:T(8,128)(2,1)S(1)}, bf16[256,256]{1,0:T(8,128)(2,1)}, u32[]{:S(2)}) copy-start(bf16[256,256]{1,0:T(8,128)(2,1)} %get-tuple-element.33.refs_0_) | copy-start | bytes 393220
  106.0 31.1 %all-to-all-start.2 = ((bf16[32,64,128]{2,1,0:T(8,128)(2,1)}), bf16[32,64,128]{2,1,0:T(8,128)(2,1)S(1)}, u32[]{:S(2)}, u32[]{:S(2)}) async-start(bf16[32,64,128]{2,1,0:T(8,128)(2,1)} %add_convert_fusion), calls=%async_computation.3 | async-start | bytes 1048576 | tf_op jit(solution)/shard_map/all_to_all | solution.py:389
  112.2 15.6 %collective-permute-start.4 = (bf16[64,512]{1,0:T(8,128)(2,1)S(1)}, bf16[64,512]{1,0:T(8,128)(2,1)S(1)}, u32[]{:S(2)}, u32[]{:S(2)}) collective-permute-start(bf16[64,512]{1,0:T(8,128)(2,1)S(1)} %get-tuple-element.52), channel_id=1, source_target_pairs={{0,504},{8,0},{16,8},{24,16},{32,24},{40,32},{48,40},{56,48},{64,5... | collective-permute-start | bytes 196616 | tf_op jit(solution)/shard_map/ppermute | solution.py:43
  114.8 13.0 %collective-permute-start.5 = (bf16[64,512]{1,0:T(8,128)(2,1)S(1)}, bf16[64,512]{1,0:T(8,128)(2,1)S(1)}, u32[]{:S(2)}, u32[]{:S(2)}) collective-permute-start(bf16[64,512]{1,0:T(8,128)(2,1)S(1)} %get-tuple-element.53), channel_id=1, source_target_pairs={{0,8},{8,16},{16,24},{24,32},{32,40},{40,48},{48,56},{56,64},{64,7... | collective-permute-start | bytes 196616 | tf_op jit(solution)/shard_map/ppermute | solution.py:43
  118.1 13.3 %collective-permute-start.6 = (bf16[64,512]{1,0:T(8,128)(2,1)S(1)}, bf16[64,512]{1,0:T(8,128)(2,1)S(1)}, u32[]{:S(2)}, u32[]{:S(2)}) collective-permute-start(bf16[64,512]{1,0:T(8,128)(2,1)S(1)} %get-tuple-element.54), channel_id=1, source_target_pairs={{0,256},{8,264},{16,272},{24,280},{32,288},{40,296},{48,304},{56,3... | collective-permute-start | bytes 196616 | tf_op jit(solution)/shard_map/ppermute | solution.py:43
  125.2 10.5 %collective-permute-start.7 = (bf16[64,512]{1,0:T(8,128)(2,1)S(1)}, bf16[64,512]{1,0:T(8,128)(2,1)S(1)}, u32[]{:S(2)}, u32[]{:S(2)}) collective-permute-start(bf16[64,512]{1,0:T(8,128)(2,1)S(1)} %get-tuple-element.55), channel_id=1, source_target_pairs={{0,264},{8,272},{16,280},{24,288},{32,296},{40,304},{48,312},{56,3... | collective-permute-start | bytes 196616 | tf_op jit(solution)/shard_map/ppermute | solution.py:43
  (7 other events, 16.3 us)
Sparse Core Ops, SparseCore 0:
  19.3 58.2 all-gather.1
  99.4 34.5 reduce-scatter.1

commit v10 on v8

--- a/solution.py
+++ b/solution.py
@@ -259,7 +259,7 @@
     put(0)[...] = dot_tn(get(0)[...], rows).astype(BF)
 
 
-def kernel_call(body, outs, args, name, mib, scalars=0, scratch=(), cut_out=None):
+def kernel_call(body, outs, args, name, mib, scalars=0, scratch=(), cut_out=None, late=None):
     shapes = [jax.ShapeDtypeStruct(s, d) for s, d in outs]
     arrays = args[scalars:]
     n_in, n_out = len(arrays), len(shapes)
@@ -281,14 +281,21 @@
                     stores[i, j] = pltpu.make_async_copy(out_buf[i].at[j], out[i].at[j], sem)
             else:
                 stores[i, None] = pltpu.make_async_copy(out_buf[i], out[i], out_sem.at[i])
-        for load in loads:
-            load.start()
+        begin = list(range(n_in))
+        if late is not None:
+            begin.remove(late[1])
+            begin.remove(late[0])
+            begin.insert(0, late[0])
+        for i in begin:
+            loads[i].start()
         waited, sent = set(), set()
 
         def get(i):
             if i not in waited:
                 waited.add(i)
                 loads[i].wait()
+                if late is not None and i == late[0]:
+                    loads[late[1]].start()
             return in_buf[i]
 
         def send(i, j=None):
@@ -375,7 +382,7 @@
         [cut] * 4 + [((TOK_DEV, k_cols), BF), ((peers,) + block, BF)],
         [normed, cosine, sine, allowed, home, grad_out, theirs, inverse, partial, mine],
         "layer", 60, 0,
-        [pltpu.VMEM((TOK_DEV, q_cols + 2 * k_cols), BF)], 5,
+        [pltpu.VMEM((TOK_DEV, q_cols + 2 * k_cols), BF)], 5, (6, 9),
     )
     total = lax.psum_scatter(terms, "tensor", scatter_dimension=0, tiled=False)
     (grad_hidden,) = kernel_call(

time: 144 us -> 144 us (level)
  no operation moved by 1% of the time
where the time goes in v10:
time: 144 us; the launch traced here: 142 us
  starting transfers between devices  52.8 us (37%)
  waiting for transfers between devices  37.9 us (26%)
  Pallas kernels  20 us (14%)
  between operations  14.4 us (10%)
  blocking collectives  11 us (8%)
  local copies, waits for them, and re-layouts  3.83 us (3%)
  other arithmetic  2.62 us (2%)
    ppermute x7, starting transfers between devices, passed_along(): return lax.ppermute(value, DP, [(i, (i + by) % size) for i in range(size)])  32.3 us
    pallas_call x6, Pallas kernels, kernel_call(): pl.pallas_call(kernel, out_shape=shapes, in_specs=[pl.BlockSpec(memory_sp...  20 us
    ppermute x7, waiting for transfers between devices, passed_along(): return lax.ppermute(value, DP, [(i, (i + by) % size) for i in range(size)])  15.9 us
    all_gather x1, waiting for transfers between devices, on_device(): mine = lax.all_gather(own_half, 'z', axis=0, tiled=True)  13.8 us
    all_to_all x1, blocking collectives, on_device(): lax.all_to_all(jnp.broadcast_to(own[None], (NX,) + own.shape), 'x', split...  11 us
    all_to_all x1, starting transfers between devices, on_device(): lax.all_to_all(copies, 'tensor', split_axis=0, concat_axis=0, tiled=True)  7.88 us
    ppermute x2, starting transfers between devices, moved(): return lax.ppermute(value, DP, pairs)  6.26 us
    all_to_all x1, starting transfers between devices, on_device(): lax.all_to_all(pair, ('z', 'x'), split_axis=0, concat_axis=0, tiled=True)  6.24 us
  transfers between devices with their start and end apart: 13, of which 9 were waited for; matrix products, arithmetic and copies ran while one was open for 3% of the time, Pallas kernels for 7%

profile of v10, /device:TPU:1, one launch (start us, length us, event | category | flops | bytes accessed | tf_op | source)
XLA Modules:
  0.0 142.5 jit_solution(14393651437427968750)
XLA Ops:
  8.1 11.0 %all_to_all.15 = bf16[4,64,768]{2,1,0:T(8,128)(2,1)} all-to-all(bf16[4,64,768]{2,1,0:T(8,128)(2,1)S(1)} %broadcast_in_dim.6), channel_id=1, replica_groups=mesh['z'=8,'x'=4,'core'=2,'tensor'=8] {'x'}, dimensions={0} | all-to-all | bytes 786432 | tf_op jit(solution)/shard_map/all_to_all | solution.py:344
  19.7 3.6 %plan.1 = (bf16[128,512]{1,0:T(8,128)(2,1)}, bf16[64,512]{1,0:T(8,128)(2,1)}, bf16[64,512]{1,0:T(8,128)(2,1)}, bf16[256,128]{1,0:T(8,128)(2,1)}, bf16[256,256]{1...) custom-call(s32[4,64]{1,0:T(4,128)} %bitcast.8, ...), custom_call_target="tpu_custom_call" | custom-call | tf_op jit(solution)/shard_map/plan/pallas_call | solution.py:315
  23.4 2.0 %broadcast_in_dim.8 = bf16[8,272,256]{2,1,0:T(8,128)(2,1)} broadcast(bf16[272,256]{1,0:T(8,128)(2,1)} %get-tuple-element.35.refs_0_), dimensions={1,2} | broadcast | bytes 1253376 | tf_op jit(solution)/shard_map/broadcast_in_dim | solution.py:364
  25.4 7.9 %all-to-all-start.1 = ((bf16[8,272,256]{2,1,0:T(8,128)(2,1)}), bf16[8,272,256]{2,1,0:T(8,128)(2,1)S(1)}, u32[]{:S(2)}, u32[]{:S(2)}) async-start(bf16[8,272,256]{2,1,0:T(8,128)(2,1)} %broadcast_in_dim.8), calls=%async_computation.1 | async-start | bytes 2228224 | tf_op jit(solution)/shard_map/all_to_all | solution.py:365
  33.3 4.1 %collective-permute-start = (bf16[128,512]{1,0:T(8,128)(2,1)S(1)}, bf16[128,512]{1,0:T(8,128)(2,1)S(1)}, u32[]{:S(2)}, u32[]{:S(2)}) collective-permute-start(bf16[128,512]{1,0:T(8,128)(2,1)S(1)} %copy-done.9), channel_id=1, source_target_pairs={{0,504},{8,0},{16,8},{24,16},{32,24},{40,32},{48,40},{56,48},{64,5... | collective-permute-start | bytes 393224 | tf_op jit(solution)/shard_map/ppermute | solution.py:43
  37.4 3.1 %collective-permute-done.refs_3_ = bf16[128,512]{1,0:T(8,128)(2,1)S(1)} collective-permute-done((bf16[128,512]{1,0:T(8,128)(2,1)S(1)}, bf16[128,512]{1,0:T(8,128)(2,1)S(1)}, u32[]{:S(2)}, u32[]{:S(2)}) %collective-permute-start) | collective-permute-done | bytes 131104 | tf_op jit(solution)/shard_map/ppermute | solution.py:43
  40.5 10.7 %collective-permute-start.2 = (bf16[128,512]{1,0:T(8,128)(2,1)S(1)}, bf16[128,512]{1,0:T(8,128)(2,1)S(1)}, u32[]{:S(2)}, u32[]{:S(2)}) collective-permute-start(bf16[128,512]{1,0:T(8,128)(2,1)S(1)} %pad_maximum_fusion), channel_id=1, source_target_pairs={{0,256},{8,264},{16,272},{24,280},{32,288},{40,296},{48,304},{56,3... | collective-permute-start | bytes 393224 | tf_op jit(solution)/shard_map/ppermute | solution.py:43
  51.3 1.9 %collective-permute-start.1 = (bf16[64,512]{1,0:T(8,128)(2,1)S(1)}, bf16[64,512]{1,0:T(8,128)(2,1)S(1)}, u32[]{:S(2)}, u32[]{:S(2)}) collective-permute-start(bf16[64,512]{1,0:T(8,128)(2,1)S(1)} %copy-done.14), channel_id=1, source_target_pairs={{0,8},{8,16},{16,24},{24,32},{32,40},{40,48},{48,56},{56,64},{64,7... | collective-permute-start | bytes 196616 | tf_op jit(solution)/shard_map/ppermute | solution.py:43
  53.2 3.0 %collective-permute-done.1.refs_4_ = bf16[64,512]{1,0:T(8,128)(2,1)S(1)} collective-permute-done((bf16[64,512]{1,0:T(8,128)(2,1)S(1)}, bf16[64,512]{1,0:T(8,128)(2,1)S(1)}, u32[]{:S(2)}, u32[]{:S(2)}) %collective-permute-start.1) | collective-permute-done | bytes 65568 | tf_op jit(solution)/shard_map/ppermute | solution.py:43
  56.2 2.1 %collective-permute-done.2.refs_5_ = bf16[128,512]{1,0:T(8,128)(2,1)S(1)} collective-permute-done((bf16[128,512]{1,0:T(8,128)(2,1)S(1)}, bf16[128,512]{1,0:T(8,128)(2,1)S(1)}, u32[]{:S(2)}, u32[]{:S(2)}) %collective-permute-start.2) | collective-permute-done | bytes 131104 | tf_op jit(solution)/shard_map/ppermute | solution.py:43
  58.3 5.5 %all-to-all-done.1.refs_0_ = bf16[8,272,256]{2,1,0:T(8,128)(2,1)S(1)} async-done(((bf16[8,272,256]{2,1,0:T(8,128)(2,1)}), bf16[8,272,256]{2,1,0:T(8,128)(2,1)S(1)}, u32[]{:S(2)}, u32[]{:S(2)}) %all-to-all-start.1) | async-done | bytes 1114144 | tf_op jit(solution)/shard_map/all_to_all | solution.py:365
  63.8 13.8 %all-gather.2.cloned.1.call-done.refs_1_.refs_9_ = bf16[2048,768]{1,0:T(8,128)(2,1)} async-done(((bf16[256,768]{1,0:T(8,128)(2,1)}), bf16[2048,768]{1,0:T(8,128)(2,1)}) %all-gather.2.cloned.1.call-update) | async-done | bytes 3145744 | tf_op jit(solution)/shard_map/all_gather | solution.py:348
  77.6 4.0 %collective-permute-start.3 = (bf16[2048,768]{1,0:T(8,128)(2,1)}, bf16[2048,768]{1,0:T(8,128)(2,1)}, u32[]{:S(2)}, u32[]{:S(2)}) collective-permute-start(bf16[2048,768]{1,0:T(8,128)(2,1)} %all-gather.2.cloned.1.call-done.refs_1_.refs_9_), channel_id=1, source_target_pairs={{0,8},{8,0},{16,24},{24,16},{32,40},{40,32},{48,56},{56,48},{64,72... | collective-permute-start | bytes 9437192 | tf_op jit(solution)/shard_map/ppermute | solution.py:34
  81.6 4.4 %norm.1 = (bf16[2,128,2048]{2,1,0:T(8,128)(2,1)}, f32[128,128]{1,0:T(8,128)}, f32[128,768]{1,0:T(8,128)}, bf16[512,128]{1,0:T(8,128)(2,1)}) custom-call(bf16[8,272,256]{2,1,0:T(8,128)(2,1)} %copy-done.3, bf16[2048,768]{1,0:T(8,128)(2,1)} %all-gather.2.cloned.1.call-done.refs_1_.refs_9_, bf16[256,128]{1,0:T(8,128)(2,1)} %get-tuple-element.41.refs_2_.refs_4_, ...), custom_call_target="tpu_custom_call" | custom-call | tf_op jit(solution)/shard_map/norm/pallas_call | solution.py:315
  87.2 7.5 %layer.1 = (bf16[64,512]{1,0:T(8,128)(2,1)}, bf16[64,512]{1,0:T(8,128)(2,1)}, bf16[64,512]{1,0:T(8,128)(2,1)}, bf16[64,512]{1,0:T(8,128)(2,1)}, bf16[128,128]{1,0:T(8,128)(2,1)}, /*index=5*/bf16[8,272,256]{2,1,0:T(8,128)(2,1)}) custom-call(bf16[2,128,2048]{2,1,0:T(8,128)(2,1)} %get-tuple-element.45.refs_0_, f32[128,128]{1,0:T(8,128)} %get-tuple-element.46.refs_1_, ...), custom_call_target="tpu_custom_call" | custom-call | tf_op jit(solution)/shard_map/layer/pallas_call | solution.py:315
  96.7 2.3 %collective-permute-start.8 = (bf16[32,64,128]{2,1,0:T(8,128)(2,1)S(1)}, bf16[32,64,128]{2,1,0:T(8,128)(2,1)S(1)}, u32[]{:S(2)}, u32[]{:S(2)}) collective-permute-start(bf16[32,64,128]{2,1,0:T(8,128)(2,1)S(1)} %get-tuple-element.60), channel_id=1, source_target_pairs={{0,8},{8,0},{16,24},{24,16},{32,40},{40,32},{48,56},{56,48},{64,72... | collective-permute-start | bytes 1572872 | tf_op jit(solution)/shard_map/ppermute | solution.py:34
  101.5 6.2 %all-to-all-start.2 = ((bf16[32,64,128]{2,1,0:T(8,128)(2,1)}), bf16[32,64,128]{2,1,0:T(8,128)(2,1)S(1)}, u32[]{:S(2)}, u32[]{:S(2)}) async-start(bf16[32,64,128]{2,1,0:T(8,128)(2,1)} %add_convert_fusion), calls=%async_computation.3 | async-start | bytes 1048576 | tf_op jit(solution)/shard_map/all_to_all | solution.py:396
  107.8 2.6 %collective-permute-start.4 = (bf16[64,512]{1,0:T(8,128)(2,1)S(1)}, bf16[64,512]{1,0:T(8,128)(2,1)S(1)}, u32[]{:S(2)}, u32[]{:S(2)}) collective-permute-start(bf16[64,512]{1,0:T(8,128)(2,1)S(1)} %copy-done.13), channel_id=1, source_target_pairs={{0,504},{8,0},{16,8},{24,16},{32,24},{40,32},{48,40},{56,48},{64,5... | collective-permute-start | bytes 196616 | tf_op jit(solution)/shard_map/ppermute | solution.py:43
  110.4 3.3 %collective-permute-start.5 = (bf16[64,512]{1,0:T(8,128)(2,1)S(1)}, bf16[64,512]{1,0:T(8,128)(2,1)S(1)}, u32[]{:S(2)}, u32[]{:S(2)}) collective-permute-start(bf16[64,512]{1,0:T(8,128)(2,1)S(1)} %copy-done.12), channel_id=1, source_target_pairs={{0,8},{8,16},{16,24},{24,32},{32,40},{40,48},{48,56},{56,64},{64,7... | collective-permute-start | bytes 196616 | tf_op jit(solution)/shard_map/ppermute | solution.py:43
  113.7 7.0 %collective-permute-start.6 = (bf16[64,512]{1,0:T(8,128)(2,1)S(1)}, bf16[64,512]{1,0:T(8,128)(2,1)S(1)}, u32[]{:S(2)}, u32[]{:S(2)}) collective-permute-start(bf16[64,512]{1,0:T(8,128)(2,1)S(1)} %copy-done.11), channel_id=1, source_target_pairs={{0,256},{8,264},{16,272},{24,280},{32,288},{40,296},{48,304},{56,3... | collective-permute-start | bytes 196616 | tf_op jit(solution)/shard_map/ppermute | solution.py:43
  120.7 2.7 %collective-permute-start.7 = (bf16[64,512]{1,0:T(8,128)(2,1)S(1)}, bf16[64,512]{1,0:T(8,128)(2,1)S(1)}, u32[]{:S(2)}, u32[]{:S(2)}) collective-permute-start(bf16[64,512]{1,0:T(8,128)(2,1)S(1)} %copy-done.10), channel_id=1, source_target_pairs={{0,264},{8,272},{16,280},{24,288},{32,296},{40,304},{48,312},{56,3... | collective-permute-start | bytes 196616 | tf_op jit(solution)/shard_map/ppermute | solution.py:43
  123.4 3.6 %collective-permute-done.6.refs_3_ = bf16[64,512]{1,0:T(8,128)(2,1)S(1)} collective-permute-done((bf16[64,512]{1,0:T(8,128)(2,1)S(1)}, bf16[64,512]{1,0:T(8,128)(2,1)S(1)}, u32[]{:S(2)}, u32[]{:S(2)}) %collective-permute-start.6) | collective-permute-done | bytes 65568 | tf_op jit(solution)/shard_map/ppermute | solution.py:43
  127.0 4.2 %collective-permute-done.7.refs_4_ = bf16[64,512]{1,0:T(8,128)(2,1)S(1)} collective-permute-done((bf16[64,512]{1,0:T(8,128)(2,1)S(1)}, bf16[64,512]{1,0:T(8,128)(2,1)S(1)}, u32[]{:S(2)}, u32[]{:S(2)}) %collective-permute-start.7) | collective-permute-done | bytes 65568 | tf_op jit(solution)/shard_map/ppermute | solution.py:43
  133.4 2.2 %finish.1 = bf16[128,512]{1,0:T(8,128)(2,1)} custom-call(bf16[272,256]{1,0:T(8,128)(2,1)} %get-tuple-element.35.refs_0_, f32[128,128]{1,0:T(8,128)} %get-tuple-element.50.refs_7_.refs_1_, bf16[272,256]{1,0:T(8,128)(2,1)} %bitcast.7, bf16[512,512]{1,0:T(8,128)(2,1)} %get-tuple-element.57.refs_3_), custom_call_target="tpu_custom_call" | custom-call | tf_op jit(solution)/shard_map/finish/pallas_call | solution.py:315
  (49 shorter events, 9.5 us)
Async XLA Ops:
  7.2 12.0 %copy-start.8 = (bf16[512]{0:T(512)(128)(2,1)S(1)}, bf16[512]{0:T(512)(128)(2,1)}, u32[]{:S(2)}) copy-start(bf16[512]{0:T(512)(128)(2,1)} %param.12) | copy-start | bytes 3076
  7.2 70.4 %all-gather.2.cloned.1.call-start = ((), (), s32[]{:S(2)}) async-start(), calls=%async_computation.4 | async-start | bytes 3538944 | tf_op jit(solution)/shard_map/all_gather | solution.py:348
  25.3 15.2 %copy-start.7 = (bf16[64,512]{1,0:T(8,128)(2,1)S(1)}, bf16[64,512]{1,0:T(8,128)(2,1)}, u32[]{:S(2)}) copy-start(bf16[64,512]{1,0:T(8,128)(2,1)} %get-tuple-element.38) | copy-start | bytes 196612
  25.4 25.9 %copy-start.14 = (bf16[64,512]{1,0:T(8,128)(2,1)S(1)}, bf16[64,512]{1,0:T(8,128)(2,1)}, u32[]{:S(2)}) copy-start(bf16[64,512]{1,0:T(8,128)(2,1)} %get-tuple-element.37) | copy-start | bytes 196612
  25.4 38.5 %all-to-all-start.1 = ((bf16[8,272,256]{2,1,0:T(8,128)(2,1)}), bf16[8,272,256]{2,1,0:T(8,128)(2,1)S(1)}, u32[]{:S(2)}, u32[]{:S(2)}) async-start(bf16[8,272,256]{2,1,0:T(8,128)(2,1)} %broadcast_in_dim.8), calls=%async_computation.1 | async-start | bytes 2228224 | tf_op jit(solution)/shard_map/all_to_all | solution.py:365
  33.2 100.1 %reduce-scatter.2.cloned.1.call-start = ((), (), s32[]{:S(2)}) async-start(), calls=%async_computation.5 | async-start | bytes 1253376 | tf_op jit(solution)/shard_map/reduce_scatter | solution.py:387
  33.3 7.2 %collective-permute-start = (bf16[128,512]{1,0:T(8,128)(2,1)S(1)}, bf16[128,512]{1,0:T(8,128)(2,1)S(1)}, u32[]{:S(2)}, u32[]{:S(2)}) collective-permute-start(bf16[128,512]{1,0:T(8,128)(2,1)S(1)} %copy-done.9), channel_id=1, source_target_pairs={{0,504},{8,0},{16,8},{24,16},{32,24},{40,32},{48,40},{56,48},{64,5... | collective-permute-start | bytes 393224 | tf_op jit(solution)/shard_map/ppermute | solution.py:43
  40.5 41.1 %copy-start.4 = (bf16[128,512]{1,0:T(8,128)(2,1)}, bf16[128,512]{1,0:T(8,128)(2,1)S(1)}, u32[]{:S(2)}) copy-start(bf16[128,512]{1,0:T(8,128)(2,1)S(1)} %collective-permute-done.refs_3_) | copy-start | bytes 393220
  40.5 17.7 %collective-permute-start.2 = (bf16[128,512]{1,0:T(8,128)(2,1)S(1)}, bf16[128,512]{1,0:T(8,128)(2,1)S(1)}, u32[]{:S(2)}, u32[]{:S(2)}) collective-permute-start(bf16[128,512]{1,0:T(8,128)(2,1)S(1)} %pad_maximum_fusion), channel_id=1, source_target_pairs={{0,256},{8,264},{16,272},{24,280},{32,288},{40,296},{48,304},{56,3... | collective-permute-start | bytes 393224 | tf_op jit(solution)/shard_map/ppermute | solution.py:43
  51.3 5.0 %collective-permute-start.1 = (bf16[64,512]{1,0:T(8,128)(2,1)S(1)}, bf16[64,512]{1,0:T(8,128)(2,1)S(1)}, u32[]{:S(2)}, u32[]{:S(2)}) collective-permute-start(bf16[64,512]{1,0:T(8,128)(2,1)S(1)} %copy-done.14), channel_id=1, source_target_pairs={{0,8},{8,16},{16,24},{24,32},{32,40},{40,48},{48,56},{56,64},{64,7... | collective-permute-start | bytes 196616 | tf_op jit(solution)/shard_map/ppermute | solution.py:43
  56.2 25.4 %copy-start.6 = (bf16[64,512]{1,0:T(8,128)(2,1)}, bf16[64,512]{1,0:T(8,128)(2,1)S(1)}, u32[]{:S(2)}) copy-start(bf16[64,512]{1,0:T(8,128)(2,1)S(1)} %collective-permute-done.1.refs_4_) | copy-start | bytes 196612
  58.3 23.3 %copy-start.5 = (bf16[128,512]{1,0:T(8,128)(2,1)}, bf16[128,512]{1,0:T(8,128)(2,1)S(1)}, u32[]{:S(2)}) copy-start(bf16[128,512]{1,0:T(8,128)(2,1)S(1)} %collective-permute-done.2.refs_5_) | copy-start | bytes 393220
  63.8 17.8 %copy-start.3 = (bf16[8,272,256]{2,1,0:T(8,128)(2,1)}, bf16[8,272,256]{2,1,0:T(8,128)(2,1)S(1)}, u32[]{:S(2)}) copy-start(bf16[8,272,256]{2,1,0:T(8,128)(2,1)S(1)} %all-to-all-done.1.refs_0_) | copy-start | bytes 3342340
  77.6 9.6 %collective-permute-start.3 = (bf16[2048,768]{1,0:T(8,128)(2,1)}, bf16[2048,768]{1,0:T(8,128)(2,1)}, u32[]{:S(2)}, u32[]{:S(2)}) collective-permute-start(bf16[2048,768]{1,0:T(8,128)(2,1)} %all-gather.2.cloned.1.call-done.refs_1_.refs_9_), channel_id=1, source_target_pairs={{0,8},{8,0},{16,24},{24,16},{32,40},{40,32},{48,56},{56,48},{64,72... | collective-permute-start | bytes 9437192 | tf_op jit(solution)/shard_map/ppermute | solution.py:34
  96.7 3.8 %collective-permute-start.8 = (bf16[32,64,128]{2,1,0:T(8,128)(2,1)S(1)}, bf16[32,64,128]{2,1,0:T(8,128)(2,1)S(1)}, u32[]{:S(2)}, u32[]{:S(2)}) collective-permute-start(bf16[32,64,128]{2,1,0:T(8,128)(2,1)S(1)} %get-tuple-element.60), channel_id=1, source_target_pairs={{0,8},{8,0},{16,24},{24,16},{32,40},{40,32},{48,56},{56,48},{64,72... | collective-permute-start | bytes 1572872 | tf_op jit(solution)/shard_map/ppermute | solution.py:34
  100.5 9.9 %copy-start.12 = (bf16[64,512]{1,0:T(8,128)(2,1)S(1)}, bf16[64,512]{1,0:T(8,128)(2,1)}, u32[]{:S(2)}) copy-start(bf16[64,512]{1,0:T(8,128)(2,1)} %get-tuple-element.53) | copy-start | bytes 196612
  100.5 13.2 %copy-start.11 = (bf16[64,512]{1,0:T(8,128)(2,1)S(1)}, bf16[64,512]{1,0:T(8,128)(2,1)}, u32[]{:S(2)}) copy-start(bf16[64,512]{1,0:T(8,128)(2,1)} %get-tuple-element.54) | copy-start | bytes 196612
  100.5 20.2 %copy-start.10 = (bf16[64,512]{1,0:T(8,128)(2,1)S(1)}, bf16[64,512]{1,0:T(8,128)(2,1)}, u32[]{:S(2)}) copy-start(bf16[64,512]{1,0:T(8,128)(2,1)} %get-tuple-element.55) | copy-start | bytes 196612
  100.5 30.7 %copy-start.1 = (bf16[256,256]{1,0:T(8,128)(2,1)S(1)}, bf16[256,256]{1,0:T(8,128)(2,1)}, u32[]{:S(2)}) copy-start(bf16[256,256]{1,0:T(8,128)(2,1)} %get-tuple-element.33.refs_0_) | copy-start | bytes 393220
  101.5 31.2 %all-to-all-start.2 = ((bf16[32,64,128]{2,1,0:T(8,128)(2,1)}), bf16[32,64,128]{2,1,0:T(8,128)(2,1)S(1)}, u32[]{:S(2)}, u32[]{:S(2)}) async-start(bf16[32,64,128]{2,1,0:T(8,128)(2,1)} %add_convert_fusion), calls=%async_computation.3 | async-start | bytes 1048576 | tf_op jit(solution)/shard_map/all_to_all | solution.py:396
  107.8 15.6 %collective-permute-start.4 = (bf16[64,512]{1,0:T(8,128)(2,1)S(1)}, bf16[64,512]{1,0:T(8,128)(2,1)S(1)}, u32[]{:S(2)}, u32[]{:S(2)}) collective-permute-start(bf16[64,512]{1,0:T(8,128)(2,1)S(1)} %copy-done.13), channel_id=1, source_target_pairs={{0,504},{8,0},{16,8},{24,16},{32,24},{40,32},{48,40},{56,48},{64,5... | collective-permute-start | bytes 196616 | tf_op jit(solution)/shard_map/ppermute | solution.py:43
  110.4 13.1 %collective-permute-start.5 = (bf16[64,512]{1,0:T(8,128)(2,1)S(1)}, bf16[64,512]{1,0:T(8,128)(2,1)S(1)}, u32[]{:S(2)}, u32[]{:S(2)}) collective-permute-start(bf16[64,512]{1,0:T(8,128)(2,1)S(1)} %copy-done.12), channel_id=1, source_target_pairs={{0,8},{8,16},{16,24},{24,32},{32,40},{40,48},{48,56},{56,64},{64,7... | collective-permute-start | bytes 196616 | tf_op jit(solution)/shard_map/ppermute | solution.py:43
  113.7 13.3 %collective-permute-start.6 = (bf16[64,512]{1,0:T(8,128)(2,1)S(1)}, bf16[64,512]{1,0:T(8,128)(2,1)S(1)}, u32[]{:S(2)}, u32[]{:S(2)}) collective-permute-start(bf16[64,512]{1,0:T(8,128)(2,1)S(1)} %copy-done.11), channel_id=1, source_target_pairs={{0,256},{8,264},{16,272},{24,280},{32,288},{40,296},{48,304},{56,3... | collective-permute-start | bytes 196616 | tf_op jit(solution)/shard_map/ppermute | solution.py:43
  120.7 10.4 %collective-permute-start.7 = (bf16[64,512]{1,0:T(8,128)(2,1)S(1)}, bf16[64,512]{1,0:T(8,128)(2,1)S(1)}, u32[]{:S(2)}, u32[]{:S(2)}) collective-permute-start(bf16[64,512]{1,0:T(8,128)(2,1)S(1)} %copy-done.10), channel_id=1, source_target_pairs={{0,264},{8,272},{16,280},{24,288},{32,296},{40,304},{48,312},{56,3... | collective-permute-start | bytes 196616 | tf_op jit(solution)/shard_map/ppermute | solution.py:43
  (4 other events, 17.7 us)
Sparse Core Ops, SparseCore 0:
  19.3 58.2 all-gather.1
  94.9 34.6 reduce-scatter.1
